TPU v7x, 32 devices: a whole 2x2x4 slice. The times are simulated.
32 devices in a mesh: groups: 2 (over y), face: 4 (over z), band: 2 (over x), sub: 2 (over core).
Axes of the slice: x: 2, y: 2, z: 4, core: 2. Of those that a mesh axis runs over, the one named last changes fastest.
Arguments:
- grid_lat: bfloat16 [32768, 512], P(('groups', 'face', 'band', 'sub')), parts along dimension 0, may hold values from -6 to 6
- grid_route: int32 [32768, 1], P(('groups', 'face', 'band', 'sub')), parts along dimension 0, may hold values from 0 to 3; in each aligned block of 1024 rows (0 to 1023, 1024 to 2047, ...) at most 384 rows name the same one
- grid_slot: int32 [32768], P(('groups', 'face', 'band', 'sub')), parts along dimension 0, may hold values from 0 to 127
- mesh_lat: bfloat16 [4096, 512], P(('groups', 'face', 'band', 'sub')), parts along dimension 0, may hold values from -6 to 6
- mesh_nbr: int32 [4096, 6], P(('groups', 'face', 'band', 'sub')), parts along dimension 0, may hold values from 0 to 255
- enc_w1: bfloat16 [512, 512], P(('band', 'sub')), may hold values from -0.25 to 0.25
- enc_w2: bfloat16 [512, 512], P(('band', 'sub')), may hold values from -0.25 to 0.25
- grid_w1: bfloat16 [512, 512], P(('band', 'sub')), may hold values from -0.25 to 0.25
- grid_w2: bfloat16 [512, 512], P(('band', 'sub')), may hold values from -0.25 to 0.25
- node_w1: bfloat16 [1024, 512], P(('band', 'sub')), may hold values from -0.1875 to 0.1875
- node_w2: bfloat16 [512, 512], P(('band', 'sub')), may hold values from -0.25 to 0.25
- proc_w1: bfloat16 [1024, 512], P(('band', 'sub')), may hold values from -0.1875 to 0.1875
- proc_w2: bfloat16 [512, 512], P(('band', 'sub')), may hold values from -0.25 to 0.25
- upd_w1: bfloat16 [1024, 512], P(('band', 'sub')), may hold values from -0.1875 to 0.1875
- upd_w2: bfloat16 [512, 512], P(('band', 'sub')), may hold values from -0.25 to 0.25
Outputs:
- grid_out: bfloat16 [32768, 512], P(('groups', 'face', 'band', 'sub')), parts along dimension 0
- mesh_out: bfloat16 [4096, 512], P(('groups', 'face', 'band', 'sub')), parts along dimension 0
There are 2 independent parts, one for each index of `groups`. A program takes and returns all parts, laid end to end along the dimension named above; an argument that names none is the same for every part. Nothing has to cross between parts.
Inputs may be any that keep to these rules, and one draw needn't show every extreme that they name: `grid_route`: among the rows of one device no face index is named more than 384 times, and some face index is named exactly 384 times.
All inputs are finite; a program needn't handle non-finite values.
Results may differ from a plain program's by a relative error of at most 0.009.
Values may be sent and summed in bfloat16 or wider, within the bound.
No kernel may reach another device: no remote copies, remote signals or barrier semaphores. Data moves between devices by JAX's collectives and lax.ppermute only.
A program may use at most 64 MiB of HBM per device.

v0:
```python
import jax
import jax.numpy as jnp
from jax import lax
from jax.sharding import PartitionSpec as P


def extended_2(cells, sides, width):
    for axis, dim in sides:
        count = lax.axis_size(axis)
        head = lax.slice_in_dim(cells, 0, width, axis=dim)
        tail = lax.slice_in_dim(cells, cells.shape[dim] - width, cells.shape[dim], axis=dim)
        cells = jnp.concatenate(
            [
                lax.ppermute(tail, axis, [(i, (i + 1) % count) for i in range(count)]),
                cells,
                lax.ppermute(head, axis, [((i + 1) % count, i) for i in range(count)]),
            ],
            axis=dim,
        )
    return cells


def layer_norm(values):
    average = jnp.mean(values, axis=-1, keepdims=True)
    centred = values - average
    spread = jnp.mean(centred * centred, axis=-1, keepdims=True)
    return centred * lax.rsqrt(spread + 1e-05)


def perceptron(inputs, weight_in, weight_out):
    hidden = jax.nn.silu(jnp.dot(inputs, weight_in, preferred_element_type=jnp.float32)).astype(
        jnp.bfloat16
    )
    return layer_norm(jnp.dot(hidden, weight_out, preferred_element_type=jnp.float32))


def shards(
    grid_lat,
    grid_route,
    grid_slot,
    mesh_lat,
    mesh_nbr,
    enc_w1,
    enc_w2,
    grid_w1,
    grid_w2,
    node_w1,
    node_w2,
    proc_w1,
    proc_w2,
    upd_w1,
    upd_w2,
):
    grid_rows = grid_lat.shape[0]
    width = grid_lat.shape[1]
    mesh_rows = mesh_lat.shape[0]
    gathered = (
        lax.all_gather(enc_w1, ("band", "sub"), axis=0, tiled=True),
        lax.all_gather(enc_w2, ("band", "sub"), axis=0, tiled=True),
        lax.all_gather(grid_w1, ("band", "sub"), axis=0, tiled=True),
        lax.all_gather(grid_w2, ("band", "sub"), axis=0, tiled=True),
        lax.all_gather(node_w1, ("band", "sub"), axis=0, tiled=True),
        lax.all_gather(node_w2, ("band", "sub"), axis=0, tiled=True),
        lax.all_gather(proc_w1, ("band", "sub"), axis=0, tiled=True),
        lax.all_gather(proc_w2, ("band", "sub"), axis=0, tiled=True),
        lax.all_gather(upd_w1, ("band", "sub"), axis=0, tiled=True),
        lax.all_gather(upd_w2, ("band", "sub"), axis=0, tiled=True),
    )
    enc_in, enc_hid, grid_in, grid_hid = gathered[:4]
    late_set = gathered[4:]
    peers = lax.axis_size("face")
    capacity = 3 * grid_rows // (2 * peers)
    routes = grid_route[:, 0]
    marks = (routes[:, None] == jnp.arange(peers, dtype=jnp.int32)[None, :]).astype(jnp.int32)
    position = jnp.sum((jnp.cumsum(marks, axis=0) - marks) * marks, axis=1)
    places = routes * capacity + position
    slot_codes = (
        jnp.full((peers * capacity,), float(mesh_rows), jnp.bfloat16)
        .at[places]
        .set(grid_slot.astype(jnp.bfloat16))
        .reshape(peers, capacity)
    )
    messages = perceptron(grid_lat, enc_in, enc_hid).astype(jnp.bfloat16)
    outgoing = (
        jnp.zeros((peers * capacity, width), jnp.bfloat16)
        .at[places]
        .set(messages)
        .reshape(peers, capacity, width)
    )
    arrived, arrived_codes = (
        lax.all_to_all(outgoing, "face", split_axis=0, concat_axis=0, tiled=True),
        lax.all_to_all(slot_codes, "face", split_axis=0, concat_axis=0, tiled=True),
    )
    arrived_msgs = arrived.reshape(-1, width)
    grid_out = (grid_lat.astype(jnp.float32) + perceptron(grid_lat, grid_in, grid_hid)).astype(
        jnp.bfloat16
    )
    node_in, node_hid, proc_in, proc_hid, upd_in, upd_hid = late_set
    selector = (
        jnp.arange(mesh_rows, dtype=jnp.float32)[:, None]
        == arrived_codes.reshape(1, -1).astype(jnp.float32)
    ).astype(jnp.bfloat16)
    collected = jnp.dot(selector, arrived_msgs, preferred_element_type=jnp.float32)
    mesh_in = jnp.concatenate([mesh_lat, collected.astype(jnp.bfloat16)], axis=1)
    mesh_mid = (mesh_lat.astype(jnp.float32) + perceptron(mesh_in, node_in, node_hid)).astype(
        jnp.bfloat16
    )
    halo_rows = mesh_rows // 2
    extended = extended_2(mesh_mid, (("face", 0),), halo_rows)
    fanin = mesh_nbr.shape[1]
    senders = extended[mesh_nbr.reshape(-1)]
    receivers = jnp.repeat(mesh_mid, fanin, axis=0)
    edges = perceptron(jnp.concatenate([senders, receivers], axis=1), proc_in, proc_hid)
    edge_sum = jnp.sum(edges.reshape(mesh_rows, fanin, width), axis=1).astype(jnp.bfloat16)
    joined = jnp.concatenate([mesh_mid, edge_sum], axis=1)
    mesh_out = (mesh_mid.astype(jnp.float32) + perceptron(joined, upd_in, upd_hid)).astype(
        jnp.bfloat16
    )
    return (grid_out, mesh_out)


def solution(mesh):
    placed = (
        P(("groups", "face", "band", "sub"), None),
        P(("groups", "face", "band", "sub"), None),
        P(("groups", "face", "band", "sub")),
        P(("groups", "face", "band", "sub"), None),
        P(("groups", "face", "band", "sub"), None),
        P(("band", "sub"), None),
        P(("band", "sub"), None),
        P(("band", "sub"), None),
        P(("band", "sub"), None),
        P(("band", "sub"), None),
        P(("band", "sub"), None),
        P(("band", "sub"), None),
        P(("band", "sub"), None),
        P(("band", "sub"), None),
        P(("band", "sub"), None),
    )
    return jax.shard_map(
        shards,
        mesh=mesh,
        in_specs=placed,
        out_specs=(
            P(("groups", "face", "band", "sub"), None),
            P(("groups", "face", "band", "sub"), None),
        ),
        check_vma=False,
    )
```

profile of v0, /device:TPU:0, one launch (start us, length us, event | category | flops | bytes accessed | tf_op | source)
XLA Modules:
  0.0 142.4 jit_solution(163914780049874758)
XLA Ops:
  13.1 7.6 %scatter_custom_fusion = bf16[1536]{0:T(1024)(128)(2,1)S(1)} fusion(s32[1024]{0:T(1024)S(1)} %bitcast.42, bf16[1024]{0:T(1024)(128)(2,1)S(1)} %convert_element_type.70, bf16[]{:T(256)} %constant.41.clone.1), kind=kCustom, calls=%fused_computation.62 | custom fusion | bytes 3074 | tf_op jit(solution)/shard_map/scatter | solution.py:80
  22.5 6.3 %all-to-all-start = ((bf16[4,2,192]{2,1,0:T(2,128)(2,1)}), bf16[4,2,192]{2,1,0:T(2,128)(2,1)S(1)}, u32[]{:S(2)}, u32[]{:S(2)}) async-start(bf16[4,2,192]{2,1,0:T(2,128)(2,1)} %reshape.177), calls=%async_computation | async-start | bytes 8192 | tf_op jit(solution)/shard_map/all_to_all | solution.py:92
  29.6 8.5 %all_gather.32 = bf16[512,512]{1,0:T(8,128)(2,1)} all-gather(bf16[128,512]{1,0:T(8,128)(2,1)} %param.20), channel_id=1, replica_groups=mesh['groups'=2,'face'=4,'band'=2,'sub'=2] {'band','sub'}, dimensions={0}, use_global_device_ids=true | all-gather | bytes 655360 | tf_op jit(solution)/shard_map/all_gather | solution.py:58
  38.0 11.3 %all_gather.33 = bf16[512,512]{1,0:T(8,128)(2,1)} all-gather(bf16[128,512]{1,0:T(8,128)(2,1)} %param.21), channel_id=1, replica_groups=mesh['groups'=2,'face'=4,'band'=2,'sub'=2] {'band','sub'}, dimensions={0}, use_global_device_ids=true | all-gather | bytes 655360 | tf_op jit(solution)/shard_map/all_gather | solution.py:59
  49.3 2.7 %fusion.55 = (f32[1024]{0:T(1024)S(1)}, f32[1024,512]{0,1:T(8,128)S(1)}) fusion(bf16[512,512]{1,0:T(8,128)(2,1)} %all_gather.33, bf16[1024,512]{1,0:T(8,128)(2,1)S(1)} %copy-done.1, bf16[512,512]{1,0:T(8,128)(2,1)} %all_gather.32), kind=kOutput, calls=%fused_computation.80 | convolution fusion | flops 1076886528 | bytes 4198400 | tf_op jit(solution)/shard_map/dot_general | solution.py:34
  53.3 7.7 %all_gather.35 = bf16[512,512]{1,0:T(8,128)(2,1)} all-gather(bf16[128,512]{1,0:T(8,128)(2,1)S(1)} %copy-done.4), channel_id=1, replica_groups=mesh['groups'=2,'face'=4,'band'=2,'sub'=2] {'band','sub'}, dimensions={0}, use_global_device_ids=true | all-gather | bytes 655360 | tf_op jit(solution)/shard_map/all_gather | solution.py:63
  61.3 2.3 %copy.23 = bf16[1024,512]{0,1:T(8,128)(2,1)} copy(bf16[1024,512]{1,0:T(8,128)(2,1)} %param.15) | data formatting | bytes 2097152 | tf_op args[0]
  64.1 6.4 %scatter_custom_fusion.1 = bf16[1536,512]{1,0:T(8,128)(2,1)} fusion(s32[1024]{0:T(1024)S(1)} %bitcast.43, bf16[1024,512]{1,0:T(8,128)(2,1)S(1)} %copy.25, bf16[]{:T(256)} %constant.45.clone.1), kind=kCustom, calls=%fused_computation.21 | custom fusion | bytes 1572866 | tf_op jit(solution)/shard_map/scatter | solution.py:87
  70.5 5.0 %all-to-all-start.1 = ((bf16[4,384,512]{2,1,0:T(8,128)(2,1)}), bf16[4,384,512]{2,1,0:T(8,128)(2,1)}, u32[]{:S(2)}, u32[]{:S(2)}) async-start(bf16[4,384,512]{2,1,0:T(8,128)(2,1)} %bitcast.5), calls=%async_computation.1 | async-start | bytes 3145728 | tf_op jit(solution)/shard_map/all_to_all | solution.py:91
  75.5 7.6 %all_gather.37 = bf16[512,512]{1,0:T(8,128)(2,1)} all-gather(bf16[128,512]{1,0:T(8,128)(2,1)S(1)} %copy-done.5), channel_id=1, replica_groups=mesh['groups'=2,'face'=4,'band'=2,'sub'=2] {'band','sub'}, dimensions={0}, use_global_device_ids=true | all-gather | bytes 655360 | tf_op jit(solution)/shard_map/all_gather | solution.py:65
  83.1 7.7 %all_gather.39 = bf16[512,512]{1,0:T(8,128)(2,1)} all-gather(bf16[128,512]{1,0:T(8,128)(2,1)S(1)} %copy-done.6), channel_id=1, replica_groups=mesh['groups'=2,'face'=4,'band'=2,'sub'=2] {'band','sub'}, dimensions={0}, use_global_device_ids=true | all-gather | bytes 655360 | tf_op jit(solution)/shard_map/all_gather | solution.py:67
  90.8 7.7 %all_gather.30 = bf16[512,512]{1,0:T(8,128)(2,1)} all-gather(bf16[128,512]{1,0:T(8,128)(2,1)S(1)} %copy-done.7), channel_id=1, replica_groups=mesh['groups'=2,'face'=4,'band'=2,'sub'=2] {'band','sub'}, dimensions={0}, use_global_device_ids=true | all-gather | bytes 655360 | tf_op jit(solution)/shard_map/all_gather | solution.py:60
  98.5 7.9 %all_gather.31 = bf16[512,512]{1,0:T(8,128)(2,1)} all-gather(bf16[128,512]{1,0:T(8,128)(2,1)S(1)} %copy-done.8), channel_id=1, replica_groups=mesh['groups'=2,'face'=4,'band'=2,'sub'=2] {'band','sub'}, dimensions={0}, use_global_device_ids=true | all-gather | bytes 655360 | tf_op jit(solution)/shard_map/all_gather | solution.py:61
  106.4 2.7 %fusion.54 = (f32[1024]{0:T(1024)S(1)}, f32[1024,512]{0,1:T(8,128)S(1)}) fusion(bf16[512,512]{1,0:T(8,128)(2,1)} %all_gather.31, bf16[1024,512]{1,0:T(8,128)(2,1)S(1)} %copy-done.2, bf16[512,512]{1,0:T(8,128)(2,1)} %all_gather.30), kind=kOutput, calls=%fused_computation.79 | convolution fusion | flops 1076886528 | bytes 4198400 | tf_op jit(solution)/shard_map/dot_general | solution.py:34
  111.0 2.1 %all-to-all-done.1 = bf16[4,384,512]{2,1,0:T(8,128)(2,1)} async-done(((bf16[4,384,512]{2,1,0:T(8,128)(2,1)}), bf16[4,384,512]{2,1,0:T(8,128)(2,1)}, u32[]{:S(2)}, u32[]{:S(2)}) %all-to-all-start.1) | async-done | bytes 1572896 | tf_op jit(solution)/shard_map/all_to_all | solution.py:91
  113.1 1.8 %convolution_convert_fusion = bf16[128,512]{1,0:T(8,128)(2,1)S(1)} fusion(bf16[1536,512]{1,0:T(8,128)(2,1)} %bitcast.6, f32[1536]{0:T(1024)S(1)} %reshape.145), kind=kOutput, calls=%fused_computation.16 | convolution fusion | flops 201588736 | bytes 1710080 | tf_op jit(solution)/shard_map/dot_general | solution.py:103
  114.9 1.9 %fusion.56 = (f32[128]{0:T(128)S(1)}, f32[128,512]{1,0:T(8,128)S(1)}) fusion(bf16[512,512]{1,0:T(8,128)(2,1)} %all_gather.35, bf16[1024,512]{1,0:T(8,128)(2,1)} %all-gather.4.cloned.1.call-done, bf16[128,512]{1,0:T(8,128)(2,1)S(1)} %convolution_convert_fusion, bf16[128,512]{1,0:T(8,128)(2,1)S(1)} %copy-done.9), kind=kOutput, calls=%fused_computation.81 | convolution fusion | flops 202243968 | bytes 2097664 | tf_op jit(solution)/shard_map/dot_general | solution.py:34
  117.3 3.8 %collective-permute-start.1 = (bf16[64,512]{1,0:T(8,128)(2,1)S(1)}, bf16[64,512]{1,0:T(8,128)(2,1)S(1)}, u32[]{:S(2)}, u32[]{:S(2)}) collective-permute-start(bf16[64,512]{1,0:T(8,128)(2,1)S(1)} %get-tuple-element.9), channel_id=1, source_target_pairs={{4,0},{8,4},{12,8},{0,12},{5,1},{9,5},{13,9},{1,13},{6,2},{10,6},{... | collective-permute-start | bytes 196616 | tf_op jit(solution)/shard_map/ppermute | solution.py:16
  121.1 1.3 copy.27
  123.4 2.7 %gather_fusion = bf16[768,512]{1,0:T(8,128)(2,1)S(1)} fusion(bf16[256,512]{1,0:T(8,128)(2,1)S(1)} %pad_maximum_fusion, s32[1024]{0:T(1024)S(1)} %pad_clamp_fusion), kind=kCustom, calls=%fused_computation | custom fusion | bytes 1575936 | tf_op jit(solution)/shard_map/gather | solution.py:111
  126.1 3.0 %fusion.59 = (f32[768]{0:T(1024)S(1)}, f32[768,512]{1,0:T(8,128)S(1)}) fusion(bf16[512,512]{1,0:T(8,128)(2,1)} %all_gather.37, bf16[1024,512]{1,0:T(8,128)(2,1)} %all-gather.6.cloned.1.call-done, bf16[768,512]{1,0:T(8,128)(2,1)S(1)} %reshape.143, bf16[768,512]{1,0:T(8,128)(2,1)S(1)} %gather_fusion), kind=kOutput, calls=%fused_computation.82 | convolution fusion | flops 1213463808 | bytes 4721664 | tf_op jit(solution)/shard_map/dot_general | solution.py:34
  129.4 1.4 %subtract_multiply_fusion = f32[768,512]{1,0:T(8,128)} fusion(f32[768,512]{1,0:T(8,128)S(1)} %get-tuple-element.17, f32[768]{0:T(1024)S(1)} %add_rsqrt_fusion, f32[768]{0:T(1024)S(1)} %broadcast_multiply_fusion), kind=kLoop, calls=%fused_computation.15 | loop fusion | flops 786432 | bytes 3151872 | tf_op jit(solution)/shard_map/mul | solution.py:27
  130.8 1.5 %reshape.144 = f32[128,6,512]{2,1,0:T(8,128)S(1)} reshape(f32[768,512]{1,0:T(8,128)} %subtract_multiply_fusion) | data formatting | bytes 3145728 | tf_op jit(solution)/shard_map/reshape | solution.py:114
  133.1 1.8 %fusion.62 = (f32[128]{0:T(128)S(1)}, f32[128,512]{1,0:T(8,128)S(1)}) fusion(bf16[512,512]{1,0:T(8,128)(2,1)S(1)} %copy-done.3, bf16[1024,512]{1,0:T(8,128)(2,1)} %all-gather.8.cloned.1.call-done, bf16[128,512]{1,0:T(8,128)(2,1)S(1)} %reduce_sum.120, bf16[128,512]{1,0:T(8,128)(2,1)S(1)} %add_convert_fusion.2), kind=kOutput, calls=%fused_computation.83 | convolution fusion | flops 202243968 | bytes 2097664 | tf_op jit(solution)/shard_map/dot_general | solution.py:34
  (79 shorter events, 15.6 us)
Async XLA Ops:
  7.2 42.1 %copy-start.1 = (bf16[1024,512]{1,0:T(8,128)(2,1)S(1)}, bf16[1024,512]{1,0:T(8,128)(2,1)}, u32[]{:S(2)}) copy-start(bf16[1024,512]{1,0:T(8,128)(2,1)} %param.15) | copy-start | bytes 3145732
  7.2 107.7 %all-gather.4.cloned.1.call-start = ((), (), s32[]{:S(2)}) async-start(), calls=%async_computation.2 | async-start | bytes 1310720 | tf_op jit(solution)/shard_map/all_gather | solution.py:62
  7.9 118.2 %all-gather.6.cloned.1.call-start = ((), (), s32[]{:S(2)}) async-start(), calls=%async_computation.3 | async-start | bytes 1310720 | tf_op jit(solution)/shard_map/all_gather | solution.py:64
  22.5 47.9 %all-to-all-start = ((bf16[4,2,192]{2,1,0:T(2,128)(2,1)}), bf16[4,2,192]{2,1,0:T(2,128)(2,1)S(1)}, u32[]{:S(2)}, u32[]{:S(2)}) async-start(bf16[4,2,192]{2,1,0:T(2,128)(2,1)} %reshape.177), calls=%async_computation | async-start | bytes 8192 | tf_op jit(solution)/shard_map/all_to_all | solution.py:92
  28.9 104.2 %all-gather.8.cloned.1.call-start = ((), (), s32[]{:S(2)}) async-start(), calls=%async_computation.4 | async-start | bytes 1310720 | tf_op jit(solution)/shard_map/all_gather | solution.py:66
  52.4 0.9 copy-start.4
  52.4 8.6 %copy-start.10 = (s32[128,6]{0,1:T(8,128)S(1)}, s32[128,6]{0,1:T(8,128)}, u32[]{:S(2)}) copy-start(s32[128,6]{0,1:T(8,128)} %param.19) | copy-start | bytes 9220
  64.1 11.4 %copy-start.5 = (bf16[128,512]{1,0:T(8,128)(2,1)S(1)}, bf16[128,512]{1,0:T(8,128)(2,1)}, u32[]{:S(2)}) copy-start(bf16[128,512]{1,0:T(8,128)(2,1)} %param.27) | copy-start | bytes 393220
  70.5 12.6 %copy-start.6 = (bf16[128,512]{1,0:T(8,128)(2,1)S(1)}, bf16[128,512]{1,0:T(8,128)(2,1)}, u32[]{:S(2)}) copy-start(bf16[128,512]{1,0:T(8,128)(2,1)} %param.29) | copy-start | bytes 393220
  70.5 20.3 %copy-start.7 = (bf16[128,512]{1,0:T(8,128)(2,1)S(1)}, bf16[128,512]{1,0:T(8,128)(2,1)}, u32[]{:S(2)}) copy-start(bf16[128,512]{1,0:T(8,128)(2,1)} %param.22) | copy-start | bytes 393220
  70.5 28.1 %copy-start.8 = (bf16[128,512]{1,0:T(8,128)(2,1)S(1)}, bf16[128,512]{1,0:T(8,128)(2,1)}, u32[]{:S(2)}) copy-start(bf16[128,512]{1,0:T(8,128)(2,1)} %param.23) | copy-start | bytes 393220
  70.5 42.6 %all-to-all-start.1 = ((bf16[4,384,512]{2,1,0:T(8,128)(2,1)}), bf16[4,384,512]{2,1,0:T(8,128)(2,1)}, u32[]{:S(2)}, u32[]{:S(2)}) async-start(bf16[4,384,512]{2,1,0:T(8,128)(2,1)} %bitcast.5), calls=%async_computation.1 | async-start | bytes 3145728 | tf_op jit(solution)/shard_map/all_to_all | solution.py:91
  75.5 31.0 %copy-start.2 = (bf16[1024,512]{1,0:T(8,128)(2,1)S(1)}, bf16[1024,512]{1,0:T(8,128)(2,1)}, u32[]{:S(2)}) copy-start(bf16[1024,512]{1,0:T(8,128)(2,1)} %param.15) | copy-start | bytes 3145732
  109.2 1.2 copy-start
  110.4 4.5 %copy-start.9 = (bf16[128,512]{1,0:T(8,128)(2,1)S(1)}, bf16[128,512]{1,0:T(8,128)(2,1)}, u32[]{:S(2)}) copy-start(bf16[128,512]{1,0:T(8,128)(2,1)} %param.18) | copy-start | bytes 393220
  117.2 6.1 %collective-permute-start = (bf16[64,512]{1,0:T(8,128)(2,1)S(1)}, bf16[64,512]{1,0:T(8,128)(2,1)S(1)}, u32[]{:S(2)}, u32[]{:S(2)}) collective-permute-start(bf16[64,512]{1,0:T(8,128)(2,1)S(1)} %get-tuple-element.8), channel_id=1, source_target_pairs={{0,4},{4,8},{8,12},{12,0},{1,5},{5,9},{9,13},{13,1},{2,6},{6,10},{... | collective-permute-start | bytes 196616 | tf_op jit(solution)/shard_map/ppermute | solution.py:14
  117.3 6.1 %collective-permute-start.1 = (bf16[64,512]{1,0:T(8,128)(2,1)S(1)}, bf16[64,512]{1,0:T(8,128)(2,1)S(1)}, u32[]{:S(2)}, u32[]{:S(2)}) collective-permute-start(bf16[64,512]{1,0:T(8,128)(2,1)S(1)} %get-tuple-element.9), channel_id=1, source_target_pairs={{4,0},{8,4},{12,8},{0,12},{5,1},{9,5},{13,9},{1,13},{6,2},{10,6},{... | collective-permute-start | bytes 196616 | tf_op jit(solution)/shard_map/ppermute | solution.py:16
  130.8 2.3 %copy-start.3 = (bf16[512,512]{1,0:T(8,128)(2,1)S(1)}, bf16[512,512]{1,0:T(8,128)(2,1)}, u32[]{:S(2)}) copy-start(bf16[512,512]{1,0:T(8,128)(2,1)} %all_gather.39) | copy-start | bytes 1572868
Sparse Core Ops, SparseCore 0:
  9.6 19.4 all-gather.3
  30.6 19.5 all-gather.5
  51.7 16.7 all-gather.7
where the time goes:
time: 143 us; the launch traced here: 142 us
  blocking collectives  58.4 us (41%)
  local copies, waits for them, and re-layouts  26 us (18%)
  starting transfers between devices  15.3 us (11%)
  between operations  14.1 us (10%)
  matrix products  14 us (10%)
  other arithmetic  9.98 us (7%)
  waiting for transfers between devices  4.77 us (3%)
    dot_general x5, matrix products, perceptron(): jnp.dot(hidden, weight_out, preferred_element_type=jnp.float32)  12.2 us
    all_gather x1, blocking collectives, shards(): lax.all_gather(enc_w2, ('band', 'sub'), axis=0, tiled=True)  11.3 us
    all_gather x1, blocking collectives, shards(): lax.all_gather(enc_w1, ('band', 'sub'), axis=0, tiled=True)  8.46 us
    all_gather x1, blocking collectives, shards(): lax.all_gather(grid_w2, ('band', 'sub'), axis=0, tiled=True)  7.91 us
    all_gather x1, blocking collectives, shards(): lax.all_gather(node_w2, ('band', 'sub'), axis=0, tiled=True)  7.73 us
    all_gather x1, blocking collectives, shards(): lax.all_gather(upd_w2, ('band', 'sub'), axis=0, tiled=True)  7.73 us
    all_gather x1, blocking collectives, shards(): lax.all_gather(grid_w1, ('band', 'sub'), axis=0, tiled=True)  7.73 us
    scatter x1, local copies, waits for them, and re-layouts, shards(): slot_codes = jnp.full((peers * capacity,), float(mesh_rows), jnp.bfloat16...  7.59 us
  transfers between devices with their start and end apart: 7, of which 2 were waited for; matrix products, arithmetic and copies ran while one was open for 32% of the time, Pallas kernels for 0%

commit v1 on v0

v1 whole, which is shorter than its diff:
```python
import functools

import jax
import jax.numpy as jnp
from jax import lax
from jax.experimental import pallas as pl
from jax.experimental.pallas import tpu as pltpu
from jax.sharding import PartitionSpec as P

MIB = 1 << 20
ANY = pl.BlockSpec(memory_space=pl.ANY)
VMEM = pl.BlockSpec(memory_space=pltpu.VMEM)


def after(value, *earlier):
    return lax.optimization_barrier((value, *earlier))[0]


def shift(value, axis, step):
    count = lax.axis_size(axis)
    return lax.ppermute(value, axis, [(i, (i + step) % count) for i in range(count)])


def spread(pack, *earlier):
    bands, subs = lax.axis_size("band"), lax.axis_size("sub")
    first = after(pack, *earlier) if earlier else pack
    rows = [pack] + [shift(first, "band", step) for step in range(1, bands)]
    pieces = []
    for row in rows:
        pieces.append(row)
        pieces.extend(shift(row, "sub", step) for step in range(1, subs))
    return pieces, rows[-1]


def load_copies(pieces, parts, sems):
    bands, subs = lax.axis_size("band"), lax.axis_size("sub")
    band, sub = lax.axis_index("band"), lax.axis_index("sub")
    copies = []
    for index, piece in enumerate(pieces):
        owner = lax.rem(band + bands - index // subs, bands) * subs + lax.rem(
            sub + subs - index % subs, subs
        )
        start = 0
        for part, (rows, whole) in enumerate(parts):
            copies.append(
                pltpu.make_async_copy(
                    piece.at[pl.ds(start, rows)],
                    whole.at[pl.ds(pl.multiple_of(owner * rows, rows), rows)],
                    sems.at[part, index],
                )
            )
            start += rows
    return copies


def silu(values):
    half = 0.5 * values
    return half + half * jnp.tanh(half)


def layer_norm(values):
    average = jnp.mean(values, axis=-1, keepdims=True)
    centred = values - average
    spread_of = jnp.mean(centred * centred, axis=-1, keepdims=True)
    return centred * lax.rsqrt(spread_of + 1e-05)


def dot(a, b):
    return jnp.dot(a, b, preferred_element_type=jnp.float32)


def encode_kernel(count, faces, mesh_rows, target_ref, lat_ref, *refs):
    in_pieces, hid_pieces = refs[:count], refs[count : 2 * count]
    outs = refs[2 * count : 2 * count + faces]
    w_in, w_hid, messages, sems_in, sems_hid = refs[2 * count + faces :]
    rows = w_in.shape[0] // count
    first = load_copies(in_pieces, [(rows, w_in)], sems_in)
    second = load_copies(hid_pieces, [(rows, w_hid)], sems_hid)
    for copy in first + second:
        copy.start()
    for copy in first + second:
        copy.wait()
    block = 256
    for start in range(0, lat_ref.shape[0], block):
        here = pl.ds(start, block)
        hidden = silu(dot(lat_ref[here], w_in[...])).astype(jnp.bfloat16)
        messages[here] = layer_norm(dot(hidden, w_hid[...])).astype(jnp.bfloat16)
    group = min(faces, 4)
    for at in range(0, faces, group):
        slots = lax.broadcasted_iota(jnp.int32, (group * mesh_rows, lat_ref.shape[0]), 0)
        chosen = jnp.where(slots + at * mesh_rows == target_ref[...], 1.0, 0.0)
        chosen = chosen.astype(jnp.bfloat16)
        sums = dot(chosen, messages[...])
        for face in range(group):
            out = outs[at + face]
            out[...] = sums[face * mesh_rows : (face + 1) * mesh_rows].astype(out.dtype)


def grid_kernel(count, lat_ref, *refs):
    pieces = refs[:count]
    out_ref, w_in, w_hid, sems = refs[count:]
    rows = w_in.shape[0] // count
    copies = load_copies(pieces, [(rows, w_in), (rows, w_hid)], sems)
    for copy in copies:
        copy.start()
    for copy in copies:
        copy.wait()
    block = 256
    for start in range(0, lat_ref.shape[0], block):
        here = pl.ds(start, block)
        lat = lat_ref[here]
        hidden = silu(dot(lat, w_in[...])).astype(jnp.bfloat16)
        out = lat.astype(jnp.float32) + layer_norm(dot(hidden, w_hid[...]))
        out_ref[here] = out.astype(jnp.bfloat16)


def node_kernel(count, faces, lat_ref, *refs):
    sums, pieces = refs[:faces], refs[faces : faces + count]
    head_ref, tail_ref, w_in, w_hid, sems = refs[faces + count :]
    width = lat_ref.shape[1]
    copies = load_copies(
        pieces, [(w_in.shape[0] // count, w_in), (w_hid.shape[0] // count, w_hid)], sems
    )
    for copy in copies:
        copy.start()
    collected = sums[0][...]
    for one in sums[1:]:
        collected = collected + one[...].astype(jnp.float32)
    for copy in copies:
        copy.wait()
    lat = lat_ref[...]
    hidden = dot(lat, w_in[:width]) + dot(collected.astype(jnp.bfloat16), w_in[width:])
    hidden = silu(hidden).astype(jnp.bfloat16)
    mid = lat.astype(jnp.float32) + layer_norm(dot(hidden, w_hid[...]))
    mid = mid.astype(jnp.bfloat16)
    half = mid.shape[0] // 2
    head_ref[...] = mid[:half]
    tail_ref[...] = mid[half:]


def edge_kernel(count, nbr_ref, before_ref, head_ref, tail_ref, after_ref, *refs):
    proc, upd = refs[:count], refs[count : 2 * count]
    out_ref, p_in, p_hid, u_in, u_hid, sems_p, sems_u = refs[2 * count :]
    copies_p = load_copies(
        proc, [(p_in.shape[0] // count, p_in), (p_hid.shape[0] // count, p_hid)], sems_p
    )
    copies_u = load_copies(
        upd, [(u_in.shape[0] // count, u_in), (u_hid.shape[0] // count, u_hid)], sems_u
    )
    for copy in copies_p + copies_u:
        copy.start()
    rows, fanin = nbr_ref.shape
    width = head_ref.shape[1]
    mid = jnp.concatenate([head_ref[...], tail_ref[...]], axis=0)
    extended = jnp.concatenate([before_ref[...], mid, after_ref[...]], axis=0)
    spots = lax.broadcasted_iota(jnp.int32, (rows, extended.shape[0]), 1)
    nbr = nbr_ref[...]
    for copy in copies_p:
        copy.wait()
    receivers = dot(mid, p_in[width:])
    total = None
    group = 2 if fanin % 2 == 0 else 1
    for at in range(0, fanin, group):
        chosen = jnp.concatenate(
            [
                jnp.where(spots == nbr[:, k : k + 1], 1.0, 0.0).astype(jnp.bfloat16)
                for k in range(at, at + group)
            ],
            axis=0,
        )
        senders = dot(chosen, extended).astype(jnp.bfloat16)
        hidden = dot(senders, p_in[:width])
        hidden = (hidden.reshape(group, rows, width) + receivers[None]).reshape(group * rows, width)
        edges = layer_norm(dot(silu(hidden).astype(jnp.bfloat16), p_hid[...]))
        for k in range(group):
            one = edges[k * rows : (k + 1) * rows]
            total = one if total is None else total + one
    for copy in copies_u:
        copy.wait()
    hidden = dot(mid, u_in[:width]) + dot(total.astype(jnp.bfloat16), u_in[width:])
    hidden = silu(hidden).astype(jnp.bfloat16)
    out = mid.astype(jnp.float32) + layer_norm(dot(hidden, u_hid[...]))
    out_ref[...] = out.astype(jnp.bfloat16)


def shards(
    grid_lat,
    grid_route,
    grid_slot,
    mesh_lat,
    mesh_nbr,
    enc_w1,
    enc_w2,
    grid_w1,
    grid_w2,
    node_w1,
    node_w2,
    proc_w1,
    proc_w2,
    upd_w1,
    upd_w2,
):
    grid_rows, width = grid_lat.shape
    mesh_rows = mesh_lat.shape[0]
    faces = lax.axis_size("face")
    count = lax.axis_size("band") * lax.axis_size("sub")
    f32, bf16 = jnp.float32, jnp.bfloat16

    def matrix(weight):
        return pltpu.VMEM((weight.shape[0] * count, weight.shape[1]), bf16)

    def sems(parts):
        return pltpu.SemaphoreType.DMA((parts, count))

    def cost(rows, depth):
        return pl.CostEstimate(
            flops=2 * rows * depth * width,
            bytes_accessed=2 * (rows + depth) * width,
            transcendentals=rows * width,
        )

    enc_in, enc_in_last = spread(enc_w1)
    enc_hid, enc_hid_last = spread(enc_w2)
    node, node_last = spread(
        jnp.concatenate([node_w1, node_w2], axis=0), enc_in_last, enc_hid_last
    )
    grid, grid_last = spread(jnp.concatenate([grid_w1, grid_w2], axis=0), node_last)
    proc, proc_last = spread(jnp.concatenate([proc_w1, proc_w2], axis=0), grid_last)
    upd, _ = spread(jnp.concatenate([upd_w1, upd_w2], axis=0), proc_last)

    me = lax.axis_index("face")
    distance = lax.rem(grid_route[:, 0] - me + faces, faces)
    targets = (distance * mesh_rows + grid_slot).reshape(1, grid_rows)

    block = (mesh_rows, width)
    sums = pl.pallas_call(
        functools.partial(encode_kernel, count, faces, mesh_rows),
        out_shape=[
            jax.ShapeDtypeStruct(block, bf16 if step else f32) for step in range(faces)
        ],
        in_specs=[VMEM, VMEM] + [ANY] * (2 * count),
        out_specs=[VMEM] * faces,
        scratch_shapes=[
            matrix(enc_w1),
            matrix(enc_w2),
            pltpu.VMEM((grid_rows, width), bf16),
            sems(1),
            sems(1),
        ],
        compiler_params=pltpu.CompilerParams(vmem_limit_bytes=32 * MIB),
        cost_estimate=cost(grid_rows, 3 * width),
        name="encode",
    )(targets, grid_lat, *enc_in, *enc_hid)
    arrived = [sums[0]] + [shift(sums[step], "face", step) for step in range(1, faces)]

    grid_out = pl.pallas_call(
        functools.partial(grid_kernel, count),
        out_shape=jax.ShapeDtypeStruct(grid_lat.shape, bf16),
        in_specs=[VMEM] + [ANY] * count,
        out_specs=VMEM,
        scratch_shapes=[matrix(grid_w1), matrix(grid_w2), sems(2)],
        compiler_params=pltpu.CompilerParams(vmem_limit_bytes=32 * MIB),
        cost_estimate=cost(grid_rows, 2 * width),
        name="grid_update",
    )(grid_lat, *grid)

    half = (mesh_rows // 2, width)
    head, tail = pl.pallas_call(
        functools.partial(node_kernel, count, faces),
        out_shape=[jax.ShapeDtypeStruct(half, bf16)] * 2,
        in_specs=[VMEM] * (1 + faces) + [ANY] * count,
        out_specs=[VMEM] * 2,
        scratch_shapes=[matrix(node_w1), matrix(node_w2), sems(2)],
        compiler_params=pltpu.CompilerParams(vmem_limit_bytes=32 * MIB),
        cost_estimate=cost(mesh_rows, 3 * width),
        name="node_update",
    )(mesh_lat, *arrived, *node)

    before = shift(tail, "face", 1)
    behind = shift(head, "face", faces - 1)
    mesh_out = pl.pallas_call(
        functools.partial(edge_kernel, count),
        out_shape=jax.ShapeDtypeStruct(mesh_lat.shape, bf16),
        in_specs=[VMEM] * 5 + [ANY] * (2 * count),
        out_specs=VMEM,
        scratch_shapes=[
            matrix(proc_w1),
            matrix(proc_w2),
            matrix(upd_w1),
            matrix(upd_w2),
            sems(2),
            sems(2),
        ],
        compiler_params=pltpu.CompilerParams(vmem_limit_bytes=32 * MIB),
        cost_estimate=cost(mesh_rows * mesh_nbr.shape[1], 3 * width),
        name="edge_update",
    )(mesh_nbr, before, head, tail, behind, *proc, *upd)
    return (grid_out, mesh_out)


def solution(mesh):
    rows = ("groups", "face", "band", "sub")
    placed = (
        P(rows, None),
        P(rows, None),
        P(rows),
        P(rows, None),
        P(rows, None),
    ) + (P(("band", "sub"), None),) * 10
    return jax.shard_map(
        shards,
        mesh=mesh,
        in_specs=placed,
        out_specs=(P(rows, None), P(rows, None)),
        check_vma=False,
    )
```

time: 143 us -> 77.4 us (0.54)
  blocking collectives: 58.4 us -> 0 us
  waiting for transfers between devices: 4.77 us -> 32.8 us
  local copies, waits for them, and re-layouts: 26 us -> 7.16 us
  Pallas kernels: 0 us -> 15.1 us
  matrix products: 14 us -> 0 us
  between operations: 14.1 us -> 0.92 us
  other arithmetic: 9.98 us -> 0.02 us
  starting transfers between devices: 15.3 us -> 21.1 us
    all_gather x7 -> x0, blocking collectives: 58.4 us -> none  [the longest x1 11.3 us: shards(): lax.all_gather(enc_w2, ('band', 'sub'), axis=0, tiled=True)]
    ppermute x2 -> x23, waiting for transfers between devices: 0.52 us -> 32.8 us  [shift(): lax.ppermute(value, axis, [(i, (i + step) % count) for i in range(count)])]
    ppermute x2 -> x23, starting transfers between devices: 3.87 us -> 21.1 us  [shift(): lax.ppermute(value, axis, [(i, (i + step) % count) for i in range(count)])]
    pallas_call x0 -> x4, Pallas kernels: none -> 15.1 us  [the longest x1 4.97 us: shards(): pl.pallas_call(functools.partial(edge_kernel, count), out_shape=jax.Shape...]
    scatter x2 -> x0, local copies, waits for them, and re-layouts: 14 us -> none  [the longest x1 7.59 us: shards(): slot_codes = jnp.full((peers * capacity,), float(mesh_rows), jnp.bfloat16...]
    dot_general x6 -> x0, matrix products: 14 us -> none  [the longest x5 12.2 us: perceptron(): jnp.dot(hidden, weight_out, preferred_element_type=jnp.float32)]
    all_to_all x2 -> x0, starting transfers between devices: 11.3 us -> none  [the longest x1 6.32 us: shards(): lax.all_to_all(slot_codes, 'face', split_axis=0, concat_axis=0, tiled=True)]
    convert_element_type x7 -> x0, other arithmetic: 3.03 us -> none  [the longest x1 0.79 us: shards(): (mesh_mid.astype(jnp.float32) + perceptron(joined, upd_in, upd_hid)).asty...]
  transfers between devices with their start and end apart: 7 -> 23, of which waited for: 2 -> 8; matrix products, arithmetic and copies ran while one was open for 32% -> 2% of each run, Pallas kernels for 0% -> 13%
where the time goes in v1:
time: 77.4 us; the launch traced here: 77.1 us
  waiting for transfers between devices  32.8 us (42%)
  starting transfers between devices  21.1 us (27%)
  Pallas kernels  15.1 us (20%)
  local copies, waits for them, and re-layouts  7.16 us (9%)
  between operations  0.92 us (1%)
    ppermute x23, waiting for transfers between devices, shift(): lax.ppermute(value, axis, [(i, (i + step) % count) for i in range(count)])  32.8 us
    ppermute x23, starting transfers between devices, shift(): lax.ppermute(value, axis, [(i, (i + step) % count) for i in range(count)])  21.1 us
    unnamed x47, local copies, waits for them, and re-layouts  7.12 us
    pallas_call x1, Pallas kernels, shards(): pl.pallas_call(functools.partial(edge_kernel, count), out_shape=jax.Shape...  4.97 us
    pallas_call x1, Pallas kernels, shards(): pl.pallas_call(functools.partial(grid_kernel, count), out_shape=jax.Shape...  4.85 us
    pallas_call x1, Pallas kernels, shards(): pl.pallas_call(functools.partial(encode_kernel, count, faces, mesh_rows),...  3.67 us
    pallas_call x1, Pallas kernels, shards(): pl.pallas_call(functools.partial(node_kernel, count, faces), out_shape=[j...  1.6 us
  transfers between devices with their start and end apart: 23, of which 8 were waited for; matrix products, arithmetic and copies ran while one was open for 2% of the time, Pallas kernels for 13%

profile of v1, /device:TPU:0, one launch (start us, length us, event | category | flops | bytes accessed | tf_op | source)
XLA Modules:
  0.0 77.1 jit_solution(13884435098722625231)
XLA Ops:
  0.6 3.0 %collective-permute-start.1 = (bf16[128,512]{1,0:T(8,128)(2,1)}, bf16[128,512]{1,0:T(8,128)(2,1)S(1)}, u32[]{:S(2)}, u32[]{:S(2)}) collective-permute-start(bf16[128,512]{1,0:T(8,128)(2,1)} %refs_0_.1), channel_id=1, source_target_pairs={{0,2},{2,0},{1,3},{3,1},{4,6},{6,4},{5,7},{7,5},{8,10},{10,8},{9,1... | collective-permute-start | bytes 393224 | tf_op jit(solution)/shard_map/ppermute | solution.py:21
  3.7 1.0 %constant_dynamic-update-slice_fusion.3 = bf16[384,512]{1,0:T(8,128)(2,1)S(1)} fusion(bf16[256,512]{1,0:T(8,128)(2,1)} %param.24), kind=kLoop, calls=%fused_computation.3 | loop fusion | bytes 524288
  4.8 3.4 %collective-permute-done.1.refs_2_ = bf16[128,512]{1,0:T(8,128)(2,1)S(1)} collective-permute-done((bf16[128,512]{1,0:T(8,128)(2,1)}, bf16[128,512]{1,0:T(8,128)(2,1)S(1)}, u32[]{:S(2)}, u32[]{:S(2)}) %collective-permute-start.1) | collective-permute-done | bytes 131104 | tf_op jit(solution)/shard_map/ppermute | solution.py:21
  8.2 2.0 %collective-permute-done.2.refs_6_ = bf16[128,512]{1,0:T(8,128)(2,1)S(1)} collective-permute-done((bf16[128,512]{1,0:T(8,128)(2,1)}, bf16[128,512]{1,0:T(8,128)(2,1)S(1)}, u32[]{:S(2)}, u32[]{:S(2)}) %collective-permute-start.2) | collective-permute-done | bytes 131104 | tf_op jit(solution)/shard_map/ppermute | solution.py:21
  10.2 1.7 %collective-permute-start.3 = (bf16[384,512]{1,0:T(8,128)(2,1)S(1)}, bf16[384,512]{1,0:T(8,128)(2,1)S(1)}, u32[]{:S(2)}, u32[]{:S(2)}) collective-permute-start(bf16[384,512]{1,0:T(8,128)(2,1)S(1)} %constant_dynamic-update-slice_fusion.2.refs_4_), channel_id=1, source_target_pairs={{0,2},{2,0},{1,3},{3,1},{4,6},{6,4},{5,7},{7,5},{8,10},{10,8},{9,1... | collective-permute-start | bytes 1179656 | tf_op jit(solution)/shard_map/ppermute | solution.py:21
  12.0 8.5 %collective-permute-done.3.refs_6_ = bf16[384,512]{1,0:T(8,128)(2,1)S(1)} collective-permute-done((bf16[384,512]{1,0:T(8,128)(2,1)S(1)}, bf16[384,512]{1,0:T(8,128)(2,1)S(1)}, u32[]{:S(2)}, u32[]{:S(2)}) %collective-permute-start.3) | collective-permute-done | bytes 393248 | tf_op jit(solution)/shard_map/ppermute | solution.py:21
  20.5 1.4 %collective-permute-start.4 = (bf16[256,512]{1,0:T(8,128)(2,1)S(1)}, bf16[256,512]{1,0:T(8,128)(2,1)}, u32[]{:S(2)}, u32[]{:S(2)}) collective-permute-start(bf16[256,512]{1,0:T(8,128)(2,1)S(1)} %constant_dynamic-update-slice_fusion.refs_0_), channel_id=1, source_target_pairs={{0,2},{2,0},{1,3},{3,1},{4,6},{6,4},{5,7},{7,5},{8,10},{10,8},{9,1... | collective-permute-start | bytes 786440 | tf_op jit(solution)/shard_map/ppermute | solution.py:21
  23.3 3.8 %collective-permute-done.4.refs_2_ = bf16[256,512]{1,0:T(8,128)(2,1)} collective-permute-done((bf16[256,512]{1,0:T(8,128)(2,1)S(1)}, bf16[256,512]{1,0:T(8,128)(2,1)}, u32[]{:S(2)}, u32[]{:S(2)}) %collective-permute-start.4) | collective-permute-done | bytes 262176 | tf_op jit(solution)/shard_map/ppermute | solution.py:21
  27.1 1.6 %collective-permute-start.18 = (bf16[384,512]{1,0:T(8,128)(2,1)S(1)}, bf16[384,512]{1,0:T(8,128)(2,1)}, u32[]{:S(2)}, u32[]{:S(2)}) collective-permute-start(bf16[384,512]{1,0:T(8,128)(2,1)S(1)} %constant_dynamic-update-slice_fusion.4.refs_0_), channel_id=1, source_target_pairs={{0,2},{2,0},{1,3},{3,1},{4,6},{6,4},{5,7},{7,5},{8,10},{10,8},{9,1... | collective-permute-start | bytes 1179656 | tf_op jit(solution)/shard_map/ppermute | solution.py:21
  29.4 6.4 %collective-permute-done.18.refs_2_ = bf16[384,512]{1,0:T(8,128)(2,1)} collective-permute-done((bf16[384,512]{1,0:T(8,128)(2,1)S(1)}, bf16[384,512]{1,0:T(8,128)(2,1)}, u32[]{:S(2)}, u32[]{:S(2)}) %collective-permute-start.18) | collective-permute-done | bytes 393248 | tf_op jit(solution)/shard_map/ppermute | solution.py:21
  37.6 1.1 %collective-permute-start.21 = (bf16[384,512]{1,0:T(8,128)(2,1)S(1)}, bf16[384,512]{1,0:T(8,128)(2,1)}, u32[]{:S(2)}, u32[]{:S(2)}) collective-permute-start(bf16[384,512]{1,0:T(8,128)(2,1)S(1)} %constant_dynamic-update-slice_fusion.6.refs_4_), channel_id=1, source_target_pairs={{0,2},{2,0},{1,3},{3,1},{4,6},{6,4},{5,7},{7,5},{8,10},{10,8},{9,1... | collective-permute-start | bytes 1179656 | tf_op jit(solution)/shard_map/ppermute | solution.py:21
  38.7 1.2 %copy-done.1 = bf16[1024,512]{1,0:T(8,128)(2,1)S(1)} copy-done((bf16[1024,512]{1,0:T(8,128)(2,1)S(1)}, bf16[1024,512]{1,0:T(8,128)(2,1)}, u32[]{:S(2)}) %copy-start.1) | copy-done | bytes 1048600
  41.7 3.7 %encode.1 = (f32[128,512]{1,0:T(8,128)S(1)}, bf16[128,512]{1,0:T(8,128)(2,1)S(1)}, bf16[128,512]{1,0:T(8,128)(2,1)S(1)}, bf16[128,512]{1,0:T(8,128)(2,1)S(1)}) custom-call(s32[1,1024]{1,0:T(1,128)S(1)} %bitcast.2, bf16[1024,512]{1,0:T(8,128)(2,1)S(1)} %copy-done.1, bf16[128,512]{1,0:T(8,128)(2,1)S(1)} %copy-done.5, bf16[128,512]{1,0:T(8,128)(2,1)S(1)} %copy-done.8, ...), custom_call_target="tpu_custom_call" | custom-call | flops 1610612736 | bytes 2621440 | tf_op jit(solution)/shard_map/encode/pallas_call | solution.py:236
  45.4 1.6 %collective-permute-start.10 = (bf16[128,512]{1,0:T(8,128)(2,1)S(1)}, bf16[128,512]{1,0:T(8,128)(2,1)S(1)}, u32[]{:S(2)}, u32[]{:S(2)}) collective-permute-start(bf16[128,512]{1,0:T(8,128)(2,1)S(1)} %get-tuple-element.15), channel_id=1, source_target_pairs={{0,4},{4,8},{8,12},{12,0},{1,5},{5,9},{9,13},{13,1},{2,6},{6,10},{... | collective-permute-start | bytes 393224 | tf_op jit(solution)/shard_map/ppermute | solution.py:21
  47.7 2.6 %collective-permute-start.11 = (bf16[128,512]{1,0:T(8,128)(2,1)S(1)}, bf16[128,512]{1,0:T(8,128)(2,1)S(1)}, u32[]{:S(2)}, u32[]{:S(2)}) collective-permute-start(bf16[128,512]{1,0:T(8,128)(2,1)S(1)} %get-tuple-element.16), channel_id=1, source_target_pairs={{0,8},{4,12},{8,0},{12,4},{1,9},{5,13},{9,1},{13,5},{2,10},{6,14},... | collective-permute-start | bytes 393224 | tf_op jit(solution)/shard_map/ppermute | solution.py:21
  50.3 3.3 %collective-permute-done.10.refs_1_ = bf16[128,512]{1,0:T(8,128)(2,1)S(1)} collective-permute-done((bf16[128,512]{1,0:T(8,128)(2,1)S(1)}, bf16[128,512]{1,0:T(8,128)(2,1)S(1)}, u32[]{:S(2)}, u32[]{:S(2)}) %collective-permute-start.10) | collective-permute-done | bytes 131104 | tf_op jit(solution)/shard_map/ppermute | solution.py:21
  53.7 1.5 %collective-permute-start.12 = (bf16[128,512]{1,0:T(8,128)(2,1)S(1)}, bf16[128,512]{1,0:T(8,128)(2,1)S(1)}, u32[]{:S(2)}, u32[]{:S(2)}) collective-permute-start(bf16[128,512]{1,0:T(8,128)(2,1)S(1)} %get-tuple-element.17), channel_id=1, source_target_pairs={{0,12},{4,0},{8,4},{12,8},{1,13},{5,1},{9,5},{13,9},{2,14},{6,2},{... | collective-permute-start | bytes 393224 | tf_op jit(solution)/shard_map/ppermute | solution.py:21
  55.1 3.6 %collective-permute-done.11.refs_2_ = bf16[128,512]{1,0:T(8,128)(2,1)S(1)} collective-permute-done((bf16[128,512]{1,0:T(8,128)(2,1)S(1)}, bf16[128,512]{1,0:T(8,128)(2,1)S(1)}, u32[]{:S(2)}, u32[]{:S(2)}) %collective-permute-start.11) | collective-permute-done | bytes 131104 | tf_op jit(solution)/shard_map/ppermute | solution.py:21
  58.7 1.8 %collective-permute-done.12.refs_3_ = bf16[128,512]{1,0:T(8,128)(2,1)S(1)} collective-permute-done((bf16[128,512]{1,0:T(8,128)(2,1)S(1)}, bf16[128,512]{1,0:T(8,128)(2,1)S(1)}, u32[]{:S(2)}, u32[]{:S(2)}) %collective-permute-start.12) | collective-permute-done | bytes 131104 | tf_op jit(solution)/shard_map/ppermute | solution.py:21
  61.7 1.6 %node_update.1 = (bf16[64,512]{1,0:T(8,128)(2,1)S(1)}, bf16[64,512]{1,0:T(8,128)(2,1)S(1)}) custom-call(bf16[128,512]{1,0:T(8,128)(2,1)S(1)} %copy-done, f32[128,512]{1,0:T(8,128)S(1)} %get-tuple-element.14.refs_0_, bf16[128,512]{1,0:T(8,128)(2,1)S(1)} %collective-permute-done.10.refs_1_, bf16[128,512]{1,0:T(8,128)(2,1)S(1)} %collective-permute-done.11.refs_2_, ...), custom_call_target="tpu_custom_call" | custom-call | flops 201326592 | bytes 1703936 | tf_op jit(solution)/shard_map/node_update/pallas_call | solution.py:268
  63.3 1.5 %collective-permute-start.15 = (bf16[64,512]{1,0:T(8,128)(2,1)S(1)}, bf16[64,512]{1,0:T(8,128)(2,1)S(1)}, u32[]{:S(2)}, u32[]{:S(2)}) collective-permute-start(bf16[64,512]{1,0:T(8,128)(2,1)S(1)} %get-tuple-element.18.tail_ref), channel_id=1, source_target_pairs={{0,4},{4,8},{8,12},{12,0},{1,5},{5,9},{9,13},{13,1},{2,6},{6,10},{... | collective-permute-start | bytes 196616 | tf_op jit(solution)/shard_map/ppermute | solution.py:21
  64.8 2.4 %collective-permute-start.16 = (bf16[64,512]{1,0:T(8,128)(2,1)S(1)}, bf16[64,512]{1,0:T(8,128)(2,1)S(1)}, u32[]{:S(2)}, u32[]{:S(2)}) collective-permute-start(bf16[64,512]{1,0:T(8,128)(2,1)S(1)} %get-tuple-element.19.head_ref), channel_id=1, source_target_pairs={{0,12},{4,0},{8,4},{12,8},{1,13},{5,1},{9,5},{13,9},{2,14},{6,2},{... | collective-permute-start | bytes 196616 | tf_op jit(solution)/shard_map/ppermute | solution.py:21
  67.2 4.8 %grid_update.1 = bf16[1024,512]{1,0:T(8,128)(2,1)} custom-call(bf16[1024,512]{1,0:T(8,128)(2,1)S(1)} %copy-done.2, bf16[256,512]{1,0:T(8,128)(2,1)S(1)} %constant_dynamic-update-slice_fusion.refs_0_, bf16[256,512]{1,0:T(8,128)(2,1)S(1)} %copy-done.4, bf16[256,512]{1,0:T(8,128)(2,1)} %collective-permute-done.4.refs_2_, ...), custom_call_target="tpu_custom_call" | custom-call | flops 1073741824 | bytes 2097152 | tf_op jit(solution)/shard_map/grid_update/pallas_call | solution.py:256
  72.1 5.0 %edge_update.1 = bf16[128,512]{1,0:T(8,128)(2,1)} custom-call(s32[128,6]{1,0:T(8,128)S(1)} %copy.17.nbr_ref, bf16[64,512]{1,0:T(8,128)(2,1)S(1)} %collective-permute-done.15.before_ref, bf16[64,512]{1,0:T(8,128)(2,1)S(1)} %get-tuple-element.19.head_ref, bf16[64,512]{1,0:T(8,128)(2,1)S(1)} %get-tuple-element.18.tail_ref, ...), custom_call_target="tpu_custom_call" | custom-call | flops 1207959552 | bytes 2359296 | tf_op jit(solution)/shard_map/edge_update/pallas_call | solution.py:281
  (79 shorter events, 7.7 us)
Async XLA Ops:
  0.6 7.5 %collective-permute-start.1 = (bf16[128,512]{1,0:T(8,128)(2,1)}, bf16[128,512]{1,0:T(8,128)(2,1)S(1)}, u32[]{:S(2)}, u32[]{:S(2)}) collective-permute-start(bf16[128,512]{1,0:T(8,128)(2,1)} %refs_0_.1), channel_id=1, source_target_pairs={{0,2},{2,0},{1,3},{3,1},{4,6},{6,4},{5,7},{7,5},{8,10},{10,8},{9,1... | collective-permute-start | bytes 393224 | tf_op jit(solution)/shard_map/ppermute | solution.py:21
  3.6 6.5 %collective-permute-start.2 = (bf16[128,512]{1,0:T(8,128)(2,1)}, bf16[128,512]{1,0:T(8,128)(2,1)S(1)}, u32[]{:S(2)}, u32[]{:S(2)}) collective-permute-start(bf16[128,512]{1,0:T(8,128)(2,1)} %refs_4_.1), channel_id=1, source_target_pairs={{0,2},{2,0},{1,3},{3,1},{4,6},{6,4},{5,7},{7,5},{8,10},{10,8},{9,1... | collective-permute-start | bytes 393224 | tf_op jit(solution)/shard_map/ppermute | solution.py:21
  10.2 10.3 %collective-permute-start.3 = (bf16[384,512]{1,0:T(8,128)(2,1)S(1)}, bf16[384,512]{1,0:T(8,128)(2,1)S(1)}, u32[]{:S(2)}, u32[]{:S(2)}) collective-permute-start(bf16[384,512]{1,0:T(8,128)(2,1)S(1)} %constant_dynamic-update-slice_fusion.2.refs_4_), channel_id=1, source_target_pairs={{0,2},{2,0},{1,3},{3,1},{4,6},{6,4},{5,7},{7,5},{8,10},{10,8},{9,1... | collective-permute-start | bytes 1179656 | tf_op jit(solution)/shard_map/ppermute | solution.py:21
  20.5 6.7 %collective-permute-start.4 = (bf16[256,512]{1,0:T(8,128)(2,1)S(1)}, bf16[256,512]{1,0:T(8,128)(2,1)}, u32[]{:S(2)}, u32[]{:S(2)}) collective-permute-start(bf16[256,512]{1,0:T(8,128)(2,1)S(1)} %constant_dynamic-update-slice_fusion.refs_0_), channel_id=1, source_target_pairs={{0,2},{2,0},{1,3},{3,1},{4,6},{6,4},{5,7},{7,5},{8,10},{10,8},{9,1... | collective-permute-start | bytes 786440 | tf_op jit(solution)/shard_map/ppermute | solution.py:21
  21.9 13.8 %collective-permute-start.6 = (bf16[128,512]{1,0:T(8,128)(2,1)S(1)}, bf16[128,512]{1,0:T(8,128)(2,1)S(1)}, u32[]{:S(2)}, u32[]{:S(2)}) collective-permute-start(bf16[128,512]{1,0:T(8,128)(2,1)S(1)} %copy-done.5), channel_id=1, source_target_pairs={{0,1},{1,0},{2,3},{3,2},{4,5},{5,4},{6,7},{7,6},{8,9},{9,8},{10,11... | collective-permute-start | bytes 393224 | tf_op jit(solution)/shard_map/ppermute | solution.py:21
  21.9 15.0 %collective-permute-start.8 = (bf16[128,512]{1,0:T(8,128)(2,1)S(1)}, bf16[128,512]{1,0:T(8,128)(2,1)S(1)}, u32[]{:S(2)}, u32[]{:S(2)}) collective-permute-start(bf16[128,512]{1,0:T(8,128)(2,1)S(1)} %copy-done.6), channel_id=1, source_target_pairs={{0,1},{1,0},{2,3},{3,2},{4,5},{5,4},{6,7},{7,6},{8,9},{9,8},{10,11... | collective-permute-start | bytes 393224 | tf_op jit(solution)/shard_map/ppermute | solution.py:21
  27.1 8.6 %collective-permute-start.18 = (bf16[384,512]{1,0:T(8,128)(2,1)S(1)}, bf16[384,512]{1,0:T(8,128)(2,1)}, u32[]{:S(2)}, u32[]{:S(2)}) collective-permute-start(bf16[384,512]{1,0:T(8,128)(2,1)S(1)} %constant_dynamic-update-slice_fusion.4.refs_0_), channel_id=1, source_target_pairs={{0,2},{2,0},{1,3},{3,1},{4,6},{6,4},{5,7},{7,5},{8,10},{10,8},{9,1... | collective-permute-start | bytes 1179656 | tf_op jit(solution)/shard_map/ppermute | solution.py:21
  28.8 8.8 %collective-permute-start.7 = (bf16[128,512]{1,0:T(8,128)(2,1)S(1)}, bf16[128,512]{1,0:T(8,128)(2,1)S(1)}, u32[]{:S(2)}, u32[]{:S(2)}) collective-permute-start(bf16[128,512]{1,0:T(8,128)(2,1)S(1)} %collective-permute-done.1.refs_2_), channel_id=1, source_target_pairs={{0,1},{1,0},{2,3},{3,2},{4,5},{5,4},{6,7},{7,6},{8,9},{9,8},{10,11... | collective-permute-start | bytes 393224 | tf_op jit(solution)/shard_map/ppermute | solution.py:21
  28.8 9.8 %collective-permute-start.9 = (bf16[128,512]{1,0:T(8,128)(2,1)S(1)}, bf16[128,512]{1,0:T(8,128)(2,1)S(1)}, u32[]{:S(2)}, u32[]{:S(2)}) collective-permute-start(bf16[128,512]{1,0:T(8,128)(2,1)S(1)} %collective-permute-done.2.refs_6_), channel_id=1, source_target_pairs={{0,1},{1,0},{2,3},{3,2},{4,5},{5,4},{6,7},{7,6},{8,9},{9,8},{10,11... | collective-permute-start | bytes 393224 | tf_op jit(solution)/shard_map/ppermute | solution.py:21
  35.7 11.3 %collective-permute-start = (bf16[256,512]{1,0:T(8,128)(2,1)S(1)}, bf16[256,512]{1,0:T(8,128)(2,1)S(1)}, u32[]{:S(2)}, u32[]{:S(2)}) collective-permute-start(bf16[256,512]{1,0:T(8,128)(2,1)S(1)} %constant_dynamic-update-slice_fusion.refs_0_), channel_id=1, source_target_pairs={{0,1},{1,0},{2,3},{3,2},{4,5},{5,4},{6,7},{7,6},{8,9},{9,8},{10,11... | collective-permute-start | bytes 786440 | tf_op jit(solution)/shard_map/ppermute | solution.py:21
  36.4 24.1 %collective-permute-start.13 = (bf16[384,512]{1,0:T(8,128)(2,1)S(1)}, bf16[384,512]{1,0:T(8,128)(2,1)S(1)}, u32[]{:S(2)}, u32[]{:S(2)}) collective-permute-start(bf16[384,512]{1,0:T(8,128)(2,1)S(1)} %constant_dynamic-update-slice_fusion.2.refs_4_), channel_id=1, source_target_pairs={{0,1},{1,0},{2,3},{3,2},{4,5},{5,4},{6,7},{7,6},{8,9},{9,8},{10,11... | collective-permute-start | bytes 1179656 | tf_op jit(solution)/shard_map/ppermute | solution.py:21
  37.6 23.6 %collective-permute-start.14 = (bf16[384,512]{1,0:T(8,128)(2,1)S(1)}, bf16[384,512]{1,0:T(8,128)(2,1)S(1)}, u32[]{:S(2)}, u32[]{:S(2)}) collective-permute-start(bf16[384,512]{1,0:T(8,128)(2,1)S(1)} %collective-permute-done.3.refs_6_), channel_id=1, source_target_pairs={{0,1},{1,0},{2,3},{3,2},{4,5},{5,4},{6,7},{7,6},{8,9},{9,8},{10,11... | collective-permute-start | bytes 1179656 | tf_op jit(solution)/shard_map/ppermute | solution.py:21
  37.6 23.5 %collective-permute-start.21 = (bf16[384,512]{1,0:T(8,128)(2,1)S(1)}, bf16[384,512]{1,0:T(8,128)(2,1)}, u32[]{:S(2)}, u32[]{:S(2)}) collective-permute-start(bf16[384,512]{1,0:T(8,128)(2,1)S(1)} %constant_dynamic-update-slice_fusion.6.refs_4_), channel_id=1, source_target_pairs={{0,2},{2,0},{1,3},{3,1},{4,6},{6,4},{5,7},{7,5},{8,10},{10,8},{9,1... | collective-permute-start | bytes 1179656 | tf_op jit(solution)/shard_map/ppermute | solution.py:21
  41.7 20.0 %copy-start = (bf16[128,512]{1,0:T(8,128)(2,1)S(1)}, bf16[128,512]{1,0:T(8,128)(2,1)}, u32[]{:S(2)}) copy-start(bf16[128,512]{1,0:T(8,128)(2,1)} %lat_ref.5) | copy-start | bytes 393220
  45.4 8.3 %collective-permute-start.10 = (bf16[128,512]{1,0:T(8,128)(2,1)S(1)}, bf16[128,512]{1,0:T(8,128)(2,1)S(1)}, u32[]{:S(2)}, u32[]{:S(2)}) collective-permute-start(bf16[128,512]{1,0:T(8,128)(2,1)S(1)} %get-tuple-element.15), channel_id=1, source_target_pairs={{0,4},{4,8},{8,12},{12,0},{1,5},{5,9},{9,13},{13,1},{2,6},{6,10},{... | collective-permute-start | bytes 393224 | tf_op jit(solution)/shard_map/ppermute | solution.py:21
  47.7 11.0 %collective-permute-start.11 = (bf16[128,512]{1,0:T(8,128)(2,1)S(1)}, bf16[128,512]{1,0:T(8,128)(2,1)S(1)}, u32[]{:S(2)}, u32[]{:S(2)}) collective-permute-start(bf16[128,512]{1,0:T(8,128)(2,1)S(1)} %get-tuple-element.16), channel_id=1, source_target_pairs={{0,8},{4,12},{8,0},{12,4},{1,9},{5,13},{9,1},{13,5},{2,10},{6,14},... | collective-permute-start | bytes 393224 | tf_op jit(solution)/shard_map/ppermute | solution.py:21
  53.7 6.9 %collective-permute-start.12 = (bf16[128,512]{1,0:T(8,128)(2,1)S(1)}, bf16[128,512]{1,0:T(8,128)(2,1)S(1)}, u32[]{:S(2)}, u32[]{:S(2)}) collective-permute-start(bf16[128,512]{1,0:T(8,128)(2,1)S(1)} %get-tuple-element.17), channel_id=1, source_target_pairs={{0,12},{4,0},{8,4},{12,8},{1,13},{5,1},{9,5},{13,9},{2,14},{6,2},{... | collective-permute-start | bytes 393224 | tf_op jit(solution)/shard_map/ppermute | solution.py:21
  58.7 4.6 %collective-permute-start.17 = (bf16[384,512]{1,0:T(8,128)(2,1)S(1)}, bf16[384,512]{1,0:T(8,128)(2,1)}, u32[]{:S(2)}, u32[]{:S(2)}) collective-permute-start(bf16[384,512]{1,0:T(8,128)(2,1)S(1)} %constant_dynamic-update-slice_fusion.4.refs_0_), channel_id=1, source_target_pairs={{0,1},{1,0},{2,3},{3,2},{4,5},{5,4},{6,7},{7,6},{8,9},{9,8},{10,11... | collective-permute-start | bytes 1179656 | tf_op jit(solution)/shard_map/ppermute | solution.py:21
  60.5 11.5 %collective-permute-start.20 = (bf16[384,512]{1,0:T(8,128)(2,1)S(1)}, bf16[384,512]{1,0:T(8,128)(2,1)}, u32[]{:S(2)}, u32[]{:S(2)}) collective-permute-start(bf16[384,512]{1,0:T(8,128)(2,1)S(1)} %constant_dynamic-update-slice_fusion.6.refs_4_), channel_id=1, source_target_pairs={{0,1},{1,0},{2,3},{3,2},{4,5},{5,4},{6,7},{7,6},{8,9},{9,8},{10,11... | collective-permute-start | bytes 1179656 | tf_op jit(solution)/shard_map/ppermute | solution.py:21
  60.5 11.6 %collective-permute-start.19 = (bf16[384,512]{1,0:T(8,128)(2,1)}, bf16[384,512]{1,0:T(8,128)(2,1)}, u32[]{:S(2)}, u32[]{:S(2)}) collective-permute-start(bf16[384,512]{1,0:T(8,128)(2,1)} %collective-permute-done.18.refs_2_), channel_id=1, source_target_pairs={{0,1},{1,0},{2,3},{3,2},{4,5},{5,4},{6,7},{7,6},{8,9},{9,8},{10,11... | collective-permute-start | bytes 1179656 | tf_op jit(solution)/shard_map/ppermute | solution.py:21
  61.0 11.1 %collective-permute-start.22 = (bf16[384,512]{1,0:T(8,128)(2,1)}, bf16[384,512]{1,0:T(8,128)(2,1)}, u32[]{:S(2)}, u32[]{:S(2)}) collective-permute-start(bf16[384,512]{1,0:T(8,128)(2,1)} %collective-permute-done.21.refs_6_), channel_id=1, source_target_pairs={{0,1},{1,0},{2,3},{3,2},{4,5},{5,4},{6,7},{7,6},{8,9},{9,8},{10,11... | collective-permute-start | bytes 1179656 | tf_op jit(solution)/shard_map/ppermute | solution.py:21
  61.1 3.7 %collective-permute-start.5 = (bf16[256,512]{1,0:T(8,128)(2,1)}, bf16[256,512]{1,0:T(8,128)(2,1)}, u32[]{:S(2)}, u32[]{:S(2)}) collective-permute-start(bf16[256,512]{1,0:T(8,128)(2,1)} %collective-permute-done.4.refs_2_), channel_id=1, source_target_pairs={{0,1},{1,0},{2,3},{3,2},{4,5},{5,4},{6,7},{7,6},{8,9},{9,8},{10,11... | collective-permute-start | bytes 786440 | tf_op jit(solution)/shard_map/ppermute | solution.py:21
  63.3 8.8 %collective-permute-start.15 = (bf16[64,512]{1,0:T(8,128)(2,1)S(1)}, bf16[64,512]{1,0:T(8,128)(2,1)S(1)}, u32[]{:S(2)}, u32[]{:S(2)}) collective-permute-start(bf16[64,512]{1,0:T(8,128)(2,1)S(1)} %get-tuple-element.18.tail_ref), channel_id=1, source_target_pairs={{0,4},{4,8},{8,12},{12,0},{1,5},{5,9},{9,13},{13,1},{2,6},{6,10},{... | collective-permute-start | bytes 196616 | tf_op jit(solution)/shard_map/ppermute | solution.py:21
  64.8 7.3 %collective-permute-start.16 = (bf16[64,512]{1,0:T(8,128)(2,1)S(1)}, bf16[64,512]{1,0:T(8,128)(2,1)S(1)}, u32[]{:S(2)}, u32[]{:S(2)}) collective-permute-start(bf16[64,512]{1,0:T(8,128)(2,1)S(1)} %get-tuple-element.19.head_ref), channel_id=1, source_target_pairs={{0,12},{4,0},{8,4},{12,8},{1,13},{5,1},{9,5},{13,9},{2,14},{6,2},{... | collective-permute-start | bytes 196616 | tf_op jit(solution)/shard_map/ppermute | solution.py:21
  (20 other events, 113.9 us)

commit v2 on v1

--- a/solution.py
+++ b/solution.py
@@ -21,36 +21,103 @@
     return lax.ppermute(value, axis, [(i, (i + step) % count) for i in range(count)])
 
 
-def spread(pack, *earlier):
+def spread(pack):
     bands, subs = lax.axis_size("band"), lax.axis_size("sub")
-    first = after(pack, *earlier) if earlier else pack
-    rows = [pack] + [shift(first, "band", step) for step in range(1, bands)]
+    rows = [pack] + [shift(pack, "band", step) for step in range(1, bands)]
     pieces = []
     for row in rows:
         pieces.append(row)
         pieces.extend(shift(row, "sub", step) for step in range(1, subs))
-    return pieces, rows[-1]
-
-
-def load_copies(pieces, parts, sems):
+    return pieces, rows[1:]
+
+
+def own_spread(pack):
+    return [pack] + [shift(pack, "sub", step) for step in range(1, lax.axis_size("sub"))]
+
+
+def relay(parts, *earlier):
+    pieces = []
+    for part in parts:
+        first = after(part, *earlier) if earlier else part
+        for far in range(lax.axis_size("groups")):
+            held = shift(first, "groups", far) if far else part
+            pieces.extend([held] + [shift(held, "sub", near) for near in range(1, lax.axis_size("sub"))])
+    return pieces
+
+
+def owner_of(band_step, sub_step):
     bands, subs = lax.axis_size("band"), lax.axis_size("sub")
-    band, sub = lax.axis_index("band"), lax.axis_index("sub")
+    return lax.rem(lax.axis_index("band") + bands - band_step, bands) * subs + lax.rem(
+        lax.axis_index("sub") + subs - sub_step, subs
+    )
+
+
+def load_copies(pieces, rows, whole, sems):
+    subs = lax.axis_size("sub")
     copies = []
     for index, piece in enumerate(pieces):
-        owner = lax.rem(band + bands - index // subs, bands) * subs + lax.rem(
-            sub + subs - index % subs, subs
-        )
+        owner = owner_of(index // subs, index % subs)
+        there = whole.at[pl.ds(pl.multiple_of(owner * rows, rows), rows)]
+        copies.append(pltpu.make_async_copy(piece, there, sems.at[index]))
+    return copies
+
+
+def pack_copies(pieces, sizes, wanted, sems):
+    subs, groups = lax.axis_size("sub"), lax.axis_size("groups")
+    block = sum(sizes) // groups
+    group = lax.axis_index("groups")
+    copies = []
+    slot = 0
+    for index, piece in enumerate(pieces):
+        if index < subs:
+            owner = owner_of(0, index)
+            held = [(part, part * block) for part in range(groups)]
+        else:
+            band_step, rest = divmod(index - subs, groups * subs)
+            far, near = divmod(rest, subs)
+            owner = owner_of(band_step + 1, near)
+            held = [(lax.rem(group + groups - far, groups), 0)]
+        for part, base in held:
+            for at, whole in wanted.items():
+                rows = sizes[at] // groups
+                start = base + sum(sizes[:at]) // groups
+                into = pl.multiple_of(owner * sizes[at] + part * rows, rows)
+                copies.append(
+                    pltpu.make_async_copy(
+                        piece.at[pl.ds(start, rows)], whole.at[pl.ds(into, rows)], sems.at[slot]
+                    )
+                )
+                slot += 1
+    return copies
+
+
+def pack_kernel(sets, *refs):
+    count = sum(sets)
+    sources, outs, sems = refs[:count], refs[count:-1], refs[-1]
+    groups = lax.axis_size("groups")
+    group = lax.axis_index("groups")
+    copies = []
+    first = 0
+    for at, amount in enumerate(sets):
+        pack, mine = outs[2 * at], outs[2 * at + 1]
         start = 0
-        for part, (rows, whole) in enumerate(parts):
-            copies.append(
-                pltpu.make_async_copy(
-                    piece.at[pl.ds(start, rows)],
-                    whole.at[pl.ds(pl.multiple_of(owner * rows, rows), rows)],
-                    sems.at[part, index],
+        for part in range(groups + 1):
+            into, chosen, base = (pack, part, start) if part < groups else (mine, group, 0)
+            for source in sources[first : first + amount]:
+                rows = source.shape[0] // groups
+                begin = chosen * rows if part < groups else pl.multiple_of(chosen * rows, rows)
+                copies.append(
+                    pltpu.make_async_copy(
+                        source.at[pl.ds(begin, rows)], into.at[pl.ds(base, rows)], sems.at[len(copies)]
+                    )
                 )
-            )
-            start += rows
-    return copies
+                base += rows
+            start = base
+        first += amount
+    for copy in copies:
+        copy.start()
+    for copy in copies:
+        copy.wait()
 
 
 def silu(values):
@@ -74,8 +141,8 @@
     outs = refs[2 * count : 2 * count + faces]
     w_in, w_hid, messages, sems_in, sems_hid = refs[2 * count + faces :]
     rows = w_in.shape[0] // count
-    first = load_copies(in_pieces, [(rows, w_in)], sems_in)
-    second = load_copies(hid_pieces, [(rows, w_hid)], sems_hid)
+    first = load_copies(in_pieces, rows, w_in, sems_in)
+    second = load_copies(hid_pieces, rows, w_hid, sems_hid)
     for copy in first + second:
         copy.start()
     for copy in first + second:
@@ -96,11 +163,9 @@
             out[...] = sums[face * mesh_rows : (face + 1) * mesh_rows].astype(out.dtype)
 
 
-def grid_kernel(count, lat_ref, *refs):
-    pieces = refs[:count]
-    out_ref, w_in, w_hid, sems = refs[count:]
-    rows = w_in.shape[0] // count
-    copies = load_copies(pieces, [(rows, w_in), (rows, w_hid)], sems)
+def grid_kernel(sizes, lat_ref, *refs):
+    pieces, (out_ref, w_in, w_hid, sems) = refs[:-4], refs[-4:]
+    copies = pack_copies(pieces, sizes, {2: w_in, 3: w_hid}, sems)
     for copy in copies:
         copy.start()
     for copy in copies:
@@ -114,13 +179,11 @@
         out_ref[here] = out.astype(jnp.bfloat16)
 
 
-def node_kernel(count, faces, lat_ref, *refs):
-    sums, pieces = refs[:faces], refs[faces : faces + count]
-    head_ref, tail_ref, w_in, w_hid, sems = refs[faces + count :]
+def node_kernel(sizes, faces, lat_ref, *refs):
+    sums, pieces = refs[:faces], refs[faces:-5]
+    head_ref, tail_ref, w_in, w_hid, sems = refs[-5:]
     width = lat_ref.shape[1]
-    copies = load_copies(
-        pieces, [(w_in.shape[0] // count, w_in), (w_hid.shape[0] // count, w_hid)], sems
-    )
+    copies = pack_copies(pieces, sizes, {0: w_in, 1: w_hid}, sems)
     for copy in copies:
         copy.start()
     collected = sums[0][...]
@@ -138,15 +201,10 @@
     tail_ref[...] = mid[half:]
 
 
-def edge_kernel(count, nbr_ref, before_ref, head_ref, tail_ref, after_ref, *refs):
-    proc, upd = refs[:count], refs[count : 2 * count]
-    out_ref, p_in, p_hid, u_in, u_hid, sems_p, sems_u = refs[2 * count :]
-    copies_p = load_copies(
-        proc, [(p_in.shape[0] // count, p_in), (p_hid.shape[0] // count, p_hid)], sems_p
-    )
-    copies_u = load_copies(
-        upd, [(u_in.shape[0] // count, u_in), (u_hid.shape[0] // count, u_hid)], sems_u
-    )
+def edge_kernel(sizes, nbr_ref, before_ref, head_ref, tail_ref, after_ref, *refs):
+    pieces, (out_ref, p_in, p_hid, u_in, u_hid, sems_p, sems_u) = refs[:-7], refs[-7:]
+    copies_p = pack_copies(pieces, sizes, {0: p_in, 1: p_hid}, sems_p)
+    copies_u = pack_copies(pieces, sizes, {2: u_in, 3: u_hid}, sems_u)
     for copy in copies_p + copies_u:
         copy.start()
     rows, fanin = nbr_ref.shape
@@ -209,8 +267,11 @@
     def matrix(weight):
         return pltpu.VMEM((weight.shape[0] * count, weight.shape[1]), bf16)
 
+    groups, subs, bands = lax.axis_size("groups"), lax.axis_size("sub"), lax.axis_size("band")
+    copies = groups * count
+
     def sems(parts):
-        return pltpu.SemaphoreType.DMA((parts, count))
+        return pltpu.SemaphoreType.DMA((parts,))
 
     def cost(rows, depth):
         return pl.CostEstimate(
@@ -219,14 +280,26 @@
             transcendentals=rows * width,
         )
 
-    enc_in, enc_in_last = spread(enc_w1)
-    enc_hid, enc_hid_last = spread(enc_w2)
-    node, node_last = spread(
-        jnp.concatenate([node_w1, node_w2], axis=0), enc_in_last, enc_hid_last
-    )
-    grid, grid_last = spread(jnp.concatenate([grid_w1, grid_w2], axis=0), node_last)
-    proc, proc_last = spread(jnp.concatenate([proc_w1, proc_w2], axis=0), grid_last)
-    upd, _ = spread(jnp.concatenate([upd_w1, upd_w2], axis=0), proc_last)
+    sets = ((node_w1, node_w2, grid_w1, grid_w2), (proc_w1, proc_w2, upd_w1, upd_w2))
+    sizes = [[weight.shape[0] for weight in one] for one in sets]
+    early, early_mine, late, late_mine = pl.pallas_call(
+        functools.partial(pack_kernel, [len(one) for one in sets]),
+        out_shape=[
+            jax.ShapeDtypeStruct((sum(one) // part, width), bf16)
+            for one in sizes
+            for part in (1, groups)
+        ],
+        in_specs=[ANY] * 8,
+        out_specs=[ANY] * 4,
+        scratch_shapes=[sems(8 * (groups + 1))],
+        name="pack",
+    )(*sets[0], *sets[1])
+
+    enc_in, enc_in_far = spread(enc_w1)
+    enc_hid, enc_hid_far = spread(enc_w2)
+    early_near, late_near = own_spread(early), own_spread(late)
+    early_sent = after(early_mine, *enc_in_far, *enc_hid_far)
+    early_far = [shift(early_sent, "band", step) for step in range(1, bands)]
 
     me = lax.axis_index("face")
     distance = lax.rem(grid_route[:, 0] - me + faces, faces)
@@ -244,57 +317,61 @@
             matrix(enc_w1),
             matrix(enc_w2),
             pltpu.VMEM((grid_rows, width), bf16),
-            sems(1),
-            sems(1),
+            sems(count),
+            sems(count),
         ],
         compiler_params=pltpu.CompilerParams(vmem_limit_bytes=32 * MIB),
         cost_estimate=cost(grid_rows, 3 * width),
         name="encode",
     )(targets, grid_lat, *enc_in, *enc_hid)
+    early_all = early_near + relay(early_far, sums[0])
+    late_sent = after(late_mine, sums[0], *early_far)
+    late_far = [shift(late_sent, "band", step) for step in range(1, bands)]
     arrived = [sums[0]] + [shift(sums[step], "face", step) for step in range(1, faces)]
 
     grid_out = pl.pallas_call(
-        functools.partial(grid_kernel, count),
+        functools.partial(grid_kernel, sizes[0]),
         out_shape=jax.ShapeDtypeStruct(grid_lat.shape, bf16),
-        in_specs=[VMEM] + [ANY] * count,
+        in_specs=[VMEM] + [ANY] * len(early_all),
         out_specs=VMEM,
-        scratch_shapes=[matrix(grid_w1), matrix(grid_w2), sems(2)],
+        scratch_shapes=[matrix(grid_w1), matrix(grid_w2), sems(2 * copies)],
         compiler_params=pltpu.CompilerParams(vmem_limit_bytes=32 * MIB),
         cost_estimate=cost(grid_rows, 2 * width),
         name="grid_update",
-    )(grid_lat, *grid)
+    )(after(grid_lat, *late_far), *early_all)
 
     half = (mesh_rows // 2, width)
     head, tail = pl.pallas_call(
-        functools.partial(node_kernel, count, faces),
+        functools.partial(node_kernel, sizes[0], faces),
         out_shape=[jax.ShapeDtypeStruct(half, bf16)] * 2,
-        in_specs=[VMEM] * (1 + faces) + [ANY] * count,
+        in_specs=[VMEM] * (1 + faces) + [ANY] * len(early_all),
         out_specs=[VMEM] * 2,
-        scratch_shapes=[matrix(node_w1), matrix(node_w2), sems(2)],
+        scratch_shapes=[matrix(node_w1), matrix(node_w2), sems(2 * copies)],
         compiler_params=pltpu.CompilerParams(vmem_limit_bytes=32 * MIB),
         cost_estimate=cost(mesh_rows, 3 * width),
         name="node_update",
-    )(mesh_lat, *arrived, *node)
+    )(mesh_lat, *arrived, *early_all)
 
     before = shift(tail, "face", 1)
     behind = shift(head, "face", faces - 1)
+    late_all = late_near + relay(late_far)
     mesh_out = pl.pallas_call(
-        functools.partial(edge_kernel, count),
+        functools.partial(edge_kernel, sizes[1]),
         out_shape=jax.ShapeDtypeStruct(mesh_lat.shape, bf16),
-        in_specs=[VMEM] * 5 + [ANY] * (2 * count),
+        in_specs=[VMEM] * 5 + [ANY] * len(late_all),
         out_specs=VMEM,
         scratch_shapes=[
             matrix(proc_w1),
             matrix(proc_w2),
             matrix(upd_w1),
             matrix(upd_w2),
-            sems(2),
-            sems(2),
+            sems(2 * copies),
+            sems(2 * copies),
         ],
         compiler_params=pltpu.CompilerParams(vmem_limit_bytes=32 * MIB),
         cost_estimate=cost(mesh_rows * mesh_nbr.shape[1], 3 * width),
         name="edge_update",
-    )(mesh_nbr, before, head, tail, behind, *proc, *upd)
+    )(mesh_nbr, before, head, tail, behind, *late_all)
     return (grid_out, mesh_out)
 
 

time: 77.4 us -> 127 us (1.64)
  Pallas kernels: 15.1 us -> 83.7 us
  waiting for transfers between devices: 32.8 us -> 20.1 us
  local copies, waits for them, and re-layouts: 7.16 us -> 0.16 us
    pallas_call x3 -> x4, Pallas kernels: 11.4 us -> 80 us  [the longest x1 66.8 us: shards(): pl.pallas_call(functools.partial(pack_kernel, [len(one) for one in sets])...]
    ppermute x23 -> x21, waiting for transfers between devices: 32.8 us -> 20.1 us  [shift(): lax.ppermute(value, axis, [(i, (i + step) % count) for i in range(count)])]
    unnamed x47 -> x21, local copies, waits for them, and re-layouts: 7.12 us -> 0.16 us
    ppermute x23 -> x21, starting transfers between devices: 21.1 us -> 22.3 us  [shift(): lax.ppermute(value, axis, [(i, (i + step) % count) for i in range(count)])]
  transfers between devices with their start and end apart: 23 -> 21, of which waited for: 8 -> 8; matrix products, arithmetic and copies ran while one was open for 2% -> 0% of each run, Pallas kernels for 13% -> 61%
where the time goes in v2:
time: 127 us
  Pallas kernels  83.7 us (66%)
  starting transfers between devices  22.3 us (18%)
  waiting for transfers between devices  20.1 us (16%)
    pallas_call x1, Pallas kernels, shards(): pl.pallas_call(functools.partial(pack_kernel, [len(one) for one in sets])...  66.8 us
    ppermute x21, starting transfers between devices, shift(): lax.ppermute(value, axis, [(i, (i + step) % count) for i in range(count)])  22.3 us
    ppermute x21, waiting for transfers between devices, shift(): lax.ppermute(value, axis, [(i, (i + step) % count) for i in range(count)])  20.1 us
    pallas_call x1, Pallas kernels, shards(): pl.pallas_call(functools.partial(edge_kernel, sizes[1]), out_shape=jax.Sh...  5.53 us
    pallas_call x1, Pallas kernels, shards(): pl.pallas_call(functools.partial(grid_kernel, sizes[0]), out_shape=jax.Sh...  4.51 us
    pallas_call x1, Pallas kernels, shards(): pl.pallas_call(functools.partial(encode_kernel, count, faces, mesh_rows),...  3.72 us
    pallas_call x1, Pallas kernels, shards(): pl.pallas_call(functools.partial(node_kernel, sizes[0], faces), out_shape...  3.15 us
  transfers between devices with their start and end apart: 21, of which 8 were waited for; matrix products, arithmetic and copies ran while one was open for 0% of the time, Pallas kernels for 61%

profile of v2, /device:TPU:0, one launch (start us, length us, event | category | flops | bytes accessed | tf_op | source)
XLA Modules:
  0.0 127.2 jit_solution(13543236082854847207)
XLA Ops:
  0.6 0.5 collective-permute-start
  1.2 2.6 %collective-permute-start.1 = (bf16[128,512]{1,0:T(8,128)(2,1)}, bf16[128,512]{1,0:T(8,128)(2,1)S(1)}, u32[]{:S(2)}, u32[]{:S(2)}) collective-permute-start(bf16[128,512]{1,0:T(8,128)(2,1)} %refs_0_.3), channel_id=1, source_target_pairs={{0,2},{2,0},{1,3},{3,1},{4,6},{6,4},{5,7},{7,5},{8,10},{10,8},{9,1... | collective-permute-start | bytes 393224 | tf_op jit(solution)/shard_map/ppermute | solution.py:21
  4.2 66.8 %pack.1 = (bf16[640,512]{1,0:T(8,128)(2,1)}, bf16[320,512]{1,0:T(8,128)(2,1)}, bf16[768,512]{1,0:T(8,128)(2,1)}, bf16[384,512]{1,0:T(8,128)(2,1)}) custom-call(bf16[256,512]{1,0:T(8,128)(2,1)} %refs_0_.2, bf16[128,512]{1,0:T(8,128)(2,1)} %refs_1_.1, bf16[128,512]{1,0:T(8,128)(2,1)} %refs_2_.1, bf16[128,512]{1,0:T(8,128)(2,1)} %refs_3_.1, ...), custom_call_target="tpu_custom_call" | custom-call | tf_op jit(solution)/shard_map/pack/pallas_call | solution.py:285
  71.1 1.8 %collective-permute-start.6 = (bf16[320,512]{1,0:T(8,128)(2,1)}, bf16[320,512]{1,0:T(8,128)(2,1)S(1)}, u32[]{:S(2)}, u32[]{:S(2)}) collective-permute-start(bf16[320,512]{1,0:T(8,128)(2,1)} %get-tuple-element.19), channel_id=1, source_target_pairs={{0,2},{2,0},{1,3},{3,1},{4,6},{6,4},{5,7},{7,5},{8,10},{10,8},{9,1... | collective-permute-start | bytes 983048 | tf_op jit(solution)/shard_map/ppermute | solution.py:21
  72.9 0.5 collective-permute-start.5
  73.4 0.8 collective-permute-done.2.refs_3_
  74.5 3.7 %encode.1 = (f32[128,512]{1,0:T(8,128)S(1)}, bf16[128,512]{1,0:T(8,128)(2,1)S(1)}, bf16[128,512]{1,0:T(8,128)(2,1)S(1)}, bf16[128,512]{1,0:T(8,128)(2,1)S(1)}) custom-call(s32[1,1024]{1,0:T(1,128)S(1)} %bitcast.2, bf16[1024,512]{1,0:T(8,128)(2,1)S(1)} %copy-done.1, bf16[128,512]{1,0:T(8,128)(2,1)S(1)} %copy-done.4, ...), custom_call_target="tpu_custom_call" | custom-call | flops 1610612736 | bytes 2621440 | tf_op jit(solution)/shard_map/encode/pallas_call | solution.py:309
  78.2 2.8 %collective-permute-done.6.refs_2_.refs_6_ = bf16[320,512]{1,0:T(8,128)(2,1)S(1)} collective-permute-done((bf16[320,512]{1,0:T(8,128)(2,1)}, bf16[320,512]{1,0:T(8,128)(2,1)S(1)}, u32[]{:S(2)}, u32[]{:S(2)}) %collective-permute-start.6) | collective-permute-done | bytes 327712 | tf_op jit(solution)/shard_map/ppermute | solution.py:21
  81.0 1.7 %collective-permute-start.7 = (bf16[384,512]{1,0:T(8,128)(2,1)S(1)}, bf16[384,512]{1,0:T(8,128)(2,1)}, u32[]{:S(2)}, u32[]{:S(2)}) collective-permute-start(bf16[384,512]{1,0:T(8,128)(2,1)S(1)} %copy-done.9), channel_id=1, source_target_pairs={{0,2},{2,0},{1,3},{3,1},{4,6},{6,4},{5,7},{7,5},{8,10},{10,8},{9,1... | collective-permute-start | bytes 1179656 | tf_op jit(solution)/shard_map/ppermute | solution.py:21
  82.8 1.6 %collective-permute-start.12 = (bf16[128,512]{1,0:T(8,128)(2,1)S(1)}, bf16[128,512]{1,0:T(8,128)(2,1)S(1)}, u32[]{:S(2)}, u32[]{:S(2)}) collective-permute-start(bf16[128,512]{1,0:T(8,128)(2,1)S(1)} %get-tuple-element.24), channel_id=1, source_target_pairs={{0,4},{4,8},{8,12},{12,0},{1,5},{5,9},{9,13},{13,1},{2,6},{6,10},{... | collective-permute-start | bytes 393224 | tf_op jit(solution)/shard_map/ppermute | solution.py:21
  84.6 6.8 %collective-permute-done.7.refs_2_ = bf16[384,512]{1,0:T(8,128)(2,1)} collective-permute-done((bf16[384,512]{1,0:T(8,128)(2,1)S(1)}, bf16[384,512]{1,0:T(8,128)(2,1)}, u32[]{:S(2)}, u32[]{:S(2)}) %collective-permute-start.7) | collective-permute-done | bytes 393248 | tf_op jit(solution)/shard_map/ppermute | solution.py:21
  91.4 1.7 %collective-permute-start.19 = (bf16[384,512]{1,0:T(8,128)(2,1)}, bf16[384,512]{1,0:T(8,128)(2,1)}, u32[]{:S(2)}, u32[]{:S(2)}) collective-permute-start(bf16[384,512]{1,0:T(8,128)(2,1)} %collective-permute-done.7.refs_2_), channel_id=1, source_target_pairs={{0,16},{16,0},{1,17},{17,1},{2,18},{18,2},{3,19},{19,3},{4,20},{20... | collective-permute-start | bytes 1179656 | tf_op jit(solution)/shard_map/ppermute | solution.py:21
  93.5 2.8 %collective-permute-start.13 = (bf16[128,512]{1,0:T(8,128)(2,1)S(1)}, bf16[128,512]{1,0:T(8,128)(2,1)S(1)}, u32[]{:S(2)}, u32[]{:S(2)}) collective-permute-start(bf16[128,512]{1,0:T(8,128)(2,1)S(1)} %get-tuple-element.25), channel_id=1, source_target_pairs={{0,8},{4,12},{8,0},{12,4},{1,9},{5,13},{9,1},{13,5},{2,10},{6,14},... | collective-permute-start | bytes 393224 | tf_op jit(solution)/shard_map/ppermute | solution.py:21
  96.3 4.6 %collective-permute-done.13.refs_2_ = bf16[128,512]{1,0:T(8,128)(2,1)S(1)} collective-permute-done((bf16[128,512]{1,0:T(8,128)(2,1)S(1)}, bf16[128,512]{1,0:T(8,128)(2,1)S(1)}, u32[]{:S(2)}, u32[]{:S(2)}) %collective-permute-start.13) | collective-permute-done | bytes 131104 | tf_op jit(solution)/shard_map/ppermute | solution.py:21
  100.8 3.6 %collective-permute-start.14 = (bf16[128,512]{1,0:T(8,128)(2,1)S(1)}, bf16[128,512]{1,0:T(8,128)(2,1)S(1)}, u32[]{:S(2)}, u32[]{:S(2)}) collective-permute-start(bf16[128,512]{1,0:T(8,128)(2,1)S(1)} %get-tuple-element.26), channel_id=1, source_target_pairs={{0,12},{4,0},{8,4},{12,8},{1,13},{5,1},{9,5},{13,9},{2,14},{6,2},{... | collective-permute-start | bytes 393224 | tf_op jit(solution)/shard_map/ppermute | solution.py:21
  104.4 2.5 %collective-permute-done.14.refs_3_ = bf16[128,512]{1,0:T(8,128)(2,1)S(1)} collective-permute-done((bf16[128,512]{1,0:T(8,128)(2,1)S(1)}, bf16[128,512]{1,0:T(8,128)(2,1)S(1)}, u32[]{:S(2)}, u32[]{:S(2)}) %collective-permute-start.14) | collective-permute-done | bytes 131104 | tf_op jit(solution)/shard_map/ppermute | solution.py:21
  107.0 1.0 collective-permute-done.10.refs_4_.refs_8_
  108.0 0.5 collective-permute-start.18
  108.7 1.3 %collective-permute-done.11.refs_5_.refs_9_ = bf16[320,512]{1,0:T(8,128)(2,1)S(1)} collective-permute-done((bf16[320,512]{1,0:T(8,128)(2,1)S(1)}, bf16[320,512]{1,0:T(8,128)(2,1)S(1)}, u32[]{:S(2)}, u32[]{:S(2)}) %collective-permute-start.11) | collective-permute-done | bytes 327712 | tf_op jit(solution)/shard_map/ppermute | solution.py:21
  110.0 3.1 %node_update.1 = (bf16[64,512]{1,0:T(8,128)(2,1)S(1)}, bf16[64,512]{1,0:T(8,128)(2,1)S(1)}) custom-call(bf16[128,512]{1,0:T(8,128)(2,1)S(1)} %copy-done.3, f32[128,512]{1,0:T(8,128)S(1)} %get-tuple-element.17.refs_0_, bf16[128,512]{1,0:T(8,128)(2,1)S(1)} %collective-permute-done.12.refs_1_, bf16[128,512]{1,0:T(8,128)(2,1)S(1)} %collective-permute-done.13.refs_2_, ...), custom_call_target="tpu_custom_call" | custom-call | flops 201326592 | bytes 1703936 | tf_op jit(solution)/shard_map/node_update/pallas_call | solution.py:344
  113.2 1.8 %collective-permute-start.15 = (bf16[64,512]{1,0:T(8,128)(2,1)S(1)}, bf16[64,512]{1,0:T(8,128)(2,1)S(1)}, u32[]{:S(2)}, u32[]{:S(2)}) collective-permute-start(bf16[64,512]{1,0:T(8,128)(2,1)S(1)} %get-tuple-element.27.tail_ref), channel_id=1, source_target_pairs={{0,4},{4,8},{8,12},{12,0},{1,5},{5,9},{9,13},{13,1},{2,6},{6,10},{... | collective-permute-start | bytes 196616 | tf_op jit(solution)/shard_map/ppermute | solution.py:21
  115.0 2.1 %collective-permute-start.16 = (bf16[64,512]{1,0:T(8,128)(2,1)S(1)}, bf16[64,512]{1,0:T(8,128)(2,1)S(1)}, u32[]{:S(2)}, u32[]{:S(2)}) collective-permute-start(bf16[64,512]{1,0:T(8,128)(2,1)S(1)} %get-tuple-element.28.head_ref), channel_id=1, source_target_pairs={{0,12},{4,0},{8,4},{12,8},{1,13},{5,1},{9,5},{13,9},{2,14},{6,2},{... | collective-permute-start | bytes 196616 | tf_op jit(solution)/shard_map/ppermute | solution.py:21
  117.1 4.5 %grid_update.1 = bf16[1024,512]{1,0:T(8,128)(2,1)} custom-call(bf16[1024,512]{1,0:T(8,128)(2,1)S(1)} %copy-done.2, bf16[640,512]{1,0:T(8,128)(2,1)S(1)} %copy-done, bf16[640,512]{1,0:T(8,128)(2,1)S(1)} %collective-permute-done.8.refs_1_.refs_5_, bf16[320,512]{1,0:T(8,128)(2,1)S(1)} %collective-permute-done.6.refs_2_.refs_6_, ...), custom_call_target="tpu_custom_call" | custom-call | flops 1073741824 | bytes 2097152 | tf_op jit(solution)/shard_map/grid_update/pallas_call | solution.py:332
  121.7 5.5 %edge_update.1 = bf16[128,512]{1,0:T(8,128)(2,1)} custom-call(s32[128,6]{1,0:T(8,128)S(1)} %copy.17.nbr_ref, bf16[64,512]{1,0:T(8,128)(2,1)S(1)} %collective-permute-done.15.before_ref, bf16[64,512]{1,0:T(8,128)(2,1)S(1)} %get-tuple-element.28.head_ref, bf16[64,512]{1,0:T(8,128)(2,1)S(1)} %get-tuple-element.27.tail_ref, ...), custom_call_target="tpu_custom_call" | custom-call | flops 1207959552 | bytes 2359296 | tf_op jit(solution)/shard_map/edge_update/pallas_call | solution.py:358
  (46 shorter events, 1.4 us)
Async XLA Ops:
  0.6 73.8 %copy-start.1 = (bf16[1024,512]{1,0:T(8,128)(2,1)S(1)}, bf16[1024,512]{1,0:T(8,128)(2,1)}, u32[]{:S(2)}) copy-start(bf16[1024,512]{1,0:T(8,128)(2,1)} %lat_ref.3) | copy-start | bytes 3145732
  0.6 72.8 %collective-permute-start = (bf16[128,512]{1,0:T(8,128)(2,1)}, bf16[128,512]{1,0:T(8,128)(2,1)S(1)}, u32[]{:S(2)}, u32[]{:S(2)}) collective-permute-start(bf16[128,512]{1,0:T(8,128)(2,1)} %refs_0_.3), channel_id=1, source_target_pairs={{0,1},{1,0},{2,3},{3,2},{4,5},{5,4},{6,7},{7,6},{8,9},{9,8},{10,11... | collective-permute-start | bytes 393224 | tf_op jit(solution)/shard_map/ppermute | solution.py:21
  1.2 69.9 %collective-permute-start.1 = (bf16[128,512]{1,0:T(8,128)(2,1)}, bf16[128,512]{1,0:T(8,128)(2,1)S(1)}, u32[]{:S(2)}, u32[]{:S(2)}) collective-permute-start(bf16[128,512]{1,0:T(8,128)(2,1)} %refs_0_.3), channel_id=1, source_target_pairs={{0,2},{2,0},{1,3},{3,1},{4,6},{6,4},{5,7},{7,5},{8,10},{10,8},{9,1... | collective-permute-start | bytes 393224 | tf_op jit(solution)/shard_map/ppermute | solution.py:21
  3.7 69.7 %collective-permute-start.3 = (bf16[128,512]{1,0:T(8,128)(2,1)}, bf16[128,512]{1,0:T(8,128)(2,1)S(1)}, u32[]{:S(2)}, u32[]{:S(2)}) collective-permute-start(bf16[128,512]{1,0:T(8,128)(2,1)} %refs_4_.3), channel_id=1, source_target_pairs={{0,1},{1,0},{2,3},{3,2},{4,5},{5,4},{6,7},{7,6},{8,9},{9,8},{10,11... | collective-permute-start | bytes 393224 | tf_op jit(solution)/shard_map/ppermute | solution.py:21
  3.9 67.2 %collective-permute-start.4 = (bf16[128,512]{1,0:T(8,128)(2,1)}, bf16[128,512]{1,0:T(8,128)(2,1)S(1)}, u32[]{:S(2)}, u32[]{:S(2)}) collective-permute-start(bf16[128,512]{1,0:T(8,128)(2,1)} %refs_4_.3), channel_id=1, source_target_pairs={{0,2},{2,0},{1,3},{3,1},{4,6},{6,4},{5,7},{7,5},{8,10},{10,8},{9,1... | collective-permute-start | bytes 393224 | tf_op jit(solution)/shard_map/ppermute | solution.py:21
  4.2 70.3 %copy-start.4 = (bf16[128,512]{1,0:T(8,128)(2,1)S(1)}, bf16[128,512]{1,0:T(8,128)(2,1)}, u32[]{:S(2)}) copy-start(bf16[128,512]{1,0:T(8,128)(2,1)} %refs_0_.3) | copy-start | bytes 393220
  4.2 70.3 %copy-start.5 = (bf16[128,512]{1,0:T(8,128)(2,1)S(1)}, bf16[128,512]{1,0:T(8,128)(2,1)}, u32[]{:S(2)}) copy-start(bf16[128,512]{1,0:T(8,128)(2,1)} %refs_4_.3) | copy-start | bytes 393220
  71.1 10.0 %collective-permute-start.6 = (bf16[320,512]{1,0:T(8,128)(2,1)}, bf16[320,512]{1,0:T(8,128)(2,1)S(1)}, u32[]{:S(2)}, u32[]{:S(2)}) collective-permute-start(bf16[320,512]{1,0:T(8,128)(2,1)} %get-tuple-element.19), channel_id=1, source_target_pairs={{0,2},{2,0},{1,3},{3,1},{4,6},{6,4},{5,7},{7,5},{8,10},{10,8},{9,1... | collective-permute-start | bytes 983048 | tf_op jit(solution)/shard_map/ppermute | solution.py:21
  72.9 1.3 %collective-permute-start.2 = (bf16[128,512]{1,0:T(8,128)(2,1)S(1)}, bf16[128,512]{1,0:T(8,128)(2,1)S(1)}, u32[]{:S(2)}, u32[]{:S(2)}) collective-permute-start(bf16[128,512]{1,0:T(8,128)(2,1)S(1)} %collective-permute-done.1.refs_2_), channel_id=1, source_target_pairs={{0,1},{1,0},{2,3},{3,2},{4,5},{5,4},{6,7},{7,6},{8,9},{9,8},{10,11... | collective-permute-start | bytes 393224 | tf_op jit(solution)/shard_map/ppermute | solution.py:21
  72.9 1.5 %collective-permute-start.5 = (bf16[128,512]{1,0:T(8,128)(2,1)S(1)}, bf16[128,512]{1,0:T(8,128)(2,1)S(1)}, u32[]{:S(2)}, u32[]{:S(2)}) collective-permute-start(bf16[128,512]{1,0:T(8,128)(2,1)S(1)} %collective-permute-done.4.refs_6_), channel_id=1, source_target_pairs={{0,1},{1,0},{2,3},{3,2},{4,5},{5,4},{6,7},{7,6},{8,9},{9,8},{10,11... | collective-permute-start | bytes 393224 | tf_op jit(solution)/shard_map/ppermute | solution.py:21
  81.0 10.4 %collective-permute-start.7 = (bf16[384,512]{1,0:T(8,128)(2,1)S(1)}, bf16[384,512]{1,0:T(8,128)(2,1)}, u32[]{:S(2)}, u32[]{:S(2)}) collective-permute-start(bf16[384,512]{1,0:T(8,128)(2,1)S(1)} %copy-done.9), channel_id=1, source_target_pairs={{0,2},{2,0},{1,3},{3,1},{4,6},{6,4},{5,7},{7,5},{8,10},{10,8},{9,1... | collective-permute-start | bytes 1179656 | tf_op jit(solution)/shard_map/ppermute | solution.py:21
  82.8 25.2 %collective-permute-start.8 = (bf16[640,512]{1,0:T(8,128)(2,1)S(1)}, bf16[640,512]{1,0:T(8,128)(2,1)S(1)}, u32[]{:S(2)}, u32[]{:S(2)}) collective-permute-start(bf16[640,512]{1,0:T(8,128)(2,1)S(1)} %copy-done), channel_id=1, source_target_pairs={{0,1},{1,0},{2,3},{3,2},{4,5},{5,4},{6,7},{7,6},{8,9},{9,8},{10,11... | collective-permute-start | bytes 1966088 | tf_op jit(solution)/shard_map/ppermute | solution.py:21
  82.8 10.7 %collective-permute-start.12 = (bf16[128,512]{1,0:T(8,128)(2,1)S(1)}, bf16[128,512]{1,0:T(8,128)(2,1)S(1)}, u32[]{:S(2)}, u32[]{:S(2)}) collective-permute-start(bf16[128,512]{1,0:T(8,128)(2,1)S(1)} %get-tuple-element.24), channel_id=1, source_target_pairs={{0,4},{4,8},{8,12},{12,0},{1,5},{5,9},{9,13},{13,1},{2,6},{6,10},{... | collective-permute-start | bytes 393224 | tf_op jit(solution)/shard_map/ppermute | solution.py:21
  84.4 37.2 %collective-permute-start.17 = (bf16[768,512]{1,0:T(8,128)(2,1)}, bf16[768,512]{1,0:T(8,128)(2,1)}, u32[]{:S(2)}, u32[]{:S(2)}) collective-permute-start(bf16[768,512]{1,0:T(8,128)(2,1)} %get-tuple-element.29.refs_0_), channel_id=1, source_target_pairs={{0,1},{1,0},{2,3},{3,2},{4,5},{5,4},{6,7},{7,6},{8,9},{9,8},{10,11... | collective-permute-start | bytes 2359304 | tf_op jit(solution)/shard_map/ppermute | solution.py:21
  91.4 17.1 %collective-permute-start.19 = (bf16[384,512]{1,0:T(8,128)(2,1)}, bf16[384,512]{1,0:T(8,128)(2,1)}, u32[]{:S(2)}, u32[]{:S(2)}) collective-permute-start(bf16[384,512]{1,0:T(8,128)(2,1)} %collective-permute-done.7.refs_2_), channel_id=1, source_target_pairs={{0,16},{16,0},{1,17},{17,1},{2,18},{18,2},{3,19},{19,3},{4,20},{20... | collective-permute-start | bytes 1179656 | tf_op jit(solution)/shard_map/ppermute | solution.py:21
  93.2 14.8 %collective-permute-start.10 = (bf16[320,512]{1,0:T(8,128)(2,1)S(1)}, bf16[320,512]{1,0:T(8,128)(2,1)S(1)}, u32[]{:S(2)}, u32[]{:S(2)}) collective-permute-start(bf16[320,512]{1,0:T(8,128)(2,1)S(1)} %collective-permute-done.6.refs_2_.refs_6_), channel_id=1, source_target_pairs={{0,16},{16,0},{1,17},{17,1},{2,18},{18,2},{3,19},{19,3},{4,20},{20... | collective-permute-start | bytes 983048 | tf_op jit(solution)/shard_map/ppermute | solution.py:21
  93.5 7.4 %collective-permute-start.13 = (bf16[128,512]{1,0:T(8,128)(2,1)S(1)}, bf16[128,512]{1,0:T(8,128)(2,1)S(1)}, u32[]{:S(2)}, u32[]{:S(2)}) collective-permute-start(bf16[128,512]{1,0:T(8,128)(2,1)S(1)} %get-tuple-element.25), channel_id=1, source_target_pairs={{0,8},{4,12},{8,0},{12,4},{1,9},{5,13},{9,1},{13,5},{2,10},{6,14},... | collective-permute-start | bytes 393224 | tf_op jit(solution)/shard_map/ppermute | solution.py:21
  100.8 6.1 %collective-permute-start.14 = (bf16[128,512]{1,0:T(8,128)(2,1)S(1)}, bf16[128,512]{1,0:T(8,128)(2,1)S(1)}, u32[]{:S(2)}, u32[]{:S(2)}) collective-permute-start(bf16[128,512]{1,0:T(8,128)(2,1)S(1)} %get-tuple-element.26), channel_id=1, source_target_pairs={{0,12},{4,0},{8,4},{12,8},{1,13},{5,1},{9,5},{13,9},{2,14},{6,2},{... | collective-permute-start | bytes 393224 | tf_op jit(solution)/shard_map/ppermute | solution.py:21
  107.0 1.8 %collective-permute-start.9 = (bf16[320,512]{1,0:T(8,128)(2,1)S(1)}, bf16[320,512]{1,0:T(8,128)(2,1)S(1)}, u32[]{:S(2)}, u32[]{:S(2)}) collective-permute-start(bf16[320,512]{1,0:T(8,128)(2,1)S(1)} %collective-permute-done.6.refs_2_.refs_6_), channel_id=1, source_target_pairs={{0,1},{1,0},{2,3},{3,2},{4,5},{5,4},{6,7},{7,6},{8,9},{9,8},{10,11... | collective-permute-start | bytes 983048 | tf_op jit(solution)/shard_map/ppermute | solution.py:21
  108.0 2.0 %collective-permute-start.11 = (bf16[320,512]{1,0:T(8,128)(2,1)S(1)}, bf16[320,512]{1,0:T(8,128)(2,1)S(1)}, u32[]{:S(2)}, u32[]{:S(2)}) collective-permute-start(bf16[320,512]{1,0:T(8,128)(2,1)S(1)} %collective-permute-done.10.refs_4_.refs_8_), channel_id=1, source_target_pairs={{0,1},{1,0},{2,3},{3,2},{4,5},{5,4},{6,7},{7,6},{8,9},{9,8},{10,11... | collective-permute-start | bytes 983048 | tf_op jit(solution)/shard_map/ppermute | solution.py:21
  108.0 13.6 %collective-permute-start.18 = (bf16[384,512]{1,0:T(8,128)(2,1)}, bf16[384,512]{1,0:T(8,128)(2,1)}, u32[]{:S(2)}, u32[]{:S(2)}) collective-permute-start(bf16[384,512]{1,0:T(8,128)(2,1)} %collective-permute-done.7.refs_2_), channel_id=1, source_target_pairs={{0,1},{1,0},{2,3},{3,2},{4,5},{5,4},{6,7},{7,6},{8,9},{9,8},{10,11... | collective-permute-start | bytes 1179656 | tf_op jit(solution)/shard_map/ppermute | solution.py:21
  108.5 13.1 %collective-permute-start.20 = (bf16[384,512]{1,0:T(8,128)(2,1)}, bf16[384,512]{1,0:T(8,128)(2,1)}, u32[]{:S(2)}, u32[]{:S(2)}) collective-permute-start(bf16[384,512]{1,0:T(8,128)(2,1)} %collective-permute-done.19.refs_4_), channel_id=1, source_target_pairs={{0,1},{1,0},{2,3},{3,2},{4,5},{5,4},{6,7},{7,6},{8,9},{9,8},{10,11... | collective-permute-start | bytes 1179656 | tf_op jit(solution)/shard_map/ppermute | solution.py:21
  113.2 8.4 %collective-permute-start.15 = (bf16[64,512]{1,0:T(8,128)(2,1)S(1)}, bf16[64,512]{1,0:T(8,128)(2,1)S(1)}, u32[]{:S(2)}, u32[]{:S(2)}) collective-permute-start(bf16[64,512]{1,0:T(8,128)(2,1)S(1)} %get-tuple-element.27.tail_ref), channel_id=1, source_target_pairs={{0,4},{4,8},{8,12},{12,0},{1,5},{5,9},{9,13},{13,1},{2,6},{6,10},{... | collective-permute-start | bytes 196616 | tf_op jit(solution)/shard_map/ppermute | solution.py:21
  115.0 6.6 %collective-permute-start.16 = (bf16[64,512]{1,0:T(8,128)(2,1)S(1)}, bf16[64,512]{1,0:T(8,128)(2,1)S(1)}, u32[]{:S(2)}, u32[]{:S(2)}) collective-permute-start(bf16[64,512]{1,0:T(8,128)(2,1)S(1)} %get-tuple-element.28.head_ref), channel_id=1, source_target_pairs={{0,12},{4,0},{8,4},{12,8},{1,13},{5,1},{9,5},{13,9},{2,14},{6,2},{... | collective-permute-start | bytes 196616 | tf_op jit(solution)/shard_map/ppermute | solution.py:21
  (7 other events, 153.9 us)

commit v3 on v2

--- a/solution.py
+++ b/solution.py
@@ -21,16 +21,6 @@
     return lax.ppermute(value, axis, [(i, (i + step) % count) for i in range(count)])
 
 
-def spread(pack):
-    bands, subs = lax.axis_size("band"), lax.axis_size("sub")
-    rows = [pack] + [shift(pack, "band", step) for step in range(1, bands)]
-    pieces = []
-    for row in rows:
-        pieces.append(row)
-        pieces.extend(shift(row, "sub", step) for step in range(1, subs))
-    return pieces, rows[1:]
-
-
 def own_spread(pack):
     return [pack] + [shift(pack, "sub", step) for step in range(1, lax.axis_size("sub"))]
 
@@ -38,10 +28,7 @@
 def relay(parts, *earlier):
     pieces = []
     for part in parts:
-        first = after(part, *earlier) if earlier else part
-        for far in range(lax.axis_size("groups")):
-            held = shift(first, "groups", far) if far else part
-            pieces.extend([held] + [shift(held, "sub", near) for near in range(1, lax.axis_size("sub"))])
+        pieces.extend(own_spread(after(part, *earlier) if earlier else part))
     return pieces
 
 
@@ -52,72 +39,46 @@
     )
 
 
-def load_copies(pieces, rows, whole, sems):
+def load_copies(pieces, start, rows, whole, sems):
     subs = lax.axis_size("sub")
     copies = []
     for index, piece in enumerate(pieces):
         owner = owner_of(index // subs, index % subs)
         there = whole.at[pl.ds(pl.multiple_of(owner * rows, rows), rows)]
-        copies.append(pltpu.make_async_copy(piece, there, sems.at[index]))
+        here = piece.at[pl.ds(start, rows)]
+        copies.append(pltpu.make_async_copy(here, there, sems.at[index]))
     return copies
 
 
 def pack_copies(pieces, sizes, wanted, sems):
-    subs, groups = lax.axis_size("sub"), lax.axis_size("groups")
-    block = sum(sizes) // groups
-    group = lax.axis_index("groups")
     copies = []
-    slot = 0
-    for index, piece in enumerate(pieces):
-        if index < subs:
-            owner = owner_of(0, index)
-            held = [(part, part * block) for part in range(groups)]
-        else:
-            band_step, rest = divmod(index - subs, groups * subs)
-            far, near = divmod(rest, subs)
-            owner = owner_of(band_step + 1, near)
-            held = [(lax.rem(group + groups - far, groups), 0)]
-        for part, base in held:
-            for at, whole in wanted.items():
-                rows = sizes[at] // groups
-                start = base + sum(sizes[:at]) // groups
-                into = pl.multiple_of(owner * sizes[at] + part * rows, rows)
-                copies.append(
-                    pltpu.make_async_copy(
-                        piece.at[pl.ds(start, rows)], whole.at[pl.ds(into, rows)], sems.at[slot]
-                    )
-                )
-                slot += 1
+    for slot, (at, whole) in enumerate(wanted.items()):
+        copies += load_copies(pieces, sum(sizes[:at]), sizes[at], whole, sems.at[slot])
     return copies
 
 
 def pack_kernel(sets, *refs):
-    count = sum(sets)
-    sources, outs, sems = refs[:count], refs[count:-1], refs[-1]
-    groups = lax.axis_size("groups")
-    group = lax.axis_index("groups")
-    copies = []
-    first = 0
-    for at, amount in enumerate(sets):
-        pack, mine = outs[2 * at], outs[2 * at + 1]
+    sources, outs = list(refs[: sum(sets)]), refs[sum(sets) :]
+    for out, amount in zip(outs, sets):
         start = 0
-        for part in range(groups + 1):
-            into, chosen, base = (pack, part, start) if part < groups else (mine, group, 0)
-            for source in sources[first : first + amount]:
-                rows = source.shape[0] // groups
-                begin = chosen * rows if part < groups else pl.multiple_of(chosen * rows, rows)
-                copies.append(
-                    pltpu.make_async_copy(
-                        source.at[pl.ds(begin, rows)], into.at[pl.ds(base, rows)], sems.at[len(copies)]
-                    )
-                )
-                base += rows
-            start = base
-        first += amount
-    for copy in copies:
-        copy.start()
-    for copy in copies:
-        copy.wait()
+        for _ in range(amount):
+            source = sources.pop(0)
+            out[start : start + source.shape[0]] = source[...]
+            start += source.shape[0]
+
+
+def pack(sets):
+    width = sets[0][0].shape[1]
+    return pl.pallas_call(
+        functools.partial(pack_kernel, [len(one) for one in sets]),
+        out_shape=[
+            jax.ShapeDtypeStruct((sum(weight.shape[0] for weight in one), width), jnp.bfloat16)
+            for one in sets
+        ],
+        in_specs=[VMEM] * sum(len(one) for one in sets),
+        out_specs=[VMEM] * len(sets),
+        name="pack",
+    )(*(weight for one in sets for weight in one))
 
 
 def silu(values):
@@ -136,16 +97,12 @@
     return jnp.dot(a, b, preferred_element_type=jnp.float32)
 
 
-def encode_kernel(count, faces, mesh_rows, target_ref, lat_ref, *refs):
-    in_pieces, hid_pieces = refs[:count], refs[count : 2 * count]
-    outs = refs[2 * count : 2 * count + faces]
-    w_in, w_hid, messages, sems_in, sems_hid = refs[2 * count + faces :]
-    rows = w_in.shape[0] // count
-    first = load_copies(in_pieces, rows, w_in, sems_in)
-    second = load_copies(hid_pieces, rows, w_hid, sems_hid)
-    for copy in first + second:
+def encode_kernel(faces, mesh_rows, sizes, target_ref, lat_ref, *refs):
+    pieces, outs, (w_in, w_hid, messages, sems) = refs[: -4 - faces], refs[-4 - faces : -4], refs[-4:]
+    copies = pack_copies(pieces, sizes, {0: w_in, 1: w_hid}, sems)
+    for copy in copies:
         copy.start()
-    for copy in first + second:
+    for copy in copies:
         copy.wait()
     block = 256
     for start in range(0, lat_ref.shape[0], block):
@@ -261,17 +218,15 @@
     grid_rows, width = grid_lat.shape
     mesh_rows = mesh_lat.shape[0]
     faces = lax.axis_size("face")
-    count = lax.axis_size("band") * lax.axis_size("sub")
+    bands = lax.axis_size("band")
+    count = bands * lax.axis_size("sub")
     f32, bf16 = jnp.float32, jnp.bfloat16
 
     def matrix(weight):
         return pltpu.VMEM((weight.shape[0] * count, weight.shape[1]), bf16)
 
-    groups, subs, bands = lax.axis_size("groups"), lax.axis_size("sub"), lax.axis_size("band")
-    copies = groups * count
-
-    def sems(parts):
-        return pltpu.SemaphoreType.DMA((parts,))
+    def sems(*shape):
+        return pltpu.SemaphoreType.DMA(shape)
 
     def cost(rows, depth):
         return pl.CostEstimate(
@@ -282,24 +237,13 @@
 
     sets = ((node_w1, node_w2, grid_w1, grid_w2), (proc_w1, proc_w2, upd_w1, upd_w2))
     sizes = [[weight.shape[0] for weight in one] for one in sets]
-    early, early_mine, late, late_mine = pl.pallas_call(
-        functools.partial(pack_kernel, [len(one) for one in sets]),
-        out_shape=[
-            jax.ShapeDtypeStruct((sum(one) // part, width), bf16)
-            for one in sizes
-            for part in (1, groups)
-        ],
-        in_specs=[ANY] * 8,
-        out_specs=[ANY] * 4,
-        scratch_shapes=[sems(8 * (groups + 1))],
-        name="pack",
-    )(*sets[0], *sets[1])
-
-    enc_in, enc_in_far = spread(enc_w1)
-    enc_hid, enc_hid_far = spread(enc_w2)
+    enc_pack, early, late = pack([(enc_w1, enc_w2), *sets])
+    enc_far = [shift(enc_pack, "band", step) for step in range(1, bands)]
+    enc_near = own_spread(enc_pack)
+    enc_all = enc_near + relay(enc_far)
+    early_sent = after(early, *enc_far)
+    early_far = [shift(early_sent, "band", step) for step in range(1, bands)]
     early_near, late_near = own_spread(early), own_spread(late)
-    early_sent = after(early_mine, *enc_in_far, *enc_hid_far)
-    early_far = [shift(early_sent, "band", step) for step in range(1, bands)]
 
     me = lax.axis_index("face")
     distance = lax.rem(grid_route[:, 0] - me + faces, faces)
@@ -307,38 +251,39 @@
 
     block = (mesh_rows, width)
     sums = pl.pallas_call(
-        functools.partial(encode_kernel, count, faces, mesh_rows),
+        functools.partial(
+            encode_kernel, faces, mesh_rows, [enc_w1.shape[0], enc_w2.shape[0]]
+        ),
         out_shape=[
             jax.ShapeDtypeStruct(block, bf16 if step else f32) for step in range(faces)
         ],
-        in_specs=[VMEM, VMEM] + [ANY] * (2 * count),
+        in_specs=[VMEM, VMEM] + [ANY] * len(enc_all),
         out_specs=[VMEM] * faces,
         scratch_shapes=[
             matrix(enc_w1),
             matrix(enc_w2),
             pltpu.VMEM((grid_rows, width), bf16),
-            sems(count),
-            sems(count),
+            sems(2, count),
         ],
         compiler_params=pltpu.CompilerParams(vmem_limit_bytes=32 * MIB),
         cost_estimate=cost(grid_rows, 3 * width),
         name="encode",
-    )(targets, grid_lat, *enc_in, *enc_hid)
-    early_all = early_near + relay(early_far, sums[0])
-    late_sent = after(late_mine, sums[0], *early_far)
+    )(targets, after(grid_lat, *early_near, *late_near), *enc_all)
+    late_sent = after(late, sums[0])
     late_far = [shift(late_sent, "band", step) for step in range(1, bands)]
     arrived = [sums[0]] + [shift(sums[step], "face", step) for step in range(1, faces)]
 
+    early_all = early_near + relay(early_far, *arrived[1:])
     grid_out = pl.pallas_call(
         functools.partial(grid_kernel, sizes[0]),
         out_shape=jax.ShapeDtypeStruct(grid_lat.shape, bf16),
         in_specs=[VMEM] + [ANY] * len(early_all),
         out_specs=VMEM,
-        scratch_shapes=[matrix(grid_w1), matrix(grid_w2), sems(2 * copies)],
+        scratch_shapes=[matrix(grid_w1), matrix(grid_w2), sems(2, count)],
         compiler_params=pltpu.CompilerParams(vmem_limit_bytes=32 * MIB),
         cost_estimate=cost(grid_rows, 2 * width),
         name="grid_update",
-    )(after(grid_lat, *late_far), *early_all)
+    )(grid_lat, *early_all)
 
     half = (mesh_rows // 2, width)
     head, tail = pl.pallas_call(
@@ -346,7 +291,7 @@
         out_shape=[jax.ShapeDtypeStruct(half, bf16)] * 2,
         in_specs=[VMEM] * (1 + faces) + [ANY] * len(early_all),
         out_specs=[VMEM] * 2,
-        scratch_shapes=[matrix(node_w1), matrix(node_w2), sems(2 * copies)],
+        scratch_shapes=[matrix(node_w1), matrix(node_w2), sems(2, count)],
         compiler_params=pltpu.CompilerParams(vmem_limit_bytes=32 * MIB),
         cost_estimate=cost(mesh_rows, 3 * width),
         name="node_update",
@@ -354,7 +299,7 @@
 
     before = shift(tail, "face", 1)
     behind = shift(head, "face", faces - 1)
-    late_all = late_near + relay(late_far)
+    late_all = late_near + relay(late_far, head)
     mesh_out = pl.pallas_call(
         functools.partial(edge_kernel, sizes[1]),
         out_shape=jax.ShapeDtypeStruct(mesh_lat.shape, bf16),
@@ -365,8 +310,8 @@
             matrix(proc_w2),
             matrix(upd_w1),
             matrix(upd_w2),
-            sems(2 * copies),
-            sems(2 * copies),
+            sems(2, count),
+            sems(2, count),
         ],
         compiler_params=pltpu.CompilerParams(vmem_limit_bytes=32 * MIB),
         cost_estimate=cost(mesh_rows * mesh_nbr.shape[1], 3 * width),

time: 127 us -> 62.4 us (0.49)
  Pallas kernels: 83.7 us -> 17.4 us
  starting transfers between devices: 22.3 us -> 15 us
  waiting for transfers between devices: 20.1 us -> 26.7 us
  local copies, waits for them, and re-layouts: 0.16 us -> 2.33 us
    pallas_call x2, Pallas kernels: 70.5 us -> 6.49 us  [the longest x1 3.69 us: shards(): pl.pallas_call(functools.partial(encode_kernel, faces, mesh_rows, [enc_w1...]
    ppermute x21 -> x14, starting transfers between devices: 22.3 us -> 15 us  [shift(): lax.ppermute(value, axis, [(i, (i + step) % count) for i in range(count)])]
    ppermute x21 -> x14, waiting for transfers between devices: 20.1 us -> 26.7 us  [shift(): lax.ppermute(value, axis, [(i, (i + step) % count) for i in range(count)])]
    unnamed x21 -> x25, local copies, waits for them, and re-layouts: 0.16 us -> 2.33 us
    pallas_call x1, Pallas kernels: 3.15 us -> 1.61 us  [shards(): pl.pallas_call(functools.partial(node_kernel, sizes[0], faces), out_shape...]
  transfers between devices with their start and end apart: 21 -> 14, of which waited for: 8 -> 7; matrix products, arithmetic and copies ran while one was open for 0% -> 0% of each run, Pallas kernels for 61% -> 16%
where the time goes in v3:
time: 62.4 us; the launch traced here: 62.2 us
  waiting for transfers between devices  26.7 us (43%)
  Pallas kernels  17.4 us (28%)
  starting transfers between devices  15 us (24%)
  local copies, waits for them, and re-layouts  2.33 us (4%)
  between operations  0.75 us (1%)
    ppermute x14, waiting for transfers between devices, shift(): lax.ppermute(value, axis, [(i, (i + step) % count) for i in range(count)])  26.7 us
    ppermute x14, starting transfers between devices, shift(): lax.ppermute(value, axis, [(i, (i + step) % count) for i in range(count)])  15 us
    pallas_call x1, Pallas kernels, shards(): pl.pallas_call(functools.partial(edge_kernel, sizes[1]), out_shape=jax.Sh...  4.88 us
    pallas_call x1, Pallas kernels, shards(): pl.pallas_call(functools.partial(grid_kernel, sizes[0]), out_shape=jax.Sh...  4.44 us
    pallas_call x1, Pallas kernels, shards(): pl.pallas_call(functools.partial(encode_kernel, faces, mesh_rows, [enc_w1...  3.69 us
    pallas_call x1, Pallas kernels, pack(): pl.pallas_call(functools.partial(pack_kernel, [len(one) for one in sets])...  2.8 us
    unnamed x25, local copies, waits for them, and re-layouts  2.33 us
    pallas_call x1, Pallas kernels, shards(): pl.pallas_call(functools.partial(node_kernel, sizes[0], faces), out_shape...  1.61 us
  transfers between devices with their start and end apart: 14, of which 7 were waited for; matrix products, arithmetic and copies ran while one was open for 0% of the time, Pallas kernels for 16%

profile of v3, /device:TPU:0, one launch (start us, length us, event | category | flops | bytes accessed | tf_op | source)
XLA Modules:
  0.0 62.2 jit_solution(5916831548024347796)
XLA Ops:
  0.6 2.8 %pack.1 = (bf16[256,512]{1,0:T(8,128)(2,1)}, bf16[640,512]{1,0:T(8,128)(2,1)}, bf16[768,512]{1,0:T(8,128)(2,1)}) custom-call(bf16[128,512]{1,0:T(8,128)(2,1)} %refs_0_.1, bf16[128,512]{1,0:T(8,128)(2,1)} %refs_1_.1, bf16[256,512]{1,0:T(8,128)(2,1)} %refs_2_.1, bf16[128,512]{1,0:T(8,128)(2,1)} %refs_3_.1, bf16[128,512]{1,0:T(8,128)(2,1)} %refs_4_.1, ...), custom_call_target="tpu_custom_call" | custom-call | tf_op jit(solution)/shard_map/pack/pallas_call | solution.py:72
  3.4 0.5 collective-permute-start.3
  3.9 2.5 %collective-permute-start.1 = (bf16[256,512]{1,0:T(8,128)(2,1)}, bf16[256,512]{1,0:T(8,128)(2,1)S(1)}, u32[]{:S(2)}, u32[]{:S(2)}) collective-permute-start(bf16[256,512]{1,0:T(8,128)(2,1)} %get-tuple-element.17.refs_0_), channel_id=1, source_target_pairs={{0,2},{2,0},{1,3},{3,1},{4,6},{6,4},{5,7},{7,5},{8,10},{10,8},{9,1... | collective-permute-start | bytes 786440 | tf_op jit(solution)/shard_map/ppermute | solution.py:21
  6.4 0.2 collective-permute-start
  6.6 0.3 collective-permute-start.4
  6.9 6.7 %collective-permute-done.1.refs_2_ = bf16[256,512]{1,0:T(8,128)(2,1)S(1)} collective-permute-done((bf16[256,512]{1,0:T(8,128)(2,1)}, bf16[256,512]{1,0:T(8,128)(2,1)S(1)}, u32[]{:S(2)}, u32[]{:S(2)}) %collective-permute-start.1) | collective-permute-done | bytes 262176 | tf_op jit(solution)/shard_map/ppermute | solution.py:21
  13.6 1.7 %collective-permute-start.2 = (bf16[640,512]{1,0:T(8,128)(2,1)}, bf16[640,512]{1,0:T(8,128)(2,1)S(1)}, u32[]{:S(2)}, u32[]{:S(2)}) collective-permute-start(bf16[640,512]{1,0:T(8,128)(2,1)} %get-tuple-element.18.refs_0_.refs_4_), channel_id=1, source_target_pairs={{0,2},{2,0},{1,3},{3,1},{4,6},{6,4},{5,7},{7,5},{8,10},{10,8},{9,1... | collective-permute-start | bytes 1966088 | tf_op jit(solution)/shard_map/ppermute | solution.py:21
  15.4 1.5 %collective-permute-done.5.refs_3_ = bf16[256,512]{1,0:T(8,128)(2,1)S(1)} collective-permute-done((bf16[256,512]{1,0:T(8,128)(2,1)S(1)}, bf16[256,512]{1,0:T(8,128)(2,1)S(1)}, u32[]{:S(2)}, u32[]{:S(2)}) %collective-permute-start.5) | collective-permute-done | bytes 262176 | tf_op jit(solution)/shard_map/ppermute | solution.py:21
  16.9 0.9 %copy-done.6 = bf16[256,512]{1,0:T(8,128)(2,1)S(1)} copy-done((bf16[256,512]{1,0:T(8,128)(2,1)S(1)}, bf16[256,512]{1,0:T(8,128)(2,1)}, u32[]{:S(2)}) %copy-start.6) | copy-done | bytes 262168
  17.8 3.7 %encode.1 = (f32[128,512]{1,0:T(8,128)S(1)}, bf16[128,512]{1,0:T(8,128)(2,1)S(1)}, bf16[128,512]{1,0:T(8,128)(2,1)S(1)}, bf16[128,512]{1,0:T(8,128)(2,1)S(1)}) custom-call(s32[1,1024]{1,0:T(1,128)S(1)} %bitcast.2, bf16[1024,512]{1,0:T(8,128)(2,1)S(1)} %copy-done.1, bf16[256,512]{1,0:T(8,128)(2,1)S(1)} %copy-done.6, ...), custom_call_target="tpu_custom_call" | custom-call | flops 1610612736 | bytes 2621440 | tf_op jit(solution)/shard_map/encode/pallas_call | solution.py:253
  21.5 1.6 %collective-permute-start.6 = (bf16[128,512]{1,0:T(8,128)(2,1)S(1)}, bf16[128,512]{1,0:T(8,128)(2,1)S(1)}, u32[]{:S(2)}, u32[]{:S(2)}) collective-permute-start(bf16[128,512]{1,0:T(8,128)(2,1)S(1)} %get-tuple-element.21), channel_id=1, source_target_pairs={{0,4},{4,8},{8,12},{12,0},{1,5},{5,9},{9,13},{13,1},{2,6},{6,10},{... | collective-permute-start | bytes 393224 | tf_op jit(solution)/shard_map/ppermute | solution.py:21
  23.1 2.6 %collective-permute-start.7 = (bf16[128,512]{1,0:T(8,128)(2,1)S(1)}, bf16[128,512]{1,0:T(8,128)(2,1)S(1)}, u32[]{:S(2)}, u32[]{:S(2)}) collective-permute-start(bf16[128,512]{1,0:T(8,128)(2,1)S(1)} %get-tuple-element.22), channel_id=1, source_target_pairs={{0,8},{4,12},{8,0},{12,4},{1,9},{5,13},{9,1},{13,5},{2,10},{6,14},... | collective-permute-start | bytes 393224 | tf_op jit(solution)/shard_map/ppermute | solution.py:21
  25.7 1.3 %collective-permute-start.8 = (bf16[128,512]{1,0:T(8,128)(2,1)S(1)}, bf16[128,512]{1,0:T(8,128)(2,1)S(1)}, u32[]{:S(2)}, u32[]{:S(2)}) collective-permute-start(bf16[128,512]{1,0:T(8,128)(2,1)S(1)} %get-tuple-element.23), channel_id=1, source_target_pairs={{0,12},{4,0},{8,4},{12,8},{1,13},{5,1},{9,5},{13,9},{2,14},{6,2},{... | collective-permute-start | bytes 393224 | tf_op jit(solution)/shard_map/ppermute | solution.py:21
  27.1 0.5 collective-permute-start.12
  27.6 3.8 %collective-permute-done.2.refs_2_.refs_6_ = bf16[640,512]{1,0:T(8,128)(2,1)S(1)} collective-permute-done((bf16[640,512]{1,0:T(8,128)(2,1)}, bf16[640,512]{1,0:T(8,128)(2,1)S(1)}, u32[]{:S(2)}, u32[]{:S(2)}) %collective-permute-start.2) | collective-permute-done | bytes 655392 | tf_op jit(solution)/shard_map/ppermute | solution.py:21
  31.4 3.3 %collective-permute-done.7.refs_2_ = bf16[128,512]{1,0:T(8,128)(2,1)S(1)} collective-permute-done((bf16[128,512]{1,0:T(8,128)(2,1)S(1)}, bf16[128,512]{1,0:T(8,128)(2,1)S(1)}, u32[]{:S(2)}, u32[]{:S(2)}) %collective-permute-start.7) | collective-permute-done | bytes 131104 | tf_op jit(solution)/shard_map/ppermute | solution.py:21
  34.7 2.1 %collective-permute-done.9.refs_3_.refs_7_ = bf16[640,512]{1,0:T(8,128)(2,1)S(1)} collective-permute-done((bf16[640,512]{1,0:T(8,128)(2,1)S(1)}, bf16[640,512]{1,0:T(8,128)(2,1)S(1)}, u32[]{:S(2)}, u32[]{:S(2)}) %collective-permute-start.9) | collective-permute-done | bytes 655392 | tf_op jit(solution)/shard_map/ppermute | solution.py:21
  36.8 1.6 %node_update.1 = (bf16[64,512]{1,0:T(8,128)(2,1)S(1)}, bf16[64,512]{1,0:T(8,128)(2,1)S(1)}) custom-call(bf16[128,512]{1,0:T(8,128)(2,1)S(1)} %copy-done.3, f32[128,512]{1,0:T(8,128)S(1)} %get-tuple-element.25.refs_0_, bf16[128,512]{1,0:T(8,128)(2,1)S(1)} %collective-permute-done.6.refs_1_, bf16[128,512]{1,0:T(8,128)(2,1)S(1)} %collective-permute-done.7.refs_2_, ...), custom_call_target="tpu_custom_call" | custom-call | flops 201326592 | bytes 1703936 | tf_op jit(solution)/shard_map/node_update/pallas_call | solution.py:289
  38.4 8.8 %collective-permute-done.12.refs_2_ = bf16[768,512]{1,0:T(8,128)(2,1)S(1)} collective-permute-done((bf16[768,512]{1,0:T(8,128)(2,1)S(1)}, bf16[768,512]{1,0:T(8,128)(2,1)S(1)}, u32[]{:S(2)}, u32[]{:S(2)}) %collective-permute-start.12) | collective-permute-done | bytes 786464 | tf_op jit(solution)/shard_map/ppermute | solution.py:21
  47.3 3.7 %collective-permute-start.11 = (bf16[64,512]{1,0:T(8,128)(2,1)S(1)}, bf16[64,512]{1,0:T(8,128)(2,1)S(1)}, u32[]{:S(2)}, u32[]{:S(2)}) collective-permute-start(bf16[64,512]{1,0:T(8,128)(2,1)S(1)} %get-tuple-element.27.head_ref), channel_id=1, source_target_pairs={{0,12},{4,0},{8,4},{12,8},{1,13},{5,1},{9,5},{13,9},{2,14},{6,2},{... | collective-permute-start | bytes 196616 | tf_op jit(solution)/shard_map/ppermute | solution.py:21
  51.0 1.2 %copy-done.2 = bf16[1024,512]{1,0:T(8,128)(2,1)S(1)} copy-done((bf16[1024,512]{1,0:T(8,128)(2,1)S(1)}, bf16[1024,512]{1,0:T(8,128)(2,1)}, u32[]{:S(2)}) %copy-start.2) | copy-done | bytes 1048600
  52.3 4.4 %grid_update.1 = bf16[1024,512]{1,0:T(8,128)(2,1)} custom-call(bf16[1024,512]{1,0:T(8,128)(2,1)S(1)} %copy-done.2, bf16[640,512]{1,0:T(8,128)(2,1)S(1)} %copy-done, bf16[640,512]{1,0:T(8,128)(2,1)S(1)} %collective-permute-done.refs_1_.refs_5_, bf16[640,512]{1,0:T(8,128)(2,1)S(1)} %collective-permute-done.2.refs_2_.refs_6_, ...), custom_call_target="tpu_custom_call" | custom-call | flops 1073741824 | bytes 2097152 | tf_op jit(solution)/shard_map/grid_update/pallas_call | solution.py:277
  56.7 0.6 collective-permute-done.10.before_ref
  57.3 4.9 %edge_update.1 = bf16[128,512]{1,0:T(8,128)(2,1)} custom-call(s32[128,6]{1,0:T(8,128)S(1)} %copy.17.nbr_ref, bf16[64,512]{1,0:T(8,128)(2,1)S(1)} %collective-permute-done.10.before_ref, bf16[64,512]{1,0:T(8,128)(2,1)S(1)} %get-tuple-element.27.head_ref, bf16[64,512]{1,0:T(8,128)(2,1)S(1)} %copy-done.8, ...), custom_call_target="tpu_custom_call" | custom-call | flops 1207959552 | bytes 2359296 | tf_op jit(solution)/shard_map/edge_update/pallas_call | solution.py:303
  (36 shorter events, 0.2 us)
Async XLA Ops:
  0.6 16.2 %copy-start.1 = (bf16[1024,512]{1,0:T(8,128)(2,1)S(1)}, bf16[1024,512]{1,0:T(8,128)(2,1)}, u32[]{:S(2)}) copy-start(bf16[1024,512]{1,0:T(8,128)(2,1)} %lat_ref.3) | copy-start | bytes 3145732
  3.4 11.9 %collective-permute-start.3 = (bf16[768,512]{1,0:T(8,128)(2,1)}, bf16[768,512]{1,0:T(8,128)(2,1)}, u32[]{:S(2)}, u32[]{:S(2)}) collective-permute-start(bf16[768,512]{1,0:T(8,128)(2,1)} %get-tuple-element.28.refs_0_), channel_id=1, source_target_pairs={{0,1},{1,0},{2,3},{3,2},{4,5},{5,4},{6,7},{7,6},{8,9},{9,8},{10,11... | collective-permute-start | bytes 2359304 | tf_op jit(solution)/shard_map/ppermute | solution.py:21
  3.9 9.7 %collective-permute-start.1 = (bf16[256,512]{1,0:T(8,128)(2,1)}, bf16[256,512]{1,0:T(8,128)(2,1)S(1)}, u32[]{:S(2)}, u32[]{:S(2)}) collective-permute-start(bf16[256,512]{1,0:T(8,128)(2,1)} %get-tuple-element.17.refs_0_), channel_id=1, source_target_pairs={{0,2},{2,0},{1,3},{3,1},{4,6},{6,4},{5,7},{7,5},{8,10},{10,8},{9,1... | collective-permute-start | bytes 786440 | tf_op jit(solution)/shard_map/ppermute | solution.py:21
  6.4 8.9 %copy-start.11 = (s32[1024,1]{0,1:T(1,128)S(1)}, s32[1024,1]{0,1:T(1,128)}, u32[]{:S(2)}) copy-start(s32[1024,1]{0,1:T(1,128)} %param.16) | copy-start | bytes 12292
  6.4 9.0 %collective-permute-start = (bf16[640,512]{1,0:T(8,128)(2,1)}, bf16[640,512]{1,0:T(8,128)(2,1)S(1)}, u32[]{:S(2)}, u32[]{:S(2)}) collective-permute-start(bf16[640,512]{1,0:T(8,128)(2,1)} %get-tuple-element.18.refs_0_.refs_4_), channel_id=1, source_target_pairs={{0,1},{1,0},{2,3},{3,2},{4,5},{5,4},{6,7},{7,6},{8,9},{9,8},{10,11... | collective-permute-start | bytes 1966088 | tf_op jit(solution)/shard_map/ppermute | solution.py:21
  6.6 8.8 %collective-permute-start.4 = (bf16[256,512]{1,0:T(8,128)(2,1)}, bf16[256,512]{1,0:T(8,128)(2,1)S(1)}, u32[]{:S(2)}, u32[]{:S(2)}) collective-permute-start(bf16[256,512]{1,0:T(8,128)(2,1)} %get-tuple-element.17.refs_0_), channel_id=1, source_target_pairs={{0,1},{1,0},{2,3},{3,2},{4,5},{5,4},{6,7},{7,6},{8,9},{9,8},{10,11... | collective-permute-start | bytes 786440 | tf_op jit(solution)/shard_map/ppermute | solution.py:21
  6.9 8.4 %copy-start.9 = (s32[1024]{0:T(1024)S(1)}, s32[1024]{0:T(1024)}, u32[]{:S(2)}) copy-start(s32[1024]{0:T(1024)} %param.17) | copy-start | bytes 12292
  13.6 17.8 %collective-permute-start.2 = (bf16[640,512]{1,0:T(8,128)(2,1)}, bf16[640,512]{1,0:T(8,128)(2,1)S(1)}, u32[]{:S(2)}, u32[]{:S(2)}) collective-permute-start(bf16[640,512]{1,0:T(8,128)(2,1)} %get-tuple-element.18.refs_0_.refs_4_), channel_id=1, source_target_pairs={{0,2},{2,0},{1,3},{3,1},{4,6},{6,4},{5,7},{7,5},{8,10},{10,8},{9,1... | collective-permute-start | bytes 1966088 | tf_op jit(solution)/shard_map/ppermute | solution.py:21
  15.3 1.5 %collective-permute-start.5 = (bf16[256,512]{1,0:T(8,128)(2,1)S(1)}, bf16[256,512]{1,0:T(8,128)(2,1)S(1)}, u32[]{:S(2)}, u32[]{:S(2)}) collective-permute-start(bf16[256,512]{1,0:T(8,128)(2,1)S(1)} %collective-permute-done.1.refs_2_), channel_id=1, source_target_pairs={{0,1},{1,0},{2,3},{3,2},{4,5},{5,4},{6,7},{7,6},{8,9},{9,8},{10,11... | collective-permute-start | bytes 786440 | tf_op jit(solution)/shard_map/ppermute | solution.py:21
  17.8 9.3 %copy-start.4 = (bf16[768,512]{1,0:T(8,128)(2,1)S(1)}, bf16[768,512]{1,0:T(8,128)(2,1)}, u32[]{:S(2)}) copy-start(bf16[768,512]{1,0:T(8,128)(2,1)} %get-tuple-element.28.refs_0_) | copy-start | bytes 2359300
  17.8 19.0 %copy-start = (bf16[640,512]{1,0:T(8,128)(2,1)S(1)}, bf16[640,512]{1,0:T(8,128)(2,1)}, u32[]{:S(2)}) copy-start(bf16[640,512]{1,0:T(8,128)(2,1)} %get-tuple-element.18.refs_0_.refs_4_) | copy-start | bytes 1966084
  17.8 19.0 %copy-start.3 = (bf16[128,512]{1,0:T(8,128)(2,1)S(1)}, bf16[128,512]{1,0:T(8,128)(2,1)}, u32[]{:S(2)}) copy-start(bf16[128,512]{1,0:T(8,128)(2,1)} %lat_ref.4) | copy-start | bytes 393220
  21.5 9.9 %collective-permute-start.6 = (bf16[128,512]{1,0:T(8,128)(2,1)S(1)}, bf16[128,512]{1,0:T(8,128)(2,1)S(1)}, u32[]{:S(2)}, u32[]{:S(2)}) collective-permute-start(bf16[128,512]{1,0:T(8,128)(2,1)S(1)} %get-tuple-element.21), channel_id=1, source_target_pairs={{0,4},{4,8},{8,12},{12,0},{1,5},{5,9},{9,13},{13,1},{2,6},{6,10},{... | collective-permute-start | bytes 393224 | tf_op jit(solution)/shard_map/ppermute | solution.py:21
  23.1 11.5 %collective-permute-start.7 = (bf16[128,512]{1,0:T(8,128)(2,1)S(1)}, bf16[128,512]{1,0:T(8,128)(2,1)S(1)}, u32[]{:S(2)}, u32[]{:S(2)}) collective-permute-start(bf16[128,512]{1,0:T(8,128)(2,1)S(1)} %get-tuple-element.22), channel_id=1, source_target_pairs={{0,8},{4,12},{8,0},{12,4},{1,9},{5,13},{9,1},{13,5},{2,10},{6,14},... | collective-permute-start | bytes 393224 | tf_op jit(solution)/shard_map/ppermute | solution.py:21
  25.7 8.9 %collective-permute-start.8 = (bf16[128,512]{1,0:T(8,128)(2,1)S(1)}, bf16[128,512]{1,0:T(8,128)(2,1)S(1)}, u32[]{:S(2)}, u32[]{:S(2)}) collective-permute-start(bf16[128,512]{1,0:T(8,128)(2,1)S(1)} %get-tuple-element.23), channel_id=1, source_target_pairs={{0,12},{4,0},{8,4},{12,8},{1,13},{5,1},{9,5},{13,9},{2,14},{6,2},{... | collective-permute-start | bytes 393224 | tf_op jit(solution)/shard_map/ppermute | solution.py:21
  27.1 20.1 %collective-permute-start.12 = (bf16[768,512]{1,0:T(8,128)(2,1)S(1)}, bf16[768,512]{1,0:T(8,128)(2,1)S(1)}, u32[]{:S(2)}, u32[]{:S(2)}) collective-permute-start(bf16[768,512]{1,0:T(8,128)(2,1)S(1)} %copy-done.4), channel_id=1, source_target_pairs={{0,2},{2,0},{1,3},{3,1},{4,6},{6,4},{5,7},{7,5},{8,10},{10,8},{9,1... | collective-permute-start | bytes 2359304 | tf_op jit(solution)/shard_map/ppermute | solution.py:21
  34.7 2.1 %collective-permute-start.9 = (bf16[640,512]{1,0:T(8,128)(2,1)S(1)}, bf16[640,512]{1,0:T(8,128)(2,1)S(1)}, u32[]{:S(2)}, u32[]{:S(2)}) collective-permute-start(bf16[640,512]{1,0:T(8,128)(2,1)S(1)} %collective-permute-done.2.refs_2_.refs_6_), channel_id=1, source_target_pairs={{0,1},{1,0},{2,3},{3,2},{4,5},{5,4},{6,7},{7,6},{8,9},{9,8},{10,11... | collective-permute-start | bytes 1966088 | tf_op jit(solution)/shard_map/ppermute | solution.py:21
  36.8 10.4 %copy-start.10 = (s32[128,6]{0,1:T(8,128)S(1)}, s32[128,6]{0,1:T(8,128)}, u32[]{:S(2)}) copy-start(s32[128,6]{0,1:T(8,128)} %param.19) | copy-start | bytes 9220
  38.4 8.8 %copy-start.7 = (bf16[64,512]{1,0:T(8,128)(2,1)}, bf16[64,512]{1,0:T(8,128)(2,1)S(1)}, u32[]{:S(2)}) copy-start(bf16[64,512]{1,0:T(8,128)(2,1)S(1)} %get-tuple-element.26.tail_ref) | copy-start | bytes 196612
  47.2 10.1 %collective-permute-start.13 = (bf16[768,512]{1,0:T(8,128)(2,1)S(1)}, bf16[768,512]{1,0:T(8,128)(2,1)}, u32[]{:S(2)}, u32[]{:S(2)}) collective-permute-start(bf16[768,512]{1,0:T(8,128)(2,1)S(1)} %collective-permute-done.12.refs_2_), channel_id=1, source_target_pairs={{0,1},{1,0},{2,3},{3,2},{4,5},{5,4},{6,7},{7,6},{8,9},{9,8},{10,11... | collective-permute-start | bytes 2359304 | tf_op jit(solution)/shard_map/ppermute | solution.py:21
  47.3 10.0 %collective-permute-start.11 = (bf16[64,512]{1,0:T(8,128)(2,1)S(1)}, bf16[64,512]{1,0:T(8,128)(2,1)S(1)}, u32[]{:S(2)}, u32[]{:S(2)}) collective-permute-start(bf16[64,512]{1,0:T(8,128)(2,1)S(1)} %get-tuple-element.27.head_ref), channel_id=1, source_target_pairs={{0,12},{4,0},{8,4},{12,8},{1,13},{5,1},{9,5},{13,9},{2,14},{6,2},{... | collective-permute-start | bytes 196616 | tf_op jit(solution)/shard_map/ppermute | solution.py:21
  51.0 6.3 %collective-permute-start.10 = (bf16[64,512]{1,0:T(8,128)(2,1)}, bf16[64,512]{1,0:T(8,128)(2,1)S(1)}, u32[]{:S(2)}, u32[]{:S(2)}) collective-permute-start(bf16[64,512]{1,0:T(8,128)(2,1)} %copy-done.7), channel_id=1, source_target_pairs={{0,4},{4,8},{8,12},{12,0},{1,5},{5,9},{9,13},{13,1},{2,6},{6,10},{... | collective-permute-start | bytes 196616 | tf_op jit(solution)/shard_map/ppermute | solution.py:21
  52.3 5.1 %copy-start.5 = (bf16[768,512]{1,0:T(8,128)(2,1)S(1)}, bf16[768,512]{1,0:T(8,128)(2,1)}, u32[]{:S(2)}) copy-start(bf16[768,512]{1,0:T(8,128)(2,1)} %get-tuple-element.28.refs_0_) | copy-start | bytes 2359300
  52.3 5.1 %copy-start.8 = (bf16[64,512]{1,0:T(8,128)(2,1)S(1)}, bf16[64,512]{1,0:T(8,128)(2,1)}, u32[]{:S(2)}) copy-start(bf16[64,512]{1,0:T(8,128)(2,1)} %copy-done.7) | copy-start | bytes 196612
  (2 other events, 2.2 us)

commit v4 on v3

--- a/solution.py
+++ b/solution.py
@@ -97,9 +97,13 @@
     return jnp.dot(a, b, preferred_element_type=jnp.float32)
 
 
-def encode_kernel(faces, mesh_rows, sizes, target_ref, lat_ref, *refs):
-    pieces, outs, (w_in, w_hid, messages, sems) = refs[: -4 - faces], refs[-4 - faces : -4], refs[-4:]
-    copies = pack_copies(pieces, sizes, {0: w_in, 1: w_hid}, sems)
+def encode_kernel(count, faces, mesh_rows, target_ref, lat_ref, *refs):
+    in_pieces, hid_pieces = refs[:count], refs[count : 2 * count]
+    outs = refs[2 * count : 2 * count + faces]
+    w_in, w_hid, messages, sems = refs[2 * count + faces :]
+    rows = w_in.shape[0] // count
+    copies = load_copies(in_pieces, 0, rows, w_in, sems.at[0])
+    copies += load_copies(hid_pieces, 0, rows, w_hid, sems.at[1])
     for copy in copies:
         copy.start()
     for copy in copies:
@@ -237,11 +241,12 @@
 
     sets = ((node_w1, node_w2, grid_w1, grid_w2), (proc_w1, proc_w2, upd_w1, upd_w2))
     sizes = [[weight.shape[0] for weight in one] for one in sets]
-    enc_pack, early, late = pack([(enc_w1, enc_w2), *sets])
-    enc_far = [shift(enc_pack, "band", step) for step in range(1, bands)]
-    enc_near = own_spread(enc_pack)
-    enc_all = enc_near + relay(enc_far)
-    early_sent = after(early, *enc_far)
+    enc_far = [[shift(one, "band", step) for step in range(1, bands)] for one in (enc_w1, enc_w2)]
+    enc_all = [
+        own_spread(one) + relay(far) for one, far in zip((enc_w1, enc_w2), enc_far)
+    ]
+    early, late = pack(sets)
+    early_sent = after(early, *enc_far[0], *enc_far[1])
     early_far = [shift(early_sent, "band", step) for step in range(1, bands)]
     early_near, late_near = own_spread(early), own_spread(late)
 
@@ -251,13 +256,11 @@
 
     block = (mesh_rows, width)
     sums = pl.pallas_call(
-        functools.partial(
-            encode_kernel, faces, mesh_rows, [enc_w1.shape[0], enc_w2.shape[0]]
-        ),
+        functools.partial(encode_kernel, count, faces, mesh_rows),
         out_shape=[
             jax.ShapeDtypeStruct(block, bf16 if step else f32) for step in range(faces)
         ],
-        in_specs=[VMEM, VMEM] + [ANY] * len(enc_all),
+        in_specs=[VMEM, VMEM] + [ANY] * (2 * count),
         out_specs=[VMEM] * faces,
         scratch_shapes=[
             matrix(enc_w1),
@@ -268,7 +271,7 @@
         compiler_params=pltpu.CompilerParams(vmem_limit_bytes=32 * MIB),
         cost_estimate=cost(grid_rows, 3 * width),
         name="encode",
-    )(targets, after(grid_lat, *early_near, *late_near), *enc_all)
+    )(targets, grid_lat, *enc_all[0], *enc_all[1])
     late_sent = after(late, sums[0])
     late_far = [shift(late_sent, "band", step) for step in range(1, bands)]
     arrived = [sums[0]] + [shift(sums[step], "face", step) for step in range(1, faces)]
@@ -299,7 +302,7 @@
 
     before = shift(tail, "face", 1)
     behind = shift(head, "face", faces - 1)
-    late_all = late_near + relay(late_far, head)
+    late_all = late_near + relay(late_far, head, grid_out)
     mesh_out = pl.pallas_call(
         functools.partial(edge_kernel, sizes[1]),
         out_shape=jax.ShapeDtypeStruct(mesh_lat.shape, bf16),

time: 62.4 us -> 55.5 us (0.89)
  waiting for transfers between devices: 26.7 us -> 20.7 us
  local copies, waits for them, and re-layouts: 2.33 us -> 0.15 us
  starting transfers between devices: 15 us -> 16.3 us
    ppermute x14 -> x17, waiting for transfers between devices: 26.7 us -> 20.7 us  [shift(): lax.ppermute(value, axis, [(i, (i + step) % count) for i in range(count)])]
    unnamed x25 -> x19, local copies, waits for them, and re-layouts: 2.33 us -> 0.15 us
    ppermute x14 -> x17, starting transfers between devices: 15 us -> 16.3 us  [shift(): lax.ppermute(value, axis, [(i, (i + step) % count) for i in range(count)])]
  transfers between devices with their start and end apart: 14 -> 17, of which waited for: 7 -> 10; matrix products, arithmetic and copies ran while one was open for 0% -> 0% of each run, Pallas kernels for 16% -> 22%
where the time goes in v4:
time: 55.5 us; the launch traced here: 55.4 us
  waiting for transfers between devices  20.7 us (37%)
  Pallas kernels  17.4 us (31%)
  starting transfers between devices  16.3 us (29%)
  between operations  0.76 us (1%)
    ppermute x17, waiting for transfers between devices, shift(): lax.ppermute(value, axis, [(i, (i + step) % count) for i in range(count)])  20.7 us
    ppermute x17, starting transfers between devices, shift(): lax.ppermute(value, axis, [(i, (i + step) % count) for i in range(count)])  16.3 us
    pallas_call x1, Pallas kernels, shards(): pl.pallas_call(functools.partial(edge_kernel, sizes[1]), out_shape=jax.Sh...  5.07 us
    pallas_call x1, Pallas kernels, shards(): pl.pallas_call(functools.partial(grid_kernel, sizes[0]), out_shape=jax.Sh...  4.47 us
    pallas_call x1, Pallas kernels, shards(): pl.pallas_call(functools.partial(encode_kernel, count, faces, mesh_rows),...  3.72 us
    pallas_call x1, Pallas kernels, pack(): pl.pallas_call(functools.partial(pack_kernel, [len(one) for one in sets])...  2.55 us
    pallas_call x1, Pallas kernels, shards(): pl.pallas_call(functools.partial(node_kernel, sizes[0], faces), out_shape...  1.58 us
  transfers between devices with their start and end apart: 17, of which 10 were waited for; matrix products, arithmetic and copies ran while one was open for 0% of the time, Pallas kernels for 22%

profile of v4, /device:TPU:0, one launch (start us, length us, event | category | flops | bytes accessed | tf_op | source)
XLA Modules:
  0.0 55.4 jit_solution(12170917672969697283)
XLA Ops:
  0.6 3.0 %collective-permute-start.1 = (bf16[128,512]{1,0:T(8,128)(2,1)}, bf16[128,512]{1,0:T(8,128)(2,1)S(1)}, u32[]{:S(2)}, u32[]{:S(2)}) collective-permute-start(bf16[128,512]{1,0:T(8,128)(2,1)} %refs_0_.3), channel_id=1, source_target_pairs={{0,2},{2,0},{1,3},{3,1},{4,6},{6,4},{5,7},{7,5},{8,10},{10,8},{9,1... | collective-permute-start | bytes 393224 | tf_op jit(solution)/shard_map/ppermute | solution.py:21
  3.7 0.5 collective-permute-start.6
  4.2 2.6 %pack.1 = (bf16[640,512]{1,0:T(8,128)(2,1)}, bf16[768,512]{1,0:T(8,128)(2,1)}) custom-call(bf16[256,512]{1,0:T(8,128)(2,1)} %refs_0_.2, bf16[128,512]{1,0:T(8,128)(2,1)} %refs_1_.1, bf16[128,512]{1,0:T(8,128)(2,1)} %refs_2_.1, bf16[128,512]{1,0:T(8,128)(2,1)} %refs_3_.1, bf16[256,512]{1,0:T(8,128)(2,1)} %refs_4_.2, bf16[128,512]{1,0:T(8,128)(2,1)} %refs_5_.1, ...), custom_call_target="tpu_custom_call" | custom-call | tf_op jit(solution)/shard_map/pack/pallas_call | solution.py:72
  6.8 1.4 %collective-permute-done.1.refs_2_ = bf16[128,512]{1,0:T(8,128)(2,1)S(1)} collective-permute-done((bf16[128,512]{1,0:T(8,128)(2,1)}, bf16[128,512]{1,0:T(8,128)(2,1)S(1)}, u32[]{:S(2)}, u32[]{:S(2)}) %collective-permute-start.1) | collective-permute-done | bytes 131104 | tf_op jit(solution)/shard_map/ppermute | solution.py:21
  8.2 2.0 %collective-permute-done.2.refs_6_ = bf16[128,512]{1,0:T(8,128)(2,1)S(1)} collective-permute-done((bf16[128,512]{1,0:T(8,128)(2,1)}, bf16[128,512]{1,0:T(8,128)(2,1)S(1)}, u32[]{:S(2)}, u32[]{:S(2)}) %collective-permute-start.2) | collective-permute-done | bytes 131104 | tf_op jit(solution)/shard_map/ppermute | solution.py:21
  10.2 1.7 %collective-permute-start.3 = (bf16[640,512]{1,0:T(8,128)(2,1)}, bf16[640,512]{1,0:T(8,128)(2,1)S(1)}, u32[]{:S(2)}, u32[]{:S(2)}) collective-permute-start(bf16[640,512]{1,0:T(8,128)(2,1)} %get-tuple-element.15.refs_0_.refs_4_), channel_id=1, source_target_pairs={{0,2},{2,0},{1,3},{3,1},{4,6},{6,4},{5,7},{7,5},{8,10},{10,8},{9,1... | collective-permute-start | bytes 1966088 | tf_op jit(solution)/shard_map/ppermute | solution.py:21
  12.5 0.8 %collective-permute-done.5.refs_3_ = bf16[128,512]{1,0:T(8,128)(2,1)S(1)} collective-permute-done((bf16[128,512]{1,0:T(8,128)(2,1)S(1)}, bf16[128,512]{1,0:T(8,128)(2,1)S(1)}, u32[]{:S(2)}, u32[]{:S(2)}) %collective-permute-start.5) | collective-permute-done | bytes 131104 | tf_op jit(solution)/shard_map/ppermute | solution.py:21
  13.6 3.7 %encode.1 = (f32[128,512]{1,0:T(8,128)S(1)}, bf16[128,512]{1,0:T(8,128)(2,1)S(1)}, bf16[128,512]{1,0:T(8,128)(2,1)S(1)}, bf16[128,512]{1,0:T(8,128)(2,1)S(1)}) custom-call(s32[1,1024]{1,0:T(1,128)S(1)} %bitcast.2, bf16[1024,512]{1,0:T(8,128)(2,1)S(1)} %copy-done.1, bf16[128,512]{1,0:T(8,128)(2,1)S(1)} %copy-done.4, ...), custom_call_target="tpu_custom_call" | custom-call | flops 1610612736 | bytes 2621440 | tf_op jit(solution)/shard_map/encode/pallas_call | solution.py:258
  17.3 1.6 %collective-permute-start.8 = (bf16[128,512]{1,0:T(8,128)(2,1)S(1)}, bf16[128,512]{1,0:T(8,128)(2,1)S(1)}, u32[]{:S(2)}, u32[]{:S(2)}) collective-permute-start(bf16[128,512]{1,0:T(8,128)(2,1)S(1)} %get-tuple-element.16), channel_id=1, source_target_pairs={{0,4},{4,8},{8,12},{12,0},{1,5},{5,9},{9,13},{13,1},{2,6},{6,10},{... | collective-permute-start | bytes 393224 | tf_op jit(solution)/shard_map/ppermute | solution.py:21
  18.9 2.6 %collective-permute-start.9 = (bf16[128,512]{1,0:T(8,128)(2,1)S(1)}, bf16[128,512]{1,0:T(8,128)(2,1)S(1)}, u32[]{:S(2)}, u32[]{:S(2)}) collective-permute-start(bf16[128,512]{1,0:T(8,128)(2,1)S(1)} %get-tuple-element.17), channel_id=1, source_target_pairs={{0,8},{4,12},{8,0},{12,4},{1,9},{5,13},{9,1},{13,5},{2,10},{6,14},... | collective-permute-start | bytes 393224 | tf_op jit(solution)/shard_map/ppermute | solution.py:21
  21.5 1.3 %collective-permute-start.10 = (bf16[128,512]{1,0:T(8,128)(2,1)S(1)}, bf16[128,512]{1,0:T(8,128)(2,1)S(1)}, u32[]{:S(2)}, u32[]{:S(2)}) collective-permute-start(bf16[128,512]{1,0:T(8,128)(2,1)S(1)} %get-tuple-element.18), channel_id=1, source_target_pairs={{0,12},{4,0},{8,4},{12,8},{1,13},{5,1},{9,5},{13,9},{2,14},{6,2},{... | collective-permute-start | bytes 393224 | tf_op jit(solution)/shard_map/ppermute | solution.py:21
  22.9 0.5 collective-permute-start.15
  23.4 2.1 %collective-permute-done.8.refs_1_ = bf16[128,512]{1,0:T(8,128)(2,1)S(1)} collective-permute-done((bf16[128,512]{1,0:T(8,128)(2,1)S(1)}, bf16[128,512]{1,0:T(8,128)(2,1)S(1)}, u32[]{:S(2)}, u32[]{:S(2)}) %collective-permute-start.8) | collective-permute-done | bytes 131104 | tf_op jit(solution)/shard_map/ppermute | solution.py:21
  25.6 5.1 %collective-permute-done.9.refs_2_ = bf16[128,512]{1,0:T(8,128)(2,1)S(1)} collective-permute-done((bf16[128,512]{1,0:T(8,128)(2,1)S(1)}, bf16[128,512]{1,0:T(8,128)(2,1)S(1)}, u32[]{:S(2)}, u32[]{:S(2)}) %collective-permute-start.9) | collective-permute-done | bytes 131104 | tf_op jit(solution)/shard_map/ppermute | solution.py:21
  30.7 0.5 collective-permute-start.14
  31.2 1.6 %collective-permute-done.11.refs_3_.refs_7_ = bf16[640,512]{1,0:T(8,128)(2,1)S(1)} collective-permute-done((bf16[640,512]{1,0:T(8,128)(2,1)S(1)}, bf16[640,512]{1,0:T(8,128)(2,1)S(1)}, u32[]{:S(2)}, u32[]{:S(2)}) %collective-permute-start.11) | collective-permute-done | bytes 655392 | tf_op jit(solution)/shard_map/ppermute | solution.py:21
  32.7 1.6 %node_update.1 = (bf16[64,512]{1,0:T(8,128)(2,1)S(1)}, bf16[64,512]{1,0:T(8,128)(2,1)S(1)}) custom-call(bf16[128,512]{1,0:T(8,128)(2,1)S(1)} %copy-done.2, f32[128,512]{1,0:T(8,128)S(1)} %get-tuple-element.20.refs_0_, bf16[128,512]{1,0:T(8,128)(2,1)S(1)} %collective-permute-done.8.refs_1_, bf16[128,512]{1,0:T(8,128)(2,1)S(1)} %collective-permute-done.9.refs_2_, ...), custom_call_target="tpu_custom_call" | custom-call | flops 201326592 | bytes 1703936 | tf_op jit(solution)/shard_map/node_update/pallas_call | solution.py:292
  34.4 4.5 %grid_update.1 = bf16[1024,512]{1,0:T(8,128)(2,1)} custom-call(bf16[1024,512]{1,0:T(8,128)(2,1)S(1)} %copy-done.1, bf16[640,512]{1,0:T(8,128)(2,1)S(1)} %copy-done, bf16[640,512]{1,0:T(8,128)(2,1)S(1)} %collective-permute-done.refs_1_.refs_5_, bf16[640,512]{1,0:T(8,128)(2,1)S(1)} %collective-permute-done.3.refs_2_.refs_6_, ...), custom_call_target="tpu_custom_call" | custom-call | flops 1073741824 | bytes 2097152 | tf_op jit(solution)/shard_map/grid_update/pallas_call | solution.py:280
  38.8 4.3 %collective-permute-done.15.refs_2_ = bf16[768,512]{1,0:T(8,128)(2,1)S(1)} collective-permute-done((bf16[768,512]{1,0:T(8,128)(2,1)S(1)}, bf16[768,512]{1,0:T(8,128)(2,1)S(1)}, u32[]{:S(2)}, u32[]{:S(2)}) %collective-permute-start.15) | collective-permute-done | bytes 786464 | tf_op jit(solution)/shard_map/ppermute | solution.py:21
  43.2 1.5 %collective-permute-start.12 = (bf16[64,512]{1,0:T(8,128)(2,1)S(1)}, bf16[64,512]{1,0:T(8,128)(2,1)S(1)}, u32[]{:S(2)}, u32[]{:S(2)}) collective-permute-start(bf16[64,512]{1,0:T(8,128)(2,1)S(1)} %get-tuple-element.21.tail_ref), channel_id=1, source_target_pairs={{0,4},{4,8},{8,12},{12,0},{1,5},{5,9},{9,13},{13,1},{2,6},{6,10},{... | collective-permute-start | bytes 196616 | tf_op jit(solution)/shard_map/ppermute | solution.py:21
  44.7 2.3 %collective-permute-start.13 = (bf16[64,512]{1,0:T(8,128)(2,1)S(1)}, bf16[64,512]{1,0:T(8,128)(2,1)S(1)}, u32[]{:S(2)}, u32[]{:S(2)}) collective-permute-start(bf16[64,512]{1,0:T(8,128)(2,1)S(1)} %get-tuple-element.22.head_ref), channel_id=1, source_target_pairs={{0,12},{4,0},{8,4},{12,8},{1,13},{5,1},{9,5},{13,9},{2,14},{6,2},{... | collective-permute-start | bytes 196616 | tf_op jit(solution)/shard_map/ppermute | solution.py:21
  47.1 2.5 %collective-permute-done.12.before_ref = bf16[64,512]{1,0:T(8,128)(2,1)S(1)} collective-permute-done((bf16[64,512]{1,0:T(8,128)(2,1)S(1)}, bf16[64,512]{1,0:T(8,128)(2,1)S(1)}, u32[]{:S(2)}, u32[]{:S(2)}) %collective-permute-start.12) | collective-permute-done | bytes 65568 | tf_op jit(solution)/shard_map/ppermute | solution.py:21
  49.6 0.7 %collective-permute-done.13.after_ref = bf16[64,512]{1,0:T(8,128)(2,1)S(1)} collective-permute-done((bf16[64,512]{1,0:T(8,128)(2,1)S(1)}, bf16[64,512]{1,0:T(8,128)(2,1)S(1)}, u32[]{:S(2)}, u32[]{:S(2)}) %collective-permute-start.13) | collective-permute-done | bytes 65568 | tf_op jit(solution)/shard_map/ppermute | solution.py:21
  50.3 5.1 %edge_update.1 = bf16[128,512]{1,0:T(8,128)(2,1)} custom-call(s32[128,6]{1,0:T(8,128)S(1)} %copy.17.nbr_ref, bf16[64,512]{1,0:T(8,128)(2,1)S(1)} %collective-permute-done.12.before_ref, bf16[64,512]{1,0:T(8,128)(2,1)S(1)} %get-tuple-element.22.head_ref, bf16[64,512]{1,0:T(8,128)(2,1)S(1)} %get-tuple-element.21.tail_ref, ...), custom_call_target="tpu_custom_call" | custom-call | flops 1207959552 | bytes 2359296 | tf_op jit(solution)/shard_map/edge_update/pallas_call | solution.py:306
  (36 shorter events, 1.0 us)
Async XLA Ops:
  0.6 12.9 %copy-start.1 = (bf16[1024,512]{1,0:T(8,128)(2,1)S(1)}, bf16[1024,512]{1,0:T(8,128)(2,1)}, u32[]{:S(2)}) copy-start(bf16[1024,512]{1,0:T(8,128)(2,1)} %lat_ref.4) | copy-start | bytes 3145732
  0.6 7.5 %collective-permute-start.1 = (bf16[128,512]{1,0:T(8,128)(2,1)}, bf16[128,512]{1,0:T(8,128)(2,1)S(1)}, u32[]{:S(2)}, u32[]{:S(2)}) collective-permute-start(bf16[128,512]{1,0:T(8,128)(2,1)} %refs_0_.3), channel_id=1, source_target_pairs={{0,2},{2,0},{1,3},{3,1},{4,6},{6,4},{5,7},{7,5},{8,10},{10,8},{9,1... | collective-permute-start | bytes 393224 | tf_op jit(solution)/shard_map/ppermute | solution.py:21
  3.6 6.5 %collective-permute-start.2 = (bf16[128,512]{1,0:T(8,128)(2,1)}, bf16[128,512]{1,0:T(8,128)(2,1)S(1)}, u32[]{:S(2)}, u32[]{:S(2)}) collective-permute-start(bf16[128,512]{1,0:T(8,128)(2,1)} %refs_4_.3), channel_id=1, source_target_pairs={{0,2},{2,0},{1,3},{3,1},{4,6},{6,4},{5,7},{7,5},{8,10},{10,8},{9,1... | collective-permute-start | bytes 393224 | tf_op jit(solution)/shard_map/ppermute | solution.py:21
  3.7 8.8 %collective-permute-start.4 = (bf16[128,512]{1,0:T(8,128)(2,1)}, bf16[128,512]{1,0:T(8,128)(2,1)S(1)}, u32[]{:S(2)}, u32[]{:S(2)}) collective-permute-start(bf16[128,512]{1,0:T(8,128)(2,1)} %refs_0_.3), channel_id=1, source_target_pairs={{0,1},{1,0},{2,3},{3,2},{4,5},{5,4},{6,7},{7,6},{8,9},{9,8},{10,11... | collective-permute-start | bytes 393224 | tf_op jit(solution)/shard_map/ppermute | solution.py:21
  3.7 8.8 %collective-permute-start.6 = (bf16[128,512]{1,0:T(8,128)(2,1)}, bf16[128,512]{1,0:T(8,128)(2,1)S(1)}, u32[]{:S(2)}, u32[]{:S(2)}) collective-permute-start(bf16[128,512]{1,0:T(8,128)(2,1)} %refs_4_.3), channel_id=1, source_target_pairs={{0,1},{1,0},{2,3},{3,2},{4,5},{5,4},{6,7},{7,6},{8,9},{9,8},{10,11... | collective-permute-start | bytes 393224 | tf_op jit(solution)/shard_map/ppermute | solution.py:21
  4.2 9.3 %copy-start.4 = (bf16[128,512]{1,0:T(8,128)(2,1)S(1)}, bf16[128,512]{1,0:T(8,128)(2,1)}, u32[]{:S(2)}) copy-start(bf16[128,512]{1,0:T(8,128)(2,1)} %refs_0_.3) | copy-start | bytes 393220
  4.2 9.3 %copy-start.5 = (bf16[128,512]{1,0:T(8,128)(2,1)S(1)}, bf16[128,512]{1,0:T(8,128)(2,1)}, u32[]{:S(2)}) copy-start(bf16[128,512]{1,0:T(8,128)(2,1)} %refs_4_.3) | copy-start | bytes 393220
  10.2 20.5 %collective-permute-start.3 = (bf16[640,512]{1,0:T(8,128)(2,1)}, bf16[640,512]{1,0:T(8,128)(2,1)S(1)}, u32[]{:S(2)}, u32[]{:S(2)}) collective-permute-start(bf16[640,512]{1,0:T(8,128)(2,1)} %get-tuple-element.15.refs_0_.refs_4_), channel_id=1, source_target_pairs={{0,2},{2,0},{1,3},{3,1},{4,6},{6,4},{5,7},{7,5},{8,10},{10,8},{9,1... | collective-permute-start | bytes 1966088 | tf_op jit(solution)/shard_map/ppermute | solution.py:21
  11.9 1.4 %collective-permute-start.5 = (bf16[128,512]{1,0:T(8,128)(2,1)S(1)}, bf16[128,512]{1,0:T(8,128)(2,1)S(1)}, u32[]{:S(2)}, u32[]{:S(2)}) collective-permute-start(bf16[128,512]{1,0:T(8,128)(2,1)S(1)} %collective-permute-done.1.refs_2_), channel_id=1, source_target_pairs={{0,1},{1,0},{2,3},{3,2},{4,5},{5,4},{6,7},{7,6},{8,9},{9,8},{10,11... | collective-permute-start | bytes 393224 | tf_op jit(solution)/shard_map/ppermute | solution.py:21
  12.0 1.5 %collective-permute-start.7 = (bf16[128,512]{1,0:T(8,128)(2,1)S(1)}, bf16[128,512]{1,0:T(8,128)(2,1)S(1)}, u32[]{:S(2)}, u32[]{:S(2)}) collective-permute-start(bf16[128,512]{1,0:T(8,128)(2,1)S(1)} %collective-permute-done.2.refs_6_), channel_id=1, source_target_pairs={{0,1},{1,0},{2,3},{3,2},{4,5},{5,4},{6,7},{7,6},{8,9},{9,8},{10,11... | collective-permute-start | bytes 393224 | tf_op jit(solution)/shard_map/ppermute | solution.py:21
  13.5 9.3 %copy-start.3 = (bf16[768,512]{1,0:T(8,128)(2,1)S(1)}, bf16[768,512]{1,0:T(8,128)(2,1)}, u32[]{:S(2)}) copy-start(bf16[768,512]{1,0:T(8,128)(2,1)} %get-tuple-element.24.refs_0_) | copy-start | bytes 2359300
  13.5 12.0 %copy-start = (bf16[640,512]{1,0:T(8,128)(2,1)S(1)}, bf16[640,512]{1,0:T(8,128)(2,1)}, u32[]{:S(2)}) copy-start(bf16[640,512]{1,0:T(8,128)(2,1)} %get-tuple-element.15.refs_0_.refs_4_) | copy-start | bytes 1966084
  13.6 19.2 %copy-start.2 = (bf16[128,512]{1,0:T(8,128)(2,1)S(1)}, bf16[128,512]{1,0:T(8,128)(2,1)}, u32[]{:S(2)}) copy-start(bf16[128,512]{1,0:T(8,128)(2,1)} %lat_ref.5) | copy-start | bytes 393220
  17.3 8.3 %collective-permute-start.8 = (bf16[128,512]{1,0:T(8,128)(2,1)S(1)}, bf16[128,512]{1,0:T(8,128)(2,1)S(1)}, u32[]{:S(2)}, u32[]{:S(2)}) collective-permute-start(bf16[128,512]{1,0:T(8,128)(2,1)S(1)} %get-tuple-element.16), channel_id=1, source_target_pairs={{0,4},{4,8},{8,12},{12,0},{1,5},{5,9},{9,13},{13,1},{2,6},{6,10},{... | collective-permute-start | bytes 393224 | tf_op jit(solution)/shard_map/ppermute | solution.py:21
  18.9 11.7 %collective-permute-start.9 = (bf16[128,512]{1,0:T(8,128)(2,1)S(1)}, bf16[128,512]{1,0:T(8,128)(2,1)S(1)}, u32[]{:S(2)}, u32[]{:S(2)}) collective-permute-start(bf16[128,512]{1,0:T(8,128)(2,1)S(1)} %get-tuple-element.17), channel_id=1, source_target_pairs={{0,8},{4,12},{8,0},{12,4},{1,9},{5,13},{9,1},{13,5},{2,10},{6,14},... | collective-permute-start | bytes 393224 | tf_op jit(solution)/shard_map/ppermute | solution.py:21
  21.5 9.1 %collective-permute-start.10 = (bf16[128,512]{1,0:T(8,128)(2,1)S(1)}, bf16[128,512]{1,0:T(8,128)(2,1)S(1)}, u32[]{:S(2)}, u32[]{:S(2)}) collective-permute-start(bf16[128,512]{1,0:T(8,128)(2,1)S(1)} %get-tuple-element.18), channel_id=1, source_target_pairs={{0,12},{4,0},{8,4},{12,8},{1,13},{5,1},{9,5},{13,9},{2,14},{6,2},{... | collective-permute-start | bytes 393224 | tf_op jit(solution)/shard_map/ppermute | solution.py:21
  22.9 20.3 %collective-permute-start.15 = (bf16[768,512]{1,0:T(8,128)(2,1)S(1)}, bf16[768,512]{1,0:T(8,128)(2,1)S(1)}, u32[]{:S(2)}, u32[]{:S(2)}) collective-permute-start(bf16[768,512]{1,0:T(8,128)(2,1)S(1)} %copy-done.3), channel_id=1, source_target_pairs={{0,2},{2,0},{1,3},{3,1},{4,6},{6,4},{5,7},{7,5},{8,10},{10,8},{9,1... | collective-permute-start | bytes 2359304 | tf_op jit(solution)/shard_map/ppermute | solution.py:21
  25.6 5.6 %collective-permute-start = (bf16[640,512]{1,0:T(8,128)(2,1)S(1)}, bf16[640,512]{1,0:T(8,128)(2,1)S(1)}, u32[]{:S(2)}, u32[]{:S(2)}) collective-permute-start(bf16[640,512]{1,0:T(8,128)(2,1)S(1)} %copy-done), channel_id=1, source_target_pairs={{0,1},{1,0},{2,3},{3,2},{4,5},{5,4},{6,7},{7,6},{8,9},{9,8},{10,11... | collective-permute-start | bytes 1966088 | tf_op jit(solution)/shard_map/ppermute | solution.py:21
  30.6 2.1 %collective-permute-start.11 = (bf16[640,512]{1,0:T(8,128)(2,1)S(1)}, bf16[640,512]{1,0:T(8,128)(2,1)S(1)}, u32[]{:S(2)}, u32[]{:S(2)}) collective-permute-start(bf16[640,512]{1,0:T(8,128)(2,1)S(1)} %collective-permute-done.3.refs_2_.refs_6_), channel_id=1, source_target_pairs={{0,1},{1,0},{2,3},{3,2},{4,5},{5,4},{6,7},{7,6},{8,9},{9,8},{10,11... | collective-permute-start | bytes 1966088 | tf_op jit(solution)/shard_map/ppermute | solution.py:21
  30.7 16.4 %collective-permute-start.14 = (bf16[768,512]{1,0:T(8,128)(2,1)S(1)}, bf16[768,512]{1,0:T(8,128)(2,1)S(1)}, u32[]{:S(2)}, u32[]{:S(2)}) collective-permute-start(bf16[768,512]{1,0:T(8,128)(2,1)S(1)} %copy-done.3), channel_id=1, source_target_pairs={{0,1},{1,0},{2,3},{3,2},{4,5},{5,4},{6,7},{7,6},{8,9},{9,8},{10,11... | collective-permute-start | bytes 2359304 | tf_op jit(solution)/shard_map/ppermute | solution.py:21
  34.3 12.6 %copy-start.7 = (s32[128,6]{0,1:T(8,128)S(1)}, s32[128,6]{0,1:T(8,128)}, u32[]{:S(2)}) copy-start(s32[128,6]{0,1:T(8,128)} %param.19) | copy-start | bytes 9220
  43.1 7.1 %collective-permute-start.16 = (bf16[768,512]{1,0:T(8,128)(2,1)S(1)}, bf16[768,512]{1,0:T(8,128)(2,1)S(1)}, u32[]{:S(2)}, u32[]{:S(2)}) collective-permute-start(bf16[768,512]{1,0:T(8,128)(2,1)S(1)} %collective-permute-done.15.refs_2_), channel_id=1, source_target_pairs={{0,1},{1,0},{2,3},{3,2},{4,5},{5,4},{6,7},{7,6},{8,9},{9,8},{10,11... | collective-permute-start | bytes 2359304 | tf_op jit(solution)/shard_map/ppermute | solution.py:21
  43.2 6.5 %collective-permute-start.12 = (bf16[64,512]{1,0:T(8,128)(2,1)S(1)}, bf16[64,512]{1,0:T(8,128)(2,1)S(1)}, u32[]{:S(2)}, u32[]{:S(2)}) collective-permute-start(bf16[64,512]{1,0:T(8,128)(2,1)S(1)} %get-tuple-element.21.tail_ref), channel_id=1, source_target_pairs={{0,4},{4,8},{8,12},{12,0},{1,5},{5,9},{9,13},{13,1},{2,6},{6,10},{... | collective-permute-start | bytes 196616 | tf_op jit(solution)/shard_map/ppermute | solution.py:21
  44.7 5.6 %collective-permute-start.13 = (bf16[64,512]{1,0:T(8,128)(2,1)S(1)}, bf16[64,512]{1,0:T(8,128)(2,1)S(1)}, u32[]{:S(2)}, u32[]{:S(2)}) collective-permute-start(bf16[64,512]{1,0:T(8,128)(2,1)S(1)} %get-tuple-element.22.head_ref), channel_id=1, source_target_pairs={{0,12},{4,0},{8,4},{12,8},{1,13},{5,1},{9,5},{13,9},{2,14},{6,2},{... | collective-permute-start | bytes 196616 | tf_op jit(solution)/shard_map/ppermute | solution.py:21
  (2 other events, 10.0 us)

commit v5 on v4

--- a/solution.py
+++ b/solution.py
@@ -39,10 +39,10 @@
     )
 
 
-def load_copies(pieces, start, rows, whole, sems):
+def load_copies(pieces, starts, rows, whole, sems):
     subs = lax.axis_size("sub")
     copies = []
-    for index, piece in enumerate(pieces):
+    for index, (piece, start) in enumerate(zip(pieces, starts)):
         owner = owner_of(index // subs, index % subs)
         there = whole.at[pl.ds(pl.multiple_of(owner * rows, rows), rows)]
         here = piece.at[pl.ds(start, rows)]
@@ -50,33 +50,37 @@
     return copies
 
 
-def pack_copies(pieces, sizes, wanted, sems):
+def pack_copies(pieces, base, sizes, wanted, sems):
+    subs = lax.axis_size("sub")
     copies = []
     for slot, (at, whole) in enumerate(wanted.items()):
-        copies += load_copies(pieces, sum(sizes[:at]), sizes[at], whole, sems.at[slot])
+        start = sum(sizes[:at])
+        starts = [base + start] * subs + [start] * (len(pieces) - subs)
+        copies += load_copies(pieces, starts, sizes[at], whole, sems.at[slot])
     return copies
 
 
 def pack_kernel(sets, *refs):
-    sources, outs = list(refs[: sum(sets)]), refs[sum(sets) :]
+    sources, outs, everything = list(refs[: sum(sets)]), refs[sum(sets) : -1], refs[-1]
+    whole_start = 0
     for out, amount in zip(outs, sets):
         start = 0
         for _ in range(amount):
-            source = sources.pop(0)
-            out[start : start + source.shape[0]] = source[...]
-            start += source.shape[0]
+            values = sources.pop(0)[...]
+            rows = values.shape[0]
+            out[start : start + rows] = values
+            everything[whole_start : whole_start + rows] = values
+            start, whole_start = start + rows, whole_start + rows
 
 
 def pack(sets):
     width = sets[0][0].shape[1]
+    rows = [sum(weight.shape[0] for weight in one) for one in sets]
     return pl.pallas_call(
         functools.partial(pack_kernel, [len(one) for one in sets]),
-        out_shape=[
-            jax.ShapeDtypeStruct((sum(weight.shape[0] for weight in one), width), jnp.bfloat16)
-            for one in sets
-        ],
+        out_shape=[jax.ShapeDtypeStruct((size, width), jnp.bfloat16) for size in rows + [sum(rows)]],
         in_specs=[VMEM] * sum(len(one) for one in sets),
-        out_specs=[VMEM] * len(sets),
+        out_specs=[VMEM] * (len(sets) + 1),
         name="pack",
     )(*(weight for one in sets for weight in one))
 
@@ -97,13 +101,12 @@
     return jnp.dot(a, b, preferred_element_type=jnp.float32)
 
 
-def encode_kernel(count, faces, mesh_rows, target_ref, lat_ref, *refs):
+def encode_kernel(count, target_ref, lat_ref, *refs):
     in_pieces, hid_pieces = refs[:count], refs[count : 2 * count]
-    outs = refs[2 * count : 2 * count + faces]
-    w_in, w_hid, messages, sems = refs[2 * count + faces :]
+    out_ref, w_in, w_hid, messages, sems = refs[2 * count :]
     rows = w_in.shape[0] // count
-    copies = load_copies(in_pieces, 0, rows, w_in, sems.at[0])
-    copies += load_copies(hid_pieces, 0, rows, w_hid, sems.at[1])
+    copies = load_copies(in_pieces, [0] * count, rows, w_in, sems.at[0])
+    copies += load_copies(hid_pieces, [0] * count, rows, w_hid, sems.at[1])
     for copy in copies:
         copy.start()
     for copy in copies:
@@ -113,20 +116,17 @@
         here = pl.ds(start, block)
         hidden = silu(dot(lat_ref[here], w_in[...])).astype(jnp.bfloat16)
         messages[here] = layer_norm(dot(hidden, w_hid[...])).astype(jnp.bfloat16)
-    group = min(faces, 4)
-    for at in range(0, faces, group):
-        slots = lax.broadcasted_iota(jnp.int32, (group * mesh_rows, lat_ref.shape[0]), 0)
-        chosen = jnp.where(slots + at * mesh_rows == target_ref[...], 1.0, 0.0)
-        chosen = chosen.astype(jnp.bfloat16)
-        sums = dot(chosen, messages[...])
-        for face in range(group):
-            out = outs[at + face]
-            out[...] = sums[face * mesh_rows : (face + 1) * mesh_rows].astype(out.dtype)
-
-
-def grid_kernel(sizes, lat_ref, *refs):
+    slots = out_ref.shape[0]
+    block = min(slots, 512)
+    for start in range(0, slots, block):
+        here = lax.broadcasted_iota(jnp.int32, (block, lat_ref.shape[0]), 0) + start
+        chosen = jnp.where(here == target_ref[...], 1.0, 0.0).astype(jnp.bfloat16)
+        out_ref[pl.ds(start, block)] = dot(chosen, messages[...]).astype(out_ref.dtype)
+
+
+def grid_kernel(base, sizes, lat_ref, *refs):
     pieces, (out_ref, w_in, w_hid, sems) = refs[:-4], refs[-4:]
-    copies = pack_copies(pieces, sizes, {2: w_in, 3: w_hid}, sems)
+    copies = pack_copies(pieces, base, sizes, {0: w_in, 1: w_hid}, sems)
     for copy in copies:
         copy.start()
     for copy in copies:
@@ -140,16 +140,17 @@
         out_ref[here] = out.astype(jnp.bfloat16)
 
 
-def node_kernel(sizes, faces, lat_ref, *refs):
-    sums, pieces = refs[:faces], refs[faces:-5]
+def node_kernel(base, sizes, lat_ref, sums_ref, *refs):
+    pieces = refs[:-5]
     head_ref, tail_ref, w_in, w_hid, sems = refs[-5:]
     width = lat_ref.shape[1]
-    copies = pack_copies(pieces, sizes, {0: w_in, 1: w_hid}, sems)
+    copies = pack_copies(pieces, base, sizes, {0: w_in, 1: w_hid}, sems)
     for copy in copies:
         copy.start()
-    collected = sums[0][...]
-    for one in sums[1:]:
-        collected = collected + one[...].astype(jnp.float32)
+    rows = lat_ref.shape[0]
+    collected = sums_ref[:rows].astype(jnp.float32)
+    for start in range(rows, sums_ref.shape[0], rows):
+        collected = collected + sums_ref[start : start + rows].astype(jnp.float32)
     for copy in copies:
         copy.wait()
     lat = lat_ref[...]
@@ -162,10 +163,10 @@
     tail_ref[...] = mid[half:]
 
 
-def edge_kernel(sizes, nbr_ref, before_ref, head_ref, tail_ref, after_ref, *refs):
+def edge_kernel(base, sizes, nbr_ref, before_ref, head_ref, tail_ref, after_ref, *refs):
     pieces, (out_ref, p_in, p_hid, u_in, u_hid, sems_p, sems_u) = refs[:-7], refs[-7:]
-    copies_p = pack_copies(pieces, sizes, {0: p_in, 1: p_hid}, sems_p)
-    copies_u = pack_copies(pieces, sizes, {2: u_in, 3: u_hid}, sems_u)
+    copies_p = pack_copies(pieces, base, sizes, {0: p_in, 1: p_hid}, sems_p)
+    copies_u = pack_copies(pieces, base, sizes, {2: u_in, 3: u_hid}, sems_u)
     for copy in copies_p + copies_u:
         copy.start()
     rows, fanin = nbr_ref.shape
@@ -224,7 +225,7 @@
     faces = lax.axis_size("face")
     bands = lax.axis_size("band")
     count = bands * lax.axis_size("sub")
-    f32, bf16 = jnp.float32, jnp.bfloat16
+    bf16 = jnp.bfloat16
 
     def matrix(weight):
         return pltpu.VMEM((weight.shape[0] * count, weight.shape[1]), bf16)
@@ -239,29 +240,28 @@
             transcendentals=rows * width,
         )
 
-    sets = ((node_w1, node_w2, grid_w1, grid_w2), (proc_w1, proc_w2, upd_w1, upd_w2))
+    sets = ((node_w1, node_w2), (grid_w1, grid_w2), (proc_w1, proc_w2, upd_w1, upd_w2))
     sizes = [[weight.shape[0] for weight in one] for one in sets]
+    bases = [sum(sum(one) for one in sizes[:at]) for at in range(len(sets))]
     enc_far = [[shift(one, "band", step) for step in range(1, bands)] for one in (enc_w1, enc_w2)]
     enc_all = [
         own_spread(one) + relay(far) for one, far in zip((enc_w1, enc_w2), enc_far)
     ]
-    early, late = pack(sets)
-    early_sent = after(early, *enc_far[0], *enc_far[1])
-    early_far = [shift(early_sent, "band", step) for step in range(1, bands)]
-    early_near, late_near = own_spread(early), own_spread(late)
-
-    me = lax.axis_index("face")
-    distance = lax.rem(grid_route[:, 0] - me + faces, faces)
-    targets = (distance * mesh_rows + grid_slot).reshape(1, grid_rows)
-
-    block = (mesh_rows, width)
+    node, grid, late, everything = pack(sets)
+    near = own_spread(everything)
+    node_sent = after(node, *enc_far[0])
+    node_far = [shift(node_sent, "band", step) for step in range(1, bands)]
+    grid_sent = after(grid, *enc_far[1])
+    grid_far = [shift(grid_sent, "band", step) for step in range(1, bands)]
+    late_sent = after(late, enc_all[0][-1], *enc_far[1])
+    late_far = [shift(late_sent, "band", step) for step in range(1, bands)]
+
+    targets = (grid_route[:, 0] * mesh_rows + grid_slot).reshape(1, grid_rows)
     sums = pl.pallas_call(
-        functools.partial(encode_kernel, count, faces, mesh_rows),
-        out_shape=[
-            jax.ShapeDtypeStruct(block, bf16 if step else f32) for step in range(faces)
-        ],
+        functools.partial(encode_kernel, count),
+        out_shape=jax.ShapeDtypeStruct((faces * mesh_rows, width), bf16),
         in_specs=[VMEM, VMEM] + [ANY] * (2 * count),
-        out_specs=[VMEM] * faces,
+        out_specs=VMEM,
         scratch_shapes=[
             matrix(enc_w1),
             matrix(enc_w2),
@@ -272,39 +272,38 @@
         cost_estimate=cost(grid_rows, 3 * width),
         name="encode",
     )(targets, grid_lat, *enc_all[0], *enc_all[1])
-    late_sent = after(late, sums[0])
-    late_far = [shift(late_sent, "band", step) for step in range(1, bands)]
-    arrived = [sums[0]] + [shift(sums[step], "face", step) for step in range(1, faces)]
-
-    early_all = early_near + relay(early_far, *arrived[1:])
+    node_all = near + relay(node_far, sums)
+    arrived = lax.all_to_all(sums, "face", split_axis=0, concat_axis=0, tiled=True)
+
+    grid_all = near + relay(grid_far, arrived)
     grid_out = pl.pallas_call(
-        functools.partial(grid_kernel, sizes[0]),
+        functools.partial(grid_kernel, bases[1], sizes[1]),
         out_shape=jax.ShapeDtypeStruct(grid_lat.shape, bf16),
-        in_specs=[VMEM] + [ANY] * len(early_all),
+        in_specs=[VMEM] + [ANY] * len(grid_all),
         out_specs=VMEM,
         scratch_shapes=[matrix(grid_w1), matrix(grid_w2), sems(2, count)],
         compiler_params=pltpu.CompilerParams(vmem_limit_bytes=32 * MIB),
         cost_estimate=cost(grid_rows, 2 * width),
         name="grid_update",
-    )(grid_lat, *early_all)
+    )(grid_lat, *grid_all)
 
     half = (mesh_rows // 2, width)
     head, tail = pl.pallas_call(
-        functools.partial(node_kernel, sizes[0], faces),
+        functools.partial(node_kernel, bases[0], sizes[0]),
         out_shape=[jax.ShapeDtypeStruct(half, bf16)] * 2,
-        in_specs=[VMEM] * (1 + faces) + [ANY] * len(early_all),
+        in_specs=[VMEM] * 2 + [ANY] * len(node_all),
         out_specs=[VMEM] * 2,
         scratch_shapes=[matrix(node_w1), matrix(node_w2), sems(2, count)],
         compiler_params=pltpu.CompilerParams(vmem_limit_bytes=32 * MIB),
         cost_estimate=cost(mesh_rows, 3 * width),
         name="node_update",
-    )(mesh_lat, *arrived, *early_all)
+    )(mesh_lat, arrived, *node_all)
 
     before = shift(tail, "face", 1)
     behind = shift(head, "face", faces - 1)
-    late_all = late_near + relay(late_far, head, grid_out)
+    late_all = near + relay(late_far, before, behind, grid_out)
     mesh_out = pl.pallas_call(
-        functools.partial(edge_kernel, sizes[1]),
+        functools.partial(edge_kernel, bases[2], sizes[2]),
         out_shape=jax.ShapeDtypeStruct(mesh_lat.shape, bf16),
         in_specs=[VMEM] * 5 + [ANY] * len(late_all),
         out_specs=VMEM,

time: 55.5 us -> 77.7 us (1.40)
  waiting for transfers between devices: 20.7 us -> 36.2 us
  local copies, waits for them, and re-layouts: 0.15 us -> 5.41 us
  Pallas kernels: 17.4 us -> 18.5 us
    ppermute x17 -> x15, waiting for transfers between devices: 20.7 us -> 36.2 us  [shift(): lax.ppermute(value, axis, [(i, (i + step) % count) for i in range(count)])]
    unnamed x19 -> x33, local copies, waits for them, and re-layouts: 0.15 us -> 5.41 us
    ppermute x17 -> x15, starting transfers between devices: 16.3 us -> 11.1 us  [shift(): lax.ppermute(value, axis, [(i, (i + step) % count) for i in range(count)])]
    all_to_all x0 -> x1, starting transfers between devices: none -> 5.12 us  [shards(): lax.all_to_all(sums, 'face', split_axis=0, concat_axis=0, tiled=True)]
  transfers between devices with their start and end apart: 17 -> 16, of which waited for: 10 -> 6; matrix products, arithmetic and copies ran while one was open for 0% -> 0% of each run, Pallas kernels for 22% -> 18%
where the time goes in v5:
time: 77.7 us; the launch traced here: 77.2 us
  waiting for transfers between devices  36.2 us (47%)
  Pallas kernels  18.5 us (24%)
  starting transfers between devices  16.3 us (21%)
  local copies, waits for them, and re-layouts  5.41 us (7%)
  between operations  0.86 us (1%)
    ppermute x15, waiting for transfers between devices, shift(): lax.ppermute(value, axis, [(i, (i + step) % count) for i in range(count)])  36.2 us
    ppermute x15, starting transfers between devices, shift(): lax.ppermute(value, axis, [(i, (i + step) % count) for i in range(count)])  11.1 us
    unnamed x33, local copies, waits for them, and re-layouts  5.41 us
    all_to_all x1, starting transfers between devices, shards(): lax.all_to_all(sums, 'face', split_axis=0, concat_axis=0, tiled=True)  5.12 us
    pallas_call x1, Pallas kernels, shards(): pl.pallas_call(functools.partial(edge_kernel, bases[2], sizes[2]), out_sh...  4.88 us
    pallas_call x1, Pallas kernels, shards(): pl.pallas_call(functools.partial(grid_kernel, bases[1], sizes[1]), out_sh...  4.85 us
    pallas_call x1, Pallas kernels, shards(): pl.pallas_call(functools.partial(encode_kernel, count), out_shape=jax.Sha...  3.68 us
    pallas_call x1, Pallas kernels, pack(): pl.pallas_call(functools.partial(pack_kernel, [len(one) for one in sets])...  2.99 us
  transfers between devices with their start and end apart: 16, of which 6 were waited for; matrix products, arithmetic and copies ran while one was open for 0% of the time, Pallas kernels for 18%

profile of v5, /device:TPU:0, one launch (start us, length us, event | category | flops | bytes accessed | tf_op | source)
XLA Modules:
  0.0 77.2 jit_solution(2864775255107950359)
XLA Ops:
  0.7 3.0 %collective-permute-start.4 = (bf16[128,512]{1,0:T(8,128)(2,1)}, bf16[128,512]{1,0:T(8,128)(2,1)S(1)}, u32[]{:S(2)}, u32[]{:S(2)}) collective-permute-start(bf16[128,512]{1,0:T(8,128)(2,1)} %refs_0_.3), channel_id=1, source_target_pairs={{0,2},{2,0},{1,3},{3,1},{4,6},{6,4},{5,7},{7,5},{8,10},{10,8},{9,1... | collective-permute-start | bytes 393224 | tf_op jit(solution)/shard_map/ppermute | solution.py:21
  3.8 3.0 %pack.1 = (bf16[384,512]{1,0:T(8,128)(2,1)}, bf16[256,512]{1,0:T(8,128)(2,1)}, bf16[768,512]{1,0:T(8,128)(2,1)}, bf16[1408,512]{1,0:T(8,128)(2,1)}) custom-call(bf16[256,512]{1,0:T(8,128)(2,1)} %refs_0_.2, bf16[128,512]{1,0:T(8,128)(2,1)} %refs_1_.1, bf16[128,512]{1,0:T(8,128)(2,1)} %refs_2_.1, bf16[128,512]{1,0:T(8,128)(2,1)} %refs_3_.1, ...), custom_call_target="tpu_custom_call" | custom-call | tf_op jit(solution)/shard_map/pack/pallas_call | solution.py:79
  7.3 0.9 %collective-permute-done.4.refs_2_ = bf16[128,512]{1,0:T(8,128)(2,1)S(1)} collective-permute-done((bf16[128,512]{1,0:T(8,128)(2,1)}, bf16[128,512]{1,0:T(8,128)(2,1)S(1)}, u32[]{:S(2)}, u32[]{:S(2)}) %collective-permute-start.4) | collective-permute-done | bytes 131104 | tf_op jit(solution)/shard_map/ppermute | solution.py:21
  8.2 2.0 %collective-permute-done.1.refs_6_ = bf16[128,512]{1,0:T(8,128)(2,1)S(1)} collective-permute-done((bf16[128,512]{1,0:T(8,128)(2,1)}, bf16[128,512]{1,0:T(8,128)(2,1)S(1)}, u32[]{:S(2)}, u32[]{:S(2)}) %collective-permute-start.1) | collective-permute-done | bytes 131104 | tf_op jit(solution)/shard_map/ppermute | solution.py:21
  10.2 0.7 copy-done.11
  10.9 0.6 collective-permute-done.7.refs_7_
  11.5 1.2 %copy-done.1 = bf16[1024,512]{1,0:T(8,128)(2,1)S(1)} copy-done((bf16[1024,512]{1,0:T(8,128)(2,1)S(1)}, bf16[1024,512]{1,0:T(8,128)(2,1)}, u32[]{:S(2)}) %copy-start.1) | copy-done | bytes 1048600
  12.8 0.9 %copy-done.12 = bf16[128,512]{1,0:T(8,128)(2,1)S(1)} copy-done((bf16[128,512]{1,0:T(8,128)(2,1)S(1)}, bf16[128,512]{1,0:T(8,128)(2,1)}, u32[]{:S(2)}) %copy-start.12) | copy-done | bytes 131096
  13.7 3.7 %encode.1 = bf16[512,512]{1,0:T(8,128)(2,1)S(1)} custom-call(s32[1,1024]{1,0:T(1,128)S(1)} %bitcast.6, bf16[1024,512]{1,0:T(8,128)(2,1)S(1)} %copy-done.1, bf16[128,512]{1,0:T(8,128)(2,1)S(1)} %copy-done.9, bf16[128,512]{1,0:T(8,128)(2,1)S(1)} %collective-permute-done.3.refs_1_, bf16[128,512]{1,0:T(8,128)(2,1)S(1)} %collective-permute-done.4.refs_2_, ...), custom_call_target="tpu_custom_call" | custom-call | flops 1610612736 | bytes 2621440 | tf_op jit(solution)/shard_map/encode/pallas_call | solution.py:260
  17.4 0.8 %copy-done.3 = bf16[512,512]{1,0:T(8,128)(2,1)} copy-done((bf16[512,512]{1,0:T(8,128)(2,1)}, bf16[512,512]{1,0:T(8,128)(2,1)S(1)}, u32[]{:S(2)}) %copy-start.3) | copy-done | bytes 524312
  18.2 5.1 %all-to-all-start = ((bf16[4,128,512]{2,1,0:T(8,128)(2,1)}), bf16[4,128,512]{2,1,0:T(8,128)(2,1)S(1)}, u32[]{:S(2)}, u32[]{:S(2)}) async-start(bf16[4,128,512]{2,1,0:T(8,128)(2,1)} %bitcast.5), calls=%async_computation | async-start | bytes 1048576 | tf_op jit(solution)/shard_map/all_to_all | solution.py:276
  23.3 1.5 %collective-permute-start.9 = (bf16[384,512]{1,0:T(8,128)(2,1)}, bf16[384,512]{1,0:T(8,128)(2,1)}, u32[]{:S(2)}, u32[]{:S(2)}) collective-permute-start(bf16[384,512]{1,0:T(8,128)(2,1)} %get-tuple-element.19), channel_id=1, source_target_pairs={{0,2},{2,0},{1,3},{3,1},{4,6},{6,4},{5,7},{7,5},{8,10},{10,8},{9,1... | collective-permute-start | bytes 1179656 | tf_op jit(solution)/shard_map/ppermute | solution.py:21
  24.8 0.5 collective-permute-start.13
  25.3 1.5 %collective-permute-start.2 = (bf16[256,512]{1,0:T(8,128)(2,1)}, bf16[256,512]{1,0:T(8,128)(2,1)}, u32[]{:S(2)}, u32[]{:S(2)}) collective-permute-start(bf16[256,512]{1,0:T(8,128)(2,1)} %get-tuple-element.16), channel_id=1, source_target_pairs={{0,2},{2,0},{1,3},{3,1},{4,6},{6,4},{5,7},{7,5},{8,10},{10,8},{9,1... | collective-permute-start | bytes 786440 | tf_op jit(solution)/shard_map/ppermute | solution.py:21
  26.8 8.8 %collective-permute-done.9.refs_2_ = bf16[384,512]{1,0:T(8,128)(2,1)} collective-permute-done((bf16[384,512]{1,0:T(8,128)(2,1)}, bf16[384,512]{1,0:T(8,128)(2,1)}, u32[]{:S(2)}, u32[]{:S(2)}) %collective-permute-start.9) | collective-permute-done | bytes 393248 | tf_op jit(solution)/shard_map/ppermute | solution.py:21
  35.6 21.4 %collective-permute-done.2.refs_2_ = bf16[256,512]{1,0:T(8,128)(2,1)} collective-permute-done((bf16[256,512]{1,0:T(8,128)(2,1)}, bf16[256,512]{1,0:T(8,128)(2,1)}, u32[]{:S(2)}, u32[]{:S(2)}) %collective-permute-start.2) | collective-permute-done | bytes 262176 | tf_op jit(solution)/shard_map/ppermute | solution.py:21
  57.0 2.2 %node_update.1 = (bf16[64,512]{1,0:T(8,128)(2,1)S(1)}, bf16[64,512]{1,0:T(8,128)(2,1)S(1)}) custom-call(bf16[128,512]{1,0:T(8,128)(2,1)S(1)} %copy-done.4, bf16[512,512]{1,0:T(8,128)(2,1)S(1)} %bitcast.4, bf16[1408,512]{1,0:T(8,128)(2,1)S(1)} %copy-done, bf16[1408,512]{1,0:T(8,128)(2,1)S(1)} %collective-permute-done.refs_1_, ...), custom_call_target="tpu_custom_call" | custom-call | flops 201326592 | bytes 1703936 | tf_op jit(solution)/shard_map/node_update/pallas_call | solution.py:291
  59.2 1.8 %collective-permute-start.11 = (bf16[64,512]{1,0:T(8,128)(2,1)S(1)}, bf16[64,512]{1,0:T(8,128)(2,1)S(1)}, u32[]{:S(2)}, u32[]{:S(2)}) collective-permute-start(bf16[64,512]{1,0:T(8,128)(2,1)S(1)} %get-tuple-element.21.tail_ref), channel_id=1, source_target_pairs={{0,4},{4,8},{8,12},{12,0},{1,5},{5,9},{9,13},{13,1},{2,6},{6,10},{... | collective-permute-start | bytes 196616 | tf_op jit(solution)/shard_map/ppermute | solution.py:21
  61.0 2.1 %collective-permute-start.12 = (bf16[64,512]{1,0:T(8,128)(2,1)S(1)}, bf16[64,512]{1,0:T(8,128)(2,1)S(1)}, u32[]{:S(2)}, u32[]{:S(2)}) collective-permute-start(bf16[64,512]{1,0:T(8,128)(2,1)S(1)} %get-tuple-element.22.head_ref), channel_id=1, source_target_pairs={{0,12},{4,0},{8,4},{12,8},{1,13},{5,1},{9,5},{13,9},{2,14},{6,2},{... | collective-permute-start | bytes 196616 | tf_op jit(solution)/shard_map/ppermute | solution.py:21
  63.1 4.8 %grid_update.1 = bf16[1024,512]{1,0:T(8,128)(2,1)} custom-call(bf16[1024,512]{1,0:T(8,128)(2,1)S(1)} %copy-done.2, bf16[1408,512]{1,0:T(8,128)(2,1)S(1)} %copy-done, bf16[1408,512]{1,0:T(8,128)(2,1)S(1)} %collective-permute-done.refs_1_, bf16[256,512]{1,0:T(8,128)(2,1)} %collective-permute-done.2.refs_2_, bf16[256,512]{1,0:T(8,128)(2,1)S(1)} %collective-permute-done.8.refs_3_), custom_call_target="tpu_custom_call" | custom-call | flops 1073741824 | bytes 2097152 | tf_op jit(solution)/shard_map/grid_update/pallas_call | solution.py:279
  68.2 2.5 %collective-permute-done.14.refs_3_ = bf16[768,512]{1,0:T(8,128)(2,1)} collective-permute-done((bf16[768,512]{1,0:T(8,128)(2,1)}, bf16[768,512]{1,0:T(8,128)(2,1)}, u32[]{:S(2)}, u32[]{:S(2)}) %collective-permute-start.14) | collective-permute-done | bytes 786464 | tf_op jit(solution)/shard_map/ppermute | solution.py:21
  70.7 0.8 %copy-done.6 = bf16[64,512]{1,0:T(8,128)(2,1)S(1)} copy-done((bf16[64,512]{1,0:T(8,128)(2,1)S(1)}, bf16[64,512]{1,0:T(8,128)(2,1)}, u32[]{:S(2)}) %copy-start.6) | copy-done | bytes 65560
  71.5 0.8 %copy-done.8 = bf16[64,512]{1,0:T(8,128)(2,1)S(1)} copy-done((bf16[64,512]{1,0:T(8,128)(2,1)S(1)}, bf16[64,512]{1,0:T(8,128)(2,1)}, u32[]{:S(2)}) %copy-start.8) | copy-done | bytes 65560
  72.4 4.9 %edge_update.1 = bf16[128,512]{1,0:T(8,128)(2,1)} custom-call(s32[128,6]{1,0:T(8,128)S(1)} %copy.17.nbr_ref, bf16[64,512]{1,0:T(8,128)(2,1)S(1)} %collective-permute-done.11.before_ref, bf16[64,512]{1,0:T(8,128)(2,1)S(1)} %copy-done.6, bf16[64,512]{1,0:T(8,128)(2,1)S(1)} %copy-done.8, bf16[64,512]{1,0:T(8,128)(2,1)S(1)} %collective-permute-done.12.after_ref, ...), custom_call_target="tpu_custom_call" | custom-call | flops 1207959552 | bytes 2359296 | tf_op jit(solution)/shard_map/edge_update/pallas_call | solution.py:305
  (48 shorter events, 0.9 us)
Async XLA Ops:
  0.6 6.6 %copy-start.10 = (bf16[128,512]{1,0:T(8,128)(2,1)S(1)}, bf16[128,512]{1,0:T(8,128)(2,1)}, u32[]{:S(2)}) copy-start(bf16[128,512]{1,0:T(8,128)(2,1)} %refs_4_.3) | copy-start | bytes 393220
  0.7 10.2 %copy-start.15 = (s32[1024,1]{0,1:T(1,128)S(1)}, s32[1024,1]{0,1:T(1,128)}, u32[]{:S(2)}) copy-start(s32[1024,1]{0,1:T(1,128)} %param.16) | copy-start | bytes 12292
  0.7 10.2 %copy-start.13 = (s32[1024]{0:T(1024)S(1)}, s32[1024]{0:T(1024)}, u32[]{:S(2)}) copy-start(s32[1024]{0:T(1024)} %param.17) | copy-start | bytes 12292
  0.7 7.5 %collective-permute-start.4 = (bf16[128,512]{1,0:T(8,128)(2,1)}, bf16[128,512]{1,0:T(8,128)(2,1)S(1)}, u32[]{:S(2)}, u32[]{:S(2)}) collective-permute-start(bf16[128,512]{1,0:T(8,128)(2,1)} %refs_0_.3), channel_id=1, source_target_pairs={{0,2},{2,0},{1,3},{3,1},{4,6},{6,4},{5,7},{7,5},{8,10},{10,8},{9,1... | collective-permute-start | bytes 393224 | tf_op jit(solution)/shard_map/ppermute | solution.py:21
  3.7 6.5 %collective-permute-start.1 = (bf16[128,512]{1,0:T(8,128)(2,1)}, bf16[128,512]{1,0:T(8,128)(2,1)S(1)}, u32[]{:S(2)}, u32[]{:S(2)}) collective-permute-start(bf16[128,512]{1,0:T(8,128)(2,1)} %refs_4_.3), channel_id=1, source_target_pairs={{0,2},{2,0},{1,3},{3,1},{4,6},{6,4},{5,7},{7,5},{8,10},{10,8},{9,1... | collective-permute-start | bytes 393224 | tf_op jit(solution)/shard_map/ppermute | solution.py:21
  6.7 50.2 %collective-permute-start = (bf16[1408,512]{1,0:T(8,128)(2,1)}, bf16[1408,512]{1,0:T(8,128)(2,1)S(1)}, u32[]{:S(2)}, u32[]{:S(2)}) collective-permute-start(bf16[1408,512]{1,0:T(8,128)(2,1)} %get-tuple-element.14.refs_0_), channel_id=1, source_target_pairs={{0,1},{1,0},{2,3},{3,2},{4,5},{5,4},{6,7},{7,6},{8,9},{9,8},{10,11... | collective-permute-start | bytes 4325384 | tf_op jit(solution)/shard_map/ppermute | solution.py:21
  6.8 4.1 %collective-permute-start.3 = (bf16[128,512]{1,0:T(8,128)(2,1)S(1)}, bf16[128,512]{1,0:T(8,128)(2,1)S(1)}, u32[]{:S(2)}, u32[]{:S(2)}) collective-permute-start(bf16[128,512]{1,0:T(8,128)(2,1)S(1)} %copy-done.9), channel_id=1, source_target_pairs={{0,1},{1,0},{2,3},{3,2},{4,5},{5,4},{6,7},{7,6},{8,9},{9,8},{10,11... | collective-permute-start | bytes 393224 | tf_op jit(solution)/shard_map/ppermute | solution.py:21
  7.3 3.6 %collective-permute-start.6 = (bf16[128,512]{1,0:T(8,128)(2,1)S(1)}, bf16[128,512]{1,0:T(8,128)(2,1)S(1)}, u32[]{:S(2)}, u32[]{:S(2)}) collective-permute-start(bf16[128,512]{1,0:T(8,128)(2,1)S(1)} %copy-done.10), channel_id=1, source_target_pairs={{0,1},{1,0},{2,3},{3,2},{4,5},{5,4},{6,7},{7,6},{8,9},{9,8},{10,11... | collective-permute-start | bytes 393224 | tf_op jit(solution)/shard_map/ppermute | solution.py:21
  8.2 2.7 %collective-permute-start.5 = (bf16[128,512]{1,0:T(8,128)(2,1)S(1)}, bf16[128,512]{1,0:T(8,128)(2,1)S(1)}, u32[]{:S(2)}, u32[]{:S(2)}) collective-permute-start(bf16[128,512]{1,0:T(8,128)(2,1)S(1)} %collective-permute-done.4.refs_2_), channel_id=1, source_target_pairs={{0,1},{1,0},{2,3},{3,2},{4,5},{5,4},{6,7},{7,6},{8,9},{9,8},{10,11... | collective-permute-start | bytes 393224 | tf_op jit(solution)/shard_map/ppermute | solution.py:21
  10.2 1.3 %collective-permute-start.7 = (bf16[128,512]{1,0:T(8,128)(2,1)S(1)}, bf16[128,512]{1,0:T(8,128)(2,1)S(1)}, u32[]{:S(2)}, u32[]{:S(2)}) collective-permute-start(bf16[128,512]{1,0:T(8,128)(2,1)S(1)} %collective-permute-done.1.refs_6_), channel_id=1, source_target_pairs={{0,1},{1,0},{2,3},{3,2},{4,5},{5,4},{6,7},{7,6},{8,9},{9,8},{10,11... | collective-permute-start | bytes 393224 | tf_op jit(solution)/shard_map/ppermute | solution.py:21
  13.7 43.3 %copy-start = (bf16[1408,512]{1,0:T(8,128)(2,1)S(1)}, bf16[1408,512]{1,0:T(8,128)(2,1)}, u32[]{:S(2)}) copy-start(bf16[1408,512]{1,0:T(8,128)(2,1)} %get-tuple-element.14.refs_0_) | copy-start | bytes 4325380
  13.7 43.3 %copy-start.4 = (bf16[128,512]{1,0:T(8,128)(2,1)S(1)}, bf16[128,512]{1,0:T(8,128)(2,1)}, u32[]{:S(2)}) copy-start(bf16[128,512]{1,0:T(8,128)(2,1)} %lat_ref.5) | copy-start | bytes 393220
  18.2 38.8 %all-to-all-start = ((bf16[4,128,512]{2,1,0:T(8,128)(2,1)}), bf16[4,128,512]{2,1,0:T(8,128)(2,1)S(1)}, u32[]{:S(2)}, u32[]{:S(2)}) async-start(bf16[4,128,512]{2,1,0:T(8,128)(2,1)} %bitcast.5), calls=%async_computation | async-start | bytes 1048576 | tf_op jit(solution)/shard_map/all_to_all | solution.py:276
  23.3 12.3 %collective-permute-start.9 = (bf16[384,512]{1,0:T(8,128)(2,1)}, bf16[384,512]{1,0:T(8,128)(2,1)}, u32[]{:S(2)}, u32[]{:S(2)}) collective-permute-start(bf16[384,512]{1,0:T(8,128)(2,1)} %get-tuple-element.19), channel_id=1, source_target_pairs={{0,2},{2,0},{1,3},{3,1},{4,6},{6,4},{5,7},{7,5},{8,10},{10,8},{9,1... | collective-permute-start | bytes 1179656 | tf_op jit(solution)/shard_map/ppermute | solution.py:21
  24.8 43.2 %collective-permute-start.13 = (bf16[768,512]{1,0:T(8,128)(2,1)}, bf16[768,512]{1,0:T(8,128)(2,1)}, u32[]{:S(2)}, u32[]{:S(2)}) collective-permute-start(bf16[768,512]{1,0:T(8,128)(2,1)} %get-tuple-element.24), channel_id=1, source_target_pairs={{0,2},{2,0},{1,3},{3,1},{4,6},{6,4},{5,7},{7,5},{8,10},{10,8},{9,1... | collective-permute-start | bytes 2359304 | tf_op jit(solution)/shard_map/ppermute | solution.py:21
  25.3 31.6 %collective-permute-start.2 = (bf16[256,512]{1,0:T(8,128)(2,1)}, bf16[256,512]{1,0:T(8,128)(2,1)}, u32[]{:S(2)}, u32[]{:S(2)}) collective-permute-start(bf16[256,512]{1,0:T(8,128)(2,1)} %get-tuple-element.16), channel_id=1, source_target_pairs={{0,2},{2,0},{1,3},{3,1},{4,6},{6,4},{5,7},{7,5},{8,10},{10,8},{9,1... | collective-permute-start | bytes 786440 | tf_op jit(solution)/shard_map/ppermute | solution.py:21
  35.6 21.4 %collective-permute-start.10 = (bf16[384,512]{1,0:T(8,128)(2,1)}, bf16[384,512]{1,0:T(8,128)(2,1)}, u32[]{:S(2)}, u32[]{:S(2)}) collective-permute-start(bf16[384,512]{1,0:T(8,128)(2,1)} %collective-permute-done.9.refs_2_), channel_id=1, source_target_pairs={{0,1},{1,0},{2,3},{3,2},{4,5},{5,4},{6,7},{7,6},{8,9},{9,8},{10,11... | collective-permute-start | bytes 1179656 | tf_op jit(solution)/shard_map/ppermute | solution.py:21
  57.0 6.1 %collective-permute-start.8 = (bf16[256,512]{1,0:T(8,128)(2,1)}, bf16[256,512]{1,0:T(8,128)(2,1)S(1)}, u32[]{:S(2)}, u32[]{:S(2)}) collective-permute-start(bf16[256,512]{1,0:T(8,128)(2,1)} %collective-permute-done.2.refs_2_), channel_id=1, source_target_pairs={{0,1},{1,0},{2,3},{3,2},{4,5},{5,4},{6,7},{7,6},{8,9},{9,8},{10,11... | collective-permute-start | bytes 786440 | tf_op jit(solution)/shard_map/ppermute | solution.py:21
  59.2 8.8 %copy-start.5 = (bf16[64,512]{1,0:T(8,128)(2,1)}, bf16[64,512]{1,0:T(8,128)(2,1)S(1)}, u32[]{:S(2)}) copy-start(bf16[64,512]{1,0:T(8,128)(2,1)S(1)} %get-tuple-element.22.head_ref) | copy-start | bytes 196612
  59.2 8.8 %copy-start.7 = (bf16[64,512]{1,0:T(8,128)(2,1)}, bf16[64,512]{1,0:T(8,128)(2,1)S(1)}, u32[]{:S(2)}) copy-start(bf16[64,512]{1,0:T(8,128)(2,1)S(1)} %get-tuple-element.21.tail_ref) | copy-start | bytes 196612
  59.2 8.8 %collective-permute-start.11 = (bf16[64,512]{1,0:T(8,128)(2,1)S(1)}, bf16[64,512]{1,0:T(8,128)(2,1)S(1)}, u32[]{:S(2)}, u32[]{:S(2)}) collective-permute-start(bf16[64,512]{1,0:T(8,128)(2,1)S(1)} %get-tuple-element.21.tail_ref), channel_id=1, source_target_pairs={{0,4},{4,8},{8,12},{12,0},{1,5},{5,9},{9,13},{13,1},{2,6},{6,10},{... | collective-permute-start | bytes 196616 | tf_op jit(solution)/shard_map/ppermute | solution.py:21
  61.0 7.1 %copy-start.14 = (s32[128,6]{0,1:T(8,128)S(1)}, s32[128,6]{0,1:T(8,128)}, u32[]{:S(2)}) copy-start(s32[128,6]{0,1:T(8,128)} %param.19) | copy-start | bytes 9220
  61.0 7.0 %collective-permute-start.12 = (bf16[64,512]{1,0:T(8,128)(2,1)S(1)}, bf16[64,512]{1,0:T(8,128)(2,1)S(1)}, u32[]{:S(2)}, u32[]{:S(2)}) collective-permute-start(bf16[64,512]{1,0:T(8,128)(2,1)S(1)} %get-tuple-element.22.head_ref), channel_id=1, source_target_pairs={{0,12},{4,0},{8,4},{12,8},{1,13},{5,1},{9,5},{13,9},{2,14},{6,2},{... | collective-permute-start | bytes 196616 | tf_op jit(solution)/shard_map/ppermute | solution.py:21
  68.0 2.7 %collective-permute-start.14 = (bf16[768,512]{1,0:T(8,128)(2,1)}, bf16[768,512]{1,0:T(8,128)(2,1)}, u32[]{:S(2)}, u32[]{:S(2)}) collective-permute-start(bf16[768,512]{1,0:T(8,128)(2,1)} %collective-permute-done.13.refs_2_), channel_id=1, source_target_pairs={{0,1},{1,0},{2,3},{3,2},{4,5},{5,4},{6,7},{7,6},{8,9},{9,8},{10,11... | collective-permute-start | bytes 2359304 | tf_op jit(solution)/shard_map/ppermute | solution.py:21
  (8 other events, 17.5 us)

commit v6 on v4

--- a/solution.py
+++ b/solution.py
@@ -8,7 +8,6 @@
 from jax.sharding import PartitionSpec as P
 
 MIB = 1 << 20
-ANY = pl.BlockSpec(memory_space=pl.ANY)
 VMEM = pl.BlockSpec(memory_space=pltpu.VMEM)
 
 
@@ -19,6 +18,21 @@
 def shift(value, axis, step):
     count = lax.axis_size(axis)
     return lax.ppermute(value, axis, [(i, (i + step) % count) for i in range(count)])
+
+
+def distances(faces):
+    if faces & (faces - 1):
+        return list(range(faces))
+    return [0] + sorted(range(1, faces), key=lambda step: (step == 1, step))
+
+
+def face_at(faces, step, me):
+    return (me + step) % faces if faces & (faces - 1) else me ^ step
+
+
+def to_face(value, step):
+    faces = lax.axis_size("face")
+    return lax.ppermute(value, "face", [(i, face_at(faces, step, i)) for i in range(faces)])
 
 
 def own_spread(pack):
@@ -39,22 +53,16 @@
     )
 
 
-def load_copies(pieces, start, rows, whole, sems):
+def place(pieces, start, rows, whole):
     subs = lax.axis_size("sub")
-    copies = []
     for index, piece in enumerate(pieces):
         owner = owner_of(index // subs, index % subs)
-        there = whole.at[pl.ds(pl.multiple_of(owner * rows, rows), rows)]
-        here = piece.at[pl.ds(start, rows)]
-        copies.append(pltpu.make_async_copy(here, there, sems.at[index]))
-    return copies
-
-
-def pack_copies(pieces, sizes, wanted, sems):
-    copies = []
-    for slot, (at, whole) in enumerate(wanted.items()):
-        copies += load_copies(pieces, sum(sizes[:at]), sizes[at], whole, sems.at[slot])
-    return copies
+        whole[pl.ds(pl.multiple_of(owner * rows, rows), rows)] = piece[start : start + rows]
+
+
+def unpack(pieces, sizes, wanted):
+    for at, whole in wanted.items():
+        place(pieces, sum(sizes[:at]), sizes[at], whole)
 
 
 def pack_kernel(sets, *refs):
@@ -100,14 +108,10 @@
 def encode_kernel(count, faces, mesh_rows, target_ref, lat_ref, *refs):
     in_pieces, hid_pieces = refs[:count], refs[count : 2 * count]
     outs = refs[2 * count : 2 * count + faces]
-    w_in, w_hid, messages, sems = refs[2 * count + faces :]
+    w_in, w_hid, messages = refs[2 * count + faces :]
     rows = w_in.shape[0] // count
-    copies = load_copies(in_pieces, 0, rows, w_in, sems.at[0])
-    copies += load_copies(hid_pieces, 0, rows, w_hid, sems.at[1])
-    for copy in copies:
-        copy.start()
-    for copy in copies:
-        copy.wait()
+    place(in_pieces, 0, rows, w_in)
+    place(hid_pieces, 0, rows, w_hid)
     block = 256
     for start in range(0, lat_ref.shape[0], block):
         here = pl.ds(start, block)
@@ -125,12 +129,8 @@
 
 
 def grid_kernel(sizes, lat_ref, *refs):
-    pieces, (out_ref, w_in, w_hid, sems) = refs[:-4], refs[-4:]
-    copies = pack_copies(pieces, sizes, {2: w_in, 3: w_hid}, sems)
-    for copy in copies:
-        copy.start()
-    for copy in copies:
-        copy.wait()
+    pieces, (out_ref, w_in, w_hid) = refs[:-3], refs[-3:]
+    unpack(pieces, sizes, {2: w_in, 3: w_hid})
     block = 256
     for start in range(0, lat_ref.shape[0], block):
         here = pl.ds(start, block)
@@ -141,17 +141,13 @@
 
 
 def node_kernel(sizes, faces, lat_ref, *refs):
-    sums, pieces = refs[:faces], refs[faces:-5]
-    head_ref, tail_ref, w_in, w_hid, sems = refs[-5:]
+    sums, pieces = refs[:faces], refs[faces:-4]
+    head_ref, tail_ref, w_in, w_hid = refs[-4:]
     width = lat_ref.shape[1]
-    copies = pack_copies(pieces, sizes, {0: w_in, 1: w_hid}, sems)
-    for copy in copies:
-        copy.start()
+    unpack(pieces, sizes, {0: w_in, 1: w_hid})
     collected = sums[0][...]
     for one in sums[1:]:
         collected = collected + one[...].astype(jnp.float32)
-    for copy in copies:
-        copy.wait()
     lat = lat_ref[...]
     hidden = dot(lat, w_in[:width]) + dot(collected.astype(jnp.bfloat16), w_in[width:])
     hidden = silu(hidden).astype(jnp.bfloat16)
@@ -163,19 +159,14 @@
 
 
 def edge_kernel(sizes, nbr_ref, before_ref, head_ref, tail_ref, after_ref, *refs):
-    pieces, (out_ref, p_in, p_hid, u_in, u_hid, sems_p, sems_u) = refs[:-7], refs[-7:]
-    copies_p = pack_copies(pieces, sizes, {0: p_in, 1: p_hid}, sems_p)
-    copies_u = pack_copies(pieces, sizes, {2: u_in, 3: u_hid}, sems_u)
-    for copy in copies_p + copies_u:
-        copy.start()
+    pieces, (out_ref, p_in, p_hid, u_in, u_hid) = refs[:-5], refs[-5:]
+    unpack(pieces, sizes, {0: p_in, 1: p_hid, 2: u_in, 3: u_hid})
     rows, fanin = nbr_ref.shape
     width = head_ref.shape[1]
     mid = jnp.concatenate([head_ref[...], tail_ref[...]], axis=0)
     extended = jnp.concatenate([before_ref[...], mid, after_ref[...]], axis=0)
     spots = lax.broadcasted_iota(jnp.int32, (rows, extended.shape[0]), 1)
     nbr = nbr_ref[...]
-    for copy in copies_p:
-        copy.wait()
     receivers = dot(mid, p_in[width:])
     total = None
     group = 2 if fanin % 2 == 0 else 1
@@ -194,8 +185,6 @@
         for k in range(group):
             one = edges[k * rows : (k + 1) * rows]
             total = one if total is None else total + one
-    for copy in copies_u:
-        copy.wait()
     hidden = dot(mid, u_in[:width]) + dot(total.astype(jnp.bfloat16), u_in[width:])
     hidden = silu(hidden).astype(jnp.bfloat16)
     out = mid.astype(jnp.float32) + layer_norm(dot(hidden, u_hid[...]))
@@ -222,15 +211,12 @@
     grid_rows, width = grid_lat.shape
     mesh_rows = mesh_lat.shape[0]
     faces = lax.axis_size("face")
-    bands = lax.axis_size("band")
-    count = bands * lax.axis_size("sub")
+    bands, subs = lax.axis_size("band"), lax.axis_size("sub")
+    count = bands * subs
     f32, bf16 = jnp.float32, jnp.bfloat16
 
     def matrix(weight):
         return pltpu.VMEM((weight.shape[0] * count, weight.shape[1]), bf16)
-
-    def sems(*shape):
-        return pltpu.SemaphoreType.DMA(shape)
 
     def cost(rows, depth):
         return pl.CostEstimate(
@@ -246,12 +232,14 @@
         own_spread(one) + relay(far) for one, far in zip((enc_w1, enc_w2), enc_far)
     ]
     early, late = pack(sets)
-    early_sent = after(early, *enc_far[0], *enc_far[1])
+    early_sent = after(early, *enc_far[1], *enc_all[0][1:], *enc_all[1][1:subs])
     early_far = [shift(early_sent, "band", step) for step in range(1, bands)]
     early_near, late_near = own_spread(early), own_spread(late)
 
     me = lax.axis_index("face")
-    distance = lax.rem(grid_route[:, 0] - me + faces, faces)
+    routes = grid_route[:, 0]
+    steps = distances(faces)
+    distance = lax.rem(routes - me + faces, faces) if faces & (faces - 1) else routes ^ me
     targets = (distance * mesh_rows + grid_slot).reshape(1, grid_rows)
 
     block = (mesh_rows, width)
@@ -260,30 +248,29 @@
         out_shape=[
             jax.ShapeDtypeStruct(block, bf16 if step else f32) for step in range(faces)
         ],
-        in_specs=[VMEM, VMEM] + [ANY] * (2 * count),
+        in_specs=[VMEM, VMEM] + [VMEM] * (2 * count),
         out_specs=[VMEM] * faces,
         scratch_shapes=[
             matrix(enc_w1),
             matrix(enc_w2),
             pltpu.VMEM((grid_rows, width), bf16),
-            sems(2, count),
         ],
-        compiler_params=pltpu.CompilerParams(vmem_limit_bytes=32 * MIB),
+        compiler_params=pltpu.CompilerParams(vmem_limit_bytes=16 * MIB),
         cost_estimate=cost(grid_rows, 3 * width),
         name="encode",
     )(targets, grid_lat, *enc_all[0], *enc_all[1])
     late_sent = after(late, sums[0])
     late_far = [shift(late_sent, "band", step) for step in range(1, bands)]
-    arrived = [sums[0]] + [shift(sums[step], "face", step) for step in range(1, faces)]
+    arrived = [sums[0]] + [to_face(sums[step], step) for step in steps[1:]]
 
     early_all = early_near + relay(early_far, *arrived[1:])
     grid_out = pl.pallas_call(
         functools.partial(grid_kernel, sizes[0]),
         out_shape=jax.ShapeDtypeStruct(grid_lat.shape, bf16),
-        in_specs=[VMEM] + [ANY] * len(early_all),
+        in_specs=[VMEM] + [VMEM] * len(early_all),
         out_specs=VMEM,
-        scratch_shapes=[matrix(grid_w1), matrix(grid_w2), sems(2, count)],
-        compiler_params=pltpu.CompilerParams(vmem_limit_bytes=32 * MIB),
+        scratch_shapes=[matrix(grid_w1), matrix(grid_w2)],
+        compiler_params=pltpu.CompilerParams(vmem_limit_bytes=16 * MIB),
         cost_estimate=cost(grid_rows, 2 * width),
         name="grid_update",
     )(grid_lat, *early_all)
@@ -292,31 +279,29 @@
     head, tail = pl.pallas_call(
         functools.partial(node_kernel, sizes[0], faces),
         out_shape=[jax.ShapeDtypeStruct(half, bf16)] * 2,
-        in_specs=[VMEM] * (1 + faces) + [ANY] * len(early_all),
+        in_specs=[VMEM] * (1 + faces) + [VMEM] * len(early_all),
         out_specs=[VMEM] * 2,
-        scratch_shapes=[matrix(node_w1), matrix(node_w2), sems(2, count)],
-        compiler_params=pltpu.CompilerParams(vmem_limit_bytes=32 * MIB),
+        scratch_shapes=[matrix(node_w1), matrix(node_w2)],
+        compiler_params=pltpu.CompilerParams(vmem_limit_bytes=16 * MIB),
         cost_estimate=cost(mesh_rows, 3 * width),
         name="node_update",
     )(mesh_lat, *arrived, *early_all)
 
     before = shift(tail, "face", 1)
     behind = shift(head, "face", faces - 1)
-    late_all = late_near + relay(late_far, head, grid_out)
+    late_all = late_near + relay(late_far, before, behind, grid_out)
     mesh_out = pl.pallas_call(
         functools.partial(edge_kernel, sizes[1]),
         out_shape=jax.ShapeDtypeStruct(mesh_lat.shape, bf16),
-        in_specs=[VMEM] * 5 + [ANY] * len(late_all),
+        in_specs=[VMEM] * 5 + [VMEM] * len(late_all),
         out_specs=VMEM,
         scratch_shapes=[
             matrix(proc_w1),
             matrix(proc_w2),
             matrix(upd_w1),
             matrix(upd_w2),
-            sems(2, count),
-            sems(2, count),
         ],
-        compiler_params=pltpu.CompilerParams(vmem_limit_bytes=32 * MIB),
+        compiler_params=pltpu.CompilerParams(vmem_limit_bytes=16 * MIB),
         cost_estimate=cost(mesh_rows * mesh_nbr.shape[1], 3 * width),
         name="edge_update",
     )(mesh_nbr, before, head, tail, behind, *late_all)

time: 55.5 us -> 52.5 us (0.946)
  Pallas kernels: 17.4 us -> 13.3 us
  waiting for transfers between devices: 20.7 us -> 22.5 us
  starting transfers between devices: 16.3 us -> 15.1 us
    ppermute x0 -> x3, waiting for transfers between devices: none -> 9.1 us  [to_face(): lax.ppermute(value, 'face', [(i, face_at(faces, step, i)) for i in range(...]
    ppermute x17 -> x14, waiting for transfers between devices: 20.7 us -> 13.4 us  [shift(): lax.ppermute(value, axis, [(i, (i + step) % count) for i in range(count)])]
    ppermute x17 -> x14, starting transfers between devices: 16.3 us -> 10.8 us  [shift(): lax.ppermute(value, axis, [(i, (i + step) % count) for i in range(count)])]
    ppermute x0 -> x3, starting transfers between devices: none -> 4.24 us  [to_face(): lax.ppermute(value, 'face', [(i, face_at(faces, step, i)) for i in range(...]
    pallas_call x1, Pallas kernels: 4.47 us -> 3.06 us  [shards(): pl.pallas_call(functools.partial(grid_kernel, sizes[0]), out_shape=jax.Sh...]
    pallas_call x1, Pallas kernels: 3.72 us -> 2.32 us  [shards(): pl.pallas_call(functools.partial(encode_kernel, count, faces, mesh_rows),...]
    pallas_call x1, Pallas kernels: 1.58 us -> 0.78 us  [shards(): pl.pallas_call(functools.partial(node_kernel, sizes[0], faces), out_shape...]
  transfers between devices with their start and end apart: 17 -> 17, of which waited for: 10 -> 8; matrix products, arithmetic and copies ran while one was open for 0% -> 0% of each run, Pallas kernels for 22% -> 17%
where the time goes in v6:
time: 52.5 us; the launch traced here: 52.3 us
  waiting for transfers between devices  22.5 us (43%)
  starting transfers between devices  15.1 us (29%)
  Pallas kernels  13.3 us (25%)
  between operations  0.77 us (1%)
  local copies, waits for them, and re-layouts  0.6 us (1%)
    ppermute x14, waiting for transfers between devices, shift(): lax.ppermute(value, axis, [(i, (i + step) % count) for i in range(count)])  13.4 us
    ppermute x14, starting transfers between devices, shift(): lax.ppermute(value, axis, [(i, (i + step) % count) for i in range(count)])  10.8 us
    ppermute x3, waiting for transfers between devices, to_face(): lax.ppermute(value, 'face', [(i, face_at(faces, step, i)) for i in range(...  9.1 us
    pallas_call x1, Pallas kernels, shards(): pl.pallas_call(functools.partial(edge_kernel, sizes[1]), out_shape=jax.Sh...  4.66 us
    ppermute x3, starting transfers between devices, to_face(): lax.ppermute(value, 'face', [(i, face_at(faces, step, i)) for i in range(...  4.24 us
    pallas_call x1, Pallas kernels, shards(): pl.pallas_call(functools.partial(grid_kernel, sizes[0]), out_shape=jax.Sh...  3.06 us
    pallas_call x1, Pallas kernels, pack(): pl.pallas_call(functools.partial(pack_kernel, [len(one) for one in sets])...  2.51 us
    pallas_call x1, Pallas kernels, shards(): pl.pallas_call(functools.partial(encode_kernel, count, faces, mesh_rows),...  2.32 us
  transfers between devices with their start and end apart: 17, of which 8 were waited for; matrix products, arithmetic and copies ran while one was open for 0% of the time, Pallas kernels for 17%

profile of v6, /device:TPU:0, one launch (start us, length us, event | category | flops | bytes accessed | tf_op | source)
XLA Modules:
  0.0 52.3 jit_solution(356336136173140805)
XLA Ops:
  0.7 3.0 %collective-permute-start.3 = (bf16[128,512]{1,0:T(8,128)(2,1)}, bf16[128,512]{1,0:T(8,128)(2,1)S(1)}, u32[]{:S(2)}, u32[]{:S(2)}) collective-permute-start(bf16[128,512]{1,0:T(8,128)(2,1)} %refs_0_.3), channel_id=1, source_target_pairs={{0,2},{2,0},{1,3},{3,1},{4,6},{6,4},{5,7},{7,5},{8,10},{10,8},{9,1... | collective-permute-start | bytes 393224 | tf_op jit(solution)/shard_map/ppermute | solution.py:20
  3.8 0.4 collective-permute-start.5
  4.2 3.7 %collective-permute-done.3.refs_2_ = bf16[128,512]{1,0:T(8,128)(2,1)S(1)} collective-permute-done((bf16[128,512]{1,0:T(8,128)(2,1)}, bf16[128,512]{1,0:T(8,128)(2,1)S(1)}, u32[]{:S(2)}, u32[]{:S(2)}) %collective-permute-start.3) | collective-permute-done | bytes 131104 | tf_op jit(solution)/shard_map/ppermute | solution.py:20
  7.9 2.5 %pack.1 = (bf16[640,512]{1,0:T(8,128)(2,1)}, bf16[768,512]{1,0:T(8,128)(2,1)}) custom-call(bf16[256,512]{1,0:T(8,128)(2,1)} %refs_0_.2, bf16[128,512]{1,0:T(8,128)(2,1)} %refs_1_.1, bf16[128,512]{1,0:T(8,128)(2,1)} %refs_2_.1, bf16[128,512]{1,0:T(8,128)(2,1)} %refs_3_.1, bf16[256,512]{1,0:T(8,128)(2,1)} %refs_4_.2, bf16[128,512]{1,0:T(8,128)(2,1)} %refs_5_.1, ...), custom_call_target="tpu_custom_call" | custom-call | tf_op jit(solution)/shard_map/pack/pallas_call | solution.py:80
  10.4 2.4 %collective-permute-start.6 = (bf16[640,512]{1,0:T(8,128)(2,1)}, bf16[640,512]{1,0:T(8,128)(2,1)S(1)}, u32[]{:S(2)}, u32[]{:S(2)}) collective-permute-start(bf16[640,512]{1,0:T(8,128)(2,1)} %get-tuple-element.15.refs_0_.refs_4_), channel_id=1, source_target_pairs={{0,2},{2,0},{1,3},{3,1},{4,6},{6,4},{5,7},{7,5},{8,10},{10,8},{9,1... | collective-permute-start | bytes 1966088 | tf_op jit(solution)/shard_map/ppermute | solution.py:20
  13.1 0.4 copy-done.6
  13.6 0.7 %collective-permute-done.7.refs_7_ = bf16[128,512]{1,0:T(8,128)(2,1)S(1)} collective-permute-done((bf16[128,512]{1,0:T(8,128)(2,1)S(1)}, bf16[128,512]{1,0:T(8,128)(2,1)S(1)}, u32[]{:S(2)}, u32[]{:S(2)}) %collective-permute-start.7) | collective-permute-done | bytes 131104 | tf_op jit(solution)/shard_map/ppermute | solution.py:20
  14.3 2.3 %encode.1 = (f32[128,512]{1,0:T(8,128)S(1)}, bf16[128,512]{1,0:T(8,128)(2,1)S(1)}, bf16[128,512]{1,0:T(8,128)(2,1)S(1)}, bf16[128,512]{1,0:T(8,128)(2,1)S(1)}) custom-call(s32[1,1024]{1,0:T(1,128)S(1)} %bitcast.2, bf16[1024,512]{1,0:T(8,128)(2,1)S(1)} %copy-done.1, bf16[128,512]{1,0:T(8,128)(2,1)S(1)} %copy-done.4, ...), custom_call_target="tpu_custom_call" | custom-call | flops 1610612736 | bytes 2621440 | tf_op jit(solution)/shard_map/encode/pallas_call | solution.py:246
  16.6 2.7 %collective-permute-start.8 = (bf16[128,512]{1,0:T(8,128)(2,1)S(1)}, bf16[128,512]{1,0:T(8,128)(2,1)S(1)}, u32[]{:S(2)}, u32[]{:S(2)}) collective-permute-start(bf16[128,512]{1,0:T(8,128)(2,1)S(1)} %get-tuple-element.16), channel_id=1, source_target_pairs={{0,8},{4,12},{8,0},{12,4},{1,9},{5,13},{9,1},{13,5},{2,10},{6,14},... | collective-permute-start | bytes 393224 | tf_op jit(solution)/shard_map/ppermute | solution.py:35
  19.3 1.3 %collective-permute-start.9 = (bf16[128,512]{1,0:T(8,128)(2,1)S(1)}, bf16[128,512]{1,0:T(8,128)(2,1)S(1)}, u32[]{:S(2)}, u32[]{:S(2)}) collective-permute-start(bf16[128,512]{1,0:T(8,128)(2,1)S(1)} %get-tuple-element.17), channel_id=1, source_target_pairs={{0,12},{4,8},{8,4},{12,0},{1,13},{5,9},{9,5},{13,1},{2,14},{6,10},... | collective-permute-start | bytes 393224 | tf_op jit(solution)/shard_map/ppermute | solution.py:35
  20.6 0.2 collective-permute-start.10
  20.8 0.2 collective-permute-start.15
  21.1 8.5 %collective-permute-done.8.refs_1_ = bf16[128,512]{1,0:T(8,128)(2,1)S(1)} collective-permute-done((bf16[128,512]{1,0:T(8,128)(2,1)S(1)}, bf16[128,512]{1,0:T(8,128)(2,1)S(1)}, u32[]{:S(2)}, u32[]{:S(2)}) %collective-permute-start.8) | collective-permute-done | bytes 131104 | tf_op jit(solution)/shard_map/ppermute | solution.py:35
  29.6 0.6 %collective-permute-done.10.refs_3_ = bf16[128,512]{1,0:T(8,128)(2,1)S(1)} collective-permute-done((bf16[128,512]{1,0:T(8,128)(2,1)S(1)}, bf16[128,512]{1,0:T(8,128)(2,1)S(1)}, u32[]{:S(2)}, u32[]{:S(2)}) %collective-permute-start.10) | collective-permute-done | bytes 131104 | tf_op jit(solution)/shard_map/ppermute | solution.py:35
  30.2 0.5 collective-permute-start.14
  30.7 1.0 %collective-permute-done.refs_1_.refs_5_ = bf16[640,512]{1,0:T(8,128)(2,1)S(1)} collective-permute-done((bf16[640,512]{1,0:T(8,128)(2,1)S(1)}, bf16[640,512]{1,0:T(8,128)(2,1)S(1)}, u32[]{:S(2)}, u32[]{:S(2)}) %collective-permute-start) | collective-permute-done | bytes 655392 | tf_op jit(solution)/shard_map/ppermute | solution.py:20
  31.7 1.9 %collective-permute-done.11.refs_3_.refs_7_ = bf16[640,512]{1,0:T(8,128)(2,1)S(1)} collective-permute-done((bf16[640,512]{1,0:T(8,128)(2,1)S(1)}, bf16[640,512]{1,0:T(8,128)(2,1)S(1)}, u32[]{:S(2)}, u32[]{:S(2)}) %collective-permute-start.11) | collective-permute-done | bytes 655392 | tf_op jit(solution)/shard_map/ppermute | solution.py:20
  33.5 0.8 %node_update.1 = (bf16[64,512]{1,0:T(8,128)(2,1)S(1)}, bf16[64,512]{1,0:T(8,128)(2,1)S(1)}) custom-call(bf16[128,512]{1,0:T(8,128)(2,1)S(1)} %copy-done.2, f32[128,512]{1,0:T(8,128)S(1)} %get-tuple-element.20.refs_0_, bf16[128,512]{1,0:T(8,128)(2,1)S(1)} %collective-permute-done.8.refs_1_, bf16[128,512]{1,0:T(8,128)(2,1)S(1)} %collective-permute-done.9.refs_2_, ...), custom_call_target="tpu_custom_call" | custom-call | flops 201326592 | bytes 1703936 | tf_op jit(solution)/shard_map/node_update/pallas_call | solution.py:279
  34.3 1.2 %collective-permute-start.12 = (bf16[64,512]{1,0:T(8,128)(2,1)S(1)}, bf16[64,512]{1,0:T(8,128)(2,1)S(1)}, u32[]{:S(2)}, u32[]{:S(2)}) collective-permute-start(bf16[64,512]{1,0:T(8,128)(2,1)S(1)} %get-tuple-element.21.tail_ref), channel_id=1, source_target_pairs={{0,4},{4,8},{8,12},{12,0},{1,5},{5,9},{9,13},{13,1},{2,6},{6,10},{... | collective-permute-start | bytes 196616 | tf_op jit(solution)/shard_map/ppermute | solution.py:20
  35.5 2.7 %collective-permute-start.13 = (bf16[64,512]{1,0:T(8,128)(2,1)S(1)}, bf16[64,512]{1,0:T(8,128)(2,1)S(1)}, u32[]{:S(2)}, u32[]{:S(2)}) collective-permute-start(bf16[64,512]{1,0:T(8,128)(2,1)S(1)} %get-tuple-element.22.head_ref), channel_id=1, source_target_pairs={{0,12},{4,0},{8,4},{12,8},{1,13},{5,1},{9,5},{13,9},{2,14},{6,2},{... | collective-permute-start | bytes 196616 | tf_op jit(solution)/shard_map/ppermute | solution.py:20
  38.2 3.1 %grid_update.1 = bf16[1024,512]{1,0:T(8,128)(2,1)} custom-call(bf16[1024,512]{1,0:T(8,128)(2,1)S(1)} %copy-done.1, bf16[640,512]{1,0:T(8,128)(2,1)S(1)} %copy-done, bf16[640,512]{1,0:T(8,128)(2,1)S(1)} %collective-permute-done.refs_1_.refs_5_, bf16[640,512]{1,0:T(8,128)(2,1)S(1)} %collective-permute-done.6.refs_2_.refs_6_, ...), custom_call_target="tpu_custom_call" | custom-call | flops 1073741824 | bytes 2097152 | tf_op jit(solution)/shard_map/grid_update/pallas_call | solution.py:267
  41.3 4.1 %collective-permute-done.15.refs_2_ = bf16[768,512]{1,0:T(8,128)(2,1)S(1)} collective-permute-done((bf16[768,512]{1,0:T(8,128)(2,1)S(1)}, bf16[768,512]{1,0:T(8,128)(2,1)S(1)}, u32[]{:S(2)}, u32[]{:S(2)}) %collective-permute-start.15) | collective-permute-done | bytes 786464 | tf_op jit(solution)/shard_map/ppermute | solution.py:20
  45.5 2.2 %collective-permute-done.16.refs_3_ = bf16[768,512]{1,0:T(8,128)(2,1)S(1)} collective-permute-done((bf16[768,512]{1,0:T(8,128)(2,1)S(1)}, bf16[768,512]{1,0:T(8,128)(2,1)S(1)}, u32[]{:S(2)}, u32[]{:S(2)}) %collective-permute-start.16) | collective-permute-done | bytes 786464 | tf_op jit(solution)/shard_map/ppermute | solution.py:20
  47.7 4.7 %edge_update.1 = bf16[128,512]{1,0:T(8,128)(2,1)} custom-call(s32[128,6]{1,0:T(8,128)S(1)} %copy.17.nbr_ref, bf16[64,512]{1,0:T(8,128)(2,1)S(1)} %collective-permute-done.12.before_ref, bf16[64,512]{1,0:T(8,128)(2,1)S(1)} %get-tuple-element.22.head_ref, bf16[64,512]{1,0:T(8,128)(2,1)S(1)} %get-tuple-element.21.tail_ref, ...), custom_call_target="tpu_custom_call" | custom-call | flops 1207959552 | bytes 2359296 | tf_op jit(solution)/shard_map/edge_update/pallas_call | solution.py:293
  (36 shorter events, 0.6 us)
Async XLA Ops:
  0.6 13.6 %copy-start.4 = (bf16[128,512]{1,0:T(8,128)(2,1)S(1)}, bf16[128,512]{1,0:T(8,128)(2,1)}, u32[]{:S(2)}) copy-start(bf16[128,512]{1,0:T(8,128)(2,1)} %refs_0_.3) | copy-start | bytes 393220
  0.6 13.6 %copy-start.5 = (bf16[128,512]{1,0:T(8,128)(2,1)S(1)}, bf16[128,512]{1,0:T(8,128)(2,1)}, u32[]{:S(2)}) copy-start(bf16[128,512]{1,0:T(8,128)(2,1)} %refs_4_.3) | copy-start | bytes 393220
  0.7 13.6 %copy-start.1 = (bf16[1024,512]{1,0:T(8,128)(2,1)S(1)}, bf16[1024,512]{1,0:T(8,128)(2,1)}, u32[]{:S(2)}) copy-start(bf16[1024,512]{1,0:T(8,128)(2,1)} %lat_ref.4) | copy-start | bytes 3145732
  0.7 7.2 %collective-permute-start.3 = (bf16[128,512]{1,0:T(8,128)(2,1)}, bf16[128,512]{1,0:T(8,128)(2,1)S(1)}, u32[]{:S(2)}, u32[]{:S(2)}) collective-permute-start(bf16[128,512]{1,0:T(8,128)(2,1)} %refs_0_.3), channel_id=1, source_target_pairs={{0,2},{2,0},{1,3},{3,1},{4,6},{6,4},{5,7},{7,5},{8,10},{10,8},{9,1... | collective-permute-start | bytes 393224 | tf_op jit(solution)/shard_map/ppermute | solution.py:20
  3.7 6.7 %collective-permute-start.2 = (bf16[128,512]{1,0:T(8,128)(2,1)}, bf16[128,512]{1,0:T(8,128)(2,1)S(1)}, u32[]{:S(2)}, u32[]{:S(2)}) collective-permute-start(bf16[128,512]{1,0:T(8,128)(2,1)} %refs_0_.3), channel_id=1, source_target_pairs={{0,1},{1,0},{2,3},{3,2},{4,5},{5,4},{6,7},{7,6},{8,9},{9,8},{10,11... | collective-permute-start | bytes 393224 | tf_op jit(solution)/shard_map/ppermute | solution.py:20
  3.7 6.7 %collective-permute-start.1 = (bf16[128,512]{1,0:T(8,128)(2,1)}, bf16[128,512]{1,0:T(8,128)(2,1)S(1)}, u32[]{:S(2)}, u32[]{:S(2)}) collective-permute-start(bf16[128,512]{1,0:T(8,128)(2,1)} %refs_4_.3), channel_id=1, source_target_pairs={{0,2},{2,0},{1,3},{3,1},{4,6},{6,4},{5,7},{7,5},{8,10},{10,8},{9,1... | collective-permute-start | bytes 393224 | tf_op jit(solution)/shard_map/ppermute | solution.py:20
  3.8 6.6 %collective-permute-start.5 = (bf16[128,512]{1,0:T(8,128)(2,1)}, bf16[128,512]{1,0:T(8,128)(2,1)S(1)}, u32[]{:S(2)}, u32[]{:S(2)}) collective-permute-start(bf16[128,512]{1,0:T(8,128)(2,1)} %refs_4_.3), channel_id=1, source_target_pairs={{0,1},{1,0},{2,3},{3,2},{4,5},{5,4},{6,7},{7,6},{8,9},{9,8},{10,11... | collective-permute-start | bytes 393224 | tf_op jit(solution)/shard_map/ppermute | solution.py:20
  7.9 2.5 %collective-permute-start.4 = (bf16[128,512]{1,0:T(8,128)(2,1)S(1)}, bf16[128,512]{1,0:T(8,128)(2,1)S(1)}, u32[]{:S(2)}, u32[]{:S(2)}) collective-permute-start(bf16[128,512]{1,0:T(8,128)(2,1)S(1)} %collective-permute-done.3.refs_2_), channel_id=1, source_target_pairs={{0,1},{1,0},{2,3},{3,2},{4,5},{5,4},{6,7},{7,6},{8,9},{9,8},{10,11... | collective-permute-start | bytes 393224 | tf_op jit(solution)/shard_map/ppermute | solution.py:20
  10.4 19.8 %collective-permute-start.6 = (bf16[640,512]{1,0:T(8,128)(2,1)}, bf16[640,512]{1,0:T(8,128)(2,1)S(1)}, u32[]{:S(2)}, u32[]{:S(2)}) collective-permute-start(bf16[640,512]{1,0:T(8,128)(2,1)} %get-tuple-element.15.refs_0_.refs_4_), channel_id=1, source_target_pairs={{0,2},{2,0},{1,3},{3,1},{4,6},{6,4},{5,7},{7,5},{8,10},{10,8},{9,1... | collective-permute-start | bytes 1966088 | tf_op jit(solution)/shard_map/ppermute | solution.py:20
  12.9 1.3 %collective-permute-start.7 = (bf16[128,512]{1,0:T(8,128)(2,1)S(1)}, bf16[128,512]{1,0:T(8,128)(2,1)S(1)}, u32[]{:S(2)}, u32[]{:S(2)}) collective-permute-start(bf16[128,512]{1,0:T(8,128)(2,1)S(1)} %collective-permute-done.1.refs_6_), channel_id=1, source_target_pairs={{0,1},{1,0},{2,3},{3,2},{4,5},{5,4},{6,7},{7,6},{8,9},{9,8},{10,11... | collective-permute-start | bytes 393224 | tf_op jit(solution)/shard_map/ppermute | solution.py:20
  14.3 6.6 %copy-start.3 = (bf16[768,512]{1,0:T(8,128)(2,1)S(1)}, bf16[768,512]{1,0:T(8,128)(2,1)}, u32[]{:S(2)}) copy-start(bf16[768,512]{1,0:T(8,128)(2,1)} %get-tuple-element.24.refs_0_) | copy-start | bytes 2359300
  14.3 15.3 %copy-start = (bf16[640,512]{1,0:T(8,128)(2,1)S(1)}, bf16[640,512]{1,0:T(8,128)(2,1)}, u32[]{:S(2)}) copy-start(bf16[640,512]{1,0:T(8,128)(2,1)} %get-tuple-element.15.refs_0_.refs_4_) | copy-start | bytes 1966084
  14.3 19.3 %copy-start.2 = (bf16[128,512]{1,0:T(8,128)(2,1)S(1)}, bf16[128,512]{1,0:T(8,128)(2,1)}, u32[]{:S(2)}) copy-start(bf16[128,512]{1,0:T(8,128)(2,1)} %lat_ref.5) | copy-start | bytes 393220
  16.6 13.0 %collective-permute-start.8 = (bf16[128,512]{1,0:T(8,128)(2,1)S(1)}, bf16[128,512]{1,0:T(8,128)(2,1)S(1)}, u32[]{:S(2)}, u32[]{:S(2)}) collective-permute-start(bf16[128,512]{1,0:T(8,128)(2,1)S(1)} %get-tuple-element.16), channel_id=1, source_target_pairs={{0,8},{4,12},{8,0},{12,4},{1,9},{5,13},{9,1},{13,5},{2,10},{6,14},... | collective-permute-start | bytes 393224 | tf_op jit(solution)/shard_map/ppermute | solution.py:35
  19.3 10.3 %collective-permute-start.9 = (bf16[128,512]{1,0:T(8,128)(2,1)S(1)}, bf16[128,512]{1,0:T(8,128)(2,1)S(1)}, u32[]{:S(2)}, u32[]{:S(2)}) collective-permute-start(bf16[128,512]{1,0:T(8,128)(2,1)S(1)} %get-tuple-element.17), channel_id=1, source_target_pairs={{0,12},{4,8},{8,4},{12,0},{1,13},{5,9},{9,5},{13,1},{2,14},{6,10},... | collective-permute-start | bytes 393224 | tf_op jit(solution)/shard_map/ppermute | solution.py:35
  20.6 9.6 %collective-permute-start.10 = (bf16[128,512]{1,0:T(8,128)(2,1)S(1)}, bf16[128,512]{1,0:T(8,128)(2,1)S(1)}, u32[]{:S(2)}, u32[]{:S(2)}) collective-permute-start(bf16[128,512]{1,0:T(8,128)(2,1)S(1)} %get-tuple-element.18), channel_id=1, source_target_pairs={{0,4},{4,0},{8,12},{12,8},{1,5},{5,1},{9,13},{13,9},{2,6},{6,2},{1... | collective-permute-start | bytes 393224 | tf_op jit(solution)/shard_map/ppermute | solution.py:35
  20.8 24.5 %collective-permute-start.15 = (bf16[768,512]{1,0:T(8,128)(2,1)S(1)}, bf16[768,512]{1,0:T(8,128)(2,1)S(1)}, u32[]{:S(2)}, u32[]{:S(2)}) collective-permute-start(bf16[768,512]{1,0:T(8,128)(2,1)S(1)} %copy-done.3), channel_id=1, source_target_pairs={{0,2},{2,0},{1,3},{3,1},{4,6},{6,4},{5,7},{7,5},{8,10},{10,8},{9,1... | collective-permute-start | bytes 2359304 | tf_op jit(solution)/shard_map/ppermute | solution.py:20
  29.6 2.1 %collective-permute-start = (bf16[640,512]{1,0:T(8,128)(2,1)S(1)}, bf16[640,512]{1,0:T(8,128)(2,1)S(1)}, u32[]{:S(2)}, u32[]{:S(2)}) collective-permute-start(bf16[640,512]{1,0:T(8,128)(2,1)S(1)} %copy-done), channel_id=1, source_target_pairs={{0,1},{1,0},{2,3},{3,2},{4,5},{5,4},{6,7},{7,6},{8,9},{9,8},{10,11... | collective-permute-start | bytes 1966088 | tf_op jit(solution)/shard_map/ppermute | solution.py:20
  30.2 3.3 %collective-permute-start.11 = (bf16[640,512]{1,0:T(8,128)(2,1)S(1)}, bf16[640,512]{1,0:T(8,128)(2,1)S(1)}, u32[]{:S(2)}, u32[]{:S(2)}) collective-permute-start(bf16[640,512]{1,0:T(8,128)(2,1)S(1)} %collective-permute-done.6.refs_2_.refs_6_), channel_id=1, source_target_pairs={{0,1},{1,0},{2,3},{3,2},{4,5},{5,4},{6,7},{7,6},{8,9},{9,8},{10,11... | collective-permute-start | bytes 1966088 | tf_op jit(solution)/shard_map/ppermute | solution.py:20
  30.2 15.3 %collective-permute-start.14 = (bf16[768,512]{1,0:T(8,128)(2,1)S(1)}, bf16[768,512]{1,0:T(8,128)(2,1)}, u32[]{:S(2)}, u32[]{:S(2)}) collective-permute-start(bf16[768,512]{1,0:T(8,128)(2,1)S(1)} %copy-done.3), channel_id=1, source_target_pairs={{0,1},{1,0},{2,3},{3,2},{4,5},{5,4},{6,7},{7,6},{8,9},{9,8},{10,11... | collective-permute-start | bytes 2359304 | tf_op jit(solution)/shard_map/ppermute | solution.py:20
  34.3 11.0 %collective-permute-start.12 = (bf16[64,512]{1,0:T(8,128)(2,1)S(1)}, bf16[64,512]{1,0:T(8,128)(2,1)S(1)}, u32[]{:S(2)}, u32[]{:S(2)}) collective-permute-start(bf16[64,512]{1,0:T(8,128)(2,1)S(1)} %get-tuple-element.21.tail_ref), channel_id=1, source_target_pairs={{0,4},{4,8},{8,12},{12,0},{1,5},{5,9},{9,13},{13,1},{2,6},{6,10},{... | collective-permute-start | bytes 196616 | tf_op jit(solution)/shard_map/ppermute | solution.py:20
  35.5 9.8 %copy-start.7 = (s32[128,6]{0,1:T(8,128)S(1)}, s32[128,6]{0,1:T(8,128)}, u32[]{:S(2)}) copy-start(s32[128,6]{0,1:T(8,128)} %param.19) | copy-start | bytes 9220
  35.5 9.8 %collective-permute-start.13 = (bf16[64,512]{1,0:T(8,128)(2,1)S(1)}, bf16[64,512]{1,0:T(8,128)(2,1)S(1)}, u32[]{:S(2)}, u32[]{:S(2)}) collective-permute-start(bf16[64,512]{1,0:T(8,128)(2,1)S(1)} %get-tuple-element.22.head_ref), channel_id=1, source_target_pairs={{0,12},{4,0},{8,4},{12,8},{1,13},{5,1},{9,5},{13,9},{2,14},{6,2},{... | collective-permute-start | bytes 196616 | tf_op jit(solution)/shard_map/ppermute | solution.py:20
  45.4 2.3 %collective-permute-start.16 = (bf16[768,512]{1,0:T(8,128)(2,1)S(1)}, bf16[768,512]{1,0:T(8,128)(2,1)S(1)}, u32[]{:S(2)}, u32[]{:S(2)}) collective-permute-start(bf16[768,512]{1,0:T(8,128)(2,1)S(1)} %collective-permute-done.15.refs_2_), channel_id=1, source_target_pairs={{0,1},{1,0},{2,3},{3,2},{4,5},{5,4},{6,7},{7,6},{8,9},{9,8},{10,11... | collective-permute-start | bytes 2359304 | tf_op jit(solution)/shard_map/ppermute | solution.py:20
  (2 other events, 3.4 us)

commit v7 on v6

--- a/solution.py
+++ b/solution.py
@@ -60,33 +60,52 @@
         whole[pl.ds(pl.multiple_of(owner * rows, rows), rows)] = piece[start : start + rows]
 
 
+def unpack_parts(pieces, base, sizes, wholes):
+    subs, groups = lax.axis_size("sub"), lax.axis_size("groups")
+    for index, piece in enumerate(pieces):
+        band_step, rest = divmod(index, groups * subs)
+        owner = owner_of(band_step + 1, rest % subs)
+        part = lax.rem(lax.axis_index("groups") + groups - rest // subs, groups)
+        start = base if rest < subs else 0
+        for size, whole in zip(sizes, wholes):
+            rows = size // groups
+            into = pl.multiple_of(owner * size + part * rows, rows)
+            whole[pl.ds(into, rows)] = piece[start : start + rows]
+            start += rows
+
+
 def unpack(pieces, sizes, wanted):
     for at, whole in wanted.items():
         place(pieces, sum(sizes[:at]), sizes[at], whole)
 
 
 def pack_kernel(sets, *refs):
-    sources, outs = list(refs[: sum(sets)]), refs[sum(sets) :]
-    for out, amount in zip(outs, sets):
+    sources, outs = refs[: -len(sets)], refs[-len(sets) :]
+    group = lax.axis_index("groups")
+    for out, members in zip(outs, sets):
         start = 0
-        for _ in range(amount):
-            source = sources.pop(0)
-            out[start : start + source.shape[0]] = source[...]
-            start += source.shape[0]
-
-
-def pack(sets):
-    width = sets[0][0].shape[1]
+        for member, rows in members:
+            source = sources[member]
+            if rows < source.shape[0]:
+                out[start : start + rows] = source[pl.ds(pl.multiple_of(group * rows, rows), rows)]
+            else:
+                out[start : start + rows] = source[...]
+            start += rows
+
+
+def pack(weights, sets):
     return pl.pallas_call(
-        functools.partial(pack_kernel, [len(one) for one in sets]),
+        functools.partial(pack_kernel, sets),
         out_shape=[
-            jax.ShapeDtypeStruct((sum(weight.shape[0] for weight in one), width), jnp.bfloat16)
-            for one in sets
+            jax.ShapeDtypeStruct(
+                (sum(rows for _, rows in members), weights[0].shape[1]), jnp.bfloat16
+            )
+            for members in sets
         ],
-        in_specs=[VMEM] * sum(len(one) for one in sets),
+        in_specs=[VMEM] * len(weights),
         out_specs=[VMEM] * len(sets),
         name="pack",
-    )(*(weight for one in sets for weight in one))
+    )(*weights)
 
 
 def silu(values):
@@ -128,9 +147,11 @@
             out[...] = sums[face * mesh_rows : (face + 1) * mesh_rows].astype(out.dtype)
 
 
-def grid_kernel(sizes, lat_ref, *refs):
+def grid_kernel(base, sizes, lat_ref, *refs):
     pieces, (out_ref, w_in, w_hid) = refs[:-3], refs[-3:]
-    unpack(pieces, sizes, {2: w_in, 3: w_hid})
+    subs = lax.axis_size("sub")
+    unpack(pieces[:subs], sizes, {2: w_in, 3: w_hid})
+    unpack_parts(pieces[subs:], base, sizes[2:], [w_in, w_hid])
     block = 256
     for start in range(0, lat_ref.shape[0], block):
         here = pl.ds(start, block)
@@ -169,7 +190,7 @@
     nbr = nbr_ref[...]
     receivers = dot(mid, p_in[width:])
     total = None
-    group = 2 if fanin % 2 == 0 else 1
+    group = fanin
     for at in range(0, fanin, group):
         chosen = jnp.concatenate(
             [
@@ -225,16 +246,27 @@
             transcendentals=rows * width,
         )
 
-    sets = ((node_w1, node_w2, grid_w1, grid_w2), (proc_w1, proc_w2, upd_w1, upd_w2))
-    sizes = [[weight.shape[0] for weight in one] for one in sets]
+    early_set = (node_w1, node_w2, grid_w1, grid_w2)
+    late_set = (proc_w1, proc_w2, upd_w1, upd_w2)
+    early_sizes = [weight.shape[0] for weight in early_set]
+    late_sizes = [weight.shape[0] for weight in late_set]
+    small = pl.CostEstimate(flops=1, bytes_accessed=1, transcendentals=0)
     enc_far = [[shift(one, "band", step) for step in range(1, bands)] for one in (enc_w1, enc_w2)]
     enc_all = [
         own_spread(one) + relay(far) for one, far in zip((enc_w1, enc_w2), enc_far)
     ]
-    early, late = pack(sets)
-    early_sent = after(early, *enc_far[1], *enc_all[0][1:], *enc_all[1][1:subs])
-    early_far = [shift(early_sent, "band", step) for step in range(1, bands)]
-    early_near, late_near = own_spread(early), own_spread(late)
+    groups = lax.axis_size("groups")
+    early_rows = list(enumerate(early_sizes))
+    late_rows = list(enumerate(late_sizes, len(early_sizes)))
+    halves = [(at, rows // groups) for at, rows in early_rows[2:]]
+    early, late, first = pack(
+        early_set + late_set, (early_rows, late_rows, early_rows[:2] + halves)
+    )
+    first_sent = after(first, *enc_far[0], *enc_far[1])
+    first_far = [shift(first_sent, "band", step) for step in range(1, bands)]
+    own_enc = enc_all[0][1:subs] + enc_all[1][1:subs]
+    early_near = own_spread(after(early, *enc_far[0], *enc_far[1], *own_enc))
+    late_near = own_spread(late)
 
     me = lax.axis_index("face")
     routes = grid_route[:, 0]
@@ -258,40 +290,48 @@
         compiler_params=pltpu.CompilerParams(vmem_limit_bytes=16 * MIB),
         cost_estimate=cost(grid_rows, 3 * width),
         name="encode",
-    )(targets, grid_lat, *enc_all[0], *enc_all[1])
+    )(after(targets, *early_near[1:]), grid_lat, *enc_all[0], *enc_all[1])
     late_sent = after(late, sums[0])
     late_far = [shift(late_sent, "band", step) for step in range(1, bands)]
     arrived = [sums[0]] + [to_face(sums[step], step) for step in steps[1:]]
 
-    early_all = early_near + relay(early_far, *arrived[1:])
+    first_all = relay(first_far, *arrived[1:])
+    node_all = early_near + first_all
+
+    half = (mesh_rows // 2, width)
+    head, tail = pl.pallas_call(
+        functools.partial(node_kernel, early_sizes, faces),
+        out_shape=[jax.ShapeDtypeStruct(half, bf16)] * 2,
+        in_specs=[VMEM] * (1 + faces) + [VMEM] * len(node_all),
+        out_specs=[VMEM] * 2,
+        scratch_shapes=[matrix(node_w1), matrix(node_w2)],
+        compiler_params=pltpu.CompilerParams(vmem_limit_bytes=16 * MIB),
+        cost_estimate=small,
+        name="node_update",
+    )(mesh_lat, *arrived, *node_all)
+
+    base = sum(early_sizes[:2])
+    grid_all = list(early_near)
+    for at, one in enumerate(first_far):
+        over = after(one[base:], *arrived[1:])
+        grid_all += first_all[at * subs : (at + 1) * subs]
+        grid_all += relay([shift(over, "groups", step) for step in range(1, groups)], head)
     grid_out = pl.pallas_call(
-        functools.partial(grid_kernel, sizes[0]),
+        functools.partial(grid_kernel, base, early_sizes),
         out_shape=jax.ShapeDtypeStruct(grid_lat.shape, bf16),
-        in_specs=[VMEM] + [VMEM] * len(early_all),
+        in_specs=[VMEM] + [VMEM] * len(grid_all),
         out_specs=VMEM,
         scratch_shapes=[matrix(grid_w1), matrix(grid_w2)],
         compiler_params=pltpu.CompilerParams(vmem_limit_bytes=16 * MIB),
-        cost_estimate=cost(grid_rows, 2 * width),
+        cost_estimate=small,
         name="grid_update",
-    )(grid_lat, *early_all)
-
-    half = (mesh_rows // 2, width)
-    head, tail = pl.pallas_call(
-        functools.partial(node_kernel, sizes[0], faces),
-        out_shape=[jax.ShapeDtypeStruct(half, bf16)] * 2,
-        in_specs=[VMEM] * (1 + faces) + [VMEM] * len(early_all),
-        out_specs=[VMEM] * 2,
-        scratch_shapes=[matrix(node_w1), matrix(node_w2)],
-        compiler_params=pltpu.CompilerParams(vmem_limit_bytes=16 * MIB),
-        cost_estimate=cost(mesh_rows, 3 * width),
-        name="node_update",
-    )(mesh_lat, *arrived, *early_all)
+    )(grid_lat, *grid_all)
 
     before = shift(tail, "face", 1)
     behind = shift(head, "face", faces - 1)
     late_all = late_near + relay(late_far, before, behind, grid_out)
     mesh_out = pl.pallas_call(
-        functools.partial(edge_kernel, sizes[1]),
+        functools.partial(edge_kernel, late_sizes),
         out_shape=jax.ShapeDtypeStruct(mesh_lat.shape, bf16),
         in_specs=[VMEM] * 5 + [VMEM] * len(late_all),
         out_specs=VMEM,

time: 52.5 us -> 53.2 us (1.013)
  waiting for transfers between devices: 22.5 us -> 19.7 us
  starting transfers between devices: 15.1 us -> 16.4 us
  local copies, waits for them, and re-layouts: 0.6 us -> 1.87 us
  Pallas kernels: 13.3 us -> 14.2 us
    ppermute x3, waiting for transfers between devices: 9.1 us -> 6.66 us  [to_face(): lax.ppermute(value, 'face', [(i, face_at(faces, step, i)) for i in range(...]
    ppermute x14 -> x16, starting transfers between devices: 10.8 us -> 12.1 us  [shift(): lax.ppermute(value, axis, [(i, (i + step) % count) for i in range(count)])]
    unnamed x19 -> x23, local copies, waits for them, and re-layouts: 0.6 us -> 1.86 us
    pallas_call x1, Pallas kernels: 2.32 us -> 3.28 us  [shards(): pl.pallas_call(functools.partial(encode_kernel, count, faces, mesh_rows),...]
    ppermute x14 -> x16, waiting for transfers between devices: 13.4 us -> 13.1 us  [shift(): lax.ppermute(value, axis, [(i, (i + step) % count) for i in range(count)])]
  transfers between devices with their start and end apart: 17 -> 19, of which waited for: 8 -> 11; matrix products, arithmetic and copies ran while one was open for 0% -> 0% of each run, Pallas kernels for 17% -> 19%
where the time goes in v7:
time: 53.2 us; the launch traced here: 52.9 us
  waiting for transfers between devices  19.7 us (37%)
  starting transfers between devices  16.4 us (31%)
  Pallas kernels  14.2 us (27%)
  local copies, waits for them, and re-layouts  1.87 us (4%)
  between operations  0.73 us (1%)
    ppermute x16, waiting for transfers between devices, shift(): lax.ppermute(value, axis, [(i, (i + step) % count) for i in range(count)])  13.1 us
    ppermute x16, starting transfers between devices, shift(): lax.ppermute(value, axis, [(i, (i + step) % count) for i in range(count)])  12.1 us
    ppermute x3, waiting for transfers between devices, to_face(): lax.ppermute(value, 'face', [(i, face_at(faces, step, i)) for i in range(...  6.66 us
    pallas_call x1, Pallas kernels, shards(): pl.pallas_call(functools.partial(edge_kernel, late_sizes), out_shape=jax....  4.39 us
    ppermute x3, starting transfers between devices, to_face(): lax.ppermute(value, 'face', [(i, face_at(faces, step, i)) for i in range(...  4.23 us
    pallas_call x1, Pallas kernels, shards(): pl.pallas_call(functools.partial(encode_kernel, count, faces, mesh_rows),...  3.28 us
    pallas_call x1, Pallas kernels, shards(): pl.pallas_call(functools.partial(grid_kernel, base, early_sizes), out_sha...  3.07 us
    pallas_call x1, Pallas kernels, pack(): pl.pallas_call(functools.partial(pack_kernel, sets), out_shape=[jax.Shape...  2.71 us
  transfers between devices with their start and end apart: 19, of which 11 were waited for; matrix products, arithmetic and copies ran while one was open for 0% of the time, Pallas kernels for 19%

profile of v7, /device:TPU:0, one launch (start us, length us, event | category | flops | bytes accessed | tf_op | source)
XLA Modules:
  0.0 52.9 jit_solution(10787994694630399044)
XLA Ops:
  0.7 3.0 %collective-permute-start = (bf16[128,512]{1,0:T(8,128)(2,1)}, bf16[128,512]{1,0:T(8,128)(2,1)S(1)}, u32[]{:S(2)}, u32[]{:S(2)}) collective-permute-start(bf16[128,512]{1,0:T(8,128)(2,1)} %refs_0_.3), channel_id=1, source_target_pairs={{0,2},{2,0},{1,3},{3,1},{4,6},{6,4},{5,7},{7,5},{8,10},{10,8},{9,1... | collective-permute-start | bytes 393224 | tf_op jit(solution)/shard_map/ppermute | solution.py:20
  4.2 2.7 %pack.1 = (bf16[640,512]{1,0:T(8,128)(2,1)}, bf16[768,512]{1,0:T(8,128)(2,1)}, bf16[512,512]{1,0:T(8,128)(2,1)}) custom-call(bf16[256,512]{1,0:T(8,128)(2,1)} %refs_0_.2, bf16[128,512]{1,0:T(8,128)(2,1)} %refs_1_.1, bf16[128,512]{1,0:T(8,128)(2,1)} %refs_2_.1, bf16[128,512]{1,0:T(8,128)(2,1)} %refs_3_.1, bf16[256,512]{1,0:T(8,128)(2,1)} %refs_4_.2, ...), custom_call_target="tpu_custom_call" | custom-call | tf_op jit(solution)/shard_map/pack/pallas_call | solution.py:97
  6.9 1.0 %collective-permute-done.refs_2_ = bf16[128,512]{1,0:T(8,128)(2,1)S(1)} collective-permute-done((bf16[128,512]{1,0:T(8,128)(2,1)}, bf16[128,512]{1,0:T(8,128)(2,1)S(1)}, u32[]{:S(2)}, u32[]{:S(2)}) %collective-permute-start) | collective-permute-done | bytes 131104 | tf_op jit(solution)/shard_map/ppermute | solution.py:20
  7.9 2.4 %collective-permute-done.1.refs_6_ = bf16[128,512]{1,0:T(8,128)(2,1)} collective-permute-done((bf16[128,512]{1,0:T(8,128)(2,1)}, bf16[128,512]{1,0:T(8,128)(2,1)}, u32[]{:S(2)}, u32[]{:S(2)}) %collective-permute-start.1) | collective-permute-done | bytes 131104 | tf_op jit(solution)/shard_map/ppermute | solution.py:20
  10.3 0.7 %copy-done.6 = bf16[128,512]{1,0:T(8,128)(2,1)} copy-done((bf16[128,512]{1,0:T(8,128)(2,1)}, bf16[128,512]{1,0:T(8,128)(2,1)S(1)}, u32[]{:S(2)}) %copy-start.6) | copy-done | bytes 131096
  11.0 1.7 %collective-permute-start.5 = (bf16[512,512]{1,0:T(8,128)(2,1)}, bf16[512,512]{1,0:T(8,128)(2,1)S(1)}, u32[]{:S(2)}, u32[]{:S(2)}) collective-permute-start(bf16[512,512]{1,0:T(8,128)(2,1)} %get-tuple-element.22), channel_id=1, source_target_pairs={{0,2},{2,0},{1,3},{3,1},{4,6},{6,4},{5,7},{7,5},{8,10},{10,8},{9,1... | collective-permute-start | bytes 1572872 | tf_op jit(solution)/shard_map/ppermute | solution.py:20
  13.4 0.7 %collective-permute-done.6.refs_3_ = bf16[128,512]{1,0:T(8,128)(2,1)S(1)} collective-permute-done((bf16[128,512]{1,0:T(8,128)(2,1)S(1)}, bf16[128,512]{1,0:T(8,128)(2,1)S(1)}, u32[]{:S(2)}, u32[]{:S(2)}) %collective-permute-start.6) | collective-permute-done | bytes 131104 | tf_op jit(solution)/shard_map/ppermute | solution.py:20
  14.5 0.9 %copy-done.7 = bf16[128,512]{1,0:T(8,128)(2,1)S(1)} copy-done((bf16[128,512]{1,0:T(8,128)(2,1)S(1)}, bf16[128,512]{1,0:T(8,128)(2,1)}, u32[]{:S(2)}) %copy-start.7) | copy-done | bytes 131096
  15.4 3.3 %encode.1 = (f32[128,512]{1,0:T(8,128)S(1)}, bf16[128,512]{1,0:T(8,128)(2,1)S(1)}, bf16[128,512]{1,0:T(8,128)(2,1)S(1)}, bf16[128,512]{1,0:T(8,128)(2,1)S(1)}) custom-call(s32[1,1024]{1,0:T(1,128)S(1)} %bitcast.2, bf16[1024,512]{1,0:T(8,128)(2,1)S(1)} %copy-done.1, bf16[128,512]{1,0:T(8,128)(2,1)S(1)} %copy-done.4, ...), custom_call_target="tpu_custom_call" | custom-call | flops 1610612736 | bytes 2621440 | tf_op jit(solution)/shard_map/encode/pallas_call | solution.py:278
  18.7 2.7 %collective-permute-start.8 = (bf16[128,512]{1,0:T(8,128)(2,1)S(1)}, bf16[128,512]{1,0:T(8,128)(2,1)S(1)}, u32[]{:S(2)}, u32[]{:S(2)}) collective-permute-start(bf16[128,512]{1,0:T(8,128)(2,1)S(1)} %get-tuple-element.24), channel_id=1, source_target_pairs={{0,8},{4,12},{8,0},{12,4},{1,9},{5,13},{9,1},{13,5},{2,10},{6,14},... | collective-permute-start | bytes 393224 | tf_op jit(solution)/shard_map/ppermute | solution.py:35
  21.3 1.3 %collective-permute-start.9 = (bf16[128,512]{1,0:T(8,128)(2,1)S(1)}, bf16[128,512]{1,0:T(8,128)(2,1)S(1)}, u32[]{:S(2)}, u32[]{:S(2)}) collective-permute-start(bf16[128,512]{1,0:T(8,128)(2,1)S(1)} %get-tuple-element.25), channel_id=1, source_target_pairs={{0,12},{4,8},{8,4},{12,0},{1,13},{5,9},{9,5},{13,1},{2,14},{6,10},... | collective-permute-start | bytes 393224 | tf_op jit(solution)/shard_map/ppermute | solution.py:35
  22.9 0.9 %collective-permute-start.17 = (bf16[768,512]{1,0:T(8,128)(2,1)S(1)}, bf16[768,512]{1,0:T(8,128)(2,1)}, u32[]{:S(2)}, u32[]{:S(2)}) collective-permute-start(bf16[768,512]{1,0:T(8,128)(2,1)S(1)} %copy-done.3), channel_id=1, source_target_pairs={{0,2},{2,0},{1,3},{3,1},{4,6},{6,4},{5,7},{7,5},{8,10},{10,8},{9,1... | collective-permute-start | bytes 2359304 | tf_op jit(solution)/shard_map/ppermute | solution.py:20
  23.8 1.9 %collective-permute-done.5.refs_6_.refs_2_ = bf16[512,512]{1,0:T(8,128)(2,1)S(1)} collective-permute-done((bf16[512,512]{1,0:T(8,128)(2,1)}, bf16[512,512]{1,0:T(8,128)(2,1)S(1)}, u32[]{:S(2)}, u32[]{:S(2)}) %collective-permute-start.5) | collective-permute-done | bytes 524320 | tf_op jit(solution)/shard_map/ppermute | solution.py:20
  25.7 6.0 %collective-permute-done.8.refs_1_ = bf16[128,512]{1,0:T(8,128)(2,1)S(1)} collective-permute-done((bf16[128,512]{1,0:T(8,128)(2,1)S(1)}, bf16[128,512]{1,0:T(8,128)(2,1)S(1)}, u32[]{:S(2)}, u32[]{:S(2)}) %collective-permute-start.8) | collective-permute-done | bytes 131104 | tf_op jit(solution)/shard_map/ppermute | solution.py:35
  31.7 0.7 %collective-permute-done.10.refs_3_ = bf16[128,512]{1,0:T(8,128)(2,1)S(1)} collective-permute-done((bf16[128,512]{1,0:T(8,128)(2,1)S(1)}, bf16[128,512]{1,0:T(8,128)(2,1)S(1)}, u32[]{:S(2)}, u32[]{:S(2)}) %collective-permute-start.10) | collective-permute-done | bytes 131104 | tf_op jit(solution)/shard_map/ppermute | solution.py:35
  32.4 1.6 %collective-permute-start.12 = (bf16[128,512]{1,0:T(8,128)(2,1)S(1)}, bf16[128,512]{1,0:T(8,128)(2,1)S(1)}, u32[]{:S(2)}, u32[]{:S(2)}) collective-permute-start(bf16[128,512]{1,0:T(8,128)(2,1)S(1)} %slice.4), channel_id=1, source_target_pairs={{0,16},{16,0},{1,17},{17,1},{2,18},{18,2},{3,19},{19,3},{4,20},{20... | collective-permute-start | bytes 393224 | tf_op jit(solution)/shard_map/ppermute | solution.py:20
  34.3 0.8 %node_update.1 = (bf16[64,512]{1,0:T(8,128)(2,1)S(1)}, bf16[64,512]{1,0:T(8,128)(2,1)S(1)}) custom-call(bf16[128,512]{1,0:T(8,128)(2,1)S(1)} %copy-done.2, f32[128,512]{1,0:T(8,128)S(1)} %get-tuple-element.29.refs_0_, bf16[128,512]{1,0:T(8,128)(2,1)S(1)} %collective-permute-done.8.refs_1_, bf16[128,512]{1,0:T(8,128)(2,1)S(1)} %collective-permute-done.9.refs_2_, ...), custom_call_target="tpu_custom_call" | custom-call | flops 1 | bytes 1 | tf_op jit(solution)/shard_map/node_update/pallas_call | solution.py:302
  35.1 3.3 %collective-permute-done.12.refs_4_ = bf16[128,512]{1,0:T(8,128)(2,1)S(1)} collective-permute-done((bf16[128,512]{1,0:T(8,128)(2,1)S(1)}, bf16[128,512]{1,0:T(8,128)(2,1)S(1)}, u32[]{:S(2)}, u32[]{:S(2)}) %collective-permute-start.12) | collective-permute-done | bytes 131104 | tf_op jit(solution)/shard_map/ppermute | solution.py:20
  38.3 2.2 %collective-permute-start.14 = (bf16[64,512]{1,0:T(8,128)(2,1)S(1)}, bf16[64,512]{1,0:T(8,128)(2,1)S(1)}, u32[]{:S(2)}, u32[]{:S(2)}) collective-permute-start(bf16[64,512]{1,0:T(8,128)(2,1)S(1)} %get-tuple-element.32.tail_ref), channel_id=1, source_target_pairs={{0,4},{4,8},{8,12},{12,0},{1,5},{5,9},{9,13},{13,1},{2,6},{6,10},{... | collective-permute-start | bytes 196616 | tf_op jit(solution)/shard_map/ppermute | solution.py:20
  40.5 1.7 %collective-permute-start.15 = (bf16[64,512]{1,0:T(8,128)(2,1)S(1)}, bf16[64,512]{1,0:T(8,128)(2,1)S(1)}, u32[]{:S(2)}, u32[]{:S(2)}) collective-permute-start(bf16[64,512]{1,0:T(8,128)(2,1)S(1)} %get-tuple-element.30.head_ref), channel_id=1, source_target_pairs={{0,12},{4,0},{8,4},{12,8},{1,13},{5,1},{9,5},{13,9},{2,14},{6,2},{... | collective-permute-start | bytes 196616 | tf_op jit(solution)/shard_map/ppermute | solution.py:20
  42.2 3.1 %grid_update.1 = bf16[1024,512]{1,0:T(8,128)(2,1)} custom-call(bf16[1024,512]{1,0:T(8,128)(2,1)S(1)} %copy-done.1, bf16[640,512]{1,0:T(8,128)(2,1)S(1)} %copy-done, bf16[640,512]{1,0:T(8,128)(2,1)S(1)} %collective-permute-done.4.refs_5_.refs_1_, bf16[512,512]{1,0:T(8,128)(2,1)S(1)} %collective-permute-done.5.refs_6_.refs_2_, ...), custom_call_target="tpu_custom_call" | custom-call | flops 1 | bytes 1 | tf_op jit(solution)/shard_map/grid_update/pallas_call | solution.py:319
  45.2 0.8 %collective-permute-done.15.after_ref = bf16[64,512]{1,0:T(8,128)(2,1)S(1)} collective-permute-done((bf16[64,512]{1,0:T(8,128)(2,1)S(1)}, bf16[64,512]{1,0:T(8,128)(2,1)S(1)}, u32[]{:S(2)}, u32[]{:S(2)}) %collective-permute-start.15) | collective-permute-done | bytes 65568 | tf_op jit(solution)/shard_map/ppermute | solution.py:20
  46.2 2.3 %collective-permute-done.18.refs_3_ = bf16[768,512]{1,0:T(8,128)(2,1)S(1)} collective-permute-done((bf16[768,512]{1,0:T(8,128)(2,1)}, bf16[768,512]{1,0:T(8,128)(2,1)S(1)}, u32[]{:S(2)}, u32[]{:S(2)}) %collective-permute-start.18) | collective-permute-done | bytes 786464 | tf_op jit(solution)/shard_map/ppermute | solution.py:20
  48.6 4.4 %edge_update.1 = bf16[128,512]{1,0:T(8,128)(2,1)} custom-call(s32[128,6]{1,0:T(8,128)S(1)} %copy.17.nbr_ref, bf16[64,512]{1,0:T(8,128)(2,1)S(1)} %collective-permute-done.14.before_ref, bf16[64,512]{1,0:T(8,128)(2,1)S(1)} %get-tuple-element.30.head_ref, bf16[64,512]{1,0:T(8,128)(2,1)S(1)} %get-tuple-element.32.tail_ref, ...), custom_call_target="tpu_custom_call" | custom-call | flops 1207959552 | bytes 2359296 | tf_op jit(solution)/shard_map/edge_update/pallas_call | solution.py:333
  (45 shorter events, 2.4 us)
Async XLA Ops:
  0.6 13.9 %copy-start.4 = (bf16[128,512]{1,0:T(8,128)(2,1)S(1)}, bf16[128,512]{1,0:T(8,128)(2,1)}, u32[]{:S(2)}) copy-start(bf16[128,512]{1,0:T(8,128)(2,1)} %refs_0_.3) | copy-start | bytes 393220
  0.6 13.8 %copy-start.5 = (bf16[128,512]{1,0:T(8,128)(2,1)S(1)}, bf16[128,512]{1,0:T(8,128)(2,1)}, u32[]{:S(2)}) copy-start(bf16[128,512]{1,0:T(8,128)(2,1)} %refs_4_.3) | copy-start | bytes 393220
  0.7 13.8 %copy-start.1 = (bf16[1024,512]{1,0:T(8,128)(2,1)S(1)}, bf16[1024,512]{1,0:T(8,128)(2,1)}, u32[]{:S(2)}) copy-start(bf16[1024,512]{1,0:T(8,128)(2,1)} %lat_ref.5) | copy-start | bytes 3145732
  0.7 7.2 %collective-permute-start = (bf16[128,512]{1,0:T(8,128)(2,1)}, bf16[128,512]{1,0:T(8,128)(2,1)S(1)}, u32[]{:S(2)}, u32[]{:S(2)}) collective-permute-start(bf16[128,512]{1,0:T(8,128)(2,1)} %refs_0_.3), channel_id=1, source_target_pairs={{0,2},{2,0},{1,3},{3,1},{4,6},{6,4},{5,7},{7,5},{8,10},{10,8},{9,1... | collective-permute-start | bytes 393224 | tf_op jit(solution)/shard_map/ppermute | solution.py:20
  3.7 4.2 %collective-permute-start.2 = (bf16[128,512]{1,0:T(8,128)(2,1)}, bf16[128,512]{1,0:T(8,128)(2,1)S(1)}, u32[]{:S(2)}, u32[]{:S(2)}) collective-permute-start(bf16[128,512]{1,0:T(8,128)(2,1)} %refs_0_.3), channel_id=1, source_target_pairs={{0,1},{1,0},{2,3},{3,2},{4,5},{5,4},{6,7},{7,6},{8,9},{9,8},{10,11... | collective-permute-start | bytes 393224 | tf_op jit(solution)/shard_map/ppermute | solution.py:20
  3.7 6.6 %collective-permute-start.1 = (bf16[128,512]{1,0:T(8,128)(2,1)}, bf16[128,512]{1,0:T(8,128)(2,1)}, u32[]{:S(2)}, u32[]{:S(2)}) collective-permute-start(bf16[128,512]{1,0:T(8,128)(2,1)} %refs_4_.3), channel_id=1, source_target_pairs={{0,2},{2,0},{1,3},{3,1},{4,6},{6,4},{5,7},{7,5},{8,10},{10,8},{9,1... | collective-permute-start | bytes 393224 | tf_op jit(solution)/shard_map/ppermute | solution.py:20
  3.8 6.5 %collective-permute-start.3 = (bf16[128,512]{1,0:T(8,128)(2,1)}, bf16[128,512]{1,0:T(8,128)(2,1)S(1)}, u32[]{:S(2)}, u32[]{:S(2)}) collective-permute-start(bf16[128,512]{1,0:T(8,128)(2,1)} %refs_4_.3), channel_id=1, source_target_pairs={{0,1},{1,0},{2,3},{3,2},{4,5},{5,4},{6,7},{7,6},{8,9},{9,8},{10,11... | collective-permute-start | bytes 393224 | tf_op jit(solution)/shard_map/ppermute | solution.py:20
  10.9 2.4 %collective-permute-start.4 = (bf16[640,512]{1,0:T(8,128)(2,1)}, bf16[640,512]{1,0:T(8,128)(2,1)S(1)}, u32[]{:S(2)}, u32[]{:S(2)}) collective-permute-start(bf16[640,512]{1,0:T(8,128)(2,1)} %get-tuple-element.20.refs_4_.refs_0_), channel_id=1, source_target_pairs={{0,1},{1,0},{2,3},{3,2},{4,5},{5,4},{6,7},{7,6},{8,9},{9,8},{10,11... | collective-permute-start | bytes 1966088 | tf_op jit(solution)/shard_map/ppermute | solution.py:20
  11.0 14.7 %collective-permute-start.5 = (bf16[512,512]{1,0:T(8,128)(2,1)}, bf16[512,512]{1,0:T(8,128)(2,1)S(1)}, u32[]{:S(2)}, u32[]{:S(2)}) collective-permute-start(bf16[512,512]{1,0:T(8,128)(2,1)} %get-tuple-element.22), channel_id=1, source_target_pairs={{0,2},{2,0},{1,3},{3,1},{4,6},{6,4},{5,7},{7,5},{8,10},{10,8},{9,1... | collective-permute-start | bytes 1572872 | tf_op jit(solution)/shard_map/ppermute | solution.py:20
  12.7 1.3 %collective-permute-start.6 = (bf16[128,512]{1,0:T(8,128)(2,1)S(1)}, bf16[128,512]{1,0:T(8,128)(2,1)S(1)}, u32[]{:S(2)}, u32[]{:S(2)}) collective-permute-start(bf16[128,512]{1,0:T(8,128)(2,1)S(1)} %collective-permute-done.refs_2_), channel_id=1, source_target_pairs={{0,1},{1,0},{2,3},{3,2},{4,5},{5,4},{6,7},{7,6},{8,9},{9,8},{10,11... | collective-permute-start | bytes 393224 | tf_op jit(solution)/shard_map/ppermute | solution.py:20
  12.9 1.6 %collective-permute-start.7 = (bf16[128,512]{1,0:T(8,128)(2,1)}, bf16[128,512]{1,0:T(8,128)(2,1)S(1)}, u32[]{:S(2)}, u32[]{:S(2)}) collective-permute-start(bf16[128,512]{1,0:T(8,128)(2,1)} %collective-permute-done.1.refs_6_), channel_id=1, source_target_pairs={{0,1},{1,0},{2,3},{3,2},{4,5},{5,4},{6,7},{7,6},{8,9},{9,8},{10,11... | collective-permute-start | bytes 393224 | tf_op jit(solution)/shard_map/ppermute | solution.py:20
  15.4 18.9 %copy-start = (bf16[640,512]{1,0:T(8,128)(2,1)S(1)}, bf16[640,512]{1,0:T(8,128)(2,1)}, u32[]{:S(2)}) copy-start(bf16[640,512]{1,0:T(8,128)(2,1)} %get-tuple-element.20.refs_4_.refs_0_) | copy-start | bytes 1966084
  18.7 13.0 %collective-permute-start.8 = (bf16[128,512]{1,0:T(8,128)(2,1)S(1)}, bf16[128,512]{1,0:T(8,128)(2,1)S(1)}, u32[]{:S(2)}, u32[]{:S(2)}) collective-permute-start(bf16[128,512]{1,0:T(8,128)(2,1)S(1)} %get-tuple-element.24), channel_id=1, source_target_pairs={{0,8},{4,12},{8,0},{12,4},{1,9},{5,13},{9,1},{13,5},{2,10},{6,14},... | collective-permute-start | bytes 393224 | tf_op jit(solution)/shard_map/ppermute | solution.py:35
  21.3 10.3 %collective-permute-start.9 = (bf16[128,512]{1,0:T(8,128)(2,1)S(1)}, bf16[128,512]{1,0:T(8,128)(2,1)S(1)}, u32[]{:S(2)}, u32[]{:S(2)}) collective-permute-start(bf16[128,512]{1,0:T(8,128)(2,1)S(1)} %get-tuple-element.25), channel_id=1, source_target_pairs={{0,12},{4,8},{8,4},{12,0},{1,13},{5,9},{9,5},{13,1},{2,14},{6,10},... | collective-permute-start | bytes 393224 | tf_op jit(solution)/shard_map/ppermute | solution.py:35
  22.7 9.7 %collective-permute-start.10 = (bf16[128,512]{1,0:T(8,128)(2,1)S(1)}, bf16[128,512]{1,0:T(8,128)(2,1)S(1)}, u32[]{:S(2)}, u32[]{:S(2)}) collective-permute-start(bf16[128,512]{1,0:T(8,128)(2,1)S(1)} %get-tuple-element.26), channel_id=1, source_target_pairs={{0,4},{4,0},{8,12},{12,8},{1,5},{5,1},{9,13},{13,9},{2,6},{6,2},{1... | collective-permute-start | bytes 393224 | tf_op jit(solution)/shard_map/ppermute | solution.py:35
  22.9 11.3 %copy-start.2 = (bf16[128,512]{1,0:T(8,128)(2,1)S(1)}, bf16[128,512]{1,0:T(8,128)(2,1)}, u32[]{:S(2)}) copy-start(bf16[128,512]{1,0:T(8,128)(2,1)} %lat_ref.4) | copy-start | bytes 393220
  22.9 23.1 %collective-permute-start.17 = (bf16[768,512]{1,0:T(8,128)(2,1)S(1)}, bf16[768,512]{1,0:T(8,128)(2,1)}, u32[]{:S(2)}, u32[]{:S(2)}) collective-permute-start(bf16[768,512]{1,0:T(8,128)(2,1)S(1)} %copy-done.3), channel_id=1, source_target_pairs={{0,2},{2,0},{1,3},{3,1},{4,6},{6,4},{5,7},{7,5},{8,10},{10,8},{9,1... | collective-permute-start | bytes 2359304 | tf_op jit(solution)/shard_map/ppermute | solution.py:20
  32.3 1.9 %collective-permute-start.11 = (bf16[512,512]{1,0:T(8,128)(2,1)S(1)}, bf16[512,512]{1,0:T(8,128)(2,1)S(1)}, u32[]{:S(2)}, u32[]{:S(2)}) collective-permute-start(bf16[512,512]{1,0:T(8,128)(2,1)S(1)} %collective-permute-done.5.refs_6_.refs_2_), channel_id=1, source_target_pairs={{0,1},{1,0},{2,3},{3,2},{4,5},{5,4},{6,7},{7,6},{8,9},{9,8},{10,11... | collective-permute-start | bytes 1572872 | tf_op jit(solution)/shard_map/ppermute | solution.py:20
  32.4 6.0 %collective-permute-start.12 = (bf16[128,512]{1,0:T(8,128)(2,1)S(1)}, bf16[128,512]{1,0:T(8,128)(2,1)S(1)}, u32[]{:S(2)}, u32[]{:S(2)}) collective-permute-start(bf16[128,512]{1,0:T(8,128)(2,1)S(1)} %slice.4), channel_id=1, source_target_pairs={{0,16},{16,0},{1,17},{17,1},{2,18},{18,2},{3,19},{19,3},{4,20},{20... | collective-permute-start | bytes 393224 | tf_op jit(solution)/shard_map/ppermute | solution.py:20
  38.3 3.8 %collective-permute-start.13 = (bf16[128,512]{1,0:T(8,128)(2,1)S(1)}, bf16[128,512]{1,0:T(8,128)(2,1)S(1)}, u32[]{:S(2)}, u32[]{:S(2)}) collective-permute-start(bf16[128,512]{1,0:T(8,128)(2,1)S(1)} %collective-permute-done.12.refs_4_), channel_id=1, source_target_pairs={{0,1},{1,0},{2,3},{3,2},{4,5},{5,4},{6,7},{7,6},{8,9},{9,8},{10,11... | collective-permute-start | bytes 393224 | tf_op jit(solution)/shard_map/ppermute | solution.py:20
  38.3 6.9 %collective-permute-start.14 = (bf16[64,512]{1,0:T(8,128)(2,1)S(1)}, bf16[64,512]{1,0:T(8,128)(2,1)S(1)}, u32[]{:S(2)}, u32[]{:S(2)}) collective-permute-start(bf16[64,512]{1,0:T(8,128)(2,1)S(1)} %get-tuple-element.32.tail_ref), channel_id=1, source_target_pairs={{0,4},{4,8},{8,12},{12,0},{1,5},{5,9},{9,13},{13,1},{2,6},{6,10},{... | collective-permute-start | bytes 196616 | tf_op jit(solution)/shard_map/ppermute | solution.py:20
  40.5 5.6 %collective-permute-start.15 = (bf16[64,512]{1,0:T(8,128)(2,1)S(1)}, bf16[64,512]{1,0:T(8,128)(2,1)S(1)}, u32[]{:S(2)}, u32[]{:S(2)}) collective-permute-start(bf16[64,512]{1,0:T(8,128)(2,1)S(1)} %get-tuple-element.30.head_ref), channel_id=1, source_target_pairs={{0,12},{4,0},{8,4},{12,8},{1,13},{5,1},{9,5},{13,9},{2,14},{6,2},{... | collective-permute-start | bytes 196616 | tf_op jit(solution)/shard_map/ppermute | solution.py:20
  42.2 4.1 %collective-permute-start.16 = (bf16[768,512]{1,0:T(8,128)(2,1)S(1)}, bf16[768,512]{1,0:T(8,128)(2,1)}, u32[]{:S(2)}, u32[]{:S(2)}) collective-permute-start(bf16[768,512]{1,0:T(8,128)(2,1)S(1)} %copy-done.3), channel_id=1, source_target_pairs={{0,1},{1,0},{2,3},{3,2},{4,5},{5,4},{6,7},{7,6},{8,9},{9,8},{10,11... | collective-permute-start | bytes 2359304 | tf_op jit(solution)/shard_map/ppermute | solution.py:20
  46.1 2.5 %collective-permute-start.18 = (bf16[768,512]{1,0:T(8,128)(2,1)}, bf16[768,512]{1,0:T(8,128)(2,1)S(1)}, u32[]{:S(2)}, u32[]{:S(2)}) collective-permute-start(bf16[768,512]{1,0:T(8,128)(2,1)} %collective-permute-done.17.refs_2_), channel_id=1, source_target_pairs={{0,1},{1,0},{2,3},{3,2},{4,5},{5,4},{6,7},{7,6},{8,9},{9,8},{10,11... | collective-permute-start | bytes 2359304 | tf_op jit(solution)/shard_map/ppermute | solution.py:20
  (6 other events, 21.8 us)

commit v8 on v7

--- a/solution.py
+++ b/solution.py
@@ -53,30 +53,35 @@
     )
 
 
-def place(pieces, start, rows, whole):
+def place(near, far, near_start, far_start, rows, whole):
     subs = lax.axis_size("sub")
-    for index, piece in enumerate(pieces):
+    for index, piece in enumerate([*near, *far]):
         owner = owner_of(index // subs, index % subs)
+        start = near_start if index < subs else far_start
         whole[pl.ds(pl.multiple_of(owner * rows, rows), rows)] = piece[start : start + rows]
 
 
-def unpack_parts(pieces, base, sizes, wholes):
+def unpack(pieces, near_start, far_start, wholes):
+    subs, count = lax.axis_size("sub"), len(pieces)
+    for whole in wholes:
+        rows = whole.shape[0] // count
+        place(pieces[:subs], pieces[subs:], near_start, far_start, rows, whole)
+        near_start, far_start = near_start + rows, far_start + rows
+
+
+def unpack_parts(pieces, start, wholes):
     subs, groups = lax.axis_size("sub"), lax.axis_size("groups")
+    count = lax.axis_size("band") * subs
     for index, piece in enumerate(pieces):
         band_step, rest = divmod(index, groups * subs)
         owner = owner_of(band_step + 1, rest % subs)
         part = lax.rem(lax.axis_index("groups") + groups - rest // subs, groups)
-        start = base if rest < subs else 0
-        for size, whole in zip(sizes, wholes):
-            rows = size // groups
-            into = pl.multiple_of(owner * size + part * rows, rows)
-            whole[pl.ds(into, rows)] = piece[start : start + rows]
-            start += rows
-
-
-def unpack(pieces, sizes, wanted):
-    for at, whole in wanted.items():
-        place(pieces, sum(sizes[:at]), sizes[at], whole)
+        begin = start if rest < subs else 0
+        for whole in wholes:
+            rows = whole.shape[0] // (count * groups)
+            into = pl.multiple_of((owner * groups + part) * rows, rows)
+            whole[pl.ds(into, rows)] = piece[begin : begin + rows]
+            begin += rows
 
 
 def pack_kernel(sets, *refs):
@@ -128,9 +133,8 @@
     in_pieces, hid_pieces = refs[:count], refs[count : 2 * count]
     outs = refs[2 * count : 2 * count + faces]
     w_in, w_hid, messages = refs[2 * count + faces :]
-    rows = w_in.shape[0] // count
-    place(in_pieces, 0, rows, w_in)
-    place(hid_pieces, 0, rows, w_hid)
+    unpack(in_pieces, 0, 0, [w_in])
+    unpack(hid_pieces, 0, 0, [w_hid])
     block = 256
     for start in range(0, lat_ref.shape[0], block):
         here = pl.ds(start, block)
@@ -147,11 +151,15 @@
             out[...] = sums[face * mesh_rows : (face + 1) * mesh_rows].astype(out.dtype)
 
 
-def grid_kernel(base, sizes, lat_ref, *refs):
+def grid_kernel(near_start, part_start, lat_ref, *refs):
     pieces, (out_ref, w_in, w_hid) = refs[:-3], refs[-3:]
     subs = lax.axis_size("sub")
-    unpack(pieces[:subs], sizes, {2: w_in, 3: w_hid})
-    unpack_parts(pieces[subs:], base, sizes[2:], [w_in, w_hid])
+    start = near_start
+    for whole in (w_in, w_hid):
+        rows = whole.shape[0] // (lax.axis_size("band") * subs)
+        place(pieces[:subs], [], start, 0, rows, whole)
+        start += rows
+    unpack_parts(pieces[subs:], part_start, [w_in, w_hid])
     block = 256
     for start in range(0, lat_ref.shape[0], block):
         here = pl.ds(start, block)
@@ -161,11 +169,11 @@
         out_ref[here] = out.astype(jnp.bfloat16)
 
 
-def node_kernel(sizes, faces, lat_ref, *refs):
+def node_kernel(faces, lat_ref, *refs):
     sums, pieces = refs[:faces], refs[faces:-4]
     head_ref, tail_ref, w_in, w_hid = refs[-4:]
     width = lat_ref.shape[1]
-    unpack(pieces, sizes, {0: w_in, 1: w_hid})
+    unpack(pieces, 0, 0, [w_in, w_hid])
     collected = sums[0][...]
     for one in sums[1:]:
         collected = collected + one[...].astype(jnp.float32)
@@ -179,9 +187,9 @@
     tail_ref[...] = mid[half:]
 
 
-def edge_kernel(sizes, nbr_ref, before_ref, head_ref, tail_ref, after_ref, *refs):
-    pieces, (out_ref, p_in, p_hid, u_in, u_hid) = refs[:-5], refs[-5:]
-    unpack(pieces, sizes, {0: p_in, 1: p_hid, 2: u_in, 3: u_hid})
+def edge_kernel(far_start, nbr_ref, before_ref, head_ref, tail_ref, after_ref, *refs):
+    pieces, (out_ref, p_in, p_hid) = refs[:-3], refs[-3:]
+    unpack(pieces, 0, far_start, [p_in, p_hid])
     rows, fanin = nbr_ref.shape
     width = head_ref.shape[1]
     mid = jnp.concatenate([head_ref[...], tail_ref[...]], axis=0)
@@ -206,9 +214,17 @@
         for k in range(group):
             one = edges[k * rows : (k + 1) * rows]
             total = one if total is None else total + one
-    hidden = dot(mid, u_in[:width]) + dot(total.astype(jnp.bfloat16), u_in[width:])
+    out_ref[...] = total.astype(jnp.bfloat16)
+
+
+def update_kernel(near_start, head_ref, tail_ref, sum_ref, *refs):
+    pieces, (out_ref, w_in, w_hid) = refs[:-3], refs[-3:]
+    unpack(pieces, near_start, 0, [w_in, w_hid])
+    width = head_ref.shape[1]
+    mid = jnp.concatenate([head_ref[...], tail_ref[...]], axis=0)
+    hidden = dot(mid, w_in[:width]) + dot(sum_ref[...], w_in[width:])
     hidden = silu(hidden).astype(jnp.bfloat16)
-    out = mid.astype(jnp.float32) + layer_norm(dot(hidden, u_hid[...]))
+    out = mid.astype(jnp.float32) + layer_norm(dot(hidden, w_hid[...]))
     out_ref[...] = out.astype(jnp.bfloat16)
 
 
@@ -246,27 +262,24 @@
             transcendentals=rows * width,
         )
 
-    early_set = (node_w1, node_w2, grid_w1, grid_w2)
-    late_set = (proc_w1, proc_w2, upd_w1, upd_w2)
-    early_sizes = [weight.shape[0] for weight in early_set]
-    late_sizes = [weight.shape[0] for weight in late_set]
     small = pl.CostEstimate(flops=1, bytes_accessed=1, transcendentals=0)
     enc_far = [[shift(one, "band", step) for step in range(1, bands)] for one in (enc_w1, enc_w2)]
     enc_all = [
         own_spread(one) + relay(far) for one, far in zip((enc_w1, enc_w2), enc_far)
     ]
     groups = lax.axis_size("groups")
-    early_rows = list(enumerate(early_sizes))
-    late_rows = list(enumerate(late_sizes, len(early_sizes)))
-    halves = [(at, rows // groups) for at, rows in early_rows[2:]]
-    early, late, first = pack(
-        early_set + late_set, (early_rows, late_rows, early_rows[:2] + halves)
+    weights = (node_w1, node_w2, grid_w1, grid_w2, proc_w1, proc_w2, upd_w1, upd_w2)
+    whole = [(at, weight.shape[0]) for at, weight in enumerate(weights)]
+    halves = [(at, rows // groups) for at, rows in whole[2:4]]
+    node_rows = node_w1.shape[0] + node_w2.shape[0]
+    proc_rows = proc_w1.shape[0] + proc_w2.shape[0]
+    early, late, first, last = pack(
+        weights, (whole[:4], whole[4:], whole[:2] + whole[4:6] + halves, whole[6:])
     )
-    first_sent = after(first, *enc_far[0], *enc_far[1])
+    own_enc = enc_all[0][1:subs] + enc_all[1][1:subs]
+    first_sent = after(first, *enc_far[0], *enc_far[1], *own_enc)
     first_far = [shift(first_sent, "band", step) for step in range(1, bands)]
-    own_enc = enc_all[0][1:subs] + enc_all[1][1:subs]
-    early_near = own_spread(after(early, *enc_far[0], *enc_far[1], *own_enc))
-    late_near = own_spread(late)
+    early_near = own_spread(early)
 
     me = lax.axis_index("face")
     routes = grid_route[:, 0]
@@ -290,61 +303,66 @@
         compiler_params=pltpu.CompilerParams(vmem_limit_bytes=16 * MIB),
         cost_estimate=cost(grid_rows, 3 * width),
         name="encode",
-    )(after(targets, *early_near[1:]), grid_lat, *enc_all[0], *enc_all[1])
-    late_sent = after(late, sums[0])
-    late_far = [shift(late_sent, "band", step) for step in range(1, bands)]
+    )(targets, grid_lat, *enc_all[0], *enc_all[1])
+    last_sent = after(last, sums[0])
+    last_far = [shift(last_sent, "band", step) for step in range(1, bands)]
     arrived = [sums[0]] + [to_face(sums[step], step) for step in steps[1:]]
-
-    first_all = relay(first_far, *arrived[1:])
-    node_all = early_near + first_all
+    first_all = relay(first_far, *arrived[1:], *early_near[1:])
 
     half = (mesh_rows // 2, width)
     head, tail = pl.pallas_call(
-        functools.partial(node_kernel, early_sizes, faces),
+        functools.partial(node_kernel, faces),
         out_shape=[jax.ShapeDtypeStruct(half, bf16)] * 2,
-        in_specs=[VMEM] * (1 + faces) + [VMEM] * len(node_all),
+        in_specs=[VMEM] * (1 + faces) + [VMEM] * count,
         out_specs=[VMEM] * 2,
         scratch_shapes=[matrix(node_w1), matrix(node_w2)],
         compiler_params=pltpu.CompilerParams(vmem_limit_bytes=16 * MIB),
         cost_estimate=small,
         name="node_update",
-    )(mesh_lat, *arrived, *node_all)
-
-    base = sum(early_sizes[:2])
-    grid_all = list(early_near)
+    )(mesh_lat, *arrived, *early_near, *first_all)
+
+    parts, crossed = [], []
     for at, one in enumerate(first_far):
-        over = after(one[base:], *arrived[1:])
-        grid_all += first_all[at * subs : (at + 1) * subs]
-        grid_all += relay([shift(over, "groups", step) for step in range(1, groups)], head)
+        over = after(one[node_rows + proc_rows :], *arrived[1:])
+        others = [shift(over, "groups", step) for step in range(1, groups)]
+        parts += first_all[at * subs : (at + 1) * subs] + relay(others, head)
+        crossed += others
+    before = shift(after(tail, *crossed), "face", 1)
+    behind = shift(after(head, *crossed), "face", faces - 1)
     grid_out = pl.pallas_call(
-        functools.partial(grid_kernel, base, early_sizes),
+        functools.partial(grid_kernel, node_rows, node_rows + proc_rows),
         out_shape=jax.ShapeDtypeStruct(grid_lat.shape, bf16),
-        in_specs=[VMEM] + [VMEM] * len(grid_all),
+        in_specs=[VMEM] * (1 + subs + len(parts)),
         out_specs=VMEM,
         scratch_shapes=[matrix(grid_w1), matrix(grid_w2)],
         compiler_params=pltpu.CompilerParams(vmem_limit_bytes=16 * MIB),
         cost_estimate=small,
         name="grid_update",
-    )(grid_lat, *grid_all)
-
-    before = shift(tail, "face", 1)
-    behind = shift(head, "face", faces - 1)
-    late_all = late_near + relay(late_far, before, behind, grid_out)
+    )(grid_lat, *early_near, *parts)
+
+    late_near = own_spread(after(late, sums[0]))
+    edge_sum = pl.pallas_call(
+        functools.partial(edge_kernel, node_rows),
+        out_shape=jax.ShapeDtypeStruct(mesh_lat.shape, bf16),
+        in_specs=[VMEM] * 5 + [VMEM] * count,
+        out_specs=VMEM,
+        scratch_shapes=[matrix(proc_w1), matrix(proc_w2)],
+        compiler_params=pltpu.CompilerParams(vmem_limit_bytes=16 * MIB),
+        cost_estimate=small,
+        name="edges",
+    )(mesh_nbr, before, head, tail, behind, *late_near, *first_all)
+
+    last_all = late_near + relay(last_far, edge_sum)
     mesh_out = pl.pallas_call(
-        functools.partial(edge_kernel, late_sizes),
+        functools.partial(update_kernel, proc_rows),
         out_shape=jax.ShapeDtypeStruct(mesh_lat.shape, bf16),
-        in_specs=[VMEM] * 5 + [VMEM] * len(late_all),
+        in_specs=[VMEM] * 3 + [VMEM] * count,
         out_specs=VMEM,
-        scratch_shapes=[
-            matrix(proc_w1),
-            matrix(proc_w2),
-            matrix(upd_w1),
-            matrix(upd_w2),
-        ],
-        compiler_params=pltpu.CompilerParams(vmem_limit_bytes=16 * MIB),
-        cost_estimate=cost(mesh_rows * mesh_nbr.shape[1], 3 * width),
-        name="edge_update",
-    )(mesh_nbr, before, head, tail, behind, *late_all)
+        scratch_shapes=[matrix(upd_w1), matrix(upd_w2)],
+        compiler_params=pltpu.CompilerParams(vmem_limit_bytes=16 * MIB),
+        cost_estimate=small,
+        name="update",
+    )(head, tail, edge_sum, *last_all)
     return (grid_out, mesh_out)
 
 

time: 53.2 us -> 60.3 us (1.13)
  waiting for transfers between devices: 19.7 us -> 23.4 us
  local copies, waits for them, and re-layouts: 1.87 us -> 4.96 us
    ppermute x3, waiting for transfers between devices: 6.66 us -> 10.1 us  [to_face(): lax.ppermute(value, 'face', [(i, face_at(faces, step, i)) for i in range(...]
    unnamed x23 -> x35, local copies, waits for them, and re-layouts: 1.86 us -> 4.95 us
    pallas_call x1, Pallas kernels: 3.28 us -> 2.3 us  [shards(): pl.pallas_call(functools.partial(encode_kernel, count, faces, mesh_rows),...]
    pallas_call x3 -> x4, Pallas kernels: 8.25 us -> 8.93 us  [the longest x1 3.08 us: shards(): pl.pallas_call(functools.partial(grid_kernel, node_rows, node_rows + proc...]
  transfers between devices with their start and end apart: 19 -> 19, of which waited for: 11 -> 10; matrix products, arithmetic and copies ran while one was open for 0% -> 1% of each run, Pallas kernels for 19% -> 20%
where the time goes in v8:
time: 60.3 us; the launch traced here: 59.9 us
  waiting for transfers between devices  23.4 us (39%)
  starting transfers between devices  16.6 us (28%)
  Pallas kernels  14.2 us (24%)
  local copies, waits for them, and re-layouts  4.96 us (8%)
  between operations  0.76 us (1%)
    ppermute x16, waiting for transfers between devices, shift(): lax.ppermute(value, axis, [(i, (i + step) % count) for i in range(count)])  13.3 us
    ppermute x16, starting transfers between devices, shift(): lax.ppermute(value, axis, [(i, (i + step) % count) for i in range(count)])  12.1 us
    ppermute x3, waiting for transfers between devices, to_face(): lax.ppermute(value, 'face', [(i, face_at(faces, step, i)) for i in range(...  10.1 us
    unnamed x35, local copies, waits for them, and re-layouts  4.95 us
    ppermute x3, starting transfers between devices, to_face(): lax.ppermute(value, 'face', [(i, face_at(faces, step, i)) for i in range(...  4.45 us
    pallas_call x1, Pallas kernels, shards(): pl.pallas_call(functools.partial(grid_kernel, node_rows, node_rows + proc...  3.08 us
    pallas_call x1, Pallas kernels, pack(): pl.pallas_call(functools.partial(pack_kernel, sets), out_shape=[jax.Shape...  2.97 us
    pallas_call x1, Pallas kernels, shards(): pl.pallas_call(functools.partial(edge_kernel, node_rows), out_shape=jax.S...  2.65 us
  transfers between devices with their start and end apart: 19, of which 10 were waited for; matrix products, arithmetic and copies ran while one was open for 1% of the time, Pallas kernels for 20%

profile of v8, /device:TPU:0, one launch (start us, length us, event | category | flops | bytes accessed | tf_op | source)
XLA Modules:
  0.0 59.9 jit_solution(13228677762024466897)
XLA Ops:
  0.7 3.0 %collective-permute-start.1 = (bf16[128,512]{1,0:T(8,128)(2,1)}, bf16[128,512]{1,0:T(8,128)(2,1)S(1)}, u32[]{:S(2)}, u32[]{:S(2)}) collective-permute-start(bf16[128,512]{1,0:T(8,128)(2,1)} %refs_0_.3), channel_id=1, source_target_pairs={{0,2},{2,0},{1,3},{3,1},{4,6},{6,4},{5,7},{7,5},{8,10},{10,8},{9,1... | collective-permute-start | bytes 393224 | tf_op jit(solution)/shard_map/ppermute | solution.py:20
  4.2 3.0 %pack.1 = (bf16[640,512]{1,0:T(8,128)(2,1)}, bf16[768,512]{1,0:T(8,128)(2,1)}, bf16[896,512]{1,0:T(8,128)(2,1)}, bf16[384,512]{1,0:T(8,128)(2,1)}) custom-call(bf16[256,512]{1,0:T(8,128)(2,1)} %refs_0_.2, bf16[128,512]{1,0:T(8,128)(2,1)} %refs_1_.1, bf16[128,512]{1,0:T(8,128)(2,1)} %refs_2_.1, bf16[128,512]{1,0:T(8,128)(2,1)} %refs_3_.1, ...), custom_call_target="tpu_custom_call" | custom-call | tf_op jit(solution)/shard_map/pack/pallas_call | solution.py:102
  7.2 1.0 %collective-permute-done.1.refs_2_ = bf16[128,512]{1,0:T(8,128)(2,1)S(1)} collective-permute-done((bf16[128,512]{1,0:T(8,128)(2,1)}, bf16[128,512]{1,0:T(8,128)(2,1)S(1)}, u32[]{:S(2)}, u32[]{:S(2)}) %collective-permute-start.1) | collective-permute-done | bytes 131104 | tf_op jit(solution)/shard_map/ppermute | solution.py:20
  8.2 2.0 %collective-permute-done.2.refs_6_ = bf16[128,512]{1,0:T(8,128)(2,1)S(1)} collective-permute-done((bf16[128,512]{1,0:T(8,128)(2,1)}, bf16[128,512]{1,0:T(8,128)(2,1)S(1)}, u32[]{:S(2)}, u32[]{:S(2)}) %collective-permute-start.2) | collective-permute-done | bytes 131104 | tf_op jit(solution)/shard_map/ppermute | solution.py:20
  10.2 1.7 %collective-permute-start.5 = (bf16[896,512]{1,0:T(8,128)(2,1)}, bf16[896,512]{1,0:T(8,128)(2,1)S(1)}, u32[]{:S(2)}, u32[]{:S(2)}) collective-permute-start(bf16[896,512]{1,0:T(8,128)(2,1)} %get-tuple-element.23), channel_id=1, source_target_pairs={{0,2},{2,0},{1,3},{3,1},{4,6},{6,4},{5,7},{7,5},{8,10},{10,8},{9,1... | collective-permute-start | bytes 2752520 | tf_op jit(solution)/shard_map/ppermute | solution.py:20
  12.6 1.2 %collective-permute-done.6.refs_3_ = bf16[128,512]{1,0:T(8,128)(2,1)S(1)} collective-permute-done((bf16[128,512]{1,0:T(8,128)(2,1)S(1)}, bf16[128,512]{1,0:T(8,128)(2,1)S(1)}, u32[]{:S(2)}, u32[]{:S(2)}) %collective-permute-start.6) | collective-permute-done | bytes 131104 | tf_op jit(solution)/shard_map/ppermute | solution.py:20
  14.4 1.2 %copy-done.6 = bf16[1024,512]{1,0:T(8,128)(2,1)S(1)} copy-done((bf16[1024,512]{1,0:T(8,128)(2,1)S(1)}, bf16[1024,512]{1,0:T(8,128)(2,1)}, u32[]{:S(2)}) %copy-start.6) | copy-done | bytes 1048600
  15.6 2.3 %encode.1 = (f32[128,512]{1,0:T(8,128)S(1)}, bf16[128,512]{1,0:T(8,128)(2,1)S(1)}, bf16[128,512]{1,0:T(8,128)(2,1)S(1)}, bf16[128,512]{1,0:T(8,128)(2,1)S(1)}) custom-call(s32[1,1024]{1,0:T(1,128)S(1)} %bitcast.2, bf16[1024,512]{1,0:T(8,128)(2,1)S(1)} %copy-done.6, bf16[128,512]{1,0:T(8,128)(2,1)S(1)} %copy-done.12, ...), custom_call_target="tpu_custom_call" | custom-call | flops 1610612736 | bytes 2621440 | tf_op jit(solution)/shard_map/encode/pallas_call | solution.py:291
  17.9 1.6 %collective-permute-start.10 = (bf16[128,512]{1,0:T(8,128)(2,1)S(1)}, bf16[128,512]{1,0:T(8,128)(2,1)S(1)}, u32[]{:S(2)}, u32[]{:S(2)}) collective-permute-start(bf16[128,512]{1,0:T(8,128)(2,1)S(1)} %get-tuple-element.26), channel_id=1, source_target_pairs={{0,4},{4,0},{8,12},{12,8},{1,5},{5,1},{9,13},{13,9},{2,6},{6,2},{1... | collective-permute-start | bytes 393224 | tf_op jit(solution)/shard_map/ppermute | solution.py:35
  19.6 2.6 %collective-permute-start.8 = (bf16[128,512]{1,0:T(8,128)(2,1)S(1)}, bf16[128,512]{1,0:T(8,128)(2,1)S(1)}, u32[]{:S(2)}, u32[]{:S(2)}) collective-permute-start(bf16[128,512]{1,0:T(8,128)(2,1)S(1)} %get-tuple-element.24), channel_id=1, source_target_pairs={{0,8},{4,12},{8,0},{12,4},{1,9},{5,13},{9,1},{13,5},{2,10},{6,14},... | collective-permute-start | bytes 393224 | tf_op jit(solution)/shard_map/ppermute | solution.py:35
  22.4 3.1 %collective-permute-done.10.refs_3_ = bf16[128,512]{1,0:T(8,128)(2,1)S(1)} collective-permute-done((bf16[128,512]{1,0:T(8,128)(2,1)S(1)}, bf16[128,512]{1,0:T(8,128)(2,1)S(1)}, u32[]{:S(2)}, u32[]{:S(2)}) %collective-permute-start.10) | collective-permute-done | bytes 131104 | tf_op jit(solution)/shard_map/ppermute | solution.py:35
  25.5 7.0 %collective-permute-done.8.refs_1_ = bf16[128,512]{1,0:T(8,128)(2,1)S(1)} collective-permute-done((bf16[128,512]{1,0:T(8,128)(2,1)S(1)}, bf16[128,512]{1,0:T(8,128)(2,1)S(1)}, u32[]{:S(2)}, u32[]{:S(2)}) %collective-permute-start.8) | collective-permute-done | bytes 131104 | tf_op jit(solution)/shard_map/ppermute | solution.py:35
  32.5 0.8 %copy-done.3 = bf16[640,512]{1,0:T(8,128)(2,1)} copy-done((bf16[640,512]{1,0:T(8,128)(2,1)}, bf16[640,512]{1,0:T(8,128)(2,1)S(1)}, u32[]{:S(2)}) %copy-start.3) | copy-done | bytes 655384
  34.4 1.6 %collective-permute-start.12 = (bf16[128,512]{1,0:T(8,128)(2,1)S(1)}, bf16[128,512]{1,0:T(8,128)(2,1)S(1)}, u32[]{:S(2)}, u32[]{:S(2)}) collective-permute-start(bf16[128,512]{1,0:T(8,128)(2,1)S(1)} %slice.4), channel_id=1, source_target_pairs={{0,16},{16,0},{1,17},{17,1},{2,18},{18,2},{3,19},{19,3},{4,20},{20... | collective-permute-start | bytes 393224 | tf_op jit(solution)/shard_map/ppermute | solution.py:20
  36.0 1.1 %copy-done.4 = bf16[640,512]{1,0:T(8,128)(2,1)S(1)} copy-done((bf16[640,512]{1,0:T(8,128)(2,1)S(1)}, bf16[640,512]{1,0:T(8,128)(2,1)}, u32[]{:S(2)}) %copy-start.4) | copy-done | bytes 655384
  37.9 1.8 %collective-permute-done.12.refs_4_ = bf16[128,512]{1,0:T(8,128)(2,1)S(1)} collective-permute-done((bf16[128,512]{1,0:T(8,128)(2,1)S(1)}, bf16[128,512]{1,0:T(8,128)(2,1)S(1)}, u32[]{:S(2)}, u32[]{:S(2)}) %collective-permute-start.12) | collective-permute-done | bytes 131104 | tf_op jit(solution)/shard_map/ppermute | solution.py:20
  39.7 3.1 %collective-permute-start.15 = (bf16[64,512]{1,0:T(8,128)(2,1)S(1)}, bf16[64,512]{1,0:T(8,128)(2,1)}, u32[]{:S(2)}, u32[]{:S(2)}) collective-permute-start(bf16[64,512]{1,0:T(8,128)(2,1)S(1)} %get-tuple-element.34.head_ref), channel_id=1, source_target_pairs={{0,12},{4,0},{8,4},{12,8},{1,13},{5,1},{9,5},{13,9},{2,14},{6,2},{... | collective-permute-start | bytes 196616 | tf_op jit(solution)/shard_map/ppermute | solution.py:20
  43.5 1.1 %collective-permute-done.15.after_ref = bf16[64,512]{1,0:T(8,128)(2,1)} collective-permute-done((bf16[64,512]{1,0:T(8,128)(2,1)S(1)}, bf16[64,512]{1,0:T(8,128)(2,1)}, u32[]{:S(2)}, u32[]{:S(2)}) %collective-permute-start.15) | collective-permute-done | bytes 65568 | tf_op jit(solution)/shard_map/ppermute | solution.py:20
  44.6 4.3 %collective-permute-done.14.before_ref = bf16[64,512]{1,0:T(8,128)(2,1)} collective-permute-done((bf16[64,512]{1,0:T(8,128)(2,1)S(1)}, bf16[64,512]{1,0:T(8,128)(2,1)}, u32[]{:S(2)}, u32[]{:S(2)}) %collective-permute-start.14) | collective-permute-done | bytes 65568 | tf_op jit(solution)/shard_map/ppermute | solution.py:20
  48.9 0.8 %copy-done.8 = s32[128,6]{1,0:T(8,128)S(1)} copy-done((s32[128,6]{1,0:T(8,128)S(1)}, s32[128,6]{1,0:T(8,128)}, u32[]{:S(2)}) %copy-start.8) | copy-done | bytes 3096
  49.8 2.6 %edges.1.sum_ref = bf16[128,512]{1,0:T(8,128)(2,1)S(1)} custom-call(s32[128,6]{1,0:T(8,128)S(1)} %copy-done.8, bf16[64,512]{1,0:T(8,128)(2,1)} %collective-permute-done.14.before_ref, bf16[64,512]{1,0:T(8,128)(2,1)S(1)} %get-tuple-element.34.head_ref, bf16[64,512]{1,0:T(8,128)(2,1)S(1)} %get-tuple-element.33.tail_ref, ...), custom_call_target="tpu_custom_call" | custom-call | flops 1 | bytes 1 | tf_op jit(solution)/shard_map/edges/pallas_call | solution.py:344
  53.0 1.4 %collective-permute-done.13.refs_5_ = bf16[128,512]{1,0:T(8,128)(2,1)S(1)} collective-permute-done((bf16[128,512]{1,0:T(8,128)(2,1)S(1)}, bf16[128,512]{1,0:T(8,128)(2,1)S(1)}, u32[]{:S(2)}, u32[]{:S(2)}) %collective-permute-start.13) | collective-permute-done | bytes 131104 | tf_op jit(solution)/shard_map/ppermute | solution.py:20
  54.4 3.1 %grid_update.1 = bf16[1024,512]{1,0:T(8,128)(2,1)} custom-call(bf16[1024,512]{1,0:T(8,128)(2,1)S(1)} %copy-done.7, bf16[640,512]{1,0:T(8,128)(2,1)S(1)} %copy-done.2, bf16[640,512]{1,0:T(8,128)(2,1)S(1)} %copy-done.5, bf16[896,512]{1,0:T(8,128)(2,1)S(1)} %collective-permute-done.5.refs_6_.refs_2_, ...), custom_call_target="tpu_custom_call" | custom-call | flops 1 | bytes 1 | tf_op jit(solution)/shard_map/grid_update/pallas_call | solution.py:332
  57.5 2.4 %update.1 = bf16[128,512]{1,0:T(8,128)(2,1)} custom-call(bf16[64,512]{1,0:T(8,128)(2,1)S(1)} %get-tuple-element.34.head_ref, bf16[64,512]{1,0:T(8,128)(2,1)S(1)} %get-tuple-element.33.tail_ref, bf16[128,512]{1,0:T(8,128)(2,1)S(1)} %edges.1.sum_ref, bf16[768,512]{1,0:T(8,128)(2,1)S(1)} %copy-done, bf16[768,512]{1,0:T(8,128)(2,1)S(1)} %collective-permute-done.16.refs_1_, ...), custom_call_target="tpu_custom_call" | custom-call | flops 1 | bytes 1 | tf_op jit(solution)/shard_map/update/pallas_call | solution.py:356
  (58 shorter events, 5.3 us)
Async XLA Ops:
  0.6 13.8 %copy-start.12 = (bf16[128,512]{1,0:T(8,128)(2,1)S(1)}, bf16[128,512]{1,0:T(8,128)(2,1)}, u32[]{:S(2)}) copy-start(bf16[128,512]{1,0:T(8,128)(2,1)} %refs_0_.3) | copy-start | bytes 393220
  0.6 13.8 %copy-start.13 = (bf16[128,512]{1,0:T(8,128)(2,1)S(1)}, bf16[128,512]{1,0:T(8,128)(2,1)}, u32[]{:S(2)}) copy-start(bf16[128,512]{1,0:T(8,128)(2,1)} %refs_4_.3) | copy-start | bytes 393220
  0.7 7.5 %collective-permute-start.1 = (bf16[128,512]{1,0:T(8,128)(2,1)}, bf16[128,512]{1,0:T(8,128)(2,1)S(1)}, u32[]{:S(2)}, u32[]{:S(2)}) collective-permute-start(bf16[128,512]{1,0:T(8,128)(2,1)} %refs_0_.3), channel_id=1, source_target_pairs={{0,2},{2,0},{1,3},{3,1},{4,6},{6,4},{5,7},{7,5},{8,10},{10,8},{9,1... | collective-permute-start | bytes 393224 | tf_op jit(solution)/shard_map/ppermute | solution.py:20
  3.7 6.5 %collective-permute-start.2 = (bf16[128,512]{1,0:T(8,128)(2,1)}, bf16[128,512]{1,0:T(8,128)(2,1)S(1)}, u32[]{:S(2)}, u32[]{:S(2)}) collective-permute-start(bf16[128,512]{1,0:T(8,128)(2,1)} %refs_4_.3), channel_id=1, source_target_pairs={{0,2},{2,0},{1,3},{3,1},{4,6},{6,4},{5,7},{7,5},{8,10},{10,8},{9,1... | collective-permute-start | bytes 393224 | tf_op jit(solution)/shard_map/ppermute | solution.py:20
  3.7 6.4 %collective-permute-start.3 = (bf16[128,512]{1,0:T(8,128)(2,1)}, bf16[128,512]{1,0:T(8,128)(2,1)S(1)}, u32[]{:S(2)}, u32[]{:S(2)}) collective-permute-start(bf16[128,512]{1,0:T(8,128)(2,1)} %refs_0_.3), channel_id=1, source_target_pairs={{0,1},{1,0},{2,3},{3,2},{4,5},{5,4},{6,7},{7,6},{8,9},{9,8},{10,11... | collective-permute-start | bytes 393224 | tf_op jit(solution)/shard_map/ppermute | solution.py:20
  3.7 6.4 %collective-permute-start.4 = (bf16[128,512]{1,0:T(8,128)(2,1)}, bf16[128,512]{1,0:T(8,128)(2,1)S(1)}, u32[]{:S(2)}, u32[]{:S(2)}) collective-permute-start(bf16[128,512]{1,0:T(8,128)(2,1)} %refs_4_.3), channel_id=1, source_target_pairs={{0,1},{1,0},{2,3},{3,2},{4,5},{5,4},{6,7},{7,6},{8,9},{9,8},{10,11... | collective-permute-start | bytes 393224 | tf_op jit(solution)/shard_map/ppermute | solution.py:20
  10.2 23.2 %collective-permute-start.5 = (bf16[896,512]{1,0:T(8,128)(2,1)}, bf16[896,512]{1,0:T(8,128)(2,1)S(1)}, u32[]{:S(2)}, u32[]{:S(2)}) collective-permute-start(bf16[896,512]{1,0:T(8,128)(2,1)} %get-tuple-element.23), channel_id=1, source_target_pairs={{0,2},{2,0},{1,3},{3,1},{4,6},{6,4},{5,7},{7,5},{8,10},{10,8},{9,1... | collective-permute-start | bytes 2752520 | tf_op jit(solution)/shard_map/ppermute | solution.py:20
  11.9 20.6 %collective-permute-start = (bf16[640,512]{1,0:T(8,128)(2,1)}, bf16[640,512]{1,0:T(8,128)(2,1)S(1)}, u32[]{:S(2)}, u32[]{:S(2)}) collective-permute-start(bf16[640,512]{1,0:T(8,128)(2,1)} %get-tuple-element.21.refs_4_.refs_0_), channel_id=1, source_target_pairs={{0,1},{1,0},{2,3},{3,2},{4,5},{5,4},{6,7},{7,6},{8,9},{9,8},{10,11... | collective-permute-start | bytes 1966088 | tf_op jit(solution)/shard_map/ppermute | solution.py:20
  11.9 1.9 %collective-permute-start.6 = (bf16[128,512]{1,0:T(8,128)(2,1)S(1)}, bf16[128,512]{1,0:T(8,128)(2,1)S(1)}, u32[]{:S(2)}, u32[]{:S(2)}) collective-permute-start(bf16[128,512]{1,0:T(8,128)(2,1)S(1)} %collective-permute-done.1.refs_2_), channel_id=1, source_target_pairs={{0,1},{1,0},{2,3},{3,2},{4,5},{5,4},{6,7},{7,6},{8,9},{9,8},{10,11... | collective-permute-start | bytes 393224 | tf_op jit(solution)/shard_map/ppermute | solution.py:20
  12.4 2.0 %collective-permute-start.7 = (bf16[128,512]{1,0:T(8,128)(2,1)S(1)}, bf16[128,512]{1,0:T(8,128)(2,1)S(1)}, u32[]{:S(2)}, u32[]{:S(2)}) collective-permute-start(bf16[128,512]{1,0:T(8,128)(2,1)S(1)} %collective-permute-done.2.refs_6_), channel_id=1, source_target_pairs={{0,1},{1,0},{2,3},{3,2},{4,5},{5,4},{6,7},{7,6},{8,9},{9,8},{10,11... | collective-permute-start | bytes 393224 | tf_op jit(solution)/shard_map/ppermute | solution.py:20
  15.6 17.7 %copy-start = (bf16[768,512]{1,0:T(8,128)(2,1)S(1)}, bf16[768,512]{1,0:T(8,128)(2,1)}, u32[]{:S(2)}) copy-start(bf16[768,512]{1,0:T(8,128)(2,1)} %get-tuple-element.36.refs_0_) | copy-start | bytes 2359300
  15.6 20.4 %copy-start.1 = (bf16[640,512]{1,0:T(8,128)(2,1)S(1)}, bf16[640,512]{1,0:T(8,128)(2,1)}, u32[]{:S(2)}) copy-start(bf16[640,512]{1,0:T(8,128)(2,1)} %get-tuple-element.21.refs_4_.refs_0_) | copy-start | bytes 1966084
  17.9 7.5 %collective-permute-start.10 = (bf16[128,512]{1,0:T(8,128)(2,1)S(1)}, bf16[128,512]{1,0:T(8,128)(2,1)S(1)}, u32[]{:S(2)}, u32[]{:S(2)}) collective-permute-start(bf16[128,512]{1,0:T(8,128)(2,1)S(1)} %get-tuple-element.26), channel_id=1, source_target_pairs={{0,4},{4,0},{8,12},{12,8},{1,5},{5,1},{9,13},{13,9},{2,6},{6,2},{1... | collective-permute-start | bytes 393224 | tf_op jit(solution)/shard_map/ppermute | solution.py:35
  19.6 12.9 %collective-permute-start.8 = (bf16[128,512]{1,0:T(8,128)(2,1)S(1)}, bf16[128,512]{1,0:T(8,128)(2,1)S(1)}, u32[]{:S(2)}, u32[]{:S(2)}) collective-permute-start(bf16[128,512]{1,0:T(8,128)(2,1)S(1)} %get-tuple-element.24), channel_id=1, source_target_pairs={{0,8},{4,12},{8,0},{12,4},{1,9},{5,13},{9,1},{13,5},{2,10},{6,14},... | collective-permute-start | bytes 393224 | tf_op jit(solution)/shard_map/ppermute | solution.py:35
  22.2 10.3 %collective-permute-start.9 = (bf16[128,512]{1,0:T(8,128)(2,1)S(1)}, bf16[128,512]{1,0:T(8,128)(2,1)S(1)}, u32[]{:S(2)}, u32[]{:S(2)}) collective-permute-start(bf16[128,512]{1,0:T(8,128)(2,1)S(1)} %get-tuple-element.25), channel_id=1, source_target_pairs={{0,12},{4,8},{8,4},{12,0},{1,13},{5,9},{9,5},{13,1},{2,14},{6,10},... | collective-permute-start | bytes 393224 | tf_op jit(solution)/shard_map/ppermute | solution.py:35
  33.3 2.7 %collective-permute-start.11 = (bf16[896,512]{1,0:T(8,128)(2,1)S(1)}, bf16[896,512]{1,0:T(8,128)(2,1)S(1)}, u32[]{:S(2)}, u32[]{:S(2)}) collective-permute-start(bf16[896,512]{1,0:T(8,128)(2,1)S(1)} %collective-permute-done.5.refs_6_.refs_2_), channel_id=1, source_target_pairs={{0,1},{1,0},{2,3},{3,2},{4,5},{5,4},{6,7},{7,6},{8,9},{9,8},{10,11... | collective-permute-start | bytes 2752520 | tf_op jit(solution)/shard_map/ppermute | solution.py:20
  33.4 10.1 %collective-permute-start.16 = (bf16[768,512]{1,0:T(8,128)(2,1)S(1)}, bf16[768,512]{1,0:T(8,128)(2,1)S(1)}, u32[]{:S(2)}, u32[]{:S(2)}) collective-permute-start(bf16[768,512]{1,0:T(8,128)(2,1)S(1)} %copy-done), channel_id=1, source_target_pairs={{0,1},{1,0},{2,3},{3,2},{4,5},{5,4},{6,7},{7,6},{8,9},{9,8},{10,11... | collective-permute-start | bytes 2359304 | tf_op jit(solution)/shard_map/ppermute | solution.py:20
  33.9 18.5 %collective-permute-start.17 = (bf16[384,512]{1,0:T(8,128)(2,1)}, bf16[384,512]{1,0:T(8,128)(2,1)}, u32[]{:S(2)}, u32[]{:S(2)}) collective-permute-start(bf16[384,512]{1,0:T(8,128)(2,1)} %get-tuple-element.38), channel_id=1, source_target_pairs={{0,2},{2,0},{1,3},{3,1},{4,6},{6,4},{5,7},{7,5},{8,10},{10,8},{9,1... | collective-permute-start | bytes 1179656 | tf_op jit(solution)/shard_map/ppermute | solution.py:20
  34.4 5.3 %collective-permute-start.12 = (bf16[128,512]{1,0:T(8,128)(2,1)S(1)}, bf16[128,512]{1,0:T(8,128)(2,1)S(1)}, u32[]{:S(2)}, u32[]{:S(2)}) collective-permute-start(bf16[128,512]{1,0:T(8,128)(2,1)S(1)} %slice.4), channel_id=1, source_target_pairs={{0,16},{16,0},{1,17},{17,1},{2,18},{18,2},{3,19},{19,3},{4,20},{20... | collective-permute-start | bytes 393224 | tf_op jit(solution)/shard_map/ppermute | solution.py:20
  39.7 5.0 %collective-permute-start.15 = (bf16[64,512]{1,0:T(8,128)(2,1)S(1)}, bf16[64,512]{1,0:T(8,128)(2,1)}, u32[]{:S(2)}, u32[]{:S(2)}) collective-permute-start(bf16[64,512]{1,0:T(8,128)(2,1)S(1)} %get-tuple-element.34.head_ref), channel_id=1, source_target_pairs={{0,12},{4,0},{8,4},{12,8},{1,13},{5,1},{9,5},{13,9},{2,14},{6,2},{... | collective-permute-start | bytes 196616 | tf_op jit(solution)/shard_map/ppermute | solution.py:20
  42.7 6.2 %collective-permute-start.14 = (bf16[64,512]{1,0:T(8,128)(2,1)S(1)}, bf16[64,512]{1,0:T(8,128)(2,1)}, u32[]{:S(2)}, u32[]{:S(2)}) collective-permute-start(bf16[64,512]{1,0:T(8,128)(2,1)S(1)} %get-tuple-element.33.tail_ref), channel_id=1, source_target_pairs={{0,4},{4,8},{8,12},{12,0},{1,5},{5,9},{9,13},{13,1},{2,6},{6,10},{... | collective-permute-start | bytes 196616 | tf_op jit(solution)/shard_map/ppermute | solution.py:20
  43.5 10.9 %copy-start.7 = (bf16[1024,512]{1,0:T(8,128)(2,1)S(1)}, bf16[1024,512]{1,0:T(8,128)(2,1)}, u32[]{:S(2)}) copy-start(bf16[1024,512]{1,0:T(8,128)(2,1)} %lat_ref.5) | copy-start | bytes 3145732
  52.4 5.1 %collective-permute-start.18 = (bf16[384,512]{1,0:T(8,128)(2,1)}, bf16[384,512]{1,0:T(8,128)(2,1)S(1)}, u32[]{:S(2)}, u32[]{:S(2)}) collective-permute-start(bf16[384,512]{1,0:T(8,128)(2,1)} %collective-permute-done.17.refs_2_), channel_id=1, source_target_pairs={{0,1},{1,0},{2,3},{3,2},{4,5},{5,4},{6,7},{7,6},{8,9},{9,8},{10,11... | collective-permute-start | bytes 1179656 | tf_op jit(solution)/shard_map/ppermute | solution.py:20
  52.5 1.9 %collective-permute-start.13 = (bf16[128,512]{1,0:T(8,128)(2,1)S(1)}, bf16[128,512]{1,0:T(8,128)(2,1)S(1)}, u32[]{:S(2)}, u32[]{:S(2)}) collective-permute-start(bf16[128,512]{1,0:T(8,128)(2,1)S(1)} %copy-done.11), channel_id=1, source_target_pairs={{0,1},{1,0},{2,3},{3,2},{4,5},{5,4},{6,7},{7,6},{8,9},{9,8},{10,11... | collective-permute-start | bytes 393224 | tf_op jit(solution)/shard_map/ppermute | solution.py:20
  (12 other events, 40.8 us)

commit v9 on v6

--- a/solution.py
+++ b/solution.py
@@ -169,7 +169,7 @@
     nbr = nbr_ref[...]
     receivers = dot(mid, p_in[width:])
     total = None
-    group = 2 if fanin % 2 == 0 else 1
+    group = fanin
     for at in range(0, fanin, group):
         chosen = jnp.concatenate(
             [
@@ -232,7 +232,7 @@
         own_spread(one) + relay(far) for one, far in zip((enc_w1, enc_w2), enc_far)
     ]
     early, late = pack(sets)
-    early_sent = after(early, *enc_far[1], *enc_all[0][1:], *enc_all[1][1:subs])
+    early_sent = after(early, *enc_far[0], *enc_far[1], *enc_all[0][1:subs], *enc_all[1][1:subs])
     early_far = [shift(early_sent, "band", step) for step in range(1, bands)]
     early_near, late_near = own_spread(early), own_spread(late)
 

time: 52.5 us -> 50.3 us (0.958)
  waiting for transfers between devices: 22.5 us -> 21.3 us
    ppermute x14, waiting for transfers between devices: 13.4 us -> 12.4 us  [shift(): lax.ppermute(value, axis, [(i, (i + step) % count) for i in range(count)])]
  transfers between devices with their start and end apart: 17 -> 17, of which waited for: 8 -> 10; matrix products, arithmetic and copies ran while one was open for 0% -> 0% of each run, Pallas kernels for 17% -> 17%
where the time goes in v9:
time: 50.3 us; the launch traced here: 50.1 us
  waiting for transfers between devices  21.3 us (42%)
  starting transfers between devices  14.9 us (30%)
  Pallas kernels  12.8 us (25%)
  between operations  0.75 us (1%)
    ppermute x14, waiting for transfers between devices, shift(): lax.ppermute(value, axis, [(i, (i + step) % count) for i in range(count)])  12.4 us
    ppermute x14, starting transfers between devices, shift(): lax.ppermute(value, axis, [(i, (i + step) % count) for i in range(count)])  10.7 us
    ppermute x3, waiting for transfers between devices, to_face(): lax.ppermute(value, 'face', [(i, face_at(faces, step, i)) for i in range(...  8.91 us
    ppermute x3, starting transfers between devices, to_face(): lax.ppermute(value, 'face', [(i, face_at(faces, step, i)) for i in range(...  4.24 us
    pallas_call x1, Pallas kernels, shards(): pl.pallas_call(functools.partial(edge_kernel, sizes[1]), out_shape=jax.Sh...  4.15 us
    pallas_call x1, Pallas kernels, shards(): pl.pallas_call(functools.partial(grid_kernel, sizes[0]), out_shape=jax.Sh...  3.06 us
    pallas_call x1, Pallas kernels, pack(): pl.pallas_call(functools.partial(pack_kernel, [len(one) for one in sets])...  2.51 us
    pallas_call x1, Pallas kernels, shards(): pl.pallas_call(functools.partial(encode_kernel, count, faces, mesh_rows),...  2.31 us
  transfers between devices with their start and end apart: 17, of which 10 were waited for; matrix products, arithmetic and copies ran while one was open for 0% of the time, Pallas kernels for 17%

profile of v9, /device:TPU:0, one launch (start us, length us, event | category | flops | bytes accessed | tf_op | source)
XLA Modules:
  0.0 50.1 jit_solution(14048322585302787827)
XLA Ops:
  0.7 3.0 %collective-permute-start.1 = (bf16[128,512]{1,0:T(8,128)(2,1)}, bf16[128,512]{1,0:T(8,128)(2,1)S(1)}, u32[]{:S(2)}, u32[]{:S(2)}) collective-permute-start(bf16[128,512]{1,0:T(8,128)(2,1)} %refs_0_.3), channel_id=1, source_target_pairs={{0,2},{2,0},{1,3},{3,1},{4,6},{6,4},{5,7},{7,5},{8,10},{10,8},{9,1... | collective-permute-start | bytes 393224 | tf_op jit(solution)/shard_map/ppermute | solution.py:20
  3.8 0.4 collective-permute-start.4
  4.2 2.5 %pack.1 = (bf16[640,512]{1,0:T(8,128)(2,1)}, bf16[768,512]{1,0:T(8,128)(2,1)}) custom-call(bf16[256,512]{1,0:T(8,128)(2,1)} %refs_0_.2, bf16[128,512]{1,0:T(8,128)(2,1)} %refs_1_.1, bf16[128,512]{1,0:T(8,128)(2,1)} %refs_2_.1, bf16[128,512]{1,0:T(8,128)(2,1)} %refs_3_.1, bf16[256,512]{1,0:T(8,128)(2,1)} %refs_4_.2, bf16[128,512]{1,0:T(8,128)(2,1)} %refs_5_.1, ...), custom_call_target="tpu_custom_call" | custom-call | tf_op jit(solution)/shard_map/pack/pallas_call | solution.py:80
  6.7 1.2 %collective-permute-done.1.refs_2_ = bf16[128,512]{1,0:T(8,128)(2,1)S(1)} collective-permute-done((bf16[128,512]{1,0:T(8,128)(2,1)}, bf16[128,512]{1,0:T(8,128)(2,1)S(1)}, u32[]{:S(2)}, u32[]{:S(2)}) %collective-permute-start.1) | collective-permute-done | bytes 131104 | tf_op jit(solution)/shard_map/ppermute | solution.py:20
  7.9 2.3 %collective-permute-done.2.refs_6_ = bf16[128,512]{1,0:T(8,128)(2,1)S(1)} collective-permute-done((bf16[128,512]{1,0:T(8,128)(2,1)}, bf16[128,512]{1,0:T(8,128)(2,1)S(1)}, u32[]{:S(2)}, u32[]{:S(2)}) %collective-permute-start.2) | collective-permute-done | bytes 131104 | tf_op jit(solution)/shard_map/ppermute | solution.py:20
  10.2 1.7 %collective-permute-start.5 = (bf16[640,512]{1,0:T(8,128)(2,1)}, bf16[640,512]{1,0:T(8,128)(2,1)S(1)}, u32[]{:S(2)}, u32[]{:S(2)}) collective-permute-start(bf16[640,512]{1,0:T(8,128)(2,1)} %get-tuple-element.15.refs_0_.refs_4_), channel_id=1, source_target_pairs={{0,2},{2,0},{1,3},{3,1},{4,6},{6,4},{5,7},{7,5},{8,10},{10,8},{9,1... | collective-permute-start | bytes 1966088 | tf_op jit(solution)/shard_map/ppermute | solution.py:20
  11.9 0.5 %collective-permute-start.7 = (bf16[128,512]{1,0:T(8,128)(2,1)S(1)}, bf16[128,512]{1,0:T(8,128)(2,1)S(1)}, u32[]{:S(2)}, u32[]{:S(2)}) collective-permute-start(bf16[128,512]{1,0:T(8,128)(2,1)S(1)} %collective-permute-done.2.refs_6_), channel_id=1, source_target_pairs={{0,1},{1,0},{2,3},{3,2},{4,5},{5,4},{6,7},{7,6},{8,9},{9,8},{10,11... | collective-permute-start | bytes 393224 | tf_op jit(solution)/shard_map/ppermute | solution.py:20
  12.6 0.7 %collective-permute-done.6.refs_3_ = bf16[128,512]{1,0:T(8,128)(2,1)S(1)} collective-permute-done((bf16[128,512]{1,0:T(8,128)(2,1)S(1)}, bf16[128,512]{1,0:T(8,128)(2,1)S(1)}, u32[]{:S(2)}, u32[]{:S(2)}) %collective-permute-start.6) | collective-permute-done | bytes 131104 | tf_op jit(solution)/shard_map/ppermute | solution.py:20
  13.5 2.3 %encode.1 = (f32[128,512]{1,0:T(8,128)S(1)}, bf16[128,512]{1,0:T(8,128)(2,1)S(1)}, bf16[128,512]{1,0:T(8,128)(2,1)S(1)}, bf16[128,512]{1,0:T(8,128)(2,1)S(1)}) custom-call(s32[1,1024]{1,0:T(1,128)S(1)} %bitcast.2, bf16[1024,512]{1,0:T(8,128)(2,1)S(1)} %copy-done.1, bf16[128,512]{1,0:T(8,128)(2,1)S(1)} %copy-done.4, ...), custom_call_target="tpu_custom_call" | custom-call | flops 1610612736 | bytes 2621440 | tf_op jit(solution)/shard_map/encode/pallas_call | solution.py:246
  15.8 2.7 %collective-permute-start.8 = (bf16[128,512]{1,0:T(8,128)(2,1)S(1)}, bf16[128,512]{1,0:T(8,128)(2,1)S(1)}, u32[]{:S(2)}, u32[]{:S(2)}) collective-permute-start(bf16[128,512]{1,0:T(8,128)(2,1)S(1)} %get-tuple-element.16), channel_id=1, source_target_pairs={{0,8},{4,12},{8,0},{12,4},{1,9},{5,13},{9,1},{13,5},{2,10},{6,14},... | collective-permute-start | bytes 393224 | tf_op jit(solution)/shard_map/ppermute | solution.py:35
  18.5 1.3 %collective-permute-start.9 = (bf16[128,512]{1,0:T(8,128)(2,1)S(1)}, bf16[128,512]{1,0:T(8,128)(2,1)S(1)}, u32[]{:S(2)}, u32[]{:S(2)}) collective-permute-start(bf16[128,512]{1,0:T(8,128)(2,1)S(1)} %get-tuple-element.17), channel_id=1, source_target_pairs={{0,12},{4,8},{8,4},{12,0},{1,13},{5,9},{9,5},{13,1},{2,14},{6,10},... | collective-permute-start | bytes 393224 | tf_op jit(solution)/shard_map/ppermute | solution.py:35
  20.1 0.5 %collective-permute-start.15 = (bf16[768,512]{1,0:T(8,128)(2,1)S(1)}, bf16[768,512]{1,0:T(8,128)(2,1)S(1)}, u32[]{:S(2)}, u32[]{:S(2)}) collective-permute-start(bf16[768,512]{1,0:T(8,128)(2,1)S(1)} %copy-done.3), channel_id=1, source_target_pairs={{0,2},{2,0},{1,3},{3,1},{4,6},{6,4},{5,7},{7,5},{8,10},{10,8},{9,1... | collective-permute-start | bytes 2359304 | tf_op jit(solution)/shard_map/ppermute | solution.py:20
  20.6 8.2 %collective-permute-done.8.refs_1_ = bf16[128,512]{1,0:T(8,128)(2,1)S(1)} collective-permute-done((bf16[128,512]{1,0:T(8,128)(2,1)S(1)}, bf16[128,512]{1,0:T(8,128)(2,1)S(1)}, u32[]{:S(2)}, u32[]{:S(2)}) %collective-permute-start.8) | collective-permute-done | bytes 131104 | tf_op jit(solution)/shard_map/ppermute | solution.py:35
  28.8 0.7 %collective-permute-done.10.refs_3_ = bf16[128,512]{1,0:T(8,128)(2,1)S(1)} collective-permute-done((bf16[128,512]{1,0:T(8,128)(2,1)S(1)}, bf16[128,512]{1,0:T(8,128)(2,1)S(1)}, u32[]{:S(2)}, u32[]{:S(2)}) %collective-permute-start.10) | collective-permute-done | bytes 131104 | tf_op jit(solution)/shard_map/ppermute | solution.py:35
  29.5 0.5 %collective-permute-start.14 = (bf16[768,512]{1,0:T(8,128)(2,1)S(1)}, bf16[768,512]{1,0:T(8,128)(2,1)}, u32[]{:S(2)}, u32[]{:S(2)}) collective-permute-start(bf16[768,512]{1,0:T(8,128)(2,1)S(1)} %copy-done.3), channel_id=1, source_target_pairs={{0,1},{1,0},{2,3},{3,2},{4,5},{5,4},{6,7},{7,6},{8,9},{9,8},{10,11... | collective-permute-start | bytes 2359304 | tf_op jit(solution)/shard_map/ppermute | solution.py:20
  30.0 0.8 %collective-permute-done.refs_1_.refs_5_ = bf16[640,512]{1,0:T(8,128)(2,1)S(1)} collective-permute-done((bf16[640,512]{1,0:T(8,128)(2,1)S(1)}, bf16[640,512]{1,0:T(8,128)(2,1)S(1)}, u32[]{:S(2)}, u32[]{:S(2)}) %collective-permute-start) | collective-permute-done | bytes 655392 | tf_op jit(solution)/shard_map/ppermute | solution.py:20
  30.9 1.9 %collective-permute-done.11.refs_3_.refs_7_ = bf16[640,512]{1,0:T(8,128)(2,1)S(1)} collective-permute-done((bf16[640,512]{1,0:T(8,128)(2,1)S(1)}, bf16[640,512]{1,0:T(8,128)(2,1)S(1)}, u32[]{:S(2)}, u32[]{:S(2)}) %collective-permute-start.11) | collective-permute-done | bytes 655392 | tf_op jit(solution)/shard_map/ppermute | solution.py:20
  32.8 0.8 %node_update.1 = (bf16[64,512]{1,0:T(8,128)(2,1)S(1)}, bf16[64,512]{1,0:T(8,128)(2,1)S(1)}) custom-call(bf16[128,512]{1,0:T(8,128)(2,1)S(1)} %copy-done.2, f32[128,512]{1,0:T(8,128)S(1)} %get-tuple-element.20.refs_0_, bf16[128,512]{1,0:T(8,128)(2,1)S(1)} %collective-permute-done.8.refs_1_, bf16[128,512]{1,0:T(8,128)(2,1)S(1)} %collective-permute-done.9.refs_2_, ...), custom_call_target="tpu_custom_call" | custom-call | flops 201326592 | bytes 1703936 | tf_op jit(solution)/shard_map/node_update/pallas_call | solution.py:279
  33.6 1.3 %collective-permute-start.12 = (bf16[64,512]{1,0:T(8,128)(2,1)S(1)}, bf16[64,512]{1,0:T(8,128)(2,1)S(1)}, u32[]{:S(2)}, u32[]{:S(2)}) collective-permute-start(bf16[64,512]{1,0:T(8,128)(2,1)S(1)} %get-tuple-element.21.tail_ref), channel_id=1, source_target_pairs={{0,4},{4,8},{8,12},{12,0},{1,5},{5,9},{9,13},{13,1},{2,6},{6,10},{... | collective-permute-start | bytes 196616 | tf_op jit(solution)/shard_map/ppermute | solution.py:20
  34.9 2.5 %collective-permute-start.13 = (bf16[64,512]{1,0:T(8,128)(2,1)S(1)}, bf16[64,512]{1,0:T(8,128)(2,1)S(1)}, u32[]{:S(2)}, u32[]{:S(2)}) collective-permute-start(bf16[64,512]{1,0:T(8,128)(2,1)S(1)} %get-tuple-element.22.head_ref), channel_id=1, source_target_pairs={{0,12},{4,0},{8,4},{12,8},{1,13},{5,1},{9,5},{13,9},{2,14},{6,2},{... | collective-permute-start | bytes 196616 | tf_op jit(solution)/shard_map/ppermute | solution.py:20
  37.4 3.1 %grid_update.1 = bf16[1024,512]{1,0:T(8,128)(2,1)} custom-call(bf16[1024,512]{1,0:T(8,128)(2,1)S(1)} %copy-done.1, bf16[640,512]{1,0:T(8,128)(2,1)S(1)} %copy-done, bf16[640,512]{1,0:T(8,128)(2,1)S(1)} %collective-permute-done.refs_1_.refs_5_, bf16[640,512]{1,0:T(8,128)(2,1)S(1)} %collective-permute-done.5.refs_2_.refs_6_, ...), custom_call_target="tpu_custom_call" | custom-call | flops 1073741824 | bytes 2097152 | tf_op jit(solution)/shard_map/grid_update/pallas_call | solution.py:267
  40.5 3.2 %collective-permute-done.15.refs_2_ = bf16[768,512]{1,0:T(8,128)(2,1)S(1)} collective-permute-done((bf16[768,512]{1,0:T(8,128)(2,1)S(1)}, bf16[768,512]{1,0:T(8,128)(2,1)S(1)}, u32[]{:S(2)}, u32[]{:S(2)}) %collective-permute-start.15) | collective-permute-done | bytes 786464 | tf_op jit(solution)/shard_map/ppermute | solution.py:20
  43.8 2.2 %collective-permute-done.16.refs_3_ = bf16[768,512]{1,0:T(8,128)(2,1)S(1)} collective-permute-done((bf16[768,512]{1,0:T(8,128)(2,1)S(1)}, bf16[768,512]{1,0:T(8,128)(2,1)S(1)}, u32[]{:S(2)}, u32[]{:S(2)}) %collective-permute-start.16) | collective-permute-done | bytes 786464 | tf_op jit(solution)/shard_map/ppermute | solution.py:20
  46.0 4.1 %edge_update.1 = bf16[128,512]{1,0:T(8,128)(2,1)} custom-call(s32[128,6]{1,0:T(8,128)S(1)} %copy.17.nbr_ref, bf16[64,512]{1,0:T(8,128)(2,1)S(1)} %collective-permute-done.12.before_ref, bf16[64,512]{1,0:T(8,128)(2,1)S(1)} %get-tuple-element.22.head_ref, bf16[64,512]{1,0:T(8,128)(2,1)S(1)} %get-tuple-element.21.tail_ref, ...), custom_call_target="tpu_custom_call" | custom-call | flops 1207959552 | bytes 2359296 | tf_op jit(solution)/shard_map/edge_update/pallas_call | solution.py:293
  (36 shorter events, 0.9 us)
Async XLA Ops:
  0.6 12.8 %copy-start.4 = (bf16[128,512]{1,0:T(8,128)(2,1)S(1)}, bf16[128,512]{1,0:T(8,128)(2,1)}, u32[]{:S(2)}) copy-start(bf16[128,512]{1,0:T(8,128)(2,1)} %refs_0_.3) | copy-start | bytes 393220
  0.6 12.8 %copy-start.5 = (bf16[128,512]{1,0:T(8,128)(2,1)S(1)}, bf16[128,512]{1,0:T(8,128)(2,1)}, u32[]{:S(2)}) copy-start(bf16[128,512]{1,0:T(8,128)(2,1)} %refs_4_.3) | copy-start | bytes 393220
  0.7 12.8 %copy-start.1 = (bf16[1024,512]{1,0:T(8,128)(2,1)S(1)}, bf16[1024,512]{1,0:T(8,128)(2,1)}, u32[]{:S(2)}) copy-start(bf16[1024,512]{1,0:T(8,128)(2,1)} %lat_ref.4) | copy-start | bytes 3145732
  0.7 7.2 %collective-permute-start.1 = (bf16[128,512]{1,0:T(8,128)(2,1)}, bf16[128,512]{1,0:T(8,128)(2,1)S(1)}, u32[]{:S(2)}, u32[]{:S(2)}) collective-permute-start(bf16[128,512]{1,0:T(8,128)(2,1)} %refs_0_.3), channel_id=1, source_target_pairs={{0,2},{2,0},{1,3},{3,1},{4,6},{6,4},{5,7},{7,5},{8,10},{10,8},{9,1... | collective-permute-start | bytes 393224 | tf_op jit(solution)/shard_map/ppermute | solution.py:20
  3.7 4.2 %collective-permute-start.3 = (bf16[128,512]{1,0:T(8,128)(2,1)}, bf16[128,512]{1,0:T(8,128)(2,1)S(1)}, u32[]{:S(2)}, u32[]{:S(2)}) collective-permute-start(bf16[128,512]{1,0:T(8,128)(2,1)} %refs_0_.3), channel_id=1, source_target_pairs={{0,1},{1,0},{2,3},{3,2},{4,5},{5,4},{6,7},{7,6},{8,9},{9,8},{10,11... | collective-permute-start | bytes 393224 | tf_op jit(solution)/shard_map/ppermute | solution.py:20
  3.7 6.5 %collective-permute-start.2 = (bf16[128,512]{1,0:T(8,128)(2,1)}, bf16[128,512]{1,0:T(8,128)(2,1)S(1)}, u32[]{:S(2)}, u32[]{:S(2)}) collective-permute-start(bf16[128,512]{1,0:T(8,128)(2,1)} %refs_4_.3), channel_id=1, source_target_pairs={{0,2},{2,0},{1,3},{3,1},{4,6},{6,4},{5,7},{7,5},{8,10},{10,8},{9,1... | collective-permute-start | bytes 393224 | tf_op jit(solution)/shard_map/ppermute | solution.py:20
  3.8 6.4 %collective-permute-start.4 = (bf16[128,512]{1,0:T(8,128)(2,1)}, bf16[128,512]{1,0:T(8,128)(2,1)S(1)}, u32[]{:S(2)}, u32[]{:S(2)}) collective-permute-start(bf16[128,512]{1,0:T(8,128)(2,1)} %refs_4_.3), channel_id=1, source_target_pairs={{0,1},{1,0},{2,3},{3,2},{4,5},{5,4},{6,7},{7,6},{8,9},{9,8},{10,11... | collective-permute-start | bytes 393224 | tf_op jit(solution)/shard_map/ppermute | solution.py:20
  10.2 19.3 %collective-permute-start.5 = (bf16[640,512]{1,0:T(8,128)(2,1)}, bf16[640,512]{1,0:T(8,128)(2,1)S(1)}, u32[]{:S(2)}, u32[]{:S(2)}) collective-permute-start(bf16[640,512]{1,0:T(8,128)(2,1)} %get-tuple-element.15.refs_0_.refs_4_), channel_id=1, source_target_pairs={{0,2},{2,0},{1,3},{3,1},{4,6},{6,4},{5,7},{7,5},{8,10},{10,8},{9,1... | collective-permute-start | bytes 1966088 | tf_op jit(solution)/shard_map/ppermute | solution.py:20
  11.9 1.3 %collective-permute-start.6 = (bf16[128,512]{1,0:T(8,128)(2,1)S(1)}, bf16[128,512]{1,0:T(8,128)(2,1)S(1)}, u32[]{:S(2)}, u32[]{:S(2)}) collective-permute-start(bf16[128,512]{1,0:T(8,128)(2,1)S(1)} %collective-permute-done.1.refs_2_), channel_id=1, source_target_pairs={{0,1},{1,0},{2,3},{3,2},{4,5},{5,4},{6,7},{7,6},{8,9},{9,8},{10,11... | collective-permute-start | bytes 393224 | tf_op jit(solution)/shard_map/ppermute | solution.py:20
  11.9 1.5 %collective-permute-start.7 = (bf16[128,512]{1,0:T(8,128)(2,1)S(1)}, bf16[128,512]{1,0:T(8,128)(2,1)S(1)}, u32[]{:S(2)}, u32[]{:S(2)}) collective-permute-start(bf16[128,512]{1,0:T(8,128)(2,1)S(1)} %collective-permute-done.2.refs_6_), channel_id=1, source_target_pairs={{0,1},{1,0},{2,3},{3,2},{4,5},{5,4},{6,7},{7,6},{8,9},{9,8},{10,11... | collective-permute-start | bytes 393224 | tf_op jit(solution)/shard_map/ppermute | solution.py:20
  13.5 6.6 %copy-start.3 = (bf16[768,512]{1,0:T(8,128)(2,1)S(1)}, bf16[768,512]{1,0:T(8,128)(2,1)}, u32[]{:S(2)}) copy-start(bf16[768,512]{1,0:T(8,128)(2,1)} %get-tuple-element.24.refs_0_) | copy-start | bytes 2359300
  13.5 15.3 %copy-start = (bf16[640,512]{1,0:T(8,128)(2,1)S(1)}, bf16[640,512]{1,0:T(8,128)(2,1)}, u32[]{:S(2)}) copy-start(bf16[640,512]{1,0:T(8,128)(2,1)} %get-tuple-element.15.refs_0_.refs_4_) | copy-start | bytes 1966084
  13.5 19.3 %copy-start.2 = (bf16[128,512]{1,0:T(8,128)(2,1)S(1)}, bf16[128,512]{1,0:T(8,128)(2,1)}, u32[]{:S(2)}) copy-start(bf16[128,512]{1,0:T(8,128)(2,1)} %lat_ref.5) | copy-start | bytes 393220
  15.8 12.9 %collective-permute-start.8 = (bf16[128,512]{1,0:T(8,128)(2,1)S(1)}, bf16[128,512]{1,0:T(8,128)(2,1)S(1)}, u32[]{:S(2)}, u32[]{:S(2)}) collective-permute-start(bf16[128,512]{1,0:T(8,128)(2,1)S(1)} %get-tuple-element.16), channel_id=1, source_target_pairs={{0,8},{4,12},{8,0},{12,4},{1,9},{5,13},{9,1},{13,5},{2,10},{6,14},... | collective-permute-start | bytes 393224 | tf_op jit(solution)/shard_map/ppermute | solution.py:35
  18.5 10.3 %collective-permute-start.9 = (bf16[128,512]{1,0:T(8,128)(2,1)S(1)}, bf16[128,512]{1,0:T(8,128)(2,1)S(1)}, u32[]{:S(2)}, u32[]{:S(2)}) collective-permute-start(bf16[128,512]{1,0:T(8,128)(2,1)S(1)} %get-tuple-element.17), channel_id=1, source_target_pairs={{0,12},{4,8},{8,4},{12,0},{1,13},{5,9},{9,5},{13,1},{2,14},{6,10},... | collective-permute-start | bytes 393224 | tf_op jit(solution)/shard_map/ppermute | solution.py:35
  19.8 9.7 %collective-permute-start.10 = (bf16[128,512]{1,0:T(8,128)(2,1)S(1)}, bf16[128,512]{1,0:T(8,128)(2,1)S(1)}, u32[]{:S(2)}, u32[]{:S(2)}) collective-permute-start(bf16[128,512]{1,0:T(8,128)(2,1)S(1)} %get-tuple-element.18), channel_id=1, source_target_pairs={{0,4},{4,0},{8,12},{12,8},{1,5},{5,1},{9,13},{13,9},{2,6},{6,2},{1... | collective-permute-start | bytes 393224 | tf_op jit(solution)/shard_map/ppermute | solution.py:35
  20.1 23.6 %collective-permute-start.15 = (bf16[768,512]{1,0:T(8,128)(2,1)S(1)}, bf16[768,512]{1,0:T(8,128)(2,1)S(1)}, u32[]{:S(2)}, u32[]{:S(2)}) collective-permute-start(bf16[768,512]{1,0:T(8,128)(2,1)S(1)} %copy-done.3), channel_id=1, source_target_pairs={{0,2},{2,0},{1,3},{3,1},{4,6},{6,4},{5,7},{7,5},{8,10},{10,8},{9,1... | collective-permute-start | bytes 2359304 | tf_op jit(solution)/shard_map/ppermute | solution.py:20
  28.8 2.1 %collective-permute-start = (bf16[640,512]{1,0:T(8,128)(2,1)S(1)}, bf16[640,512]{1,0:T(8,128)(2,1)S(1)}, u32[]{:S(2)}, u32[]{:S(2)}) collective-permute-start(bf16[640,512]{1,0:T(8,128)(2,1)S(1)} %copy-done), channel_id=1, source_target_pairs={{0,1},{1,0},{2,3},{3,2},{4,5},{5,4},{6,7},{7,6},{8,9},{9,8},{10,11... | collective-permute-start | bytes 1966088 | tf_op jit(solution)/shard_map/ppermute | solution.py:20
  29.5 3.2 %collective-permute-start.11 = (bf16[640,512]{1,0:T(8,128)(2,1)S(1)}, bf16[640,512]{1,0:T(8,128)(2,1)S(1)}, u32[]{:S(2)}, u32[]{:S(2)}) collective-permute-start(bf16[640,512]{1,0:T(8,128)(2,1)S(1)} %collective-permute-done.5.refs_2_.refs_6_), channel_id=1, source_target_pairs={{0,1},{1,0},{2,3},{3,2},{4,5},{5,4},{6,7},{7,6},{8,9},{9,8},{10,11... | collective-permute-start | bytes 1966088 | tf_op jit(solution)/shard_map/ppermute | solution.py:20
  29.5 14.3 %collective-permute-start.14 = (bf16[768,512]{1,0:T(8,128)(2,1)S(1)}, bf16[768,512]{1,0:T(8,128)(2,1)}, u32[]{:S(2)}, u32[]{:S(2)}) collective-permute-start(bf16[768,512]{1,0:T(8,128)(2,1)S(1)} %copy-done.3), channel_id=1, source_target_pairs={{0,1},{1,0},{2,3},{3,2},{4,5},{5,4},{6,7},{7,6},{8,9},{9,8},{10,11... | collective-permute-start | bytes 2359304 | tf_op jit(solution)/shard_map/ppermute | solution.py:20
  33.6 10.1 %collective-permute-start.12 = (bf16[64,512]{1,0:T(8,128)(2,1)S(1)}, bf16[64,512]{1,0:T(8,128)(2,1)S(1)}, u32[]{:S(2)}, u32[]{:S(2)}) collective-permute-start(bf16[64,512]{1,0:T(8,128)(2,1)S(1)} %get-tuple-element.21.tail_ref), channel_id=1, source_target_pairs={{0,4},{4,8},{8,12},{12,0},{1,5},{5,9},{9,13},{13,1},{2,6},{6,10},{... | collective-permute-start | bytes 196616 | tf_op jit(solution)/shard_map/ppermute | solution.py:20
  34.9 8.8 %copy-start.7 = (s32[128,6]{0,1:T(8,128)S(1)}, s32[128,6]{0,1:T(8,128)}, u32[]{:S(2)}) copy-start(s32[128,6]{0,1:T(8,128)} %param.19) | copy-start | bytes 9220
  34.9 8.8 %collective-permute-start.13 = (bf16[64,512]{1,0:T(8,128)(2,1)S(1)}, bf16[64,512]{1,0:T(8,128)(2,1)S(1)}, u32[]{:S(2)}, u32[]{:S(2)}) collective-permute-start(bf16[64,512]{1,0:T(8,128)(2,1)S(1)} %get-tuple-element.22.head_ref), channel_id=1, source_target_pairs={{0,12},{4,0},{8,4},{12,8},{1,13},{5,1},{9,5},{13,9},{2,14},{6,2},{... | collective-permute-start | bytes 196616 | tf_op jit(solution)/shard_map/ppermute | solution.py:20
  43.7 2.3 %collective-permute-start.16 = (bf16[768,512]{1,0:T(8,128)(2,1)S(1)}, bf16[768,512]{1,0:T(8,128)(2,1)S(1)}, u32[]{:S(2)}, u32[]{:S(2)}) collective-permute-start(bf16[768,512]{1,0:T(8,128)(2,1)S(1)} %collective-permute-done.15.refs_2_), channel_id=1, source_target_pairs={{0,1},{1,0},{2,3},{3,2},{4,5},{5,4},{6,7},{7,6},{8,9},{9,8},{10,11... | collective-permute-start | bytes 2359304 | tf_op jit(solution)/shard_map/ppermute | solution.py:20
  (2 other events, 2.9 us)

commit v10 on v9

--- a/solution.py
+++ b/solution.py
@@ -53,40 +53,57 @@
     )
 
 
-def place(pieces, start, rows, whole):
+def unpack(pieces, sizes, wanted):
     subs = lax.axis_size("sub")
     for index, piece in enumerate(pieces):
         owner = owner_of(index // subs, index % subs)
-        whole[pl.ds(pl.multiple_of(owner * rows, rows), rows)] = piece[start : start + rows]
-
-
-def unpack(pieces, sizes, wanted):
-    for at, whole in wanted.items():
-        place(pieces, sum(sizes[:at]), sizes[at], whole)
+        for at, whole in wanted.items():
+            rows, start = sizes[at], sum(sizes[:at])
+            whole[pl.ds(pl.multiple_of(owner * rows, rows), rows)] = piece[start : start + rows]
+
+
+def unpack_parts(pieces, wholes):
+    subs, groups = lax.axis_size("sub"), lax.axis_size("groups")
+    count = lax.axis_size("band") * subs
+    for index, piece in enumerate(pieces):
+        band_step, rest = divmod(index, groups * subs)
+        owner = owner_of(band_step + 1, rest % subs)
+        part = lax.rem(lax.axis_index("groups") + groups - rest // subs, groups)
+        begin = 0
+        for whole in wholes:
+            rows = whole.shape[0] // (count * groups)
+            into = pl.multiple_of((owner * groups + part) * rows, rows)
+            whole[pl.ds(into, rows)] = piece[begin : begin + rows]
+            begin += rows
 
 
 def pack_kernel(sets, *refs):
-    sources, outs = list(refs[: sum(sets)]), refs[sum(sets) :]
-    for out, amount in zip(outs, sets):
+    sources, outs = refs[: -len(sets)], refs[-len(sets) :]
+    group = lax.axis_index("groups")
+    for out, members in zip(outs, sets):
         start = 0
-        for _ in range(amount):
-            source = sources.pop(0)
-            out[start : start + source.shape[0]] = source[...]
-            start += source.shape[0]
-
-
-def pack(sets):
-    width = sets[0][0].shape[1]
+        for member, rows in members:
+            source = sources[member]
+            if rows < source.shape[0]:
+                out[start : start + rows] = source[pl.ds(pl.multiple_of(group * rows, rows), rows)]
+            else:
+                out[start : start + rows] = source[...]
+            start += rows
+
+
+def pack(weights, sets):
     return pl.pallas_call(
-        functools.partial(pack_kernel, [len(one) for one in sets]),
+        functools.partial(pack_kernel, sets),
         out_shape=[
-            jax.ShapeDtypeStruct((sum(weight.shape[0] for weight in one), width), jnp.bfloat16)
-            for one in sets
+            jax.ShapeDtypeStruct(
+                (sum(rows for _, rows in members), weights[0].shape[1]), jnp.bfloat16
+            )
+            for members in sets
         ],
-        in_specs=[VMEM] * sum(len(one) for one in sets),
+        in_specs=[VMEM] * len(weights),
         out_specs=[VMEM] * len(sets),
         name="pack",
-    )(*(weight for one in sets for weight in one))
+    )(*weights)
 
 
 def silu(values):
@@ -110,8 +127,8 @@
     outs = refs[2 * count : 2 * count + faces]
     w_in, w_hid, messages = refs[2 * count + faces :]
     rows = w_in.shape[0] // count
-    place(in_pieces, 0, rows, w_in)
-    place(hid_pieces, 0, rows, w_hid)
+    unpack(in_pieces, [rows], {0: w_in})
+    unpack(hid_pieces, [rows], {0: w_hid})
     block = 256
     for start in range(0, lat_ref.shape[0], block):
         here = pl.ds(start, block)
@@ -159,8 +176,11 @@
 
 
 def edge_kernel(sizes, nbr_ref, before_ref, head_ref, tail_ref, after_ref, *refs):
-    pieces, (out_ref, p_in, p_hid, u_in, u_hid) = refs[:-5], refs[-5:]
-    unpack(pieces, sizes, {0: p_in, 1: p_hid, 2: u_in, 3: u_hid})
+    pieces, wholes = refs[:-5], refs[-4:]
+    out_ref, (p_in, p_hid, u_in, u_hid) = refs[-5], wholes
+    subs = lax.axis_size("sub")
+    unpack(pieces[:subs], sizes, dict(enumerate(wholes)))
+    unpack_parts(pieces[subs:], wholes)
     rows, fanin = nbr_ref.shape
     width = head_ref.shape[1]
     mid = jnp.concatenate([head_ref[...], tail_ref[...]], axis=0)
@@ -225,15 +245,20 @@
             transcendentals=rows * width,
         )
 
-    sets = ((node_w1, node_w2, grid_w1, grid_w2), (proc_w1, proc_w2, upd_w1, upd_w2))
-    sizes = [[weight.shape[0] for weight in one] for one in sets]
+    weights = (node_w1, node_w2, grid_w1, grid_w2, proc_w1, proc_w2, upd_w1, upd_w2)
+    sizes = [weight.shape[0] for weight in weights]
+    groups = lax.axis_size("groups")
+    small = pl.CostEstimate(flops=1, bytes_accessed=1, transcendentals=0)
+    rows = list(enumerate(sizes))
+    halves = [(at, size // groups) for at, size in rows[4:]]
+    early, late, part = pack(weights, (rows[:4], rows[4:], halves))
     enc_far = [[shift(one, "band", step) for step in range(1, bands)] for one in (enc_w1, enc_w2)]
     enc_all = [
-        own_spread(one) + relay(far) for one, far in zip((enc_w1, enc_w2), enc_far)
+        own_spread(one) + relay(far, part) for one, far in zip((enc_w1, enc_w2), enc_far)
     ]
-    early, late = pack(sets)
-    early_sent = after(early, *enc_far[0], *enc_far[1], *enc_all[0][1:subs], *enc_all[1][1:subs])
-    early_far = [shift(early_sent, "band", step) for step in range(1, bands)]
+    own_enc = enc_all[0][1:subs] + enc_all[1][1:subs]
+    part_sent = after(part, *enc_far[0], *enc_far[1], *own_enc)
+    part_far = [shift(part_sent, "band", step) for step in range(1, bands)]
     early_near, late_near = own_spread(early), own_spread(late)
 
     me = lax.axis_index("face")
@@ -259,13 +284,18 @@
         cost_estimate=cost(grid_rows, 3 * width),
         name="encode",
     )(targets, grid_lat, *enc_all[0], *enc_all[1])
-    late_sent = after(late, sums[0])
-    late_far = [shift(late_sent, "band", step) for step in range(1, bands)]
+    early_sent = after(early, sums[0])
+    early_far = [shift(early_sent, "band", step) for step in range(1, bands)]
     arrived = [sums[0]] + [to_face(sums[step], step) for step in steps[1:]]
-
-    early_all = early_near + relay(early_far, *arrived[1:])
+    parts, crossed = [], []
+    for one in part_far:
+        over = after(one, arrived[steps.index(1)])
+        others = [shift(over, "groups", step) for step in range(1, groups)]
+        parts += [one] + others
+        crossed += others
+    early_all = early_near + relay(early_far, *arrived[1:], *crossed)
     grid_out = pl.pallas_call(
-        functools.partial(grid_kernel, sizes[0]),
+        functools.partial(grid_kernel, sizes[:4]),
         out_shape=jax.ShapeDtypeStruct(grid_lat.shape, bf16),
         in_specs=[VMEM] + [VMEM] * len(early_all),
         out_specs=VMEM,
@@ -277,7 +307,7 @@
 
     half = (mesh_rows // 2, width)
     head, tail = pl.pallas_call(
-        functools.partial(node_kernel, sizes[0], faces),
+        functools.partial(node_kernel, sizes[:4], faces),
         out_shape=[jax.ShapeDtypeStruct(half, bf16)] * 2,
         in_specs=[VMEM] * (1 + faces) + [VMEM] * len(early_all),
         out_specs=[VMEM] * 2,
@@ -289,9 +319,9 @@
 
     before = shift(tail, "face", 1)
     behind = shift(head, "face", faces - 1)
-    late_all = late_near + relay(late_far, before, behind, grid_out)
+    late_all = late_near + relay(parts, head)
     mesh_out = pl.pallas_call(
-        functools.partial(edge_kernel, sizes[1]),
+        functools.partial(edge_kernel, sizes[4:]),
         out_shape=jax.ShapeDtypeStruct(mesh_lat.shape, bf16),
         in_specs=[VMEM] * 5 + [VMEM] * len(late_all),
         out_specs=VMEM,

time: 50.3 us -> 56.1 us (1.12)
  starting transfers between devices: 14.9 us -> 19.8 us
  local copies, waits for them, and re-layouts: 0.31 us -> 2.01 us
  waiting for transfers between devices: 21.3 us -> 19.8 us
  Pallas kernels: 12.8 us -> 13.5 us
    ppermute x14 -> x16, waiting for transfers between devices: 12.4 us -> 8.63 us  [shift(): lax.ppermute(value, axis, [(i, (i + step) % count) for i in range(count)])]
    ppermute x14 -> x16, starting transfers between devices: 10.7 us -> 14.3 us  [shift(): lax.ppermute(value, axis, [(i, (i + step) % count) for i in range(count)])]
    ppermute x3, waiting for transfers between devices: 8.91 us -> 11.2 us  [to_face(): lax.ppermute(value, 'face', [(i, face_at(faces, step, i)) for i in range(...]
    unnamed x19 -> x25, local copies, waits for them, and re-layouts: 0.31 us -> 2.01 us
    ppermute x3, starting transfers between devices: 4.24 us -> 5.51 us  [to_face(): lax.ppermute(value, 'face', [(i, face_at(faces, step, i)) for i in range(...]
    pallas_call x4, Pallas kernels: 10.5 us -> 11.2 us  [the longest x1 4.63 us: shards(): pl.pallas_call(functools.partial(edge_kernel, sizes[4:]), out_shape=jax.S...]
  transfers between devices with their start and end apart: 17 -> 19, of which waited for: 10 -> 7; matrix products, arithmetic and copies ran while one was open for 0% -> 0% of each run, Pallas kernels for 17% -> 16%
where the time goes in v10:
time: 56.1 us; the launch traced here: 55.9 us
  starting transfers between devices  19.8 us (35%)
  waiting for transfers between devices  19.8 us (35%)
  Pallas kernels  13.5 us (24%)
  local copies, waits for them, and re-layouts  2.01 us (4%)
  between operations  0.81 us (1%)
    ppermute x16, starting transfers between devices, shift(): lax.ppermute(value, axis, [(i, (i + step) % count) for i in range(count)])  14.3 us
    ppermute x3, waiting for transfers between devices, to_face(): lax.ppermute(value, 'face', [(i, face_at(faces, step, i)) for i in range(...  11.2 us
    ppermute x16, waiting for transfers between devices, shift(): lax.ppermute(value, axis, [(i, (i + step) % count) for i in range(count)])  8.63 us
    ppermute x3, starting transfers between devices, to_face(): lax.ppermute(value, 'face', [(i, face_at(faces, step, i)) for i in range(...  5.51 us
    pallas_call x1, Pallas kernels, shards(): pl.pallas_call(functools.partial(edge_kernel, sizes[4:]), out_shape=jax.S...  4.63 us
    pallas_call x1, Pallas kernels, shards(): pl.pallas_call(functools.partial(grid_kernel, sizes[:4]), out_shape=jax.S...  3.06 us
    pallas_call x1, Pallas kernels, pack(): pl.pallas_call(functools.partial(pack_kernel, sets), out_shape=[jax.Shape...  2.69 us
    pallas_call x1, Pallas kernels, shards(): pl.pallas_call(functools.partial(encode_kernel, count, faces, mesh_rows),...  2.31 us
  transfers between devices with their start and end apart: 19, of which 7 were waited for; matrix products, arithmetic and copies ran while one was open for 0% of the time, Pallas kernels for 16%

profile of v10, /device:TPU:0, one launch (start us, length us, event | category | flops | bytes accessed | tf_op | source)
XLA Modules:
  0.0 55.9 jit_solution(6052843783937535115)
XLA Ops:
  0.6 3.0 %collective-permute-start.5 = (bf16[128,512]{1,0:T(8,128)(2,1)}, bf16[128,512]{1,0:T(8,128)(2,1)S(1)}, u32[]{:S(2)}, u32[]{:S(2)}) collective-permute-start(bf16[128,512]{1,0:T(8,128)(2,1)} %refs_4_.3), channel_id=1, source_target_pairs={{0,2},{2,0},{1,3},{3,1},{4,6},{6,4},{5,7},{7,5},{8,10},{10,8},{9,1... | collective-permute-start | bytes 393224 | tf_op jit(solution)/shard_map/ppermute | solution.py:20
  3.7 0.5 collective-permute-start.4
  4.2 2.7 %pack.1 = (bf16[640,512]{1,0:T(8,128)(2,1)}, bf16[768,512]{1,0:T(8,128)(2,1)}, bf16[384,512]{1,0:T(8,128)(2,1)}) custom-call(bf16[256,512]{1,0:T(8,128)(2,1)} %refs_0_.2, bf16[128,512]{1,0:T(8,128)(2,1)} %refs_1_.1, bf16[128,512]{1,0:T(8,128)(2,1)} %refs_2_.1, bf16[128,512]{1,0:T(8,128)(2,1)} %refs_3_.1, bf16[256,512]{1,0:T(8,128)(2,1)} %refs_4_.2, ...), custom_call_target="tpu_custom_call" | custom-call | tf_op jit(solution)/shard_map/pack/pallas_call | solution.py:95
  6.9 1.3 %collective-permute-done.5.refs_6_ = bf16[128,512]{1,0:T(8,128)(2,1)S(1)} collective-permute-done((bf16[128,512]{1,0:T(8,128)(2,1)}, bf16[128,512]{1,0:T(8,128)(2,1)S(1)}, u32[]{:S(2)}, u32[]{:S(2)}) %collective-permute-start.5) | collective-permute-done | bytes 131104 | tf_op jit(solution)/shard_map/ppermute | solution.py:20
  8.2 2.0 %collective-permute-done.2.refs_2_ = bf16[128,512]{1,0:T(8,128)(2,1)S(1)} collective-permute-done((bf16[128,512]{1,0:T(8,128)(2,1)}, bf16[128,512]{1,0:T(8,128)(2,1)S(1)}, u32[]{:S(2)}, u32[]{:S(2)}) %collective-permute-start.2) | collective-permute-done | bytes 131104 | tf_op jit(solution)/shard_map/ppermute | solution.py:20
  10.2 0.5 collective-permute-start.6
  10.7 1.8 %collective-permute-start.11 = (bf16[384,512]{1,0:T(8,128)(2,1)}, bf16[384,512]{1,0:T(8,128)(2,1)}, u32[]{:S(2)}, u32[]{:S(2)}) collective-permute-start(bf16[384,512]{1,0:T(8,128)(2,1)} %get-tuple-element.28), channel_id=1, source_target_pairs={{0,2},{2,0},{1,3},{3,1},{4,6},{6,4},{5,7},{7,5},{8,10},{10,8},{9,1... | collective-permute-start | bytes 1179656 | tf_op jit(solution)/shard_map/ppermute | solution.py:20
  12.6 2.3 %encode.1 = (f32[128,512]{1,0:T(8,128)S(1)}, bf16[128,512]{1,0:T(8,128)(2,1)S(1)}, bf16[128,512]{1,0:T(8,128)(2,1)S(1)}, bf16[128,512]{1,0:T(8,128)(2,1)S(1)}) custom-call(s32[1,1024]{1,0:T(1,128)S(1)} %bitcast.2, bf16[1024,512]{1,0:T(8,128)(2,1)S(1)} %copy-done.1, bf16[128,512]{1,0:T(8,128)(2,1)S(1)} %copy-done.5, ...), custom_call_target="tpu_custom_call" | custom-call | flops 1610612736 | bytes 2621440 | tf_op jit(solution)/shard_map/encode/pallas_call | solution.py:271
  14.9 1.0 %collective-permute-start.7 = (bf16[640,512]{1,0:T(8,128)(2,1)S(1)}, bf16[640,512]{1,0:T(8,128)(2,1)S(1)}, u32[]{:S(2)}, u32[]{:S(2)}) collective-permute-start(bf16[640,512]{1,0:T(8,128)(2,1)S(1)} %copy-done), channel_id=1, source_target_pairs={{0,2},{2,0},{1,3},{3,1},{4,6},{6,4},{5,7},{7,5},{8,10},{10,8},{9,1... | collective-permute-start | bytes 1966088 | tf_op jit(solution)/shard_map/ppermute | solution.py:20
  15.9 1.6 %collective-permute-start.10 = (bf16[128,512]{1,0:T(8,128)(2,1)S(1)}, bf16[128,512]{1,0:T(8,128)(2,1)S(1)}, u32[]{:S(2)}, u32[]{:S(2)}) collective-permute-start(bf16[128,512]{1,0:T(8,128)(2,1)S(1)} %get-tuple-element.27), channel_id=1, source_target_pairs={{0,4},{4,0},{8,12},{12,8},{1,5},{5,1},{9,13},{13,9},{2,6},{6,2},{1... | collective-permute-start | bytes 393224 | tf_op jit(solution)/shard_map/ppermute | solution.py:35
  17.5 3.9 %collective-permute-done.10.refs_3_ = bf16[128,512]{1,0:T(8,128)(2,1)S(1)} collective-permute-done((bf16[128,512]{1,0:T(8,128)(2,1)S(1)}, bf16[128,512]{1,0:T(8,128)(2,1)S(1)}, u32[]{:S(2)}, u32[]{:S(2)}) %collective-permute-start.10) | collective-permute-done | bytes 131104 | tf_op jit(solution)/shard_map/ppermute | solution.py:35
  21.3 1.8 %collective-permute-done.11.refs_2_ = bf16[384,512]{1,0:T(8,128)(2,1)} collective-permute-done((bf16[384,512]{1,0:T(8,128)(2,1)}, bf16[384,512]{1,0:T(8,128)(2,1)}, u32[]{:S(2)}, u32[]{:S(2)}) %collective-permute-start.11) | collective-permute-done | bytes 393248 | tf_op jit(solution)/shard_map/ppermute | solution.py:20
  23.1 1.8 %collective-permute-start.12 = (bf16[384,512]{1,0:T(8,128)(2,1)}, bf16[384,512]{1,0:T(8,128)(2,1)}, u32[]{:S(2)}, u32[]{:S(2)}) collective-permute-start(bf16[384,512]{1,0:T(8,128)(2,1)} %collective-permute-done.11.refs_2_), channel_id=1, source_target_pairs={{0,16},{16,0},{1,17},{17,1},{2,18},{18,2},{3,19},{19,3},{4,20},{20... | collective-permute-start | bytes 1179656 | tf_op jit(solution)/shard_map/ppermute | solution.py:20
  24.9 2.6 %collective-permute-start.8 = (bf16[128,512]{1,0:T(8,128)(2,1)S(1)}, bf16[128,512]{1,0:T(8,128)(2,1)S(1)}, u32[]{:S(2)}, u32[]{:S(2)}) collective-permute-start(bf16[128,512]{1,0:T(8,128)(2,1)S(1)} %get-tuple-element.25), channel_id=1, source_target_pairs={{0,8},{4,12},{8,0},{12,4},{1,9},{5,13},{9,1},{13,5},{2,10},{6,14},... | collective-permute-start | bytes 393224 | tf_op jit(solution)/shard_map/ppermute | solution.py:35
  27.5 1.3 %collective-permute-start.9 = (bf16[128,512]{1,0:T(8,128)(2,1)S(1)}, bf16[128,512]{1,0:T(8,128)(2,1)S(1)}, u32[]{:S(2)}, u32[]{:S(2)}) collective-permute-start(bf16[128,512]{1,0:T(8,128)(2,1)S(1)} %get-tuple-element.26), channel_id=1, source_target_pairs={{0,12},{4,8},{8,4},{12,0},{1,13},{5,9},{9,5},{13,1},{2,14},{6,10},... | collective-permute-start | bytes 393224 | tf_op jit(solution)/shard_map/ppermute | solution.py:35
  28.8 7.3 %collective-permute-done.8.refs_1_ = bf16[128,512]{1,0:T(8,128)(2,1)S(1)} collective-permute-done((bf16[128,512]{1,0:T(8,128)(2,1)S(1)}, bf16[128,512]{1,0:T(8,128)(2,1)S(1)}, u32[]{:S(2)}, u32[]{:S(2)}) %collective-permute-start.8) | collective-permute-done | bytes 131104 | tf_op jit(solution)/shard_map/ppermute | solution.py:35
  36.7 1.6 %collective-permute-done.13.refs_3_.refs_7_ = bf16[640,512]{1,0:T(8,128)(2,1)S(1)} collective-permute-done((bf16[640,512]{1,0:T(8,128)(2,1)S(1)}, bf16[640,512]{1,0:T(8,128)(2,1)S(1)}, u32[]{:S(2)}, u32[]{:S(2)}) %collective-permute-start.13) | collective-permute-done | bytes 655392 | tf_op jit(solution)/shard_map/ppermute | solution.py:20
  38.3 0.8 %node_update.1 = (bf16[64,512]{1,0:T(8,128)(2,1)S(1)}, bf16[64,512]{1,0:T(8,128)(2,1)S(1)}) custom-call(bf16[128,512]{1,0:T(8,128)(2,1)S(1)} %copy-done.3, f32[128,512]{1,0:T(8,128)S(1)} %get-tuple-element.23.refs_0_, bf16[128,512]{1,0:T(8,128)(2,1)S(1)} %collective-permute-done.8.refs_1_, bf16[128,512]{1,0:T(8,128)(2,1)S(1)} %collective-permute-done.9.refs_2_, ...), custom_call_target="tpu_custom_call" | custom-call | flops 201326592 | bytes 1703936 | tf_op jit(solution)/shard_map/node_update/pallas_call | solution.py:309
  39.1 0.6 %copy-done.7 = bf16[64,512]{1,0:T(8,128)(2,1)} copy-done((bf16[64,512]{1,0:T(8,128)(2,1)}, bf16[64,512]{1,0:T(8,128)(2,1)S(1)}, u32[]{:S(2)}) %copy-start.7) | copy-done | bytes 65560
  40.4 4.6 %collective-permute-start.15 = (bf16[64,512]{1,0:T(8,128)(2,1)S(1)}, bf16[64,512]{1,0:T(8,128)(2,1)S(1)}, u32[]{:S(2)}, u32[]{:S(2)}) collective-permute-start(bf16[64,512]{1,0:T(8,128)(2,1)S(1)} %get-tuple-element.32.head_ref), channel_id=1, source_target_pairs={{0,12},{4,0},{8,4},{12,8},{1,13},{5,1},{9,5},{13,9},{2,14},{6,2},{... | collective-permute-start | bytes 196616 | tf_op jit(solution)/shard_map/ppermute | solution.py:20
  45.0 1.2 %copy-done.2 = bf16[1024,512]{1,0:T(8,128)(2,1)S(1)} copy-done((bf16[1024,512]{1,0:T(8,128)(2,1)S(1)}, bf16[1024,512]{1,0:T(8,128)(2,1)}, u32[]{:S(2)}) %copy-start.2) | copy-done | bytes 1048600
  46.2 3.1 %grid_update.1 = bf16[1024,512]{1,0:T(8,128)(2,1)} custom-call(bf16[1024,512]{1,0:T(8,128)(2,1)S(1)} %copy-done.2, bf16[640,512]{1,0:T(8,128)(2,1)S(1)} %copy-done, bf16[640,512]{1,0:T(8,128)(2,1)S(1)} %collective-permute-done.refs_1_.refs_5_, bf16[640,512]{1,0:T(8,128)(2,1)S(1)} %collective-permute-done.7.refs_2_.refs_6_, ...), custom_call_target="tpu_custom_call" | custom-call | flops 1073741824 | bytes 2097152 | tf_op jit(solution)/shard_map/grid_update/pallas_call | solution.py:297
  49.3 2.0 %collective-permute-done.14.before_ref = bf16[64,512]{1,0:T(8,128)(2,1)S(1)} collective-permute-done((bf16[64,512]{1,0:T(8,128)(2,1)}, bf16[64,512]{1,0:T(8,128)(2,1)S(1)}, u32[]{:S(2)}, u32[]{:S(2)}) %collective-permute-start.14) | collective-permute-done | bytes 65568 | tf_op jit(solution)/shard_map/ppermute | solution.py:20
  51.3 4.6 %edge_update.1 = bf16[128,512]{1,0:T(8,128)(2,1)} custom-call(s32[128,6]{1,0:T(8,128)S(1)} %copy.17.nbr_ref, bf16[64,512]{1,0:T(8,128)(2,1)S(1)} %collective-permute-done.14.before_ref, bf16[64,512]{1,0:T(8,128)(2,1)S(1)} %get-tuple-element.32.head_ref, bf16[64,512]{1,0:T(8,128)(2,1)S(1)} %copy-done.8, ...), custom_call_target="tpu_custom_call" | custom-call | flops 1207959552 | bytes 2359296 | tf_op jit(solution)/shard_map/edge_update/pallas_call | solution.py:323
  (46 shorter events, 1.4 us)
Async XLA Ops:
  0.6 11.9 %copy-start.1 = (bf16[1024,512]{1,0:T(8,128)(2,1)S(1)}, bf16[1024,512]{1,0:T(8,128)(2,1)}, u32[]{:S(2)}) copy-start(bf16[1024,512]{1,0:T(8,128)(2,1)} %lat_ref.4) | copy-start | bytes 3145732
  0.6 7.5 %collective-permute-start.5 = (bf16[128,512]{1,0:T(8,128)(2,1)}, bf16[128,512]{1,0:T(8,128)(2,1)S(1)}, u32[]{:S(2)}, u32[]{:S(2)}) collective-permute-start(bf16[128,512]{1,0:T(8,128)(2,1)} %refs_4_.3), channel_id=1, source_target_pairs={{0,2},{2,0},{1,3},{3,1},{4,6},{6,4},{5,7},{7,5},{8,10},{10,8},{9,1... | collective-permute-start | bytes 393224 | tf_op jit(solution)/shard_map/ppermute | solution.py:20
  3.6 6.5 %collective-permute-start.2 = (bf16[128,512]{1,0:T(8,128)(2,1)}, bf16[128,512]{1,0:T(8,128)(2,1)S(1)}, u32[]{:S(2)}, u32[]{:S(2)}) collective-permute-start(bf16[128,512]{1,0:T(8,128)(2,1)} %refs_0_.3), channel_id=1, source_target_pairs={{0,2},{2,0},{1,3},{3,1},{4,6},{6,4},{5,7},{7,5},{8,10},{10,8},{9,1... | collective-permute-start | bytes 393224 | tf_op jit(solution)/shard_map/ppermute | solution.py:20
  3.7 7.0 %collective-permute-start.1 = (bf16[128,512]{1,0:T(8,128)(2,1)}, bf16[128,512]{1,0:T(8,128)(2,1)S(1)}, u32[]{:S(2)}, u32[]{:S(2)}) collective-permute-start(bf16[128,512]{1,0:T(8,128)(2,1)} %refs_0_.3), channel_id=1, source_target_pairs={{0,1},{1,0},{2,3},{3,2},{4,5},{5,4},{6,7},{7,6},{8,9},{9,8},{10,11... | collective-permute-start | bytes 393224 | tf_op jit(solution)/shard_map/ppermute | solution.py:20
  3.7 7.0 %collective-permute-start.4 = (bf16[128,512]{1,0:T(8,128)(2,1)}, bf16[128,512]{1,0:T(8,128)(2,1)S(1)}, u32[]{:S(2)}, u32[]{:S(2)}) collective-permute-start(bf16[128,512]{1,0:T(8,128)(2,1)} %refs_4_.3), channel_id=1, source_target_pairs={{0,1},{1,0},{2,3},{3,2},{4,5},{5,4},{6,7},{7,6},{8,9},{9,8},{10,11... | collective-permute-start | bytes 393224 | tf_op jit(solution)/shard_map/ppermute | solution.py:20
  4.2 8.3 %copy-start.5 = (bf16[128,512]{1,0:T(8,128)(2,1)S(1)}, bf16[128,512]{1,0:T(8,128)(2,1)}, u32[]{:S(2)}) copy-start(bf16[128,512]{1,0:T(8,128)(2,1)} %refs_0_.3) | copy-start | bytes 393220
  4.2 8.3 %copy-start.6 = (bf16[128,512]{1,0:T(8,128)(2,1)S(1)}, bf16[128,512]{1,0:T(8,128)(2,1)}, u32[]{:S(2)}) copy-start(bf16[128,512]{1,0:T(8,128)(2,1)} %refs_4_.3) | copy-start | bytes 393220
  10.2 2.4 %collective-permute-start.3 = (bf16[128,512]{1,0:T(8,128)(2,1)S(1)}, bf16[128,512]{1,0:T(8,128)(2,1)S(1)}, u32[]{:S(2)}, u32[]{:S(2)}) collective-permute-start(bf16[128,512]{1,0:T(8,128)(2,1)S(1)} %collective-permute-done.2.refs_2_), channel_id=1, source_target_pairs={{0,1},{1,0},{2,3},{3,2},{4,5},{5,4},{6,7},{7,6},{8,9},{9,8},{10,11... | collective-permute-start | bytes 393224 | tf_op jit(solution)/shard_map/ppermute | solution.py:20
  10.2 2.4 %collective-permute-start.6 = (bf16[128,512]{1,0:T(8,128)(2,1)S(1)}, bf16[128,512]{1,0:T(8,128)(2,1)S(1)}, u32[]{:S(2)}, u32[]{:S(2)}) collective-permute-start(bf16[128,512]{1,0:T(8,128)(2,1)S(1)} %collective-permute-done.5.refs_6_), channel_id=1, source_target_pairs={{0,1},{1,0},{2,3},{3,2},{4,5},{5,4},{6,7},{7,6},{8,9},{9,8},{10,11... | collective-permute-start | bytes 393224 | tf_op jit(solution)/shard_map/ppermute | solution.py:20
  10.7 12.4 %collective-permute-start.11 = (bf16[384,512]{1,0:T(8,128)(2,1)}, bf16[384,512]{1,0:T(8,128)(2,1)}, u32[]{:S(2)}, u32[]{:S(2)}) collective-permute-start(bf16[384,512]{1,0:T(8,128)(2,1)} %get-tuple-element.28), channel_id=1, source_target_pairs={{0,2},{2,0},{1,3},{3,1},{4,6},{6,4},{5,7},{7,5},{8,10},{10,8},{9,1... | collective-permute-start | bytes 1179656 | tf_op jit(solution)/shard_map/ppermute | solution.py:20
  12.6 23.6 %copy-start.4 = (bf16[768,512]{1,0:T(8,128)(2,1)S(1)}, bf16[768,512]{1,0:T(8,128)(2,1)}, u32[]{:S(2)}) copy-start(bf16[768,512]{1,0:T(8,128)(2,1)} %get-tuple-element.33.refs_0_) | copy-start | bytes 2359300
  12.6 25.7 %copy-start.3 = (bf16[128,512]{1,0:T(8,128)(2,1)S(1)}, bf16[128,512]{1,0:T(8,128)(2,1)}, u32[]{:S(2)}) copy-start(bf16[128,512]{1,0:T(8,128)(2,1)} %lat_ref.5) | copy-start | bytes 393220
  14.9 21.2 %collective-permute-start.7 = (bf16[640,512]{1,0:T(8,128)(2,1)S(1)}, bf16[640,512]{1,0:T(8,128)(2,1)S(1)}, u32[]{:S(2)}, u32[]{:S(2)}) collective-permute-start(bf16[640,512]{1,0:T(8,128)(2,1)S(1)} %copy-done), channel_id=1, source_target_pairs={{0,2},{2,0},{1,3},{3,1},{4,6},{6,4},{5,7},{7,5},{8,10},{10,8},{9,1... | collective-permute-start | bytes 1966088 | tf_op jit(solution)/shard_map/ppermute | solution.py:20
  15.9 5.4 %collective-permute-start.10 = (bf16[128,512]{1,0:T(8,128)(2,1)S(1)}, bf16[128,512]{1,0:T(8,128)(2,1)S(1)}, u32[]{:S(2)}, u32[]{:S(2)}) collective-permute-start(bf16[128,512]{1,0:T(8,128)(2,1)S(1)} %get-tuple-element.27), channel_id=1, source_target_pairs={{0,4},{4,0},{8,12},{12,8},{1,5},{5,1},{9,13},{13,9},{2,6},{6,2},{1... | collective-permute-start | bytes 393224 | tf_op jit(solution)/shard_map/ppermute | solution.py:35
  23.1 13.0 %collective-permute-start.12 = (bf16[384,512]{1,0:T(8,128)(2,1)}, bf16[384,512]{1,0:T(8,128)(2,1)}, u32[]{:S(2)}, u32[]{:S(2)}) collective-permute-start(bf16[384,512]{1,0:T(8,128)(2,1)} %collective-permute-done.11.refs_2_), channel_id=1, source_target_pairs={{0,16},{16,0},{1,17},{17,1},{2,18},{18,2},{3,19},{19,3},{4,20},{20... | collective-permute-start | bytes 1179656 | tf_op jit(solution)/shard_map/ppermute | solution.py:20
  24.9 11.2 %collective-permute-start.8 = (bf16[128,512]{1,0:T(8,128)(2,1)S(1)}, bf16[128,512]{1,0:T(8,128)(2,1)S(1)}, u32[]{:S(2)}, u32[]{:S(2)}) collective-permute-start(bf16[128,512]{1,0:T(8,128)(2,1)S(1)} %get-tuple-element.25), channel_id=1, source_target_pairs={{0,8},{4,12},{8,0},{12,4},{1,9},{5,13},{9,1},{13,5},{2,10},{6,14},... | collective-permute-start | bytes 393224 | tf_op jit(solution)/shard_map/ppermute | solution.py:35
  27.5 8.6 %collective-permute-start.9 = (bf16[128,512]{1,0:T(8,128)(2,1)S(1)}, bf16[128,512]{1,0:T(8,128)(2,1)S(1)}, u32[]{:S(2)}, u32[]{:S(2)}) collective-permute-start(bf16[128,512]{1,0:T(8,128)(2,1)S(1)} %get-tuple-element.26), channel_id=1, source_target_pairs={{0,12},{4,8},{8,4},{12,0},{1,13},{5,9},{9,5},{13,1},{2,14},{6,10},... | collective-permute-start | bytes 393224 | tf_op jit(solution)/shard_map/ppermute | solution.py:35
  28.8 7.9 %collective-permute-start = (bf16[640,512]{1,0:T(8,128)(2,1)S(1)}, bf16[640,512]{1,0:T(8,128)(2,1)S(1)}, u32[]{:S(2)}, u32[]{:S(2)}) collective-permute-start(bf16[640,512]{1,0:T(8,128)(2,1)S(1)} %copy-done), channel_id=1, source_target_pairs={{0,1},{1,0},{2,3},{3,2},{4,5},{5,4},{6,7},{7,6},{8,9},{9,8},{10,11... | collective-permute-start | bytes 1966088 | tf_op jit(solution)/shard_map/ppermute | solution.py:20
  36.1 2.2 %collective-permute-start.13 = (bf16[640,512]{1,0:T(8,128)(2,1)S(1)}, bf16[640,512]{1,0:T(8,128)(2,1)S(1)}, u32[]{:S(2)}, u32[]{:S(2)}) collective-permute-start(bf16[640,512]{1,0:T(8,128)(2,1)S(1)} %collective-permute-done.7.refs_2_.refs_6_), channel_id=1, source_target_pairs={{0,1},{1,0},{2,3},{3,2},{4,5},{5,4},{6,7},{7,6},{8,9},{9,8},{10,11... | collective-permute-start | bytes 1966088 | tf_op jit(solution)/shard_map/ppermute | solution.py:20
  36.2 13.1 %collective-permute-start.16 = (bf16[768,512]{1,0:T(8,128)(2,1)S(1)}, bf16[768,512]{1,0:T(8,128)(2,1)}, u32[]{:S(2)}, u32[]{:S(2)}) collective-permute-start(bf16[768,512]{1,0:T(8,128)(2,1)S(1)} %copy-done.4), channel_id=1, source_target_pairs={{0,1},{1,0},{2,3},{3,2},{4,5},{5,4},{6,7},{7,6},{8,9},{9,8},{10,11... | collective-permute-start | bytes 2359304 | tf_op jit(solution)/shard_map/ppermute | solution.py:20
  39.7 11.5 %collective-permute-start.17 = (bf16[384,512]{1,0:T(8,128)(2,1)}, bf16[384,512]{1,0:T(8,128)(2,1)}, u32[]{:S(2)}, u32[]{:S(2)}) collective-permute-start(bf16[384,512]{1,0:T(8,128)(2,1)} %collective-permute-done.11.refs_2_), channel_id=1, source_target_pairs={{0,1},{1,0},{2,3},{3,2},{4,5},{5,4},{6,7},{7,6},{8,9},{9,8},{10,11... | collective-permute-start | bytes 1179656 | tf_op jit(solution)/shard_map/ppermute | solution.py:20
  39.9 11.4 %collective-permute-start.18 = (bf16[384,512]{1,0:T(8,128)(2,1)}, bf16[384,512]{1,0:T(8,128)(2,1)}, u32[]{:S(2)}, u32[]{:S(2)}) collective-permute-start(bf16[384,512]{1,0:T(8,128)(2,1)} %collective-permute-done.12.refs_4_), channel_id=1, source_target_pairs={{0,1},{1,0},{2,3},{3,2},{4,5},{5,4},{6,7},{7,6},{8,9},{9,8},{10,11... | collective-permute-start | bytes 1179656 | tf_op jit(solution)/shard_map/ppermute | solution.py:20
  40.4 10.9 %collective-permute-start.15 = (bf16[64,512]{1,0:T(8,128)(2,1)S(1)}, bf16[64,512]{1,0:T(8,128)(2,1)S(1)}, u32[]{:S(2)}, u32[]{:S(2)}) collective-permute-start(bf16[64,512]{1,0:T(8,128)(2,1)S(1)} %get-tuple-element.32.head_ref), channel_id=1, source_target_pairs={{0,12},{4,0},{8,4},{12,8},{1,13},{5,1},{9,5},{13,9},{2,14},{6,2},{... | collective-permute-start | bytes 196616 | tf_op jit(solution)/shard_map/ppermute | solution.py:20
  45.0 6.3 %collective-permute-start.14 = (bf16[64,512]{1,0:T(8,128)(2,1)}, bf16[64,512]{1,0:T(8,128)(2,1)S(1)}, u32[]{:S(2)}, u32[]{:S(2)}) collective-permute-start(bf16[64,512]{1,0:T(8,128)(2,1)} %copy-done.7), channel_id=1, source_target_pairs={{0,4},{4,8},{8,12},{12,0},{1,5},{5,9},{9,13},{13,1},{2,6},{6,10},{... | collective-permute-start | bytes 196616 | tf_op jit(solution)/shard_map/ppermute | solution.py:20
  (7 other events, 20.2 us)

commit v11 on v9

--- a/solution.py
+++ b/solution.py
@@ -158,33 +158,45 @@
     tail_ref[...] = mid[half:]
 
 
-def edge_kernel(sizes, nbr_ref, before_ref, head_ref, tail_ref, after_ref, *refs):
-    pieces, (out_ref, p_in, p_hid, u_in, u_hid) = refs[:-5], refs[-5:]
-    unpack(pieces, sizes, {0: p_in, 1: p_hid, 2: u_in, 3: u_hid})
+def share(inputs_ref, piece, index, rows):
+    subs = lax.axis_size("sub")
+    start = pl.multiple_of(owner_of(index // subs, index % subs) * rows, rows)
+    return dot(inputs_ref[:, pl.ds(start, rows)], piece[:rows])
+
+
+def prepare_kernel(here, depth, nbr_ref, before_ref, head_ref, tail_ref, after_ref, *refs):
+    pieces, (inputs_ref, hidden_ref) = refs[:-2], refs[-2:]
     rows, fanin = nbr_ref.shape
     width = head_ref.shape[1]
     mid = jnp.concatenate([head_ref[...], tail_ref[...]], axis=0)
     extended = jnp.concatenate([before_ref[...], mid, after_ref[...]], axis=0)
     spots = lax.broadcasted_iota(jnp.int32, (rows, extended.shape[0]), 1)
     nbr = nbr_ref[...]
-    receivers = dot(mid, p_in[width:])
-    total = None
-    group = fanin
-    for at in range(0, fanin, group):
-        chosen = jnp.concatenate(
-            [
-                jnp.where(spots == nbr[:, k : k + 1], 1.0, 0.0).astype(jnp.bfloat16)
-                for k in range(at, at + group)
-            ],
-            axis=0,
-        )
-        senders = dot(chosen, extended).astype(jnp.bfloat16)
-        hidden = dot(senders, p_in[:width])
-        hidden = (hidden.reshape(group, rows, width) + receivers[None]).reshape(group * rows, width)
-        edges = layer_norm(dot(silu(hidden).astype(jnp.bfloat16), p_hid[...]))
-        for k in range(group):
-            one = edges[k * rows : (k + 1) * rows]
-            total = one if total is None else total + one
+    for k in range(fanin):
+        chosen = jnp.where(spots == nbr[:, k : k + 1], 1.0, 0.0).astype(jnp.bfloat16)
+        edges = pl.ds(k * rows, rows)
+        inputs_ref[edges, :width] = dot(chosen, extended).astype(jnp.bfloat16)
+        inputs_ref[edges, width:] = mid
+    hidden = None
+    for index, piece in zip(here, pieces):
+        one = share(inputs_ref, piece, index, depth)
+        hidden = one if hidden is None else hidden + one
+    hidden_ref[...] = hidden
+
+
+def edge_kernel(sizes, missing, head_ref, tail_ref, inputs_ref, hidden_ref, *refs):
+    pieces, (out_ref, p_hid, u_in, u_hid) = refs[:-4], refs[-4:]
+    unpack(pieces, sizes, {1: p_hid, 2: u_in, 3: u_hid})
+    width = head_ref.shape[1]
+    mid = jnp.concatenate([head_ref[...], tail_ref[...]], axis=0)
+    rows = mid.shape[0]
+    hidden = hidden_ref[...]
+    for index in missing:
+        hidden = hidden + share(inputs_ref, pieces[index], index, sizes[0])
+    edges = layer_norm(dot(silu(hidden).astype(jnp.bfloat16), p_hid[...]))
+    total = edges[:rows]
+    for start in range(rows, edges.shape[0], rows):
+        total = total + edges[start : start + rows]
     hidden = dot(mid, u_in[:width]) + dot(total.astype(jnp.bfloat16), u_in[width:])
     hidden = silu(hidden).astype(jnp.bfloat16)
     out = mid.astype(jnp.float32) + layer_norm(dot(hidden, u_hid[...]))
@@ -290,21 +302,31 @@
     before = shift(tail, "face", 1)
     behind = shift(head, "face", faces - 1)
     late_all = late_near + relay(late_far, before, behind, grid_out)
+    here = [at for at in range(count) if at < subs or at % subs == 0]
+    missing = [at for at in range(count) if at not in here]
+    edges = mesh_rows * mesh_nbr.shape[1]
+    inputs, hidden = pl.pallas_call(
+        functools.partial(prepare_kernel, here, proc_w1.shape[0]),
+        out_shape=[
+            jax.ShapeDtypeStruct((edges, 2 * width), bf16),
+            jax.ShapeDtypeStruct((edges, width), jnp.float32),
+        ],
+        in_specs=[VMEM] * (5 + len(here)),
+        out_specs=[VMEM] * 2,
+        compiler_params=pltpu.CompilerParams(vmem_limit_bytes=16 * MIB),
+        cost_estimate=cost(edges, 2 * width),
+        name="prepare",
+    )(mesh_nbr, before, head, tail, behind, *(late_all[at] for at in here))
     mesh_out = pl.pallas_call(
-        functools.partial(edge_kernel, sizes[1]),
+        functools.partial(edge_kernel, sizes[1], missing),
         out_shape=jax.ShapeDtypeStruct(mesh_lat.shape, bf16),
-        in_specs=[VMEM] * 5 + [VMEM] * len(late_all),
+        in_specs=[VMEM] * (4 + count),
         out_specs=VMEM,
-        scratch_shapes=[
-            matrix(proc_w1),
-            matrix(proc_w2),
-            matrix(upd_w1),
-            matrix(upd_w2),
-        ],
-        compiler_params=pltpu.CompilerParams(vmem_limit_bytes=16 * MIB),
-        cost_estimate=cost(mesh_rows * mesh_nbr.shape[1], 3 * width),
+        scratch_shapes=[matrix(proc_w2), matrix(upd_w1), matrix(upd_w2)],
+        compiler_params=pltpu.CompilerParams(vmem_limit_bytes=16 * MIB),
+        cost_estimate=cost(edges, 2 * width),
         name="edge_update",
-    )(mesh_nbr, before, head, tail, behind, *late_all)
+    )(head, tail, inputs, hidden, *late_all)
     return (grid_out, mesh_out)
 
 

time: 50.3 us -> 50.3 us (level)
  waiting for transfers between devices: 21.3 us -> 16.4 us
  local copies, waits for them, and re-layouts: 0.31 us -> 3.16 us
  other arithmetic: 0.01 us -> 1.38 us
  Pallas kernels: 12.8 us -> 13.4 us
    ppermute x14, waiting for transfers between devices: 12.4 us -> 6.64 us  [shift(): lax.ppermute(value, axis, [(i, (i + step) % count) for i in range(count)])]
    unnamed x19 -> x17, local copies, waits for them, and re-layouts: 0.31 us -> 3.16 us
    ppermute x3, waiting for transfers between devices: 8.91 us -> 9.72 us  [to_face(): lax.ppermute(value, 'face', [(i, face_at(faces, step, i)) for i in range(...]
    mul x1, other arithmetic: 0.01 us -> 0.69 us  [shards(): targets = (distance * mesh_rows + grid_slot).reshape(1, grid_rows)]
    add x1, other arithmetic: 0.01 us -> 0.69 us  [shards(): targets = (distance * mesh_rows + grid_slot).reshape(1, grid_rows)]
    pallas_call x1 -> x2, Pallas kernels: 4.15 us -> 4.69 us  [the longest x1 3.58 us: shards(): pl.pallas_call(functools.partial(edge_kernel, sizes[1], missing), out_sha...]
  transfers between devices with their start and end apart: 17 -> 17, of which waited for: 10 -> 7; matrix products, arithmetic and copies ran while one was open for 0% -> 3% of each run, Pallas kernels for 17% -> 20%
where the time goes in v11:
time: 50.3 us; the launch traced here: 50 us
  waiting for transfers between devices  16.4 us (33%)
  starting transfers between devices  15.1 us (30%)
  Pallas kernels  13.4 us (27%)
  local copies, waits for them, and re-layouts  3.16 us (6%)
  other arithmetic  1.38 us (3%)
  between operations  0.69 us (1%)
    ppermute x14, starting transfers between devices, shift(): lax.ppermute(value, axis, [(i, (i + step) % count) for i in range(count)])  10.6 us
    ppermute x3, waiting for transfers between devices, to_face(): lax.ppermute(value, 'face', [(i, face_at(faces, step, i)) for i in range(...  9.72 us
    ppermute x14, waiting for transfers between devices, shift(): lax.ppermute(value, axis, [(i, (i + step) % count) for i in range(count)])  6.64 us
    ppermute x3, starting transfers between devices, to_face(): lax.ppermute(value, 'face', [(i, face_at(faces, step, i)) for i in range(...  4.45 us
    pallas_call x1, Pallas kernels, shards(): pl.pallas_call(functools.partial(edge_kernel, sizes[1], missing), out_sha...  3.58 us
    unnamed x17, local copies, waits for them, and re-layouts  3.16 us
    pallas_call x1, Pallas kernels, shards(): pl.pallas_call(functools.partial(grid_kernel, sizes[0]), out_shape=jax.Sh...  3.06 us
    pallas_call x1, Pallas kernels, pack(): pl.pallas_call(functools.partial(pack_kernel, [len(one) for one in sets])...  2.51 us
  transfers between devices with their start and end apart: 17, of which 7 were waited for; matrix products, arithmetic and copies ran while one was open for 3% of the time, Pallas kernels for 20%

profile of v11, /device:TPU:0, one launch (start us, length us, event | category | flops | bytes accessed | tf_op | source)
XLA Modules:
  0.0 50.0 jit_solution(6895081644862142911)
XLA Ops:
  0.6 3.0 %collective-permute-start.1 = (bf16[128,512]{1,0:T(8,128)(2,1)}, bf16[128,512]{1,0:T(8,128)(2,1)S(1)}, u32[]{:S(2)}, u32[]{:S(2)}) collective-permute-start(bf16[128,512]{1,0:T(8,128)(2,1)} %refs_0_.3), channel_id=1, source_target_pairs={{0,2},{2,0},{1,3},{3,1},{4,6},{6,4},{5,7},{7,5},{8,10},{10,8},{9,1... | collective-permute-start | bytes 393224 | tf_op jit(solution)/shard_map/ppermute | solution.py:20
  4.2 2.5 %pack.1 = (bf16[640,512]{1,0:T(8,128)(2,1)}, bf16[768,512]{1,0:T(8,128)(2,1)}) custom-call(bf16[256,512]{1,0:T(8,128)(2,1)} %refs_0_.2, bf16[128,512]{1,0:T(8,128)(2,1)} %refs_1_.1, bf16[128,512]{1,0:T(8,128)(2,1)} %refs_2_.1, bf16[128,512]{1,0:T(8,128)(2,1)} %refs_3_.1, bf16[256,512]{1,0:T(8,128)(2,1)} %refs_4_.2, bf16[128,512]{1,0:T(8,128)(2,1)} %refs_5_.1, ...), custom_call_target="tpu_custom_call" | custom-call | tf_op jit(solution)/shard_map/pack/pallas_call | solution.py:80
  6.7 1.4 %collective-permute-done.1.refs_2_ = bf16[128,512]{1,0:T(8,128)(2,1)S(1)} collective-permute-done((bf16[128,512]{1,0:T(8,128)(2,1)}, bf16[128,512]{1,0:T(8,128)(2,1)S(1)}, u32[]{:S(2)}, u32[]{:S(2)}) %collective-permute-start.1) | collective-permute-done | bytes 131104 | tf_op jit(solution)/shard_map/ppermute | solution.py:20
  8.2 2.0 %collective-permute-done.2.refs_6_ = bf16[128,512]{1,0:T(8,128)(2,1)S(1)} collective-permute-done((bf16[128,512]{1,0:T(8,128)(2,1)}, bf16[128,512]{1,0:T(8,128)(2,1)S(1)}, u32[]{:S(2)}, u32[]{:S(2)}) %collective-permute-start.2) | collective-permute-done | bytes 131104 | tf_op jit(solution)/shard_map/ppermute | solution.py:20
  10.2 1.7 %collective-permute-start.5 = (bf16[640,512]{1,0:T(8,128)(2,1)}, bf16[640,512]{1,0:T(8,128)(2,1)S(1)}, u32[]{:S(2)}, u32[]{:S(2)}) collective-permute-start(bf16[640,512]{1,0:T(8,128)(2,1)} %get-tuple-element.17.refs_0_.refs_4_), channel_id=1, source_target_pairs={{0,2},{2,0},{1,3},{3,1},{4,6},{6,4},{5,7},{7,5},{8,10},{10,8},{9,1... | collective-permute-start | bytes 1966088 | tf_op jit(solution)/shard_map/ppermute | solution.py:20
  11.9 0.5 %collective-permute-start.7 = (bf16[128,512]{1,0:T(8,128)(2,1)S(1)}, bf16[128,512]{1,0:T(8,128)(2,1)S(1)}, u32[]{:S(2)}, u32[]{:S(2)}) collective-permute-start(bf16[128,512]{1,0:T(8,128)(2,1)S(1)} %collective-permute-done.2.refs_6_), channel_id=1, source_target_pairs={{0,1},{1,0},{2,3},{3,2},{4,5},{5,4},{6,7},{7,6},{8,9},{9,8},{10,11... | collective-permute-start | bytes 393224 | tf_op jit(solution)/shard_map/ppermute | solution.py:20
  12.4 0.7 %xor_multiply_fusion = s32[1024,1]{0,1:T(1,128)S(1)} fusion(s32[1024,1]{0,1:T(1,128)} %param.16, s32[]{:T(128)S(6)} %axis_index.15), kind=kLoop, calls=%fused_computation | loop fusion | flops 2048 | bytes 8196 | tf_op jit(solution)/shard_map/mul | solution.py:255
  13.1 0.7 %add.3 = s32[1024]{0:T(1024)S(1)} add(s32[1024]{0:T(1024)S(1)} %bitcast.3, s32[1024]{0:T(1024)} %param.17) | non-fusion elementwise | flops 1024 | bytes 12288 | tf_op jit(solution)/shard_map/add | solution.py:255
  13.8 1.2 %copy-done.1 = bf16[1024,512]{1,0:T(8,128)(2,1)S(1)} copy-done((bf16[1024,512]{1,0:T(8,128)(2,1)S(1)}, bf16[1024,512]{1,0:T(8,128)(2,1)}, u32[]{:S(2)}) %copy-start.1) | copy-done | bytes 1048600
  15.0 0.9 %copy-done.5 = bf16[128,512]{1,0:T(8,128)(2,1)S(1)} copy-done((bf16[128,512]{1,0:T(8,128)(2,1)S(1)}, bf16[128,512]{1,0:T(8,128)(2,1)}, u32[]{:S(2)}) %copy-start.5) | copy-done | bytes 131096
  15.9 0.9 %copy-done.6 = bf16[128,512]{1,0:T(8,128)(2,1)S(1)} copy-done((bf16[128,512]{1,0:T(8,128)(2,1)S(1)}, bf16[128,512]{1,0:T(8,128)(2,1)}, u32[]{:S(2)}) %copy-start.6) | copy-done | bytes 131096
  16.8 2.3 %encode.1 = (f32[128,512]{1,0:T(8,128)S(1)}, bf16[128,512]{1,0:T(8,128)(2,1)S(1)}, bf16[128,512]{1,0:T(8,128)(2,1)S(1)}, bf16[128,512]{1,0:T(8,128)(2,1)S(1)}) custom-call(s32[1,1024]{1,0:T(1,128)S(1)} %bitcast.2, bf16[1024,512]{1,0:T(8,128)(2,1)S(1)} %copy-done.1, bf16[128,512]{1,0:T(8,128)(2,1)S(1)} %copy-done.5, ...), custom_call_target="tpu_custom_call" | custom-call | flops 1610612736 | bytes 2621440 | tf_op jit(solution)/shard_map/encode/pallas_call | solution.py:258
  19.2 1.6 %collective-permute-start.10 = (bf16[128,512]{1,0:T(8,128)(2,1)S(1)}, bf16[128,512]{1,0:T(8,128)(2,1)S(1)}, u32[]{:S(2)}, u32[]{:S(2)}) collective-permute-start(bf16[128,512]{1,0:T(8,128)(2,1)S(1)} %get-tuple-element.20), channel_id=1, source_target_pairs={{0,4},{4,0},{8,12},{12,8},{1,5},{5,1},{9,13},{13,9},{2,6},{6,2},{1... | collective-permute-start | bytes 393224 | tf_op jit(solution)/shard_map/ppermute | solution.py:35
  20.8 2.6 %collective-permute-start.8 = (bf16[128,512]{1,0:T(8,128)(2,1)S(1)}, bf16[128,512]{1,0:T(8,128)(2,1)S(1)}, u32[]{:S(2)}, u32[]{:S(2)}) collective-permute-start(bf16[128,512]{1,0:T(8,128)(2,1)S(1)} %get-tuple-element.18), channel_id=1, source_target_pairs={{0,8},{4,12},{8,0},{12,4},{1,9},{5,13},{9,1},{13,5},{2,10},{6,14},... | collective-permute-start | bytes 393224 | tf_op jit(solution)/shard_map/ppermute | solution.py:35
  24.0 2.4 %collective-permute-done.10.refs_3_ = bf16[128,512]{1,0:T(8,128)(2,1)S(1)} collective-permute-done((bf16[128,512]{1,0:T(8,128)(2,1)S(1)}, bf16[128,512]{1,0:T(8,128)(2,1)S(1)}, u32[]{:S(2)}, u32[]{:S(2)}) %collective-permute-start.10) | collective-permute-done | bytes 131104 | tf_op jit(solution)/shard_map/ppermute | solution.py:35
  26.4 7.3 %collective-permute-done.8.refs_1_ = bf16[128,512]{1,0:T(8,128)(2,1)S(1)} collective-permute-done((bf16[128,512]{1,0:T(8,128)(2,1)S(1)}, bf16[128,512]{1,0:T(8,128)(2,1)S(1)}, u32[]{:S(2)}, u32[]{:S(2)}) %collective-permute-start.8) | collective-permute-done | bytes 131104 | tf_op jit(solution)/shard_map/ppermute | solution.py:35
  34.2 1.6 %collective-permute-done.11.refs_3_.refs_7_ = bf16[640,512]{1,0:T(8,128)(2,1)S(1)} collective-permute-done((bf16[640,512]{1,0:T(8,128)(2,1)S(1)}, bf16[640,512]{1,0:T(8,128)(2,1)S(1)}, u32[]{:S(2)}, u32[]{:S(2)}) %collective-permute-start.11) | collective-permute-done | bytes 655392 | tf_op jit(solution)/shard_map/ppermute | solution.py:20
  35.8 0.8 %node_update.1 = (bf16[64,512]{1,0:T(8,128)(2,1)S(1)}, bf16[64,512]{1,0:T(8,128)(2,1)S(1)}) custom-call(bf16[128,512]{1,0:T(8,128)(2,1)S(1)} %copy-done.4, f32[128,512]{1,0:T(8,128)S(1)} %get-tuple-element.22.refs_0_, bf16[128,512]{1,0:T(8,128)(2,1)S(1)} %collective-permute-done.8.refs_1_, bf16[128,512]{1,0:T(8,128)(2,1)S(1)} %collective-permute-done.9.refs_2_, ...), custom_call_target="tpu_custom_call" | custom-call | flops 201326592 | bytes 1703936 | tf_op jit(solution)/shard_map/node_update/pallas_call | solution.py:291
  36.6 2.2 %collective-permute-start.12 = (bf16[64,512]{1,0:T(8,128)(2,1)S(1)}, bf16[64,512]{1,0:T(8,128)(2,1)S(1)}, u32[]{:S(2)}, u32[]{:S(2)}) collective-permute-start(bf16[64,512]{1,0:T(8,128)(2,1)S(1)} %get-tuple-element.24.tail_ref), channel_id=1, source_target_pairs={{0,4},{4,8},{8,12},{12,0},{1,5},{5,9},{9,13},{13,1},{2,6},{6,10},{... | collective-permute-start | bytes 196616 | tf_op jit(solution)/shard_map/ppermute | solution.py:20
  38.8 1.7 %collective-permute-start.13 = (bf16[64,512]{1,0:T(8,128)(2,1)S(1)}, bf16[64,512]{1,0:T(8,128)(2,1)S(1)}, u32[]{:S(2)}, u32[]{:S(2)}) collective-permute-start(bf16[64,512]{1,0:T(8,128)(2,1)S(1)} %get-tuple-element.23.head_ref), channel_id=1, source_target_pairs={{0,12},{4,0},{8,4},{12,8},{1,13},{5,1},{9,5},{13,9},{2,14},{6,2},{... | collective-permute-start | bytes 196616 | tf_op jit(solution)/shard_map/ppermute | solution.py:20
  40.5 3.1 %grid_update.1 = bf16[1024,512]{1,0:T(8,128)(2,1)} custom-call(bf16[1024,512]{1,0:T(8,128)(2,1)S(1)} %copy-done.2, bf16[640,512]{1,0:T(8,128)(2,1)S(1)} %copy-done, bf16[640,512]{1,0:T(8,128)(2,1)S(1)} %collective-permute-done.refs_1_.refs_5_, bf16[640,512]{1,0:T(8,128)(2,1)S(1)} %collective-permute-done.5.refs_2_.refs_6_, ...), custom_call_target="tpu_custom_call" | custom-call | flops 1073741824 | bytes 2097152 | tf_op jit(solution)/shard_map/grid_update/pallas_call | solution.py:279
  44.1 1.1 %prepare.1 = (bf16[768,1024]{1,0:T(8,128)(2,1)S(1)}, f32[768,512]{1,0:T(8,128)S(1)}) custom-call(s32[128,6]{1,0:T(8,128)S(1)} %copy.17.nbr_ref, bf16[64,512]{1,0:T(8,128)(2,1)S(1)} %collective-permute-done.12.before_ref, bf16[64,512]{1,0:T(8,128)(2,1)S(1)} %get-tuple-element.23.head_ref, bf16[64,512]{1,0:T(8,128)(2,1)S(1)} %get-tuple-element.24.tail_ref, ...), custom_call_target="tpu_custom_call" | custom-call | flops 805306368 | bytes 1835008 | tf_op jit(solution)/shard_map/prepare/pallas_call | solution.py:308
  45.3 1.2 %collective-permute-done.16.refs_3_ = bf16[768,512]{1,0:T(8,128)(2,1)} collective-permute-done((bf16[768,512]{1,0:T(8,128)(2,1)S(1)}, bf16[768,512]{1,0:T(8,128)(2,1)}, u32[]{:S(2)}, u32[]{:S(2)}) %collective-permute-start.16) | collective-permute-done | bytes 786464 | tf_op jit(solution)/shard_map/ppermute | solution.py:20
  46.4 3.6 %edge_update.1 = bf16[128,512]{1,0:T(8,128)(2,1)} custom-call(bf16[64,512]{1,0:T(8,128)(2,1)S(1)} %get-tuple-element.23.head_ref, bf16[64,512]{1,0:T(8,128)(2,1)S(1)} %get-tuple-element.24.tail_ref, bf16[768,1024]{1,0:T(8,128)(2,1)S(1)} %get-tuple-element.28.inputs_ref, f32[768,512]{1,0:T(8,128)S(1)} %get-tuple-element.29.hidden_ref, ...), custom_call_target="tpu_custom_call" | custom-call | flops 805306368 | bytes 1835008 | tf_op jit(solution)/shard_map/edge_update/pallas_call | solution.py:320
  (35 shorter events, 2.3 us)
Async XLA Ops:
  0.6 7.5 %collective-permute-start.1 = (bf16[128,512]{1,0:T(8,128)(2,1)}, bf16[128,512]{1,0:T(8,128)(2,1)S(1)}, u32[]{:S(2)}, u32[]{:S(2)}) collective-permute-start(bf16[128,512]{1,0:T(8,128)(2,1)} %refs_0_.3), channel_id=1, source_target_pairs={{0,2},{2,0},{1,3},{3,1},{4,6},{6,4},{5,7},{7,5},{8,10},{10,8},{9,1... | collective-permute-start | bytes 393224 | tf_op jit(solution)/shard_map/ppermute | solution.py:20
  3.6 6.5 %collective-permute-start.2 = (bf16[128,512]{1,0:T(8,128)(2,1)}, bf16[128,512]{1,0:T(8,128)(2,1)S(1)}, u32[]{:S(2)}, u32[]{:S(2)}) collective-permute-start(bf16[128,512]{1,0:T(8,128)(2,1)} %refs_4_.3), channel_id=1, source_target_pairs={{0,2},{2,0},{1,3},{3,1},{4,6},{6,4},{5,7},{7,5},{8,10},{10,8},{9,1... | collective-permute-start | bytes 393224 | tf_op jit(solution)/shard_map/ppermute | solution.py:20
  3.7 6.4 %collective-permute-start.3 = (bf16[128,512]{1,0:T(8,128)(2,1)}, bf16[128,512]{1,0:T(8,128)(2,1)S(1)}, u32[]{:S(2)}, u32[]{:S(2)}) collective-permute-start(bf16[128,512]{1,0:T(8,128)(2,1)} %refs_0_.3), channel_id=1, source_target_pairs={{0,1},{1,0},{2,3},{3,2},{4,5},{5,4},{6,7},{7,6},{8,9},{9,8},{10,11... | collective-permute-start | bytes 393224 | tf_op jit(solution)/shard_map/ppermute | solution.py:20
  3.7 6.4 %collective-permute-start.4 = (bf16[128,512]{1,0:T(8,128)(2,1)}, bf16[128,512]{1,0:T(8,128)(2,1)S(1)}, u32[]{:S(2)}, u32[]{:S(2)}) collective-permute-start(bf16[128,512]{1,0:T(8,128)(2,1)} %refs_4_.3), channel_id=1, source_target_pairs={{0,1},{1,0},{2,3},{3,2},{4,5},{5,4},{6,7},{7,6},{8,9},{9,8},{10,11... | collective-permute-start | bytes 393224 | tf_op jit(solution)/shard_map/ppermute | solution.py:20
  10.2 23.6 %collective-permute-start.5 = (bf16[640,512]{1,0:T(8,128)(2,1)}, bf16[640,512]{1,0:T(8,128)(2,1)S(1)}, u32[]{:S(2)}, u32[]{:S(2)}) collective-permute-start(bf16[640,512]{1,0:T(8,128)(2,1)} %get-tuple-element.17.refs_0_.refs_4_), channel_id=1, source_target_pairs={{0,2},{2,0},{1,3},{3,1},{4,6},{6,4},{5,7},{7,5},{8,10},{10,8},{9,1... | collective-permute-start | bytes 1966088 | tf_op jit(solution)/shard_map/ppermute | solution.py:20
  11.9 1.9 %collective-permute-start.6 = (bf16[128,512]{1,0:T(8,128)(2,1)S(1)}, bf16[128,512]{1,0:T(8,128)(2,1)S(1)}, u32[]{:S(2)}, u32[]{:S(2)}) collective-permute-start(bf16[128,512]{1,0:T(8,128)(2,1)S(1)} %collective-permute-done.1.refs_2_), channel_id=1, source_target_pairs={{0,1},{1,0},{2,3},{3,2},{4,5},{5,4},{6,7},{7,6},{8,9},{9,8},{10,11... | collective-permute-start | bytes 393224 | tf_op jit(solution)/shard_map/ppermute | solution.py:20
  11.9 1.9 %collective-permute-start.7 = (bf16[128,512]{1,0:T(8,128)(2,1)S(1)}, bf16[128,512]{1,0:T(8,128)(2,1)S(1)}, u32[]{:S(2)}, u32[]{:S(2)}) collective-permute-start(bf16[128,512]{1,0:T(8,128)(2,1)S(1)} %collective-permute-done.2.refs_6_), channel_id=1, source_target_pairs={{0,1},{1,0},{2,3},{3,2},{4,5},{5,4},{6,7},{7,6},{8,9},{9,8},{10,11... | collective-permute-start | bytes 393224 | tf_op jit(solution)/shard_map/ppermute | solution.py:20
  13.8 1.2 %copy-start.1 = (bf16[1024,512]{1,0:T(8,128)(2,1)S(1)}, bf16[1024,512]{1,0:T(8,128)(2,1)}, u32[]{:S(2)}) copy-start(bf16[1024,512]{1,0:T(8,128)(2,1)} %lat_ref.4) | copy-start | bytes 3145732
  15.0 0.9 %copy-start.5 = (bf16[128,512]{1,0:T(8,128)(2,1)S(1)}, bf16[128,512]{1,0:T(8,128)(2,1)}, u32[]{:S(2)}) copy-start(bf16[128,512]{1,0:T(8,128)(2,1)} %refs_0_.3) | copy-start | bytes 393220
  16.8 6.8 %copy-start.3 = (bf16[768,512]{1,0:T(8,128)(2,1)S(1)}, bf16[768,512]{1,0:T(8,128)(2,1)}, u32[]{:S(2)}) copy-start(bf16[768,512]{1,0:T(8,128)(2,1)} %get-tuple-element.26.refs_0_) | copy-start | bytes 2359300
  16.8 9.6 %copy-start = (bf16[640,512]{1,0:T(8,128)(2,1)S(1)}, bf16[640,512]{1,0:T(8,128)(2,1)}, u32[]{:S(2)}) copy-start(bf16[640,512]{1,0:T(8,128)(2,1)} %get-tuple-element.17.refs_0_.refs_4_) | copy-start | bytes 1966084
  16.8 19.0 %copy-start.4 = (bf16[128,512]{1,0:T(8,128)(2,1)S(1)}, bf16[128,512]{1,0:T(8,128)(2,1)}, u32[]{:S(2)}) copy-start(bf16[128,512]{1,0:T(8,128)(2,1)} %lat_ref.5) | copy-start | bytes 393220
  19.2 7.2 %collective-permute-start.10 = (bf16[128,512]{1,0:T(8,128)(2,1)S(1)}, bf16[128,512]{1,0:T(8,128)(2,1)S(1)}, u32[]{:S(2)}, u32[]{:S(2)}) collective-permute-start(bf16[128,512]{1,0:T(8,128)(2,1)S(1)} %get-tuple-element.20), channel_id=1, source_target_pairs={{0,4},{4,0},{8,12},{12,8},{1,5},{5,1},{9,13},{13,9},{2,6},{6,2},{1... | collective-permute-start | bytes 393224 | tf_op jit(solution)/shard_map/ppermute | solution.py:35
  20.8 12.9 %collective-permute-start.8 = (bf16[128,512]{1,0:T(8,128)(2,1)S(1)}, bf16[128,512]{1,0:T(8,128)(2,1)S(1)}, u32[]{:S(2)}, u32[]{:S(2)}) collective-permute-start(bf16[128,512]{1,0:T(8,128)(2,1)S(1)} %get-tuple-element.18), channel_id=1, source_target_pairs={{0,8},{4,12},{8,0},{12,4},{1,9},{5,13},{9,1},{13,5},{2,10},{6,14},... | collective-permute-start | bytes 393224 | tf_op jit(solution)/shard_map/ppermute | solution.py:35
  23.4 10.3 %collective-permute-start.9 = (bf16[128,512]{1,0:T(8,128)(2,1)S(1)}, bf16[128,512]{1,0:T(8,128)(2,1)S(1)}, u32[]{:S(2)}, u32[]{:S(2)}) collective-permute-start(bf16[128,512]{1,0:T(8,128)(2,1)S(1)} %get-tuple-element.19), channel_id=1, source_target_pairs={{0,12},{4,8},{8,4},{12,0},{1,13},{5,9},{9,5},{13,1},{2,14},{6,10},... | collective-permute-start | bytes 393224 | tf_op jit(solution)/shard_map/ppermute | solution.py:35
  23.6 16.9 %copy-start.2 = (bf16[1024,512]{1,0:T(8,128)(2,1)S(1)}, bf16[1024,512]{1,0:T(8,128)(2,1)}, u32[]{:S(2)}) copy-start(bf16[1024,512]{1,0:T(8,128)(2,1)} %lat_ref.4) | copy-start | bytes 3145732
  23.6 20.0 %collective-permute-start.15 = (bf16[768,512]{1,0:T(8,128)(2,1)S(1)}, bf16[768,512]{1,0:T(8,128)(2,1)S(1)}, u32[]{:S(2)}, u32[]{:S(2)}) collective-permute-start(bf16[768,512]{1,0:T(8,128)(2,1)S(1)} %copy-done.3), channel_id=1, source_target_pairs={{0,2},{2,0},{1,3},{3,1},{4,6},{6,4},{5,7},{7,5},{8,10},{10,8},{9,1... | collective-permute-start | bytes 2359304 | tf_op jit(solution)/shard_map/ppermute | solution.py:20
  26.4 7.8 %collective-permute-start = (bf16[640,512]{1,0:T(8,128)(2,1)S(1)}, bf16[640,512]{1,0:T(8,128)(2,1)S(1)}, u32[]{:S(2)}, u32[]{:S(2)}) collective-permute-start(bf16[640,512]{1,0:T(8,128)(2,1)S(1)} %copy-done), channel_id=1, source_target_pairs={{0,1},{1,0},{2,3},{3,2},{4,5},{5,4},{6,7},{7,6},{8,9},{9,8},{10,11... | collective-permute-start | bytes 1966088 | tf_op jit(solution)/shard_map/ppermute | solution.py:20
  33.7 2.1 %collective-permute-start.11 = (bf16[640,512]{1,0:T(8,128)(2,1)S(1)}, bf16[640,512]{1,0:T(8,128)(2,1)S(1)}, u32[]{:S(2)}, u32[]{:S(2)}) collective-permute-start(bf16[640,512]{1,0:T(8,128)(2,1)S(1)} %collective-permute-done.5.refs_2_.refs_6_), channel_id=1, source_target_pairs={{0,1},{1,0},{2,3},{3,2},{4,5},{5,4},{6,7},{7,6},{8,9},{9,8},{10,11... | collective-permute-start | bytes 1966088 | tf_op jit(solution)/shard_map/ppermute | solution.py:20
  33.7 10.4 %collective-permute-start.14 = (bf16[768,512]{1,0:T(8,128)(2,1)S(1)}, bf16[768,512]{1,0:T(8,128)(2,1)S(1)}, u32[]{:S(2)}, u32[]{:S(2)}) collective-permute-start(bf16[768,512]{1,0:T(8,128)(2,1)S(1)} %copy-done.3), channel_id=1, source_target_pairs={{0,1},{1,0},{2,3},{3,2},{4,5},{5,4},{6,7},{7,6},{8,9},{9,8},{10,11... | collective-permute-start | bytes 2359304 | tf_op jit(solution)/shard_map/ppermute | solution.py:20
  36.6 7.0 %collective-permute-start.12 = (bf16[64,512]{1,0:T(8,128)(2,1)S(1)}, bf16[64,512]{1,0:T(8,128)(2,1)S(1)}, u32[]{:S(2)}, u32[]{:S(2)}) collective-permute-start(bf16[64,512]{1,0:T(8,128)(2,1)S(1)} %get-tuple-element.24.tail_ref), channel_id=1, source_target_pairs={{0,4},{4,8},{8,12},{12,0},{1,5},{5,9},{9,13},{13,1},{2,6},{6,10},{... | collective-permute-start | bytes 196616 | tf_op jit(solution)/shard_map/ppermute | solution.py:20
  38.8 5.2 %copy-start.7 = (s32[128,6]{0,1:T(8,128)S(1)}, s32[128,6]{0,1:T(8,128)}, u32[]{:S(2)}) copy-start(s32[128,6]{0,1:T(8,128)} %param.19) | copy-start | bytes 9220
  38.8 5.2 %collective-permute-start.13 = (bf16[64,512]{1,0:T(8,128)(2,1)S(1)}, bf16[64,512]{1,0:T(8,128)(2,1)S(1)}, u32[]{:S(2)}, u32[]{:S(2)}) collective-permute-start(bf16[64,512]{1,0:T(8,128)(2,1)S(1)} %get-tuple-element.23.head_ref), channel_id=1, source_target_pairs={{0,12},{4,0},{8,4},{12,8},{1,13},{5,1},{9,5},{13,9},{2,14},{6,2},{... | collective-permute-start | bytes 196616 | tf_op jit(solution)/shard_map/ppermute | solution.py:20
  44.0 2.4 %collective-permute-start.16 = (bf16[768,512]{1,0:T(8,128)(2,1)S(1)}, bf16[768,512]{1,0:T(8,128)(2,1)}, u32[]{:S(2)}, u32[]{:S(2)}) collective-permute-start(bf16[768,512]{1,0:T(8,128)(2,1)S(1)} %collective-permute-done.15.refs_2_), channel_id=1, source_target_pairs={{0,1},{1,0},{2,3},{3,2},{4,5},{5,4},{6,7},{7,6},{8,9},{9,8},{10,11... | collective-permute-start | bytes 2359304 | tf_op jit(solution)/shard_map/ppermute | solution.py:20
  (1 other events, 0.9 us)

commit v12 on v11

--- a/solution.py
+++ b/solution.py
@@ -9,6 +9,7 @@
 
 MIB = 1 << 20
 VMEM = pl.BlockSpec(memory_space=pltpu.VMEM)
+HBM = pl.BlockSpec(memory_space=pltpu.HBM)
 
 
 def after(value, *earlier):
@@ -105,22 +106,44 @@
     return jnp.dot(a, b, preferred_element_type=jnp.float32)
 
 
-def encode_kernel(count, faces, mesh_rows, target_ref, lat_ref, *refs):
+def encode_kernel(count, faces, mesh_rows, route_ref, slot_ref, lat_hbm, *refs):
     in_pieces, hid_pieces = refs[:count], refs[count : 2 * count]
     outs = refs[2 * count : 2 * count + faces]
-    w_in, w_hid, messages = refs[2 * count + faces :]
+    w_in, w_hid, messages, lat_ref, sems = refs[2 * count + faces :]
     rows = w_in.shape[0] // count
-    place(in_pieces, 0, rows, w_in)
-    place(hid_pieces, 0, rows, w_hid)
     block = 256
-    for start in range(0, lat_ref.shape[0], block):
+    starts = range(0, lat_ref.shape[0], block)
+    copies = [
+        pltpu.make_async_copy(lat_hbm.at[pl.ds(at, block)], lat_ref.at[pl.ds(at, block)], sems.at[2 + at // block])
+        for at in starts
+    ]
+    own = pl.ds(pl.multiple_of(owner_of(0, 0) * rows, rows), rows)
+    own_copies = [
+        pltpu.make_async_copy(pieces[0], whole.at[own], sems.at[at])
+        for at, (pieces, whole) in enumerate([(in_pieces, w_in), (hid_pieces, w_hid)])
+    ]
+    for copy in own_copies + copies:
+        copy.start()
+    subs = lax.axis_size("sub")
+    for pieces, whole in ((in_pieces, w_in), (hid_pieces, w_hid)):
+        for index in range(1, count):
+            owner = owner_of(index // subs, index % subs)
+            whole[pl.ds(pl.multiple_of(owner * rows, rows), rows)] = pieces[index][...]
+    me = lax.axis_index("face")
+    routes = route_ref[...]
+    distance = lax.rem(routes - me + faces, faces) if faces & (faces - 1) else routes ^ me
+    targets = distance * mesh_rows + slot_ref[...]
+    for copy in own_copies:
+        copy.wait()
+    for copy, start in zip(copies, starts):
         here = pl.ds(start, block)
+        copy.wait()
         hidden = silu(dot(lat_ref[here], w_in[...])).astype(jnp.bfloat16)
         messages[here] = layer_norm(dot(hidden, w_hid[...])).astype(jnp.bfloat16)
     group = min(faces, 4)
     for at in range(0, faces, group):
         slots = lax.broadcasted_iota(jnp.int32, (group * mesh_rows, lat_ref.shape[0]), 0)
-        chosen = jnp.where(slots + at * mesh_rows == target_ref[...], 1.0, 0.0)
+        chosen = jnp.where(slots + at * mesh_rows == targets, 1.0, 0.0)
         chosen = chosen.astype(jnp.bfloat16)
         sums = dot(chosen, messages[...])
         for face in range(group):
@@ -248,29 +271,26 @@
     early_far = [shift(early_sent, "band", step) for step in range(1, bands)]
     early_near, late_near = own_spread(early), own_spread(late)
 
-    me = lax.axis_index("face")
-    routes = grid_route[:, 0]
     steps = distances(faces)
-    distance = lax.rem(routes - me + faces, faces) if faces & (faces - 1) else routes ^ me
-    targets = (distance * mesh_rows + grid_slot).reshape(1, grid_rows)
-
     block = (mesh_rows, width)
     sums = pl.pallas_call(
         functools.partial(encode_kernel, count, faces, mesh_rows),
         out_shape=[
             jax.ShapeDtypeStruct(block, bf16 if step else f32) for step in range(faces)
         ],
-        in_specs=[VMEM, VMEM] + [VMEM] * (2 * count),
+        in_specs=[VMEM] * 2 + ([HBM] + [HBM] + [VMEM] * (count - 1) + [HBM] + [VMEM] * (count - 1)),
         out_specs=[VMEM] * faces,
         scratch_shapes=[
             matrix(enc_w1),
             matrix(enc_w2),
             pltpu.VMEM((grid_rows, width), bf16),
+            pltpu.VMEM((grid_rows, width), bf16),
+            pltpu.SemaphoreType.DMA((2 + grid_rows // 256,)),
         ],
         compiler_params=pltpu.CompilerParams(vmem_limit_bytes=16 * MIB),
         cost_estimate=cost(grid_rows, 3 * width),
         name="encode",
-    )(targets, grid_lat, *enc_all[0], *enc_all[1])
+    )(grid_route.reshape(1, grid_rows), grid_slot.reshape(1, grid_rows), grid_lat, *enc_all[0], *enc_all[1])
     late_sent = after(late, sums[0])
     late_far = [shift(late_sent, "band", step) for step in range(1, bands)]
     arrived = [sums[0]] + [to_face(sums[step], step) for step in steps[1:]]

time: 50.3 us -> 51.6 us (1.026)
  other arithmetic: 1.38 us -> 0 us
  local copies, waits for them, and re-layouts: 3.16 us -> 4.54 us
  waiting for transfers between devices: 16.4 us -> 17.2 us
    pallas_call x1, Pallas kernels: 2.31 us -> 3.85 us  [shards(): pl.pallas_call(functools.partial(encode_kernel, count, faces, mesh_rows),...]
    unnamed x17 -> x21, local copies, waits for them, and re-layouts: 3.16 us -> 4.54 us
    pallas_call x1, Pallas kernels: 3.58 us -> 2.47 us  [shards(): pl.pallas_call(functools.partial(edge_kernel, sizes[1], missing), out_sha...]
    ppermute x14, waiting for transfers between devices: 6.64 us -> 7.53 us  [shift(): lax.ppermute(value, axis, [(i, (i + step) % count) for i in range(count)])]
    mul x1 -> x0, other arithmetic: 0.69 us -> none  [shards(): targets = (distance * mesh_rows + grid_slot).reshape(1, grid_rows)]
    add x1 -> x0, other arithmetic: 0.69 us -> none  [shards(): targets = (distance * mesh_rows + grid_slot).reshape(1, grid_rows)]
  transfers between devices with their start and end apart: 17 -> 17, of which waited for: 7 -> 9; matrix products, arithmetic and copies ran while one was open for 3% -> 0% of each run, Pallas kernels for 20% -> 22%
where the time goes in v12:
time: 51.6 us; the launch traced here: 51.3 us
  waiting for transfers between devices  17.2 us (33%)
  starting transfers between devices  15.1 us (29%)
  Pallas kernels  13.8 us (27%)
  local copies, waits for them, and re-layouts  4.54 us (9%)
  between operations  0.69 us (1%)
    ppermute x14, starting transfers between devices, shift(): lax.ppermute(value, axis, [(i, (i + step) % count) for i in range(count)])  10.6 us
    ppermute x3, waiting for transfers between devices, to_face(): lax.ppermute(value, 'face', [(i, face_at(faces, step, i)) for i in range(...  9.7 us
    ppermute x14, waiting for transfers between devices, shift(): lax.ppermute(value, axis, [(i, (i + step) % count) for i in range(count)])  7.53 us
    unnamed x21, local copies, waits for them, and re-layouts  4.54 us
    ppermute x3, starting transfers between devices, to_face(): lax.ppermute(value, 'face', [(i, face_at(faces, step, i)) for i in range(...  4.45 us
    pallas_call x1, Pallas kernels, shards(): pl.pallas_call(functools.partial(encode_kernel, count, faces, mesh_rows),...  3.85 us
    pallas_call x1, Pallas kernels, shards(): pl.pallas_call(functools.partial(grid_kernel, sizes[0]), out_shape=jax.Sh...  3.06 us
    pallas_call x1, Pallas kernels, pack(): pl.pallas_call(functools.partial(pack_kernel, [len(one) for one in sets])...  2.51 us
  transfers between devices with their start and end apart: 17, of which 9 were waited for; matrix products, arithmetic and copies ran while one was open for 0% of the time, Pallas kernels for 22%

profile of v12, /device:TPU:0, one launch (start us, length us, event | category | flops | bytes accessed | tf_op | source)
XLA Modules:
  0.0 51.3 jit_solution(7597398148127008984)
XLA Ops:
  0.6 3.0 %collective-permute-start.1 = (bf16[128,512]{1,0:T(8,128)(2,1)}, bf16[128,512]{1,0:T(8,128)(2,1)S(1)}, u32[]{:S(2)}, u32[]{:S(2)}) collective-permute-start(bf16[128,512]{1,0:T(8,128)(2,1)} %refs_0_.3), channel_id=1, source_target_pairs={{0,2},{2,0},{1,3},{3,1},{4,6},{6,4},{5,7},{7,5},{8,10},{10,8},{9,1... | collective-permute-start | bytes 393224 | tf_op jit(solution)/shard_map/ppermute | solution.py:21
  4.2 2.5 %pack.1 = (bf16[640,512]{1,0:T(8,128)(2,1)}, bf16[768,512]{1,0:T(8,128)(2,1)}) custom-call(bf16[256,512]{1,0:T(8,128)(2,1)} %refs_0_.2, bf16[128,512]{1,0:T(8,128)(2,1)} %refs_1_.1, bf16[128,512]{1,0:T(8,128)(2,1)} %refs_2_.1, bf16[128,512]{1,0:T(8,128)(2,1)} %refs_3_.1, bf16[256,512]{1,0:T(8,128)(2,1)} %refs_4_.2, bf16[128,512]{1,0:T(8,128)(2,1)} %refs_5_.1, ...), custom_call_target="tpu_custom_call" | custom-call | tf_op jit(solution)/shard_map/pack/pallas_call | solution.py:81
  6.7 1.4 %collective-permute-done.1.refs_2_ = bf16[128,512]{1,0:T(8,128)(2,1)S(1)} collective-permute-done((bf16[128,512]{1,0:T(8,128)(2,1)}, bf16[128,512]{1,0:T(8,128)(2,1)S(1)}, u32[]{:S(2)}, u32[]{:S(2)}) %collective-permute-start.1) | collective-permute-done | bytes 131104 | tf_op jit(solution)/shard_map/ppermute | solution.py:21
  8.2 2.0 %collective-permute-done.2.refs_6_ = bf16[128,512]{1,0:T(8,128)(2,1)S(1)} collective-permute-done((bf16[128,512]{1,0:T(8,128)(2,1)}, bf16[128,512]{1,0:T(8,128)(2,1)S(1)}, u32[]{:S(2)}, u32[]{:S(2)}) %collective-permute-start.2) | collective-permute-done | bytes 131104 | tf_op jit(solution)/shard_map/ppermute | solution.py:21
  10.2 1.7 %collective-permute-start.5 = (bf16[640,512]{1,0:T(8,128)(2,1)}, bf16[640,512]{1,0:T(8,128)(2,1)S(1)}, u32[]{:S(2)}, u32[]{:S(2)}) collective-permute-start(bf16[640,512]{1,0:T(8,128)(2,1)} %get-tuple-element.17.refs_0_.refs_4_), channel_id=1, source_target_pairs={{0,2},{2,0},{1,3},{3,1},{4,6},{6,4},{5,7},{7,5},{8,10},{10,8},{9,1... | collective-permute-start | bytes 1966088 | tf_op jit(solution)/shard_map/ppermute | solution.py:21
  12.4 0.8 %collective-permute-done.6.refs_3_ = bf16[128,512]{1,0:T(8,128)(2,1)S(1)} collective-permute-done((bf16[128,512]{1,0:T(8,128)(2,1)S(1)}, bf16[128,512]{1,0:T(8,128)(2,1)S(1)}, u32[]{:S(2)}, u32[]{:S(2)}) %collective-permute-start.6) | collective-permute-done | bytes 131104 | tf_op jit(solution)/shard_map/ppermute | solution.py:21
  13.4 1.2 %copy-done.1 = bf16[1024,512]{1,0:T(8,128)(2,1)S(1)} copy-done((bf16[1024,512]{1,0:T(8,128)(2,1)S(1)}, bf16[1024,512]{1,0:T(8,128)(2,1)}, u32[]{:S(2)}) %copy-start.1) | copy-done | bytes 1048600
  14.7 0.9 %copy-done.5 = bf16[128,512]{1,0:T(8,128)(2,1)S(1)} copy-done((bf16[128,512]{1,0:T(8,128)(2,1)S(1)}, bf16[128,512]{1,0:T(8,128)(2,1)}, u32[]{:S(2)}) %copy-start.5) | copy-done | bytes 131096
  15.6 0.9 %copy-done.6 = bf16[128,512]{1,0:T(8,128)(2,1)S(1)} copy-done((bf16[128,512]{1,0:T(8,128)(2,1)S(1)}, bf16[128,512]{1,0:T(8,128)(2,1)}, u32[]{:S(2)}) %copy-start.6) | copy-done | bytes 131096
  16.5 0.7 %copy-done.7 = s32[1024,1]{0,1:T(1,128)S(1)} copy-done((s32[1024,1]{0,1:T(1,128)S(1)}, s32[1024,1]{0,1:T(1,128)}, u32[]{:S(2)}) %copy-start.7) | copy-done | bytes 4120
  17.2 0.7 %copy-done.8 = s32[1024]{0:T(1024)S(1)} copy-done((s32[1024]{0:T(1024)S(1)}, s32[1024]{0:T(1024)}, u32[]{:S(2)}) %copy-start.8) | copy-done | bytes 4120
  17.9 3.9 %encode.1 = (f32[128,512]{1,0:T(8,128)S(1)}, bf16[128,512]{1,0:T(8,128)(2,1)S(1)}, bf16[128,512]{1,0:T(8,128)(2,1)S(1)}, bf16[128,512]{1,0:T(8,128)(2,1)S(1)}) custom-call(s32[1,1024]{1,0:T(1,128)S(1)} %bitcast.2, s32[1,1024]{1,0:T(1,128)S(1)} %bitcast.3, bf16[1024,512]{1,0:T(8,128)(2,1)S(1)} %copy-done.1, bf16[128,512]{1,0:T(8,128)(2,1)S(1)} %copy-done.5, ...), custom_call_target="tpu_custom_call" | custom-call | flops 1610612736 | bytes 2621440 | tf_op jit(solution)/shard_map/encode/pallas_call | solution.py:276
  21.7 1.6 %collective-permute-start.10 = (bf16[128,512]{1,0:T(8,128)(2,1)S(1)}, bf16[128,512]{1,0:T(8,128)(2,1)S(1)}, u32[]{:S(2)}, u32[]{:S(2)}) collective-permute-start(bf16[128,512]{1,0:T(8,128)(2,1)S(1)} %get-tuple-element.20), channel_id=1, source_target_pairs={{0,4},{4,0},{8,12},{12,8},{1,5},{5,1},{9,13},{13,9},{2,6},{6,2},{1... | collective-permute-start | bytes 393224 | tf_op jit(solution)/shard_map/ppermute | solution.py:36
  23.4 2.6 %collective-permute-start.8 = (bf16[128,512]{1,0:T(8,128)(2,1)S(1)}, bf16[128,512]{1,0:T(8,128)(2,1)S(1)}, u32[]{:S(2)}, u32[]{:S(2)}) collective-permute-start(bf16[128,512]{1,0:T(8,128)(2,1)S(1)} %get-tuple-element.18), channel_id=1, source_target_pairs={{0,8},{4,12},{8,0},{12,4},{1,9},{5,13},{9,1},{13,5},{2,10},{6,14},... | collective-permute-start | bytes 393224 | tf_op jit(solution)/shard_map/ppermute | solution.py:36
  26.6 3.0 %collective-permute-done.10.refs_3_ = bf16[128,512]{1,0:T(8,128)(2,1)S(1)} collective-permute-done((bf16[128,512]{1,0:T(8,128)(2,1)S(1)}, bf16[128,512]{1,0:T(8,128)(2,1)S(1)}, u32[]{:S(2)}, u32[]{:S(2)}) %collective-permute-start.10) | collective-permute-done | bytes 131104 | tf_op jit(solution)/shard_map/ppermute | solution.py:36
  29.6 6.7 %collective-permute-done.8.refs_1_ = bf16[128,512]{1,0:T(8,128)(2,1)S(1)} collective-permute-done((bf16[128,512]{1,0:T(8,128)(2,1)S(1)}, bf16[128,512]{1,0:T(8,128)(2,1)S(1)}, u32[]{:S(2)}, u32[]{:S(2)}) %collective-permute-start.8) | collective-permute-done | bytes 131104 | tf_op jit(solution)/shard_map/ppermute | solution.py:36
  36.8 1.6 %collective-permute-done.11.refs_3_.refs_7_ = bf16[640,512]{1,0:T(8,128)(2,1)S(1)} collective-permute-done((bf16[640,512]{1,0:T(8,128)(2,1)S(1)}, bf16[640,512]{1,0:T(8,128)(2,1)S(1)}, u32[]{:S(2)}, u32[]{:S(2)}) %collective-permute-start.11) | collective-permute-done | bytes 655392 | tf_op jit(solution)/shard_map/ppermute | solution.py:21
  38.4 0.8 %node_update.1 = (bf16[64,512]{1,0:T(8,128)(2,1)S(1)}, bf16[64,512]{1,0:T(8,128)(2,1)S(1)}) custom-call(bf16[128,512]{1,0:T(8,128)(2,1)S(1)} %copy-done.4, f32[128,512]{1,0:T(8,128)S(1)} %get-tuple-element.22.refs_0_, bf16[128,512]{1,0:T(8,128)(2,1)S(1)} %collective-permute-done.8.refs_1_, bf16[128,512]{1,0:T(8,128)(2,1)S(1)} %collective-permute-done.9.refs_2_, ...), custom_call_target="tpu_custom_call" | custom-call | flops 201326592 | bytes 1703936 | tf_op jit(solution)/shard_map/node_update/pallas_call | solution.py:311
  39.2 2.5 %collective-permute-start.12 = (bf16[64,512]{1,0:T(8,128)(2,1)S(1)}, bf16[64,512]{1,0:T(8,128)(2,1)S(1)}, u32[]{:S(2)}, u32[]{:S(2)}) collective-permute-start(bf16[64,512]{1,0:T(8,128)(2,1)S(1)} %get-tuple-element.24.tail_ref), channel_id=1, source_target_pairs={{0,4},{4,8},{8,12},{12,0},{1,5},{5,9},{9,13},{13,1},{2,6},{6,10},{... | collective-permute-start | bytes 196616 | tf_op jit(solution)/shard_map/ppermute | solution.py:21
  41.7 1.4 %collective-permute-start.13 = (bf16[64,512]{1,0:T(8,128)(2,1)S(1)}, bf16[64,512]{1,0:T(8,128)(2,1)S(1)}, u32[]{:S(2)}, u32[]{:S(2)}) collective-permute-start(bf16[64,512]{1,0:T(8,128)(2,1)S(1)} %get-tuple-element.23.head_ref), channel_id=1, source_target_pairs={{0,12},{4,0},{8,4},{12,8},{1,13},{5,1},{9,5},{13,9},{2,14},{6,2},{... | collective-permute-start | bytes 196616 | tf_op jit(solution)/shard_map/ppermute | solution.py:21
  43.1 3.1 %grid_update.1 = bf16[1024,512]{1,0:T(8,128)(2,1)} custom-call(bf16[1024,512]{1,0:T(8,128)(2,1)S(1)} %copy-done.2, bf16[640,512]{1,0:T(8,128)(2,1)S(1)} %copy-done, bf16[640,512]{1,0:T(8,128)(2,1)S(1)} %collective-permute-done.refs_1_.refs_5_, bf16[640,512]{1,0:T(8,128)(2,1)S(1)} %collective-permute-done.5.refs_2_.refs_6_, ...), custom_call_target="tpu_custom_call" | custom-call | flops 1073741824 | bytes 2097152 | tf_op jit(solution)/shard_map/grid_update/pallas_call | solution.py:299
  46.7 1.1 %prepare.1 = (bf16[768,1024]{1,0:T(8,128)(2,1)S(1)}, f32[768,512]{1,0:T(8,128)S(1)}) custom-call(s32[128,6]{1,0:T(8,128)S(1)} %copy.17.nbr_ref, bf16[64,512]{1,0:T(8,128)(2,1)S(1)} %collective-permute-done.12.before_ref, bf16[64,512]{1,0:T(8,128)(2,1)S(1)} %get-tuple-element.23.head_ref, bf16[64,512]{1,0:T(8,128)(2,1)S(1)} %get-tuple-element.24.tail_ref, ...), custom_call_target="tpu_custom_call" | custom-call | flops 805306368 | bytes 1835008 | tf_op jit(solution)/shard_map/prepare/pallas_call | solution.py:328
  47.8 1.1 %collective-permute-done.16.refs_3_ = bf16[768,512]{1,0:T(8,128)(2,1)S(1)} collective-permute-done((bf16[768,512]{1,0:T(8,128)(2,1)S(1)}, bf16[768,512]{1,0:T(8,128)(2,1)S(1)}, u32[]{:S(2)}, u32[]{:S(2)}) %collective-permute-start.16) | collective-permute-done | bytes 786464 | tf_op jit(solution)/shard_map/ppermute | solution.py:21
  48.9 2.5 %edge_update.1 = bf16[128,512]{1,0:T(8,128)(2,1)} custom-call(bf16[64,512]{1,0:T(8,128)(2,1)S(1)} %get-tuple-element.23.head_ref, bf16[64,512]{1,0:T(8,128)(2,1)S(1)} %get-tuple-element.24.tail_ref, bf16[768,1024]{1,0:T(8,128)(2,1)S(1)} %get-tuple-element.28.inputs_ref, f32[768,512]{1,0:T(8,128)S(1)} %get-tuple-element.29.hidden_ref, ...), custom_call_target="tpu_custom_call" | custom-call | flops 805306368 | bytes 1835008 | tf_op jit(solution)/shard_map/edge_update/pallas_call | solution.py:340
  (37 shorter events, 3.0 us)
Async XLA Ops:
  0.6 7.5 %collective-permute-start.1 = (bf16[128,512]{1,0:T(8,128)(2,1)}, bf16[128,512]{1,0:T(8,128)(2,1)S(1)}, u32[]{:S(2)}, u32[]{:S(2)}) collective-permute-start(bf16[128,512]{1,0:T(8,128)(2,1)} %refs_0_.3), channel_id=1, source_target_pairs={{0,2},{2,0},{1,3},{3,1},{4,6},{6,4},{5,7},{7,5},{8,10},{10,8},{9,1... | collective-permute-start | bytes 393224 | tf_op jit(solution)/shard_map/ppermute | solution.py:21
  3.6 6.5 %collective-permute-start.2 = (bf16[128,512]{1,0:T(8,128)(2,1)}, bf16[128,512]{1,0:T(8,128)(2,1)S(1)}, u32[]{:S(2)}, u32[]{:S(2)}) collective-permute-start(bf16[128,512]{1,0:T(8,128)(2,1)} %refs_4_.3), channel_id=1, source_target_pairs={{0,2},{2,0},{1,3},{3,1},{4,6},{6,4},{5,7},{7,5},{8,10},{10,8},{9,1... | collective-permute-start | bytes 393224 | tf_op jit(solution)/shard_map/ppermute | solution.py:21
  3.7 6.4 %collective-permute-start.3 = (bf16[128,512]{1,0:T(8,128)(2,1)}, bf16[128,512]{1,0:T(8,128)(2,1)S(1)}, u32[]{:S(2)}, u32[]{:S(2)}) collective-permute-start(bf16[128,512]{1,0:T(8,128)(2,1)} %refs_0_.3), channel_id=1, source_target_pairs={{0,1},{1,0},{2,3},{3,2},{4,5},{5,4},{6,7},{7,6},{8,9},{9,8},{10,11... | collective-permute-start | bytes 393224 | tf_op jit(solution)/shard_map/ppermute | solution.py:21
  3.7 6.4 %collective-permute-start.4 = (bf16[128,512]{1,0:T(8,128)(2,1)}, bf16[128,512]{1,0:T(8,128)(2,1)S(1)}, u32[]{:S(2)}, u32[]{:S(2)}) collective-permute-start(bf16[128,512]{1,0:T(8,128)(2,1)} %refs_4_.3), channel_id=1, source_target_pairs={{0,1},{1,0},{2,3},{3,2},{4,5},{5,4},{6,7},{7,6},{8,9},{9,8},{10,11... | collective-permute-start | bytes 393224 | tf_op jit(solution)/shard_map/ppermute | solution.py:21
  10.2 26.1 %collective-permute-start.5 = (bf16[640,512]{1,0:T(8,128)(2,1)}, bf16[640,512]{1,0:T(8,128)(2,1)S(1)}, u32[]{:S(2)}, u32[]{:S(2)}) collective-permute-start(bf16[640,512]{1,0:T(8,128)(2,1)} %get-tuple-element.17.refs_0_.refs_4_), channel_id=1, source_target_pairs={{0,2},{2,0},{1,3},{3,1},{4,6},{6,4},{5,7},{7,5},{8,10},{10,8},{9,1... | collective-permute-start | bytes 1966088 | tf_op jit(solution)/shard_map/ppermute | solution.py:21
  11.9 1.3 %collective-permute-start.6 = (bf16[128,512]{1,0:T(8,128)(2,1)S(1)}, bf16[128,512]{1,0:T(8,128)(2,1)S(1)}, u32[]{:S(2)}, u32[]{:S(2)}) collective-permute-start(bf16[128,512]{1,0:T(8,128)(2,1)S(1)} %collective-permute-done.1.refs_2_), channel_id=1, source_target_pairs={{0,1},{1,0},{2,3},{3,2},{4,5},{5,4},{6,7},{7,6},{8,9},{9,8},{10,11... | collective-permute-start | bytes 393224 | tf_op jit(solution)/shard_map/ppermute | solution.py:21
  11.9 1.5 %collective-permute-start.7 = (bf16[128,512]{1,0:T(8,128)(2,1)S(1)}, bf16[128,512]{1,0:T(8,128)(2,1)S(1)}, u32[]{:S(2)}, u32[]{:S(2)}) collective-permute-start(bf16[128,512]{1,0:T(8,128)(2,1)S(1)} %collective-permute-done.2.refs_6_), channel_id=1, source_target_pairs={{0,1},{1,0},{2,3},{3,2},{4,5},{5,4},{6,7},{7,6},{8,9},{9,8},{10,11... | collective-permute-start | bytes 393224 | tf_op jit(solution)/shard_map/ppermute | solution.py:21
  13.4 1.2 %copy-start.1 = (bf16[1024,512]{1,0:T(8,128)(2,1)S(1)}, bf16[1024,512]{1,0:T(8,128)(2,1)}, u32[]{:S(2)}) copy-start(bf16[1024,512]{1,0:T(8,128)(2,1)} %lat_ref.2) | copy-start | bytes 3145732
  15.6 0.9 %copy-start.6 = (bf16[128,512]{1,0:T(8,128)(2,1)S(1)}, bf16[128,512]{1,0:T(8,128)(2,1)}, u32[]{:S(2)}) copy-start(bf16[128,512]{1,0:T(8,128)(2,1)} %refs_4_.3) | copy-start | bytes 393220
  17.8 8.3 %copy-start.3 = (bf16[768,512]{1,0:T(8,128)(2,1)S(1)}, bf16[768,512]{1,0:T(8,128)(2,1)}, u32[]{:S(2)}) copy-start(bf16[768,512]{1,0:T(8,128)(2,1)} %get-tuple-element.26.refs_0_) | copy-start | bytes 2359300
  17.9 11.7 %copy-start = (bf16[640,512]{1,0:T(8,128)(2,1)S(1)}, bf16[640,512]{1,0:T(8,128)(2,1)}, u32[]{:S(2)}) copy-start(bf16[640,512]{1,0:T(8,128)(2,1)} %get-tuple-element.17.refs_0_.refs_4_) | copy-start | bytes 1966084
  17.9 20.5 %copy-start.4 = (bf16[128,512]{1,0:T(8,128)(2,1)S(1)}, bf16[128,512]{1,0:T(8,128)(2,1)}, u32[]{:S(2)}) copy-start(bf16[128,512]{1,0:T(8,128)(2,1)} %lat_ref.3) | copy-start | bytes 393220
  21.7 7.9 %collective-permute-start.10 = (bf16[128,512]{1,0:T(8,128)(2,1)S(1)}, bf16[128,512]{1,0:T(8,128)(2,1)S(1)}, u32[]{:S(2)}, u32[]{:S(2)}) collective-permute-start(bf16[128,512]{1,0:T(8,128)(2,1)S(1)} %get-tuple-element.20), channel_id=1, source_target_pairs={{0,4},{4,0},{8,12},{12,8},{1,5},{5,1},{9,13},{13,9},{2,6},{6,2},{1... | collective-permute-start | bytes 393224 | tf_op jit(solution)/shard_map/ppermute | solution.py:36
  23.4 12.9 %collective-permute-start.8 = (bf16[128,512]{1,0:T(8,128)(2,1)S(1)}, bf16[128,512]{1,0:T(8,128)(2,1)S(1)}, u32[]{:S(2)}, u32[]{:S(2)}) collective-permute-start(bf16[128,512]{1,0:T(8,128)(2,1)S(1)} %get-tuple-element.18), channel_id=1, source_target_pairs={{0,8},{4,12},{8,0},{12,4},{1,9},{5,13},{9,1},{13,5},{2,10},{6,14},... | collective-permute-start | bytes 393224 | tf_op jit(solution)/shard_map/ppermute | solution.py:36
  25.9 10.3 %collective-permute-start.9 = (bf16[128,512]{1,0:T(8,128)(2,1)S(1)}, bf16[128,512]{1,0:T(8,128)(2,1)S(1)}, u32[]{:S(2)}, u32[]{:S(2)}) collective-permute-start(bf16[128,512]{1,0:T(8,128)(2,1)S(1)} %get-tuple-element.19), channel_id=1, source_target_pairs={{0,12},{4,8},{8,4},{12,0},{1,13},{5,9},{9,5},{13,1},{2,14},{6,10},... | collective-permute-start | bytes 393224 | tf_op jit(solution)/shard_map/ppermute | solution.py:36
  26.2 16.9 %copy-start.2 = (bf16[1024,512]{1,0:T(8,128)(2,1)S(1)}, bf16[1024,512]{1,0:T(8,128)(2,1)}, u32[]{:S(2)}) copy-start(bf16[1024,512]{1,0:T(8,128)(2,1)} %lat_ref.2) | copy-start | bytes 3145732
  26.2 20.0 %collective-permute-start.15 = (bf16[768,512]{1,0:T(8,128)(2,1)S(1)}, bf16[768,512]{1,0:T(8,128)(2,1)S(1)}, u32[]{:S(2)}, u32[]{:S(2)}) collective-permute-start(bf16[768,512]{1,0:T(8,128)(2,1)S(1)} %copy-done.3), channel_id=1, source_target_pairs={{0,2},{2,0},{1,3},{3,1},{4,6},{6,4},{5,7},{7,5},{8,10},{10,8},{9,1... | collective-permute-start | bytes 2359304 | tf_op jit(solution)/shard_map/ppermute | solution.py:21
  29.6 7.2 %collective-permute-start = (bf16[640,512]{1,0:T(8,128)(2,1)S(1)}, bf16[640,512]{1,0:T(8,128)(2,1)S(1)}, u32[]{:S(2)}, u32[]{:S(2)}) collective-permute-start(bf16[640,512]{1,0:T(8,128)(2,1)S(1)} %copy-done), channel_id=1, source_target_pairs={{0,1},{1,0},{2,3},{3,2},{4,5},{5,4},{6,7},{7,6},{8,9},{9,8},{10,11... | collective-permute-start | bytes 1966088 | tf_op jit(solution)/shard_map/ppermute | solution.py:21
  36.3 2.1 %collective-permute-start.11 = (bf16[640,512]{1,0:T(8,128)(2,1)S(1)}, bf16[640,512]{1,0:T(8,128)(2,1)S(1)}, u32[]{:S(2)}, u32[]{:S(2)}) collective-permute-start(bf16[640,512]{1,0:T(8,128)(2,1)S(1)} %collective-permute-done.5.refs_2_.refs_6_), channel_id=1, source_target_pairs={{0,1},{1,0},{2,3},{3,2},{4,5},{5,4},{6,7},{7,6},{8,9},{9,8},{10,11... | collective-permute-start | bytes 1966088 | tf_op jit(solution)/shard_map/ppermute | solution.py:21
  36.3 10.4 %collective-permute-start.14 = (bf16[768,512]{1,0:T(8,128)(2,1)S(1)}, bf16[768,512]{1,0:T(8,128)(2,1)S(1)}, u32[]{:S(2)}, u32[]{:S(2)}) collective-permute-start(bf16[768,512]{1,0:T(8,128)(2,1)S(1)} %copy-done.3), channel_id=1, source_target_pairs={{0,1},{1,0},{2,3},{3,2},{4,5},{5,4},{6,7},{7,6},{8,9},{9,8},{10,11... | collective-permute-start | bytes 2359304 | tf_op jit(solution)/shard_map/ppermute | solution.py:21
  39.2 6.9 %collective-permute-start.12 = (bf16[64,512]{1,0:T(8,128)(2,1)S(1)}, bf16[64,512]{1,0:T(8,128)(2,1)S(1)}, u32[]{:S(2)}, u32[]{:S(2)}) collective-permute-start(bf16[64,512]{1,0:T(8,128)(2,1)S(1)} %get-tuple-element.24.tail_ref), channel_id=1, source_target_pairs={{0,4},{4,8},{8,12},{12,0},{1,5},{5,9},{9,13},{13,1},{2,6},{6,10},{... | collective-permute-start | bytes 196616 | tf_op jit(solution)/shard_map/ppermute | solution.py:21
  41.7 4.9 %copy-start.9 = (s32[128,6]{0,1:T(8,128)S(1)}, s32[128,6]{0,1:T(8,128)}, u32[]{:S(2)}) copy-start(s32[128,6]{0,1:T(8,128)} %param.19) | copy-start | bytes 9220
  41.7 4.9 %collective-permute-start.13 = (bf16[64,512]{1,0:T(8,128)(2,1)S(1)}, bf16[64,512]{1,0:T(8,128)(2,1)S(1)}, u32[]{:S(2)}, u32[]{:S(2)}) collective-permute-start(bf16[64,512]{1,0:T(8,128)(2,1)S(1)} %get-tuple-element.23.head_ref), channel_id=1, source_target_pairs={{0,12},{4,0},{8,4},{12,8},{1,13},{5,1},{9,5},{13,9},{2,14},{6,2},{... | collective-permute-start | bytes 196616 | tf_op jit(solution)/shard_map/ppermute | solution.py:21
  46.6 2.3 %collective-permute-start.16 = (bf16[768,512]{1,0:T(8,128)(2,1)S(1)}, bf16[768,512]{1,0:T(8,128)(2,1)S(1)}, u32[]{:S(2)}, u32[]{:S(2)}) collective-permute-start(bf16[768,512]{1,0:T(8,128)(2,1)S(1)} %collective-permute-done.15.refs_2_), channel_id=1, source_target_pairs={{0,1},{1,0},{2,3},{3,2},{4,5},{5,4},{6,7},{7,6},{8,9},{9,8},{10,11... | collective-permute-start | bytes 2359304 | tf_op jit(solution)/shard_map/ppermute | solution.py:21
  (3 other events, 2.3 us)
